TPU v7x, 32 devices: a whole 2x2x4 slice. The times are simulated.
32 devices in a mesh: groups: 2 (over x), row: 16 (over z, y, core).
Axes of the slice: x: 2, y: 2, z: 4, core: 2. Of those that a mesh axis runs over, the one named last changes fastest.
Arguments:
- basis: float32 [32768, 512], P(('groups', 'row')), parts along dimension 0, may hold values from -0.0625 to 0.0625
- weights: bfloat16 [32, 2048, 4096], P(('groups', 'row')), parts along dimension 0, may hold values from -6 to 6
Outputs:
- rotated: bfloat16 [1024, 8192], P(('groups', 'row')), parts along dimension 0
There are 2 independent parts, one for each index of `groups`. A program takes and returns all parts, laid end to end along the dimension named above; each array names one. Nothing has to cross between parts.
All inputs are finite; a program needn't handle non-finite values.
Results may differ from a plain program's by a relative error of at most 0.001.
Values may be sent and summed in bfloat16 or wider, within the bound.
No kernel may reach another device: no remote copies, remote signals or barrier semaphores. Data moves between devices by JAX's collectives and lax.ppermute only.
A program may use at most 128 MiB of HBM per device.

v0:
```python
import jax
import jax.numpy as jnp
import numpy as np
from jax import lax
from jax.sharding import PartitionSpec as P


def swapped(block, axis, apart):
    count = lax.axis_size(axis)
    route = []
    for low in range(count):
        high = low | 1 << apart
        if high != low and high < count:
            route += [(low, high), (high, low)]
    return lax.ppermute(block, axis, route)


def slot_order(blocks, column_index):
    slot_count = blocks.shape[0]
    order = jnp.bitwise_xor(column_index, jnp.arange(slot_count, dtype=jnp.int32))
    return jnp.take(blocks, order, axis=0)


def cube_exchange(blocks, low_bits, swap_fn):
    slot_count = blocks.shape[0]
    for bit_no in range(low_bits):
        chosen = np.array(
            [position for position in range(slot_count) if position >> bit_no & 1], dtype=np.int32
        )
        arrived = swap_fn(blocks[chosen], bit_no)
        blocks = blocks.at[chosen].set(arrived)
    return blocks


def contract_rows(left, right):
    return lax.dot_general(
        left,
        right,
        (((0,), (0,)), ((), ())),
        precision=lax.Precision.HIGHEST,
        preferred_element_type=jnp.float32,
    )


def on_device(basis, weights):
    axis_len = lax.axis_size("row")
    col_blocks = axis_len // 8
    low_bits = col_blocks.bit_length() - 1
    my_index = lax.axis_index("row")
    my_column = jnp.bitwise_and(my_index, col_blocks - 1)
    block = weights[0]
    own_count = block.shape[0] // col_blocks
    pieces = slot_order(block.reshape(col_blocks, own_count, block.shape[1]), my_column)

    def swap_slab(sent, bit_no):
        return swapped(sent, "row", bit_no)

    pieces = slot_order(cube_exchange(pieces, low_bits, swap_slab), my_column)
    wide_slab = jnp.transpose(pieces, (1, 0, 2)).reshape(own_count, -1).astype(jnp.float32)
    summed = lax.psum_scatter(
        contract_rows(basis, wide_slab), "row", scatter_dimension=0, tiled=True
    )
    return summed.astype(jnp.bfloat16)


def solution(mesh):
    in_specs = (P(("groups", "row"), None), P(("groups", "row"), None, None))
    out_specs = P(("groups", "row"), None)
    return jax.shard_map(
        on_device, mesh=mesh, in_specs=in_specs, out_specs=out_specs, check_vma=False
    )
```

profile of v0, /device:TPU:0, one launch (start us, length us, event | category | flops | bytes accessed | tf_op | source)
XLA Modules:
  0.0 402.1 jit_solution(15594523570893838887)
XLA Ops:
  6.5 0.0 copy-start
  6.5 0.0 reduce-scatter.4.cloned.1.call-start
  6.6 3.2 mini-gather-slice.29
  9.8 10.9 %fusion.1 = (bf16[2,1024,896]{2,1,0:T(8,128)(2,1)}, bf16[2,1024,896]{2,1,0:T(8,128)(2,1)}, bf16[2,1024,896]{2,1,0:T(8,128)(2,1)}, bf16[2,1024,896]{2,1,0:T(8,128)(2,1)}) fusion(bf16[2,1024,4096]{2,1,0:T(8,128)(2,1)} %bitcast.10), kind=kLoop, calls=%fused_computation.28 | loop fusion | bytes 29360128 | tf_op jit(solution)/shard_map/jit(_take)/gather | solution.py:21
  20.7 3.6 gather_fusion.4
  24.3 4.8 %gather_fusion.3 = bf16[2,1024,896]{2,1,0:T(8,128)(2,1)} fusion(bf16[2,1024,896]{2,1,0:T(8,128)(2,1)} %get-tuple-element.33, s32[1024]{0:T(1024)S(1)} %pad_clamp_fusion), kind=kCustom, calls=%fused_computation.3.clone | custom fusion | bytes 7340040 | tf_op jit(solution)/shard_map/jit(_take)/gather | solution.py:21
  29.1 4.8 %gather_fusion.2 = bf16[2,1024,896]{2,1,0:T(8,128)(2,1)} fusion(bf16[2,1024,896]{2,1,0:T(8,128)(2,1)} %get-tuple-element.34, s32[1024]{0:T(1024)S(1)} %pad_clamp_fusion), kind=kCustom, calls=%fused_computation.2.clone | custom fusion | bytes 7340040 | tf_op jit(solution)/shard_map/jit(_take)/gather | solution.py:21
  33.9 4.9 %gather_fusion.1 = bf16[2,1024,896]{2,1,0:T(8,128)(2,1)} fusion(bf16[2,1024,896]{2,1,0:T(8,128)(2,1)} %get-tuple-element.35, s32[1024]{0:T(1024)S(1)} %pad_clamp_fusion), kind=kCustom, calls=%fused_computation.1.clone | custom fusion | bytes 7340040 | tf_op jit(solution)/shard_map/jit(_take)/gather | solution.py:21
  38.8 4.9 %gather_fusion = bf16[2,1024,896]{2,1,0:T(8,128)(2,1)} fusion(bf16[2,1024,896]{2,1,0:T(8,128)(2,1)} %get-tuple-element.36, s32[1024]{0:T(1024)S(1)} %pad_clamp_fusion), kind=kCustom, calls=%fused_computation.clone | custom fusion | bytes 7340040 | tf_op jit(solution)/shard_map/jit(_take)/gather | solution.py:21
  43.7 0.0 copy-start.6
  43.7 2.8 constant_dynamic-update-slice_fusion.4
  46.5 0.4 copy-done.6
  46.8 0.0 copy-start.4
  46.8 0.6 constant_dynamic-update-slice_fusion.3
  47.5 1.4 copy-done.4
  48.9 0.0 copy-start.2
  48.9 0.6 constant_dynamic-update-slice_fusion.2
  49.5 1.4 copy-done.2
  50.9 0.0 copy-start.7
  50.9 0.6 constant_dynamic-update-slice_fusion.1
  51.6 0.9 copy-done.7
  52.5 0.3 constant_dynamic-update-slice_fusion
  52.8 7.0 %broadcast_select_fusion = bf16[2,1024,4096]{2,1,0:T(8,128)(2,1)} fusion(bf16[2,1024,4096]{2,1,0:T(8,128)(2,1)S(1)} %constant_dynamic-update-slice_fusion, pred[2]{0:T(512)(128)(4,1)S(1)} %compare_and_fusion), kind=kLoop, calls=%fused_computation.11 | loop fusion | flops 8388608 | bytes 33554432 | tf_op jit(solution)/shard_map/jit(_take)/select_n | solution.py:21
  59.8 7.7 %slice.50 = bf16[1,1024,4096]{2,1,0:T(8,128)(2,1)} slice(bf16[2,1024,4096]{2,1,0:T(8,128)(2,1)} %broadcast_select_fusion), slice={[1:2], [0:1024], [0:4096]} | slice | bytes 16777216 | tf_op jit(solution)/shard_map/gather | solution.py:30
  67.5 0.5 collective-permute-start
  68.0 13.1 %collective-permute-done = bf16[1,1024,4096]{2,1,0:T(8,128)(2,1)} collective-permute-done((bf16[1,1024,4096]{2,1,0:T(8,128)(2,1)}, bf16[1,1024,4096]{2,1,0:T(8,128)(2,1)}, u32[]{:S(2)}, u32[]{:S(2)}) %collective-permute-start) | collective-permute-done | bytes 8388640 | tf_op jit(solution)/shard_map/ppermute | solution.py:15
  81.1 7.7 %constant_dynamic-update-slice_fusion.10 = bf16[2,1024,4096]{2,1,0:T(8,128)(2,1)} fusion(bf16[2,1024,4096]{2,1,0:T(8,128)(2,1)} %broadcast_select_fusion, bf16[1,1024,4096]{2,1,0:T(8,128)(2,1)} %collective-permute-done), kind=kLoop, calls=%fused_computation.26 | loop fusion | bytes 16777216 | tf_op jit(solution)/shard_map/scatter | solution.py:31
  88.8 3.0 mini-gather-slice.34
  91.8 10.8 %fusion = (bf16[2,1024,896]{2,1,0:T(8,128)(2,1)}, bf16[2,1024,896]{2,1,0:T(8,128)(2,1)}, bf16[2,1024,896]{2,1,0:T(8,128)(2,1)}, bf16[2,1024,896]{2,1,0:T(8,128)(2,1)}) fusion(bf16[2,1024,4096]{2,1,0:T(8,128)(2,1)} %constant_dynamic-update-slice_fusion.10), kind=kLoop, calls=%fused_computation.27 | loop fusion | bytes 29360128 | tf_op jit(solution)/shard_map/jit(_take)/gather | solution.py:21
  102.6 4.8 %gather_fusion.8 = bf16[2,1024,896]{2,1,0:T(8,128)(2,1)} fusion(bf16[2,1024,896]{2,1,0:T(8,128)(2,1)} %get-tuple-element.29, s32[1024]{0:T(1024)S(1)} %pad_clamp_fusion), kind=kCustom, calls=%fused_computation.8.clone | custom fusion | bytes 7340040 | tf_op jit(solution)/shard_map/jit(_take)/gather | solution.py:21
  107.4 3.6 gather_fusion.9
  111.0 4.8 %gather_fusion.7 = bf16[2,1024,896]{2,1,0:T(8,128)(2,1)} fusion(bf16[2,1024,896]{2,1,0:T(8,128)(2,1)} %get-tuple-element.30, s32[1024]{0:T(1024)S(1)} %pad_clamp_fusion), kind=kCustom, calls=%fused_computation.7.clone | custom fusion | bytes 7340040 | tf_op jit(solution)/shard_map/jit(_take)/gather | solution.py:21
  115.9 4.9 %gather_fusion.6 = bf16[2,1024,896]{2,1,0:T(8,128)(2,1)} fusion(bf16[2,1024,896]{2,1,0:T(8,128)(2,1)} %get-tuple-element.31, s32[1024]{0:T(1024)S(1)} %pad_clamp_fusion), kind=kCustom, calls=%fused_computation.6.clone | custom fusion | bytes 7340040 | tf_op jit(solution)/shard_map/jit(_take)/gather | solution.py:21
  120.8 4.9 %gather_fusion.5 = bf16[2,1024,896]{2,1,0:T(8,128)(2,1)} fusion(bf16[2,1024,896]{2,1,0:T(8,128)(2,1)} %get-tuple-element.32, s32[1024]{0:T(1024)S(1)} %pad_clamp_fusion), kind=kCustom, calls=%fused_computation.5.clone | custom fusion | bytes 7340040 | tf_op jit(solution)/shard_map/jit(_take)/gather | solution.py:21
  125.7 0.0 copy-start.5
  125.7 2.8 constant_dynamic-update-slice_fusion.9
  128.5 0.4 copy-done.5
  128.8 0.0 copy-start.3
  128.8 0.6 constant_dynamic-update-slice_fusion.8
  129.5 1.4 copy-done.3
  130.9 0.0 copy-start.1
  130.9 0.6 constant_dynamic-update-slice_fusion.7
  131.5 1.4 copy-done.1
  132.9 0.0 copy-start.8
  132.9 0.6 constant_dynamic-update-slice_fusion.6
  133.5 0.9 copy-done.8
  134.5 0.3 constant_dynamic-update-slice_fusion.5
  134.8 7.1 %select_bitcast_fusion = bf16[1024,2,4096]{2,0,1:T(8,128)(2,1)} fusion(bf16[2,1024,4096]{2,1,0:T(8,128)(2,1)S(1)} %constant_dynamic-update-slice_fusion.5, pred[2]{0:T(512)(128)(4,1)S(1)} %compare_and_fusion), kind=kLoop, calls=%fused_computation.10 | loop fusion | flops 8388608 | bytes 33554432 | tf_op jit(solution)/shard_map/transpose | solution.py:59
  142.0 21.2 %copy.12 = bf16[1024,2,4096]{0,2,1:T(8,128)(2,1)} copy(bf16[1024,2,4096]{2,0,1:T(8,128)(2,1)} %select_bitcast_fusion) | data formatting | bytes 33554432 | tf_op jit(solution)/shard_map/transpose | solution.py:59
  163.2 0.0 copy-done
  163.2 31.3 %convolution_bitcast_fusion = f32[512,8192]{0,1:T(8,128)} fusion(bf16[1024,8192]{0,1:T(8,128)(2,1)} %bitcast.11, f32[1024,512]{1,0:T(8,128)S(1)} %copy-done), kind=kOutput, calls=%fused_computation.12 | convolution fusion | flops 51539607552 | bytes 35651584 | tf_op jit(solution)/shard_map/dot_general | solution.py:36
  194.5 17.4 %copy.14 = f32[512,8192]{1,0:T(8,128)} copy(f32[512,8192]{0,1:T(8,128)} %convolution_bitcast_fusion) | data formatting | bytes 33554432
  211.9 0.0 reduce-scatter.4.cloned.1.call-update
  211.9 181.3 %reduce-scatter.4.cloned.1.call-done = f32[32,8192]{1,0:T(8,128)} async-done(((f32[512,8192]{1,0:T(8,128)}), f32[32,8192]{1,0:T(8,128)}) %reduce-scatter.4.cloned.1.call-update) | async-done | bytes 1048592 | tf_op jit(solution)/shard_map/reduce_scatter | solution.py:60
  393.2 2.1 convert_element_type.4
  (3 shorter events, 0.0 us)
Async XLA Ops:
  6.5 156.7 %copy-start = (f32[1024,512]{1,0:T(8,128)S(1)}, f32[1024,512]{1,0:T(8,128)}, u32[]{:S(2)}) copy-start(f32[1024,512]{1,0:T(8,128)} %param.9) | copy-start | bytes 6291460
  6.5 386.7 %reduce-scatter.4.cloned.1.call-start = ((), (), s32[]{:S(2)}) async-start(), calls=%async_computation.1 | async-start | bytes 17825792 | tf_op jit(solution)/shard_map/reduce_scatter | solution.py:60
  43.7 3.1 copy-start.6
  46.8 2.0 copy-start.4
  48.9 2.0 copy-start.2
  50.9 1.6 copy-start.7
  67.5 13.6 %collective-permute-start = (bf16[1,1024,4096]{2,1,0:T(8,128)(2,1)}, bf16[1,1024,4096]{2,1,0:T(8,128)(2,1)}, u32[]{:S(2)}, u32[]{:S(2)}) collective-permute-start(bf16[1,1024,4096]{2,1,0:T(8,128)(2,1)} %slice.50), channel_id=1, source_target_pairs={{0,1},{1,0},{2,3},{3,2},{4,5},{5,4},{6,7},{7,6},{8,9},{9,8},{10,11... | collective-permute-start | bytes 25165832 | tf_op jit(solution)/shard_map/ppermute | solution.py:15
  125.7 3.1 copy-start.5
  128.8 2.0 copy-start.3
  130.9 2.0 copy-start.1
  132.9 1.6 copy-start.8
Sparse Core Ops, SparseCore 0:
  212.0 181.1 reduce-scatter.3
where the time goes:
time: 404 us; the launch traced here: 402 us
  waiting for transfers between devices  194 us (48%)
  local copies, waits for them, and re-layouts  146 us (36%)
  matrix products  31.3 us (8%)
  other arithmetic  16.2 us (4%)
  between operations  13.5 us (3%)
    reduce_scatter x1, waiting for transfers between devices, on_device(): lax.psum_scatter(contract_rows(basis, wide_slab), 'row', scatter_dimensio...  181 us
    gather x14, local copies, waits for them, and re-layouts, slot_order(): return jnp.take(blocks, order, axis=0)  74 us
    unnamed x27, local copies, waits for them, and re-layouts  35 us
    dot_general x1, matrix products, contract_rows(): lax.dot_general(left, right, (((0,), (0,)), ((), ())), precision=lax.Prec...  31.3 us
    transpose x1, local copies, waits for them, and re-layouts, on_device(): jnp.transpose(pieces, (1, 0, 2)).reshape(own_count, -1).astype(jnp.float32)  21.2 us
    ppermute x1, waiting for transfers between devices, swapped(): return lax.ppermute(block, axis, route)  13.1 us
  transfers between devices with their start and end apart: 2, of which 2 were waited for; matrix products, arithmetic and copies ran while one was open for 0% of the time, Pallas kernels for 0%

commit v1 on v0

v1 whole, which is shorter than its diff:
```python
import functools

import jax
import jax.numpy as jnp
from jax import lax
from jax.experimental import pallas as pl
from jax.experimental.pallas import tpu as pltpu
from jax.sharding import PartitionSpec as P

LANES = 128
SCALE_ROWS = 16
HALF_SPAN = 125.0
SPAN = 250.0
TINY = 2.0**-110
MIB = 1 << 20


def column_bound(values):
    top = jnp.maximum(jnp.max(jnp.abs(values), axis=0, keepdims=True), TINY)
    return (top * 1.008).astype(jnp.bfloat16).astype(jnp.float32)


def encode(values, bound):
    level = jnp.exp2(jnp.abs(values) * (SPAN / bound) - HALF_SPAN)
    return jnp.where(values < 0, -level, level).astype(jnp.bfloat16)


def decode(coded, bound):
    coded = coded.astype(jnp.float32)
    size = (jnp.log2(jnp.abs(coded)) + HALF_SPAN) * (bound * (1.0 / SPAN))
    return jnp.where(coded < 0, -size, size)


def reversed_bits(value, bits):
    out = 0
    for bit in range(bits):
        out |= (value >> bit & 1) << (bits - 1 - bit)
    return out


def split_places(order, bits):
    stay = list(range(1 << bits))
    stages = []
    for bit in order:
        leave = [p for p in stay if reversed_bits(p, bits) >> bit & 1]
        stay = [p for p in stay if not reversed_bits(p, bits) >> bit & 1]
        stages.append((leave, stay))
    return stages


def put_message(message_ref, values, tiles, count):
    bounds = []
    for tile in range(tiles):
        sent = values[tile]
        bound = column_bound(sent)
        message_ref[tile * count : (tile + 1) * count, :] = encode(sent, bound)
        bounds.append(bound)
    bounds.append(jnp.zeros((SCALE_ROWS - tiles, LANES), jnp.float32))
    message_ref[tiles * count :, :] = jnp.concatenate(bounds, axis=0).astype(jnp.bfloat16)


def prepare_kernel(blocks, bits, place_ref, basis_ref, out_ref, turned):
    turned[...] = basis_ref[...].T
    rows = turned.shape[0]
    step = rows // blocks
    for place in range(blocks):
        source = jnp.bitwise_xor(place_ref[0], reversed_bits(place, bits))
        part = turned[pl.ds(pl.multiple_of(source * step, step), step), :]
        high = part.astype(jnp.bfloat16)
        low = (part - high.astype(jnp.float32)).astype(jnp.bfloat16)
        out_ref[place * step : (place + 1) * step, :] = high
        out_ref[rows + place * step : rows + (place + 1) * step, :] = low


def prepare(basis, place, blocks, bits):
    depth, rows = basis.shape
    wide = min(depth, 256)
    return pl.pallas_call(
        functools.partial(prepare_kernel, blocks, bits),
        grid_spec=pltpu.PrefetchScalarGridSpec(
            num_scalar_prefetch=1,
            grid=(depth // wide,),
            in_specs=[pl.BlockSpec((wide, rows), lambda i, s: (i, 0))],
            out_specs=pl.BlockSpec((2 * rows, wide), lambda i, s: (0, i)),
            scratch_shapes=[pltpu.VMEM((rows, wide), jnp.float32)],
        ),
        out_shape=jax.ShapeDtypeStruct((2 * rows, depth), jnp.bfloat16),
        cost_estimate=pl.CostEstimate(
            flops=2 * depth * rows, bytes_accessed=8 * depth * rows, transcendentals=0
        ),
        name="split_basis",
    )(place, basis)


def product_kernel(pieces, step, leave, stay, place_ref, *refs):
    left = refs[:pieces]
    right = refs[pieces : 2 * pieces]
    message_ref, kept_ref = refs[2 * pieces :]
    total = None
    for a_ref, w_ref in zip(left, right):
        part = jnp.dot(a_ref[...], w_ref[0], preferred_element_type=jnp.float32)
        total = part if total is None else total + part
    rows = total.shape[0] // 2
    total = total[:rows] + total[rows:]
    tiles = total.shape[1] // LANES
    sent = []
    count = len(stay) * step
    for tile in range(tiles):
        column = total[:, tile * LANES : (tile + 1) * LANES]
        sent.append(jnp.concatenate([column[p * step : (p + 1) * step] for p in leave], axis=0))
        for slot, p in enumerate(stay):
            at = tile * count + slot * step
            kept_ref[at : at + step, :] = column[p * step : (p + 1) * step]
    put_message(message_ref, sent, tiles, len(leave) * step)


def product(left, weights, column, start, width, wide, step, leave, stay):
    pieces = len(left)
    rows2, depth = left[0].shape
    steps = width // wide
    tiles = wide // LANES
    sent_rows = tiles * len(leave) * step + SCALE_ROWS
    kept_rows = tiles * len(stay) * step
    first = start // wide

    def weight_spec(distance):
        return pl.BlockSpec(
            (1, depth, wide), lambda j, s: (0, jnp.bitwise_xor(s[0], distance), first + j)
        )

    return pl.pallas_call(
        functools.partial(product_kernel, pieces, step, leave, stay),
        grid_spec=pltpu.PrefetchScalarGridSpec(
            num_scalar_prefetch=1,
            grid=(steps,),
            in_specs=[
                pl.BlockSpec((rows2, depth), lambda j, s: (0, 0), pipeline_mode=pl.Buffered(1))
                for _ in left
            ]
            + [weight_spec(distance) for distance in range(pieces)],
            out_specs=[
                pl.BlockSpec((sent_rows, LANES), lambda j, s: (j, 0)),
                pl.BlockSpec((kept_rows, LANES), lambda j, s: (j, 0)),
            ],
        ),
        out_shape=[
            jax.ShapeDtypeStruct((steps * sent_rows, LANES), jnp.bfloat16),
            jax.ShapeDtypeStruct((steps * kept_rows, LANES), jnp.float32),
        ],
        compiler_params=pltpu.CompilerParams(vmem_limit_bytes=40 * MIB),
        cost_estimate=pl.CostEstimate(
            flops=2 * rows2 * depth * pieces * width,
            bytes_accessed=2 * depth * pieces * width + 4 * rows2 * width,
            transcendentals=rows2 * width // 4,
        ),
        name="product",
    )(column, *left, *([weights] * pieces))


def received(message_ref, kept_ref, tile, tiles, count):
    bounds = message_ref[tiles * count :, :].astype(jnp.float32)
    coded = message_ref[tile * count : (tile + 1) * count, :]
    return kept_ref[tile * count : (tile + 1) * count, :] + decode(coded, bounds[tile : tile + 1])


def middle_kernel(tiles, step, old, leave, stay, message_ref, kept_ref, out_ref, next_ref):
    sent = []
    count = len(stay) * step
    for tile in range(tiles):
        column = received(message_ref, kept_ref, tile, tiles, len(old) * step)
        blocks = {p: column[i * step : (i + 1) * step] for i, p in enumerate(old)}
        sent.append(jnp.concatenate([blocks[p] for p in leave], axis=0))
        for slot, p in enumerate(stay):
            at = tile * count + slot * step
            next_ref[at : at + step, :] = blocks[p]
    put_message(out_ref, sent, tiles, len(leave) * step)


def middle(message, kept, width, wide, step, old, leave, stay):
    steps = width // wide
    tiles = wide // LANES
    in_rows = tiles * len(old) * step
    sent_rows = tiles * len(leave) * step + SCALE_ROWS
    kept_rows = tiles * len(stay) * step
    return pl.pallas_call(
        functools.partial(middle_kernel, tiles, step, old, leave, stay),
        grid=(steps,),
        in_specs=[
            pl.BlockSpec((in_rows + SCALE_ROWS, LANES), lambda j: (j, 0)),
            pl.BlockSpec((in_rows, LANES), lambda j: (j, 0)),
        ],
        out_specs=[
            pl.BlockSpec((sent_rows, LANES), lambda j: (j, 0)),
            pl.BlockSpec((kept_rows, LANES), lambda j: (j, 0)),
        ],
        out_shape=[
            jax.ShapeDtypeStruct((steps * sent_rows, LANES), jnp.bfloat16),
            jax.ShapeDtypeStruct((steps * kept_rows, LANES), jnp.float32),
        ],
        cost_estimate=pl.CostEstimate(
            flops=20 * steps * in_rows * LANES,
            bytes_accessed=9 * steps * in_rows * LANES,
            transcendentals=2 * steps * in_rows * LANES,
        ),
        name="add_and_split",
    )(message, kept)


def last_kernel(tiles, pieces, place_ref, message_ref, kept_ref, *refs):
    outs = refs[:pieces]
    whole = refs[pieces]
    count = whole.shape[0]
    share = count // pieces
    for tile in range(tiles):
        whole[:, tile * LANES : (tile + 1) * LANES] = received(
            message_ref, kept_ref, tile, tiles, count
        )
    for distance in range(pieces):
        owner = jnp.bitwise_xor(place_ref[0], distance)
        rows = whole[pl.ds(pl.multiple_of(owner * share, share), share), :]
        outs[distance][...] = rows.astype(jnp.bfloat16)


def last(message, kept, column, width, wide, step, pieces):
    steps = width // wide
    tiles = wide // LANES
    in_rows = tiles * step
    share = step // pieces
    return pl.pallas_call(
        functools.partial(last_kernel, tiles, pieces),
        grid_spec=pltpu.PrefetchScalarGridSpec(
            num_scalar_prefetch=1,
            grid=(steps,),
            in_specs=[
                pl.BlockSpec((in_rows + SCALE_ROWS, LANES), lambda j, s: (j, 0)),
                pl.BlockSpec((in_rows, LANES), lambda j, s: (j, 0)),
            ],
            out_specs=[pl.BlockSpec((share, wide), lambda j, s: (0, j))] * pieces,
            scratch_shapes=[pltpu.VMEM((step, wide), jnp.float32)],
        ),
        out_shape=[jax.ShapeDtypeStruct((share, width), jnp.bfloat16)] * pieces,
        cost_estimate=pl.CostEstimate(
            flops=10 * steps * in_rows * LANES,
            bytes_accessed=8 * steps * in_rows * LANES,
            transcendentals=steps * in_rows * LANES,
        ),
        name="add_last",
    )(column, message, kept)


def swapped(block, apart):
    count = lax.axis_size("row")
    return lax.ppermute(block, "row", [(i, i ^ apart) for i in range(count)])


def on_device(basis, weights):
    axis_len = lax.axis_size("row")
    depth, rows = basis.shape
    pieces = weights.shape[1] // depth
    blocks = axis_len // pieces
    bits = blocks.bit_length() - 1
    piece_bits = pieces.bit_length() - 1
    step = rows // blocks
    width = weights.shape[2]
    me = lax.axis_index("row").astype(jnp.int32)
    column = jnp.bitwise_and(me, pieces - 1)
    place = jnp.right_shift(me, piece_bits)[None]
    column_at = column[None]

    own = prepare(basis, place, blocks, bits)
    left = [own] + [swapped(own, distance) for distance in range(1, pieces)]

    chunk = width // 4
    wide = min(chunk, 512)
    plain = list(range(bits))
    orders = [plain] * 4
    if bits > 1:
        orders[1] = [1, 0] + plain[2:]

    finished = []
    for index, order in enumerate(orders):
        stages = split_places(order, bits)
        message, kept = product(
            left, weights, column_at, index * chunk, chunk, wide, step, *stages[0]
        )
        for number, bit in enumerate(order):
            message = swapped(message, pieces << bit)
            if number + 1 < bits:
                message, kept = middle(
                    message, kept, chunk, wide, step, stages[number][1], *stages[number + 1]
                )
        parts = last(message, kept, column_at, chunk, wide, step, pieces)
        finished.append(
            [parts[0]] + [swapped(parts[distance], distance) for distance in range(1, pieces)]
        )
    out = [jnp.concatenate(parts, axis=1) for parts in zip(*finished)]
    for bit in range(piece_bits):
        odd = jnp.right_shift(column, bit) & 1 == 1
        out = [jnp.where(odd, out[q ^ 1 << bit], out[q]) for q in range(pieces)]
    return jnp.concatenate(out, axis=1)


def solution(mesh):
    in_specs = (P(("groups", "row"), None), P(("groups", "row"), None, None))
    out_specs = P(("groups", "row"), None)
    return jax.shard_map(
        on_device, mesh=mesh, in_specs=in_specs, out_specs=out_specs, check_vma=False
    )
```

time: 404 us -> 109 us (0.27)
  waiting for transfers between devices: 194 us -> 17.8 us
  local copies, waits for them, and re-layouts: 146 us -> 16 us
  Pallas kernels: 0 us -> 55.3 us
  matrix products: 31.3 us -> 0 us
  starting transfers between devices: 0.45 us -> 18.6 us
  other arithmetic: 16.2 us -> 0.87 us
  between operations: 13.5 us -> 0.15 us
    reduce_scatter x1 -> x0, waiting for transfers between devices: 181 us -> none  [on_device(): lax.psum_scatter(contract_rows(basis, wide_slab), 'row', scatter_dimensio...]
    gather x15 -> x0, local copies, waits for them, and re-layouts: 81.7 us -> none  [the longest x14 74 us: slot_order(): return jnp.take(blocks, order, axis=0)]
    pallas_call x0 -> x17, Pallas kernels: none -> 55.3 us  [the longest x4 27 us: product(): pl.pallas_call(functools.partial(product_kernel, pieces, step, leave, sta...]
    dot_general x1 -> x0, matrix products: 31.3 us -> none  [contract_rows(): lax.dot_general(left, right, (((0,), (0,)), ((), ())), precision=lax.Prec...]
    transpose x1 -> x0, local copies, waits for them, and re-layouts: 21.2 us -> none  [on_device(): jnp.transpose(pieces, (1, 0, 2)).reshape(own_count, -1).astype(jnp.float32)]
    unnamed x27 -> x36, local copies, waits for them, and re-layouts: 35 us -> 15.1 us
    ppermute x1 -> x17, starting transfers between devices: 0.45 us -> 18.6 us  [swapped(): return lax.ppermute(block, 'row', [(i, i ^ apart) for i in range(count)])]
    scatter x1 -> x0, local copies, waits for them, and re-layouts: 7.72 us -> none  [cube_exchange(): blocks = blocks.at[chosen].set(arrived)]
  transfers between devices with their start and end apart: 2 -> 17, of which waited for: 2 -> 5; matrix products, arithmetic and copies ran while one was open for 0% -> 3% of each run, Pallas kernels for 0% -> 41%
where the time goes in v1:
time: 109 us
  Pallas kernels  55.3 us (51%)
  starting transfers between devices  18.6 us (17%)
  waiting for transfers between devices  17.8 us (16%)
  local copies, waits for them, and re-layouts  16 us (15%)
    pallas_call x4, Pallas kernels, product(): pl.pallas_call(functools.partial(product_kernel, pieces, step, leave, sta...  27 us
    ppermute x17, starting transfers between devices, swapped(): return lax.ppermute(block, 'row', [(i, i ^ apart) for i in range(count)])  18.6 us
    ppermute x17, waiting for transfers between devices, swapped(): return lax.ppermute(block, 'row', [(i, i ^ apart) for i in range(count)])  17.8 us
    pallas_call x8, Pallas kernels, middle(): pl.pallas_call(functools.partial(middle_kernel, tiles, step, old, leave,...  17.2 us
    unnamed x36, local copies, waits for them, and re-layouts  15.1 us
    pallas_call x4, Pallas kernels, last(): pl.pallas_call(functools.partial(last_kernel, tiles, pieces), grid_spec=p...  6.86 us
    pallas_call x1, Pallas kernels, prepare(): pl.pallas_call(functools.partial(prepare_kernel, blocks, bits), grid_spec...  4.36 us
  transfers between devices with their start and end apart: 17, of which 5 were waited for; matrix products, arithmetic and copies ran while one was open for 3% of the time, Pallas kernels for 41%

profile of v1, /device:TPU:0, one launch (start us, length us, event | category | flops | bytes accessed | tf_op | source)
XLA Modules:
  0.0 108.8 jit_solution(16120521856801873404)
XLA Ops:
  0.0 4.4 %split_basis.1.refs_0_ = bf16[1024,1024]{1,0:T(8,128)(2,1)} custom-call(s32[1]{0:T(128)} %bitcast.1.place_ref, f32[1024,512]{1,0:T(8,128)} %basis_ref.1), custom_call_target="tpu_custom_call" | custom-call | flops 1048576 | bytes 4194304 | tf_op jit(solution)/shard_map/split_basis/pallas_call | solution.py:78
  4.4 0.5 collective-permute-start
  4.8 4.0 %collective-permute-done.refs_1_ = bf16[1024,1024]{1,0:T(8,128)(2,1)S(1)} collective-permute-done((bf16[1024,1024]{1,0:T(8,128)(2,1)}, bf16[1024,1024]{1,0:T(8,128)(2,1)S(1)}, u32[]{:S(2)}, u32[]{:S(2)}) %collective-permute-start) | collective-permute-done | bytes 2097184 | tf_op jit(solution)/shard_map/ppermute | solution.py:253
  8.8 1.6 %copy-done = bf16[1024,1024]{1,0:T(8,128)(2,1)S(1)} copy-done((bf16[1024,1024]{1,0:T(8,128)(2,1)S(1)}, bf16[1024,1024]{1,0:T(8,128)(2,1)}, u32[]{:S(2)}) %copy-start) | copy-done | bytes 2097176
  10.4 6.6 %product.4 = (bf16[2080,128]{1,0:T(8,128)(2,1)S(1)}, f32[2048,128]{1,0:T(8,128)S(1)}) custom-call(s32[1]{0:T(128)} %bitcast.place_ref, bf16[1024,1024]{1,0:T(8,128)(2,1)S(1)} %copy-done, bf16[1024,1024]{1,0:T(8,128)(2,1)S(1)} %collective-permute-done.refs_1_, bf16[1,2048,4096]{2,1,0:T(8,128)(2,1)} %refs_3_.7, bf16[1,2048,4096]{2,1,0:T(8,128)(2,1)} %refs_3_.7), custom_call_target="tpu_custom_call" | custom-call | flops 4294967296 | bytes 8388608 | tf_op jit(solution)/shard_map/product/pallas_call | solution.py:131
  17.0 1.0 copy-done.1
  18.0 2.9 %collective-permute-start.1 = (bf16[2080,128]{1,0:T(8,128)(2,1)S(1)}, bf16[2080,128]{1,0:T(8,128)(2,1)}, u32[]{:S(2)}, u32[]{:S(2)}) collective-permute-start(bf16[2080,128]{1,0:T(8,128)(2,1)S(1)} %get-tuple-element.37), channel_id=1, source_target_pairs={{0,2},{1,3},{2,0},{3,1},{4,6},{5,7},{6,4},{7,5},{8,10},{9,11},{10,... | collective-permute-start | bytes 1597448 | tf_op jit(solution)/shard_map/ppermute | solution.py:253
  20.9 7.3 %product.6 = (bf16[2080,128]{1,0:T(8,128)(2,1)}, f32[2048,128]{1,0:T(8,128)S(1)}) custom-call(s32[1]{0:T(128)} %bitcast.place_ref, bf16[1024,1024]{1,0:T(8,128)(2,1)S(1)} %copy-done, bf16[1024,1024]{1,0:T(8,128)(2,1)S(1)} %collective-permute-done.refs_1_, bf16[1,2048,4096]{2,1,0:T(8,128)(2,1)} %refs_3_.7, bf16[1,2048,4096]{2,1,0:T(8,128)(2,1)} %refs_3_.7), custom_call_target="tpu_custom_call" | custom-call | flops 4294967296 | bytes 8388608 | tf_op jit(solution)/shard_map/product/pallas_call | solution.py:131
  28.1 1.0 copy-done.3
  29.1 0.0 collective-permute-start.9
  29.1 6.6 %product.7 = (bf16[2080,128]{1,0:T(8,128)(2,1)S(1)}, f32[2048,128]{1,0:T(8,128)S(1)}) custom-call(s32[1]{0:T(128)} %bitcast.place_ref, bf16[1024,1024]{1,0:T(8,128)(2,1)S(1)} %copy-done, bf16[1024,1024]{1,0:T(8,128)(2,1)S(1)} %collective-permute-done.refs_1_, bf16[1,2048,4096]{2,1,0:T(8,128)(2,1)} %refs_3_.7, bf16[1,2048,4096]{2,1,0:T(8,128)(2,1)} %refs_3_.7), custom_call_target="tpu_custom_call" | custom-call | flops 4294967296 | bytes 8388608 | tf_op jit(solution)/shard_map/product/pallas_call | solution.py:131
  35.7 1.0 copy-done.4
  36.7 2.0 %collective-permute-start.13 = (bf16[2080,128]{1,0:T(8,128)(2,1)S(1)}, bf16[2080,128]{1,0:T(8,128)(2,1)S(1)}, u32[]{:S(2)}, u32[]{:S(2)}) collective-permute-start(bf16[2080,128]{1,0:T(8,128)(2,1)S(1)} %get-tuple-element.58), channel_id=1, source_target_pairs={{0,2},{1,3},{2,0},{3,1},{4,6},{5,7},{6,4},{7,5},{8,10},{9,11},{10,... | collective-permute-start | bytes 1597448 | tf_op jit(solution)/shard_map/ppermute | solution.py:253
  38.7 6.6 %product.5 = (bf16[2080,128]{1,0:T(8,128)(2,1)S(1)}, f32[2048,128]{1,0:T(8,128)S(1)}) custom-call(s32[1]{0:T(128)} %bitcast.place_ref, bf16[1024,1024]{1,0:T(8,128)(2,1)S(1)} %copy-done, bf16[1024,1024]{1,0:T(8,128)(2,1)S(1)} %collective-permute-done.refs_1_, bf16[1,2048,4096]{2,1,0:T(8,128)(2,1)} %refs_3_.7, bf16[1,2048,4096]{2,1,0:T(8,128)(2,1)} %refs_3_.7), custom_call_target="tpu_custom_call" | custom-call | flops 4294967296 | bytes 8388608 | tf_op jit(solution)/shard_map/product/pallas_call | solution.py:131
  45.2 1.0 copy-done.2
  46.2 1.6 %collective-permute-start.5 = (bf16[2080,128]{1,0:T(8,128)(2,1)S(1)}, bf16[2080,128]{1,0:T(8,128)(2,1)S(1)}, u32[]{:S(2)}, u32[]{:S(2)}) collective-permute-start(bf16[2080,128]{1,0:T(8,128)(2,1)S(1)} %get-tuple-element.44), channel_id=1, source_target_pairs={{0,4},{1,5},{2,6},{3,7},{4,0},{5,1},{6,2},{7,3},{8,12},{9,13},{10,... | collective-permute-start | bytes 1597448 | tf_op jit(solution)/shard_map/ppermute | solution.py:253
  47.8 8.3 %collective-permute-done.13.message_ref = bf16[2080,128]{1,0:T(8,128)(2,1)S(1)} collective-permute-done((bf16[2080,128]{1,0:T(8,128)(2,1)S(1)}, bf16[2080,128]{1,0:T(8,128)(2,1)S(1)}, u32[]{:S(2)}, u32[]{:S(2)}) %collective-permute-start.13) | collective-permute-done | bytes 532512 | tf_op jit(solution)/shard_map/ppermute | solution.py:253
  56.1 0.8 copy-done.6
  56.9 2.3 %add_and_split.14 = (bf16[1056,128]{1,0:T(8,128)(2,1)}, f32[1024,128]{1,0:T(8,128)}) custom-call(bf16[2080,128]{1,0:T(8,128)(2,1)} %copy-done.6, f32[2048,128]{1,0:T(8,128)} %copy-done.4), custom_call_target="tpu_custom_call" | custom-call | flops 5242880 | bytes 2359296 | tf_op jit(solution)/shard_map/add_and_split/pallas_call | solution.py:185
  59.2 1.8 %collective-permute-start.14 = (bf16[1056,128]{1,0:T(8,128)(2,1)}, bf16[1056,128]{1,0:T(8,128)(2,1)S(1)}, u32[]{:S(2)}, u32[]{:S(2)}) collective-permute-start(bf16[1056,128]{1,0:T(8,128)(2,1)} %get-tuple-element.60), channel_id=1, source_target_pairs={{0,4},{1,5},{2,6},{3,7},{4,0},{5,1},{6,2},{7,3},{8,12},{9,13},{10,... | collective-permute-start | bytes 811016 | tf_op jit(solution)/shard_map/ppermute | solution.py:253
  61.0 0.0 collective-permute-done.9.message_ref
  61.0 2.3 %add_and_split.12 = (bf16[1056,128]{1,0:T(8,128)(2,1)}, f32[1024,128]{1,0:T(8,128)}) custom-call(bf16[2080,128]{1,0:T(8,128)(2,1)} %collective-permute-done.9.message_ref, f32[2048,128]{1,0:T(8,128)} %copy-done.3), custom_call_target="tpu_custom_call" | custom-call | flops 5242880 | bytes 2359296 | tf_op jit(solution)/shard_map/add_and_split/pallas_call | solution.py:185
  63.3 0.2 collective-permute-start.10
  63.6 0.0 collective-permute-done.1.message_ref
  63.6 2.3 %add_and_split.8 = (bf16[1056,128]{1,0:T(8,128)(2,1)}, f32[1024,128]{1,0:T(8,128)}) custom-call(bf16[2080,128]{1,0:T(8,128)(2,1)} %collective-permute-done.1.message_ref, f32[2048,128]{1,0:T(8,128)} %copy-done.1), custom_call_target="tpu_custom_call" | custom-call | flops 5242880 | bytes 2359296 | tf_op jit(solution)/shard_map/add_and_split/pallas_call | solution.py:185
  65.9 1.8 %collective-permute-start.2 = (bf16[1056,128]{1,0:T(8,128)(2,1)}, bf16[1056,128]{1,0:T(8,128)(2,1)S(1)}, u32[]{:S(2)}, u32[]{:S(2)}) collective-permute-start(bf16[1056,128]{1,0:T(8,128)(2,1)} %get-tuple-element.39), channel_id=1, source_target_pairs={{0,4},{1,5},{2,6},{3,7},{4,0},{5,1},{6,2},{7,3},{8,12},{9,13},{10,... | collective-permute-start | bytes 811016 | tf_op jit(solution)/shard_map/ppermute | solution.py:253
  67.7 0.0 collective-permute-done.5.message_ref
  67.7 0.8 copy-done.5
  68.5 2.3 %add_and_split.10 = (bf16[1056,128]{1,0:T(8,128)(2,1)}, f32[1024,128]{1,0:T(8,128)}) custom-call(bf16[2080,128]{1,0:T(8,128)(2,1)} %copy-done.5, f32[2048,128]{1,0:T(8,128)} %copy-done.2), custom_call_target="tpu_custom_call" | custom-call | flops 5242880 | bytes 2359296 | tf_op jit(solution)/shard_map/add_and_split/pallas_call | solution.py:185
  70.8 1.5 %collective-permute-start.6 = (bf16[1056,128]{1,0:T(8,128)(2,1)}, bf16[1056,128]{1,0:T(8,128)(2,1)S(1)}, u32[]{:S(2)}, u32[]{:S(2)}) collective-permute-start(bf16[1056,128]{1,0:T(8,128)(2,1)} %get-tuple-element.46), channel_id=1, source_target_pairs={{0,2},{1,3},{2,0},{3,1},{4,6},{5,7},{6,4},{7,5},{8,10},{9,11},{10,... | collective-permute-start | bytes 811016 | tf_op jit(solution)/shard_map/ppermute | solution.py:253
  72.4 0.7 copy-done.7
  73.1 2.0 %add_and_split.15 = (bf16[544,128]{1,0:T(8,128)(2,1)}, f32[512,128]{1,0:T(8,128)}) custom-call(bf16[1056,128]{1,0:T(8,128)(2,1)} %copy-done.7, f32[1024,128]{1,0:T(8,128)} %get-tuple-element.61.kept_ref), custom_call_target="tpu_custom_call" | custom-call | flops 2621440 | bytes 1179648 | tf_op jit(solution)/shard_map/add_and_split/pallas_call | solution.py:185
  75.0 2.6 %collective-permute-start.15 = (bf16[544,128]{1,0:T(8,128)(2,1)}, bf16[544,128]{1,0:T(8,128)(2,1)S(1)}, u32[]{:S(2)}, u32[]{:S(2)}) collective-permute-start(bf16[544,128]{1,0:T(8,128)(2,1)} %get-tuple-element.62), channel_id=1, source_target_pairs={{0,8},{1,9},{2,10},{3,11},{4,12},{5,13},{6,14},{7,15},{8,0},{9,1},... | collective-permute-start | bytes 417800 | tf_op jit(solution)/shard_map/ppermute | solution.py:253
  77.6 0.0 collective-permute-done.10.message_ref
  77.6 0.7 copy-done.8
  78.3 2.0 %add_and_split.13 = (bf16[544,128]{1,0:T(8,128)(2,1)}, f32[512,128]{1,0:T(8,128)}) custom-call(bf16[1056,128]{1,0:T(8,128)(2,1)} %copy-done.8, f32[1024,128]{1,0:T(8,128)} %get-tuple-element.54.kept_ref), custom_call_target="tpu_custom_call" | custom-call | flops 2621440 | bytes 1179648 | tf_op jit(solution)/shard_map/add_and_split/pallas_call | solution.py:185
  80.3 0.3 collective-permute-start.11
  80.6 0.7 collective-permute-done.2.message_ref
  81.3 0.7 copy-done.9
  82.0 2.0 %add_and_split.9 = (bf16[544,128]{1,0:T(8,128)(2,1)}, f32[512,128]{1,0:T(8,128)}) custom-call(bf16[1056,128]{1,0:T(8,128)(2,1)} %copy-done.9, f32[1024,128]{1,0:T(8,128)} %get-tuple-element.40.kept_ref), custom_call_target="tpu_custom_call" | custom-call | flops 2621440 | bytes 1179648 | tf_op jit(solution)/shard_map/add_and_split/pallas_call | solution.py:185
  84.0 2.0 %collective-permute-start.3 = (bf16[544,128]{1,0:T(8,128)(2,1)}, bf16[544,128]{1,0:T(8,128)(2,1)S(1)}, u32[]{:S(2)}, u32[]{:S(2)}) collective-permute-start(bf16[544,128]{1,0:T(8,128)(2,1)} %get-tuple-element.41), channel_id=1, source_target_pairs={{0,8},{1,9},{2,10},{3,11},{4,12},{5,13},{6,14},{7,15},{8,0},{9,1},... | collective-permute-start | bytes 417800 | tf_op jit(solution)/shard_map/ppermute | solution.py:253
  85.9 0.0 collective-permute-done.6.message_ref
  85.9 0.7 copy-done.10
  86.6 2.0 %add_and_split.11 = (bf16[544,128]{1,0:T(8,128)(2,1)}, f32[512,128]{1,0:T(8,128)}) custom-call(bf16[1056,128]{1,0:T(8,128)(2,1)} %copy-done.10, f32[1024,128]{1,0:T(8,128)} %get-tuple-element.47.kept_ref), custom_call_target="tpu_custom_call" | custom-call | flops 2621440 | bytes 1179648 | tf_op jit(solution)/shard_map/add_and_split/pallas_call | solution.py:185
  88.6 1.0 collective-permute-start.7
  89.6 0.0 collective-permute-done.15.message_ref
  89.6 0.7 copy-done.11
  90.2 1.7 %add_last.7 = (bf16[32,1024]{1,0:T(8,128)(2,1)}, bf16[32,1024]{1,0:T(8,128)(2,1)}) custom-call(s32[1]{0:T(128)} %bitcast.place_ref, bf16[544,128]{1,0:T(8,128)(2,1)} %copy-done.11, f32[512,128]{1,0:T(8,128)} %get-tuple-element.63.kept_ref), custom_call_target="tpu_custom_call" | custom-call | flops 655360 | bytes 524288 | tf_op jit(solution)/shard_map/add_last/pallas_call | solution.py:229
  92.0 0.0 collective-permute-start.16
  92.0 2.8 %collective-permute-done.11.message_ref = bf16[544,128]{1,0:T(8,128)(2,1)S(1)} collective-permute-done((bf16[544,128]{1,0:T(8,128)(2,1)}, bf16[544,128]{1,0:T(8,128)(2,1)S(1)}, u32[]{:S(2)}, u32[]{:S(2)}) %collective-permute-start.11) | collective-permute-done | bytes 139296 | tf_op jit(solution)/shard_map/ppermute | solution.py:253
  94.7 0.7 copy-done.12
  95.4 1.7 %add_last.6 = (bf16[32,1024]{1,0:T(8,128)(2,1)}, bf16[32,1024]{1,0:T(8,128)(2,1)}) custom-call(s32[1]{0:T(128)} %bitcast.place_ref, bf16[544,128]{1,0:T(8,128)(2,1)} %copy-done.12, f32[512,128]{1,0:T(8,128)} %get-tuple-element.56.kept_ref), custom_call_target="tpu_custom_call" | custom-call | flops 655360 | bytes 524288 | tf_op jit(solution)/shard_map/add_last/pallas_call | solution.py:229
  97.1 0.0 collective-permute-start.12
  97.1 2.1 %collective-permute-done.3.message_ref = bf16[544,128]{1,0:T(8,128)(2,1)S(1)} collective-permute-done((bf16[544,128]{1,0:T(8,128)(2,1)}, bf16[544,128]{1,0:T(8,128)(2,1)S(1)}, u32[]{:S(2)}, u32[]{:S(2)}) %collective-permute-start.3) | collective-permute-done | bytes 139296 | tf_op jit(solution)/shard_map/ppermute | solution.py:253
  99.2 0.7 copy-done.13
  99.9 1.7 %add_last.4 = (bf16[32,1024]{1,0:T(8,128)(2,1)}, bf16[32,1024]{1,0:T(8,128)(2,1)}) custom-call(s32[1]{0:T(128)} %bitcast.place_ref, bf16[544,128]{1,0:T(8,128)(2,1)} %copy-done.13, f32[512,128]{1,0:T(8,128)} %get-tuple-element.42.kept_ref), custom_call_target="tpu_custom_call" | custom-call | flops 655360 | bytes 524288 | tf_op jit(solution)/shard_map/add_last/pallas_call | solution.py:229
  101.6 0.8 constant_dynamic-update-slice_fusion.7
  102.4 0.7 copy-done.14
  103.1 1.7 %add_last.5 = (bf16[32,1024]{1,0:T(8,128)(2,1)}, bf16[32,1024]{1,0:T(8,128)(2,1)}) custom-call(s32[1]{0:T(128)} %bitcast.place_ref, bf16[544,128]{1,0:T(8,128)(2,1)} %copy-done.14, f32[512,128]{1,0:T(8,128)} %get-tuple-element.49.kept_ref), custom_call_target="tpu_custom_call" | custom-call | flops 655360 | bytes 524288 | tf_op jit(solution)/shard_map/add_last/pallas_call | solution.py:229
  104.8 0.5 collective-permute-start.4
  105.3 0.8 constant_dynamic-update-slice_fusion.6
  106.1 0.8 constant_dynamic-update-slice_fusion.5
  107.0 0.8 constant_dynamic-update-slice_fusion.4
  108.0 0.8 pad_maximum_fusion
  (27 shorter events, 0.1 us)
Async XLA Ops:
  4.4 4.5 %collective-permute-start = (bf16[1024,1024]{1,0:T(8,128)(2,1)}, bf16[1024,1024]{1,0:T(8,128)(2,1)S(1)}, u32[]{:S(2)}, u32[]{:S(2)}) collective-permute-start(bf16[1024,1024]{1,0:T(8,128)(2,1)} %split_basis.1.refs_0_), channel_id=1, source_target_pairs={{0,1},{1,0},{2,3},{3,2},{4,5},{5,4},{6,7},{7,6},{8,9},{9,8},{10,11... | collective-permute-start | bytes 6291464 | tf_op jit(solution)/shard_map/ppermute | solution.py:253
  8.8 1.6 %copy-start = (bf16[1024,1024]{1,0:T(8,128)(2,1)S(1)}, bf16[1024,1024]{1,0:T(8,128)(2,1)}, u32[]{:S(2)}) copy-start(bf16[1024,1024]{1,0:T(8,128)(2,1)} %split_basis.1.refs_0_) | copy-start | bytes 6291460
  17.0 1.0 copy-start.1
  18.0 45.6 %collective-permute-start.1 = (bf16[2080,128]{1,0:T(8,128)(2,1)S(1)}, bf16[2080,128]{1,0:T(8,128)(2,1)}, u32[]{:S(2)}, u32[]{:S(2)}) collective-permute-start(bf16[2080,128]{1,0:T(8,128)(2,1)S(1)} %get-tuple-element.37), channel_id=1, source_target_pairs={{0,2},{1,3},{2,0},{3,1},{4,6},{5,7},{6,4},{7,5},{8,10},{9,11},{10,... | collective-permute-start | bytes 1597448 | tf_op jit(solution)/shard_map/ppermute | solution.py:253
  28.1 1.0 copy-start.3
  29.1 31.9 %collective-permute-start.9 = (bf16[2080,128]{1,0:T(8,128)(2,1)}, bf16[2080,128]{1,0:T(8,128)(2,1)}, u32[]{:S(2)}, u32[]{:S(2)}) collective-permute-start(bf16[2080,128]{1,0:T(8,128)(2,1)} %get-tuple-element.51), channel_id=1, source_target_pairs={{0,2},{1,3},{2,0},{3,1},{4,6},{5,7},{6,4},{7,5},{8,10},{9,11},{10,... | collective-permute-start | bytes 1597448 | tf_op jit(solution)/shard_map/ppermute | solution.py:253
  35.7 1.0 copy-start.4
  36.7 19.4 %collective-permute-start.13 = (bf16[2080,128]{1,0:T(8,128)(2,1)S(1)}, bf16[2080,128]{1,0:T(8,128)(2,1)S(1)}, u32[]{:S(2)}, u32[]{:S(2)}) collective-permute-start(bf16[2080,128]{1,0:T(8,128)(2,1)S(1)} %get-tuple-element.58), channel_id=1, source_target_pairs={{0,2},{1,3},{2,0},{3,1},{4,6},{5,7},{6,4},{7,5},{8,10},{9,11},{10,... | collective-permute-start | bytes 1597448 | tf_op jit(solution)/shard_map/ppermute | solution.py:253
  45.2 1.0 copy-start.2
  46.2 21.5 %collective-permute-start.5 = (bf16[2080,128]{1,0:T(8,128)(2,1)S(1)}, bf16[2080,128]{1,0:T(8,128)(2,1)S(1)}, u32[]{:S(2)}, u32[]{:S(2)}) collective-permute-start(bf16[2080,128]{1,0:T(8,128)(2,1)S(1)} %get-tuple-element.44), channel_id=1, source_target_pairs={{0,4},{1,5},{2,6},{3,7},{4,0},{5,1},{6,2},{7,3},{8,12},{9,13},{10,... | collective-permute-start | bytes 1597448 | tf_op jit(solution)/shard_map/ppermute | solution.py:253
  56.1 0.8 copy-start.6
  59.2 13.2 %collective-permute-start.14 = (bf16[1056,128]{1,0:T(8,128)(2,1)}, bf16[1056,128]{1,0:T(8,128)(2,1)S(1)}, u32[]{:S(2)}, u32[]{:S(2)}) collective-permute-start(bf16[1056,128]{1,0:T(8,128)(2,1)} %get-tuple-element.60), channel_id=1, source_target_pairs={{0,4},{1,5},{2,6},{3,7},{4,0},{5,1},{6,2},{7,3},{8,12},{9,13},{10,... | collective-permute-start | bytes 811016 | tf_op jit(solution)/shard_map/ppermute | solution.py:253
  63.3 14.3 %collective-permute-start.10 = (bf16[1056,128]{1,0:T(8,128)(2,1)}, bf16[1056,128]{1,0:T(8,128)(2,1)S(1)}, u32[]{:S(2)}, u32[]{:S(2)}) collective-permute-start(bf16[1056,128]{1,0:T(8,128)(2,1)} %get-tuple-element.53), channel_id=1, source_target_pairs={{0,4},{1,5},{2,6},{3,7},{4,0},{5,1},{6,2},{7,3},{8,12},{9,13},{10,... | collective-permute-start | bytes 811016 | tf_op jit(solution)/shard_map/ppermute | solution.py:253
  65.9 15.4 %collective-permute-start.2 = (bf16[1056,128]{1,0:T(8,128)(2,1)}, bf16[1056,128]{1,0:T(8,128)(2,1)S(1)}, u32[]{:S(2)}, u32[]{:S(2)}) collective-permute-start(bf16[1056,128]{1,0:T(8,128)(2,1)} %get-tuple-element.39), channel_id=1, source_target_pairs={{0,4},{1,5},{2,6},{3,7},{4,0},{5,1},{6,2},{7,3},{8,12},{9,13},{10,... | collective-permute-start | bytes 811016 | tf_op jit(solution)/shard_map/ppermute | solution.py:253
  67.7 0.8 copy-start.5
  70.8 15.1 %collective-permute-start.6 = (bf16[1056,128]{1,0:T(8,128)(2,1)}, bf16[1056,128]{1,0:T(8,128)(2,1)S(1)}, u32[]{:S(2)}, u32[]{:S(2)}) collective-permute-start(bf16[1056,128]{1,0:T(8,128)(2,1)} %get-tuple-element.46), channel_id=1, source_target_pairs={{0,2},{1,3},{2,0},{3,1},{4,6},{5,7},{6,4},{7,5},{8,10},{9,11},{10,... | collective-permute-start | bytes 811016 | tf_op jit(solution)/shard_map/ppermute | solution.py:253
  72.4 0.7 copy-start.7
  75.0 14.5 %collective-permute-start.15 = (bf16[544,128]{1,0:T(8,128)(2,1)}, bf16[544,128]{1,0:T(8,128)(2,1)S(1)}, u32[]{:S(2)}, u32[]{:S(2)}) collective-permute-start(bf16[544,128]{1,0:T(8,128)(2,1)} %get-tuple-element.62), channel_id=1, source_target_pairs={{0,8},{1,9},{2,10},{3,11},{4,12},{5,13},{6,14},{7,15},{8,0},{9,1},... | collective-permute-start | bytes 417800 | tf_op jit(solution)/shard_map/ppermute | solution.py:253
  77.6 0.7 copy-start.8
  80.3 14.4 %collective-permute-start.11 = (bf16[544,128]{1,0:T(8,128)(2,1)}, bf16[544,128]{1,0:T(8,128)(2,1)S(1)}, u32[]{:S(2)}, u32[]{:S(2)}) collective-permute-start(bf16[544,128]{1,0:T(8,128)(2,1)} %get-tuple-element.55), channel_id=1, source_target_pairs={{0,8},{1,9},{2,10},{3,11},{4,12},{5,13},{6,14},{7,15},{8,0},{9,1},... | collective-permute-start | bytes 417800 | tf_op jit(solution)/shard_map/ppermute | solution.py:253
  81.3 0.7 copy-start.9
  84.0 15.2 %collective-permute-start.3 = (bf16[544,128]{1,0:T(8,128)(2,1)}, bf16[544,128]{1,0:T(8,128)(2,1)S(1)}, u32[]{:S(2)}, u32[]{:S(2)}) collective-permute-start(bf16[544,128]{1,0:T(8,128)(2,1)} %get-tuple-element.41), channel_id=1, source_target_pairs={{0,8},{1,9},{2,10},{3,11},{4,12},{5,13},{6,14},{7,15},{8,0},{9,1},... | collective-permute-start | bytes 417800 | tf_op jit(solution)/shard_map/ppermute | solution.py:253
  85.9 0.7 copy-start.10
  88.6 13.8 %collective-permute-start.7 = (bf16[544,128]{1,0:T(8,128)(2,1)}, bf16[544,128]{1,0:T(8,128)(2,1)S(1)}, u32[]{:S(2)}, u32[]{:S(2)}) collective-permute-start(bf16[544,128]{1,0:T(8,128)(2,1)} %get-tuple-element.48), channel_id=1, source_target_pairs={{0,8},{1,9},{2,10},{3,11},{4,12},{5,13},{6,14},{7,15},{8,0},{9,1},... | collective-permute-start | bytes 417800 | tf_op jit(solution)/shard_map/ppermute | solution.py:253
  89.6 0.7 copy-start.11
  92.0 15.9 %collective-permute-start.16 = (bf16[32,1024]{1,0:T(8,128)(2,1)}, bf16[32,1024]{1,0:T(8,128)(2,1)S(1)}, u32[]{:S(2)}, u32[]{:S(2)}) collective-permute-start(bf16[32,1024]{1,0:T(8,128)(2,1)} %get-tuple-element.64), channel_id=1, source_target_pairs={{0,1},{1,0},{2,3},{3,2},{4,5},{5,4},{6,7},{7,6},{8,9},{9,8},{10,11... | collective-permute-start | bytes 196616 | tf_op jit(solution)/shard_map/ppermute | solution.py:253
  94.7 0.7 copy-start.12
  97.1 10.8 %collective-permute-start.12 = (bf16[32,1024]{1,0:T(8,128)(2,1)}, bf16[32,1024]{1,0:T(8,128)(2,1)S(1)}, u32[]{:S(2)}, u32[]{:S(2)}) collective-permute-start(bf16[32,1024]{1,0:T(8,128)(2,1)} %get-tuple-element.57), channel_id=1, source_target_pairs={{0,1},{1,0},{2,3},{3,2},{4,5},{5,4},{6,7},{7,6},{8,9},{9,8},{10,11... | collective-permute-start | bytes 196616 | tf_op jit(solution)/shard_map/ppermute | solution.py:253
  99.2 0.7 copy-start.13
  102.4 0.7 copy-start.14
  104.8 3.1 %collective-permute-start.8 = (bf16[32,1024]{1,0:T(8,128)(2,1)}, bf16[32,1024]{1,0:T(8,128)(2,1)S(1)}, u32[]{:S(2)}, u32[]{:S(2)}) collective-permute-start(bf16[32,1024]{1,0:T(8,128)(2,1)} %get-tuple-element.50), channel_id=1, source_target_pairs={{0,1},{1,0},{2,3},{3,2},{4,5},{5,4},{6,7},{7,6},{8,9},{9,8},{10,11... | collective-permute-start | bytes 196616 | tf_op jit(solution)/shard_map/ppermute | solution.py:253
  104.8 3.0 %collective-permute-start.4 = (bf16[32,1024]{1,0:T(8,128)(2,1)}, bf16[32,1024]{1,0:T(8,128)(2,1)S(1)}, u32[]{:S(2)}, u32[]{:S(2)}) collective-permute-start(bf16[32,1024]{1,0:T(8,128)(2,1)} %get-tuple-element.43), channel_id=1, source_target_pairs={{0,1},{1,0},{2,3},{3,2},{4,5},{5,4},{6,7},{7,6},{8,9},{9,8},{10,11... | collective-permute-start | bytes 196616 | tf_op jit(solution)/shard_map/ppermute | solution.py:253

commit v2 on v0

v2 whole, which is shorter than its diff:
```python
import functools

import jax
import jax.numpy as jnp
from jax import lax
from jax.experimental import pallas as pl
from jax.experimental.pallas import tpu as pltpu
from jax.sharding import PartitionSpec as P

LANES = 128
SCALE_ROWS = 16
COLUMNS = 256
HALF_SPAN = 125.0
SPAN = 250.0
TINY = 2.0**-110
MIB = 1 << 20

ORDER = [
    (0, 0), (1, 0), (2, 0), (0, 1), (3, 0), (1, 1), (0, 2), (2, 1),
    (0, 3), (2, 2), (3, 1), (1, 2), (2, 3), (3, 2), (1, 3), (3, 3),
]


def column_bound(values):
    top = jnp.maximum(jnp.max(jnp.abs(values), axis=0, keepdims=True), TINY)
    return (top * 1.008).astype(jnp.bfloat16).astype(jnp.float32)


def encode(values, bound):
    level = jnp.exp2(jnp.abs(values) * (SPAN / bound) - HALF_SPAN)
    return jnp.where(values < 0, -level, level).astype(jnp.bfloat16)


def decode(coded, bound):
    coded = coded.astype(jnp.float32)
    size = (jnp.log2(jnp.abs(coded)) + HALF_SPAN) * (bound * (1.0 / SPAN))
    return jnp.where(coded < 0, -size, size)


def reversed_bits(value, bits):
    out = 0
    for bit in range(bits):
        out |= (value >> bit & 1) << (bits - 1 - bit)
    return out


def split_places(order, bits):
    stay = list(range(1 << bits))
    stages = []
    for bit in order:
        leave = [p for p in stay if reversed_bits(p, bits) >> bit & 1]
        stay = [p for p in stay if not reversed_bits(p, bits) >> bit & 1]
        stages.append((leave, stay))
    return stages


def scale_rows(tiles):
    return -(-tiles // SCALE_ROWS) * SCALE_ROWS


def put_bounds(message_ref, bounds, count):
    tiles = len(bounds)
    spare = scale_rows(tiles) - tiles
    if spare:
        bounds = bounds + [jnp.zeros((spare, LANES), jnp.float32)]
    message_ref[tiles * count :, :] = jnp.concatenate(bounds, axis=0).astype(jnp.bfloat16)


def put_tile(message_ref, kept_ref, tile, blocks, step, leave, stay):
    sent = jnp.concatenate([blocks[p] for p in leave], axis=0)
    bound = column_bound(sent)
    count = len(leave) * step
    message_ref[tile * count : (tile + 1) * count, :] = encode(sent, bound)
    for slot, p in enumerate(stay):
        at = (tile * len(stay) + slot) * step
        kept_ref[at : at + step, :] = blocks[p]
    return bound


def call(kernel, name, ins, outs, after, scratch=(), limit=4, cost=(0, 0, 0)):
    count = len(ins)

    def run(*refs):
        kernel(*refs[:count], *refs[count + len(after) :])

    vmem = pl.BlockSpec(memory_space=pltpu.VMEM)
    return pl.pallas_call(
        run,
        in_specs=[pl.BlockSpec(memory_space=pltpu.SMEM)]
        + [vmem] * (count - 1)
        + [pl.BlockSpec(memory_space=pl.ANY)] * len(after),
        out_specs=[vmem] * len(outs),
        out_shape=outs,
        scratch_shapes=scratch,
        compiler_params=pltpu.CompilerParams(vmem_limit_bytes=limit * MIB),
        cost_estimate=pl.CostEstimate(
            flops=cost[0], bytes_accessed=cost[1], transcendentals=cost[2]
        ),
        name=name,
    )(*ins, *after)


def prepare_kernel(blocks, bits, place_ref, basis_ref, out_ref, turned):
    depth, rows = basis_ref.shape
    step = rows // blocks
    wide = min(depth, 256)
    for at in range(0, depth, wide):
        turned[:, at : at + wide] = basis_ref[at : at + wide, :].T
    for place in range(blocks):
        source = jnp.bitwise_xor(place_ref[1], reversed_bits(place, bits))
        part = turned[pl.ds(pl.multiple_of(source * step, step), step), :]
        high = part.astype(jnp.bfloat16)
        low = (part - high.astype(jnp.float32)).astype(jnp.bfloat16)
        out_ref[place * step : (place + 1) * step, :] = high
        out_ref[rows + place * step : rows + (place + 1) * step, :] = low


def prepare(basis, places, blocks, bits):
    depth, rows = basis.shape
    return call(
        functools.partial(prepare_kernel, blocks, bits),
        "split_basis",
        [places, basis],
        [jax.ShapeDtypeStruct((2 * rows, depth), jnp.bfloat16)],
        [],
        [pltpu.VMEM((rows, depth), jnp.float32)],
        limit=6,
        cost=(2 * depth * rows, 8 * depth * rows, 0),
    )[0]


def product_kernel(pieces, start, width, step, leave, stay, place_ref, w_ref, *refs):
    left = refs[:pieces]
    message_ref, kept_ref = refs[pieces:]
    depth = left[0].shape[1]
    wide = min(width, COLUMNS)
    bounds = []
    for at in range(0, width, wide):
        total = None
        for distance, a_ref in enumerate(left):
            owner = jnp.bitwise_xor(place_ref[0], distance)
            rows = pl.ds(pl.multiple_of(owner * depth, depth), depth)
            part = jnp.dot(
                a_ref[...],
                w_ref[0, rows, start + at : start + at + wide],
                preferred_element_type=jnp.float32,
            )
            total = part if total is None else total + part
        half = total.shape[0] // 2
        total = total[:half] + total[half:]
        for lane in range(0, wide, LANES):
            column = total[:, lane : lane + LANES]
            blocks = {p: column[p * step : (p + 1) * step] for p in leave + stay}
            tile = (at + lane) // LANES
            bounds.append(put_tile(message_ref, kept_ref, tile, blocks, step, leave, stay))
    put_bounds(message_ref, bounds, len(leave) * step)


def outputs(width, step, leave, stay):
    tiles = width // LANES
    sent = tiles * len(leave) * step + scale_rows(tiles)
    return [
        jax.ShapeDtypeStruct((sent, LANES), jnp.bfloat16),
        jax.ShapeDtypeStruct((tiles * len(stay) * step, LANES), jnp.float32),
    ]


def product(left, weights, places, start, width, step, leave, stay, after):
    rows2, depth = left[0].shape
    return call(
        functools.partial(product_kernel, len(left), start, width, step, leave, stay),
        "product",
        [places, weights, *left],
        outputs(width, step, leave, stay),
        after,
        limit=8,
        cost=(
            2 * rows2 * depth * len(left) * width,
            2 * depth * len(left) * width + 4 * rows2 * width,
            rows2 * width // 4,
        ),
    )


def received(message_ref, kept_ref, tile, tiles, count):
    coded = message_ref[tile * count : (tile + 1) * count, :]
    group = tile // SCALE_ROWS * SCALE_ROWS
    at = tiles * count + group
    bounds = message_ref[at : at + SCALE_ROWS, :].astype(jnp.float32)
    bound = bounds[tile - group : tile - group + 1]
    return kept_ref[tile * count : (tile + 1) * count, :] + decode(coded, bound)


def middle_kernel(tiles, step, old, leave, stay, place_ref, message_ref, kept_ref, out_ref, next_ref):
    bounds = []
    for tile in range(tiles):
        column = received(message_ref, kept_ref, tile, tiles, len(old) * step)
        blocks = {p: column[i * step : (i + 1) * step] for i, p in enumerate(old)}
        bounds.append(put_tile(out_ref, next_ref, tile, blocks, step, leave, stay))
    put_bounds(out_ref, bounds, len(leave) * step)


def middle(message, kept, places, width, step, old, leave, stay, after):
    size = width * len(old) * step
    return call(
        functools.partial(middle_kernel, width // LANES, step, old, leave, stay),
        "add_and_split",
        [places, message, kept],
        outputs(width, step, leave, stay),
        after,
        cost=(20 * size, 9 * size, 2 * size),
    )


def last_kernel(tiles, pieces, place_ref, message_ref, kept_ref, *refs):
    outs = refs[:pieces]
    whole = refs[pieces]
    count = whole.shape[0]
    share = count // pieces
    for tile in range(tiles):
        whole[:, tile * LANES : (tile + 1) * LANES] = received(
            message_ref, kept_ref, tile, tiles, count
        )
    for distance in range(pieces):
        owner = jnp.bitwise_xor(place_ref[0], distance)
        rows = whole[pl.ds(pl.multiple_of(owner * share, share), share), :]
        outs[distance][...] = rows.astype(jnp.bfloat16)


def last(message, kept, places, width, step, pieces, after):
    size = width * step
    share = jax.ShapeDtypeStruct((step // pieces, width), jnp.bfloat16)
    return call(
        functools.partial(last_kernel, width // LANES, pieces),
        "add_last",
        [places, message, kept],
        [share] * pieces,
        after,
        [pltpu.VMEM((step, width), jnp.float32)],
        cost=(10 * size, 8 * size, size),
    )


def lay_kernel(pieces, width, place_ref, *refs):
    out_ref = refs[-1]
    at = 0
    for first in range(0, len(refs) - 1, pieces):
        for distance in range(pieces):
            part = refs[first + distance]
            owner = jnp.bitwise_xor(place_ref[0], distance)
            columns = pl.ds(pl.multiple_of(owner * width + at, LANES), part.shape[1])
            out_ref[:, columns] = part[...]
        at += part.shape[1]


def lay(parts, places, pieces, width):
    flat = [part for chunk in parts for part in chunk]
    rows = flat[0].shape[0]
    return call(
        functools.partial(lay_kernel, pieces, width),
        "lay_out",
        [places, *flat],
        [jax.ShapeDtypeStruct((rows, pieces * width), jnp.bfloat16)],
        [],
        cost=(0, 4 * rows * pieces * width, 0),
    )[0]


def swapped(block, apart):
    count = lax.axis_size("row")
    return lax.ppermute(block, "row", [(i, i ^ apart) for i in range(count)])


def on_device(basis, weights):
    axis_len = lax.axis_size("row")
    depth, rows = basis.shape
    pieces = weights.shape[1] // depth
    blocks = axis_len // pieces
    bits = blocks.bit_length() - 1
    piece_bits = pieces.bit_length() - 1
    step = rows // blocks
    width = weights.shape[2]
    me = lax.axis_index("row").astype(jnp.int32)
    column = jnp.bitwise_and(me, pieces - 1)
    places = jnp.stack([column, jnp.right_shift(me, piece_bits)])

    own = prepare(basis, places, blocks, bits)
    left = [own] + [swapped(own, distance) for distance in range(1, pieces)]

    chunk = width // 4
    plain = list(range(bits))
    orders = [plain] * 4
    if bits > 1:
        orders[1] = [1, 0] + plain[2:]
    stages = [split_places(order, bits) for order in orders]

    state = {}
    after = []
    finished = {}
    for index, number in ORDER:
        order = orders[index]
        if number == 0:
            out = product(
                left, weights, places, index * chunk, chunk, step, *stages[index][0], after
            )
        elif number < bits:
            message, kept = state[index]
            old = stages[index][number - 1][1]
            out = middle(message, kept, places, chunk, step, old, *stages[index][number], after)
        else:
            message, kept = state[index]
            out = last(message, kept, places, chunk, step, pieces, after)
            finished[index] = [out[0]] + [swapped(out[d], d) for d in range(1, pieces)]
            after = [out[0]]
            continue
        state[index] = swapped(out[0], pieces << order[number]), out[1]
        after = [out[1]]
    return lay([finished[index] for index in range(4)], places, pieces, width)


def solution(mesh):
    in_specs = (P(("groups", "row"), None), P(("groups", "row"), None, None))
    out_specs = P(("groups", "row"), None)
    return jax.shard_map(
        on_device, mesh=mesh, in_specs=in_specs, out_specs=out_specs, check_vma=False
    )
```

time: 404 us -> 88.2 us (0.22)
  waiting for transfers between devices: 194 us -> 27.2 us
  local copies, waits for them, and re-layouts: 146 us -> 7.36 us
  Pallas kernels: 0 us -> 34.4 us
  matrix products: 31.3 us -> 0 us
  starting transfers between devices: 0.45 us -> 18.9 us
  other arithmetic: 16.2 us -> 0.07 us
  between operations: 13.5 us -> 0.19 us
    reduce_scatter x1 -> x0, waiting for transfers between devices: 181 us -> none  [on_device(): lax.psum_scatter(contract_rows(basis, wide_slab), 'row', scatter_dimensio...]
    gather x15 -> x0, local copies, waits for them, and re-layouts: 81.7 us -> none  [the longest x14 74 us: slot_order(): return jnp.take(blocks, order, axis=0)]
    pallas_call x0 -> x18, Pallas kernels: none -> 34.4 us  [call(): pl.pallas_call(run, in_specs=[pl.BlockSpec(memory_space=pltpu.SMEM)] + [v...]
    dot_general x1 -> x0, matrix products: 31.3 us -> none  [contract_rows(): lax.dot_general(left, right, (((0,), (0,)), ((), ())), precision=lax.Prec...]
    unnamed x27 -> x4, local copies, waits for them, and re-layouts: 35 us -> 7.36 us
    transpose x1 -> x0, local copies, waits for them, and re-layouts: 21.2 us -> none  [on_device(): jnp.transpose(pieces, (1, 0, 2)).reshape(own_count, -1).astype(jnp.float32)]
    ppermute x1 -> x17, starting transfers between devices: 0.45 us -> 18.9 us  [swapped(): return lax.ppermute(block, 'row', [(i, i ^ apart) for i in range(count)])]
    ppermute x1 -> x17, waiting for transfers between devices: 13.1 us -> 27.2 us  [swapped(): return lax.ppermute(block, 'row', [(i, i ^ apart) for i in range(count)])]
  transfers between devices with their start and end apart: 2 -> 17, of which waited for: 2 -> 10; matrix products, arithmetic and copies ran while one was open for 0% -> 0% of each run, Pallas kernels for 0% -> 30%
where the time goes in v2:
time: 88.2 us; the launch traced here: 88.1 us
  Pallas kernels  34.4 us (39%)
  waiting for transfers between devices  27.2 us (31%)
  starting transfers between devices  18.9 us (21%)
  local copies, waits for them, and re-layouts  7.36 us (8%)
    pallas_call x18, Pallas kernels, call(): pl.pallas_call(run, in_specs=[pl.BlockSpec(memory_space=pltpu.SMEM)] + [v...  34.4 us
    ppermute x17, waiting for transfers between devices, swapped(): return lax.ppermute(block, 'row', [(i, i ^ apart) for i in range(count)])  27.2 us
    ppermute x17, starting transfers between devices, swapped(): return lax.ppermute(block, 'row', [(i, i ^ apart) for i in range(count)])  18.9 us
    unnamed x4, local copies, waits for them, and re-layouts  7.36 us
  transfers between devices with their start and end apart: 17, of which 10 were waited for; matrix products, arithmetic and copies ran while one was open for 0% of the time, Pallas kernels for 30%

profile of v2, /device:TPU:0, one launch (start us, length us, event | category | flops | bytes accessed | tf_op | source)
XLA Modules:
  0.0 88.1 jit_solution(7222721818269784905)
XLA Ops:
  0.0 0.1 pad_add_fusion.refs_0_
  0.1 0.0 copy-start.1
  0.1 1.6 %copy-done.1 = f32[1024,512]{1,0:T(8,128)S(1)} copy-done((f32[1024,512]{1,0:T(8,128)S(1)}, f32[1024,512]{1,0:T(8,128)}, u32[]{:S(2)}) %copy-start.1) | copy-done | bytes 2097176
  1.7 1.6 %split_basis.1.refs_2_ = bf16[1024,1024]{1,0:T(8,128)(2,1)S(1)} custom-call(s32[2]{0:T(128)S(1)} %pad_add_fusion.refs_0_, f32[1024,512]{1,0:T(8,128)S(1)} %copy-done.1), custom_call_target="tpu_custom_call" | custom-call | flops 1048576 | bytes 4194304 | tf_op jit(solution)/shard_map/split_basis/pallas_call | solution.py:87
  3.3 0.5 collective-permute-start
  3.8 3.8 %collective-permute-done.refs_3_ = bf16[1024,1024]{1,0:T(8,128)(2,1)S(1)} collective-permute-done((bf16[1024,1024]{1,0:T(8,128)(2,1)S(1)}, bf16[1024,1024]{1,0:T(8,128)(2,1)S(1)}, u32[]{:S(2)}, u32[]{:S(2)}) %collective-permute-start) | collective-permute-done | bytes 2097184 | tf_op jit(solution)/shard_map/ppermute | solution.py:271
  7.6 0.0 copy-start
  7.6 5.8 %copy-done = bf16[1,2048,4096]{2,1,0:T(8,128)(2,1)S(1)} copy-done((bf16[1,2048,4096]{2,1,0:T(8,128)(2,1)S(1)}, bf16[1,2048,4096]{2,1,0:T(8,128)(2,1)}, u32[]{:S(2)}) %copy-start) | copy-done | bytes 16777240
  13.3 5.4 %product.4 = (bf16[2064,128]{1,0:T(8,128)(2,1)S(1)}, f32[2048,128]{1,0:T(8,128)S(1)}) custom-call(s32[2]{0:T(128)S(1)} %pad_add_fusion.refs_0_, bf16[1,2048,4096]{2,1,0:T(8,128)(2,1)S(1)} %copy-done, bf16[1024,1024]{1,0:T(8,128)(2,1)S(1)} %split_basis.1.refs_2_, bf16[1024,1024]{1,0:T(8,128)(2,1)S(1)} %collective-permute-done.refs_3_), custom_call_target="tpu_custom_call" | custom-call | flops 4294967296 | bytes 8388608 | tf_op jit(solution)/shard_map/product/pallas_call | solution.py:87
  18.7 3.0 %collective-permute-start.1 = (bf16[2064,128]{1,0:T(8,128)(2,1)S(1)}, bf16[2064,128]{1,0:T(8,128)(2,1)S(1)}, u32[]{:S(2)}, u32[]{:S(2)}) collective-permute-start(bf16[2064,128]{1,0:T(8,128)(2,1)S(1)} %get-tuple-element.37), channel_id=1, source_target_pairs={{0,2},{1,3},{2,0},{3,1},{4,6},{5,7},{6,4},{7,5},{8,10},{9,11},{10,... | collective-permute-start | bytes 1585160 | tf_op jit(solution)/shard_map/ppermute | solution.py:271
  21.6 5.3 %product.5 = (bf16[2064,128]{1,0:T(8,128)(2,1)S(1)}, f32[2048,128]{1,0:T(8,128)S(1)}) custom-call(s32[2]{0:T(128)S(1)} %pad_add_fusion.refs_0_, bf16[1,2048,4096]{2,1,0:T(8,128)(2,1)S(1)} %copy-done, bf16[1024,1024]{1,0:T(8,128)(2,1)S(1)} %split_basis.1.refs_2_, bf16[1024,1024]{1,0:T(8,128)(2,1)S(1)} %collective-permute-done.refs_3_, ...), custom_call_target="tpu_custom_call" | custom-call | flops 4294967296 | bytes 8388608 | tf_op jit(solution)/shard_map/product/pallas_call | solution.py:87
  27.0 1.7 %collective-permute-start.3 = (bf16[2064,128]{1,0:T(8,128)(2,1)S(1)}, bf16[2064,128]{1,0:T(8,128)(2,1)S(1)}, u32[]{:S(2)}, u32[]{:S(2)}) collective-permute-start(bf16[2064,128]{1,0:T(8,128)(2,1)S(1)} %get-tuple-element.43), channel_id=1, source_target_pairs={{0,4},{1,5},{2,6},{3,7},{4,0},{5,1},{6,2},{7,3},{8,12},{9,13},{10,... | collective-permute-start | bytes 1585160 | tf_op jit(solution)/shard_map/ppermute | solution.py:271
  28.6 5.4 %product.6 = (bf16[2064,128]{1,0:T(8,128)(2,1)S(1)}, f32[2048,128]{1,0:T(8,128)S(1)}) custom-call(s32[2]{0:T(128)S(1)} %pad_add_fusion.refs_0_, bf16[1,2048,4096]{2,1,0:T(8,128)(2,1)S(1)} %copy-done, bf16[1024,1024]{1,0:T(8,128)(2,1)S(1)} %split_basis.1.refs_2_, bf16[1024,1024]{1,0:T(8,128)(2,1)S(1)} %collective-permute-done.refs_3_, ...), custom_call_target="tpu_custom_call" | custom-call | flops 4294967296 | bytes 8388608 | tf_op jit(solution)/shard_map/product/pallas_call | solution.py:87
  34.0 0.6 collective-permute-start.5
  34.6 0.0 collective-permute-done.1.refs_1_
  34.6 1.0 %add_and_split.8 = (bf16[1040,128]{1,0:T(8,128)(2,1)S(1)}, f32[1024,128]{1,0:T(8,128)S(1)}) custom-call(s32[2]{0:T(128)S(1)} %pad_add_fusion.refs_0_, bf16[2064,128]{1,0:T(8,128)(2,1)S(1)} %collective-permute-done.1.refs_1_, f32[2048,128]{1,0:T(8,128)S(1)} %get-tuple-element.38.refs_4_.refs_2_, f32[2048,128]{1,0:T(8,128)S(1)} %get-tuple-element.40.refs_3_.refs_2_), custom_call_target="tpu_custom_call" | custom-call | flops 5242880 | bytes 2359296 | tf_op jit(solution)/shard_map/add_and_split/pallas_call | solution.py:87
  35.6 1.2 %collective-permute-start.2 = (bf16[1040,128]{1,0:T(8,128)(2,1)S(1)}, bf16[1040,128]{1,0:T(8,128)(2,1)S(1)}, u32[]{:S(2)}, u32[]{:S(2)}) collective-permute-start(bf16[1040,128]{1,0:T(8,128)(2,1)S(1)} %get-tuple-element.41), channel_id=1, source_target_pairs={{0,4},{1,5},{2,6},{3,7},{4,0},{5,1},{6,2},{7,3},{8,12},{9,13},{10,... | collective-permute-start | bytes 798728 | tf_op jit(solution)/shard_map/ppermute | solution.py:271
  36.8 5.3 %product.7 = (bf16[2064,128]{1,0:T(8,128)(2,1)S(1)}, f32[2048,128]{1,0:T(8,128)S(1)}) custom-call(s32[2]{0:T(128)S(1)} %pad_add_fusion.refs_0_, bf16[1,2048,4096]{2,1,0:T(8,128)(2,1)S(1)} %copy-done, bf16[1024,1024]{1,0:T(8,128)(2,1)S(1)} %split_basis.1.refs_2_, bf16[1024,1024]{1,0:T(8,128)(2,1)S(1)} %collective-permute-done.refs_3_, ...), custom_call_target="tpu_custom_call" | custom-call | flops 4294967296 | bytes 8388608 | tf_op jit(solution)/shard_map/product/pallas_call | solution.py:87
  42.2 1.7 %collective-permute-start.8 = (bf16[2064,128]{1,0:T(8,128)(2,1)S(1)}, bf16[2064,128]{1,0:T(8,128)(2,1)S(1)}, u32[]{:S(2)}, u32[]{:S(2)}) collective-permute-start(bf16[2064,128]{1,0:T(8,128)(2,1)S(1)} %get-tuple-element.53), channel_id=1, source_target_pairs={{0,2},{1,3},{2,0},{3,1},{4,6},{5,7},{6,4},{7,5},{8,10},{9,11},{10,... | collective-permute-start | bytes 1585160 | tf_op jit(solution)/shard_map/ppermute | solution.py:271
  44.0 0.0 collective-permute-done.3.refs_1_
  44.0 1.2 %add_and_split.9 = (bf16[1040,128]{1,0:T(8,128)(2,1)S(1)}, f32[1024,128]{1,0:T(8,128)S(1)}) custom-call(s32[2]{0:T(128)S(1)} %pad_add_fusion.refs_0_, bf16[2064,128]{1,0:T(8,128)(2,1)S(1)} %collective-permute-done.3.refs_1_, f32[2048,128]{1,0:T(8,128)S(1)} %get-tuple-element.39.refs_4_.refs_2_, f32[2048,128]{1,0:T(8,128)S(1)} %get-tuple-element.44.refs_3_.refs_2_), custom_call_target="tpu_custom_call" | custom-call | flops 5242880 | bytes 2359296 | tf_op jit(solution)/shard_map/add_and_split/pallas_call | solution.py:87
  45.2 1.4 %collective-permute-done.2.refs_1_ = bf16[1040,128]{1,0:T(8,128)(2,1)S(1)} collective-permute-done((bf16[1040,128]{1,0:T(8,128)(2,1)S(1)}, bf16[1040,128]{1,0:T(8,128)(2,1)S(1)}, u32[]{:S(2)}, u32[]{:S(2)}) %collective-permute-start.2) | collective-permute-done | bytes 266272 | tf_op jit(solution)/shard_map/ppermute | solution.py:271
  46.5 0.8 add_and_split.10
  47.3 1.7 %collective-permute-done.5.refs_1_ = bf16[2064,128]{1,0:T(8,128)(2,1)S(1)} collective-permute-done((bf16[2064,128]{1,0:T(8,128)(2,1)S(1)}, bf16[2064,128]{1,0:T(8,128)(2,1)S(1)}, u32[]{:S(2)}, u32[]{:S(2)}) %collective-permute-start.5) | collective-permute-done | bytes 528416 | tf_op jit(solution)/shard_map/ppermute | solution.py:271
  49.0 1.0 %add_and_split.11 = (bf16[1040,128]{1,0:T(8,128)(2,1)S(1)}, f32[1024,128]{1,0:T(8,128)S(1)}) custom-call(s32[2]{0:T(128)S(1)} %pad_add_fusion.refs_0_, bf16[2064,128]{1,0:T(8,128)(2,1)S(1)} %collective-permute-done.5.refs_1_, f32[2048,128]{1,0:T(8,128)S(1)} %get-tuple-element.40.refs_3_.refs_2_, f32[512,128]{1,0:T(8,128)S(1)} %get-tuple-element.47.refs_3_.refs_2_), custom_call_target="tpu_custom_call" | custom-call | flops 5242880 | bytes 2359296 | tf_op jit(solution)/shard_map/add_and_split/pallas_call | solution.py:87
  50.0 0.5 collective-permute-start.9
  50.5 2.6 %collective-permute-start.4 = (bf16[528,128]{1,0:T(8,128)(2,1)S(1)}, bf16[528,128]{1,0:T(8,128)(2,1)S(1)}, u32[]{:S(2)}, u32[]{:S(2)}) collective-permute-start(bf16[528,128]{1,0:T(8,128)(2,1)S(1)} %get-tuple-element.46), channel_id=1, source_target_pairs={{0,8},{1,9},{2,10},{3,11},{4,12},{5,13},{6,14},{7,15},{8,0},{9,1},... | collective-permute-start | bytes 405512 | tf_op jit(solution)/shard_map/ppermute | solution.py:271
  53.2 0.5 collective-permute-start.7
  53.7 4.2 %collective-permute-done.4.refs_1_ = bf16[528,128]{1,0:T(8,128)(2,1)S(1)} collective-permute-done((bf16[528,128]{1,0:T(8,128)(2,1)S(1)}, bf16[528,128]{1,0:T(8,128)(2,1)S(1)}, u32[]{:S(2)}, u32[]{:S(2)}) %collective-permute-start.4) | collective-permute-done | bytes 135200 | tf_op jit(solution)/shard_map/ppermute | solution.py:271
  57.9 0.6 add_last.4
  58.5 0.1 collective-permute-done.9.refs_1_
  58.6 0.8 add_and_split.12
  59.4 0.9 %collective-permute-done.8.refs_1_ = bf16[2064,128]{1,0:T(8,128)(2,1)S(1)} collective-permute-done((bf16[2064,128]{1,0:T(8,128)(2,1)S(1)}, bf16[2064,128]{1,0:T(8,128)(2,1)S(1)}, u32[]{:S(2)}, u32[]{:S(2)}) %collective-permute-start.8) | collective-permute-done | bytes 528416 | tf_op jit(solution)/shard_map/ppermute | solution.py:271
  60.3 1.0 %add_and_split.13 = (bf16[1040,128]{1,0:T(8,128)(2,1)S(1)}, f32[1024,128]{1,0:T(8,128)S(1)}) custom-call(s32[2]{0:T(128)S(1)} %pad_add_fusion.refs_0_, bf16[2064,128]{1,0:T(8,128)(2,1)S(1)} %collective-permute-done.8.refs_1_, f32[2048,128]{1,0:T(8,128)S(1)} %get-tuple-element.44.refs_3_.refs_2_, f32[512,128]{1,0:T(8,128)S(1)} %get-tuple-element.55.refs_3_.refs_2_), custom_call_target="tpu_custom_call" | custom-call | flops 5242880 | bytes 2359296 | tf_op jit(solution)/shard_map/add_and_split/pallas_call | solution.py:87
  61.4 2.4 %collective-permute-start.11 = (bf16[1040,128]{1,0:T(8,128)(2,1)S(1)}, bf16[1040,128]{1,0:T(8,128)(2,1)S(1)}, u32[]{:S(2)}, u32[]{:S(2)}) collective-permute-start(bf16[1040,128]{1,0:T(8,128)(2,1)S(1)} %get-tuple-element.59), channel_id=1, source_target_pairs={{0,4},{1,5},{2,6},{3,7},{4,0},{5,1},{6,2},{7,3},{8,12},{9,13},{10,... | collective-permute-start | bytes 798728 | tf_op jit(solution)/shard_map/ppermute | solution.py:271
  63.8 1.0 %collective-permute-start.12 = (bf16[528,128]{1,0:T(8,128)(2,1)S(1)}, bf16[528,128]{1,0:T(8,128)(2,1)S(1)}, u32[]{:S(2)}, u32[]{:S(2)}) collective-permute-start(bf16[528,128]{1,0:T(8,128)(2,1)S(1)} %get-tuple-element.60), channel_id=1, source_target_pairs={{0,8},{1,9},{2,10},{3,11},{4,12},{5,13},{6,14},{7,15},{8,0},{9,1},... | collective-permute-start | bytes 405512 | tf_op jit(solution)/shard_map/ppermute | solution.py:271
  64.7 0.0 collective-permute-done.7.refs_1_
  64.7 0.8 add_and_split.14
  65.5 2.5 %collective-permute-start.10 = (bf16[528,128]{1,0:T(8,128)(2,1)S(1)}, bf16[528,128]{1,0:T(8,128)(2,1)S(1)}, u32[]{:S(2)}, u32[]{:S(2)}) collective-permute-start(bf16[528,128]{1,0:T(8,128)(2,1)S(1)} %get-tuple-element.57), channel_id=1, source_target_pairs={{0,8},{1,9},{2,10},{3,11},{4,12},{5,13},{6,14},{7,15},{8,0},{9,1},... | collective-permute-start | bytes 405512 | tf_op jit(solution)/shard_map/ppermute | solution.py:271
  68.0 9.3 %collective-permute-done.12.refs_1_ = bf16[528,128]{1,0:T(8,128)(2,1)S(1)} collective-permute-done((bf16[528,128]{1,0:T(8,128)(2,1)S(1)}, bf16[528,128]{1,0:T(8,128)(2,1)S(1)}, u32[]{:S(2)}, u32[]{:S(2)}) %collective-permute-start.12) | collective-permute-done | bytes 135200 | tf_op jit(solution)/shard_map/ppermute | solution.py:271
  77.3 0.6 add_last.5
  77.9 0.0 collective-permute-done.11.refs_1_
  78.0 0.8 add_and_split.15
  78.8 0.1 collective-permute-start.15
  78.8 0.1 collective-permute-start.6
  78.9 0.5 collective-permute-start.14
  79.4 0.6 collective-permute-done.10.refs_1_
  80.1 0.6 add_last.6
  80.7 0.1 collective-permute-start.13
  80.8 4.0 %collective-permute-done.15.refs_1_ = bf16[528,128]{1,0:T(8,128)(2,1)S(1)} collective-permute-done((bf16[528,128]{1,0:T(8,128)(2,1)S(1)}, bf16[528,128]{1,0:T(8,128)(2,1)S(1)}, u32[]{:S(2)}, u32[]{:S(2)}) %collective-permute-start.15) | collective-permute-done | bytes 135200 | tf_op jit(solution)/shard_map/ppermute | solution.py:271
  84.7 0.6 add_last.7
  85.4 0.1 collective-permute-start.16
  85.5 0.0 collective-permute-done.6.refs_2_
  85.5 0.0 collective-permute-done.14.refs_6_
  85.5 0.0 collective-permute-done.13.refs_4_
  85.5 1.2 %collective-permute-done.16.refs_8_ = bf16[32,1024]{1,0:T(8,128)(2,1)S(1)} collective-permute-done((bf16[32,1024]{1,0:T(8,128)(2,1)S(1)}, bf16[32,1024]{1,0:T(8,128)(2,1)S(1)}, u32[]{:S(2)}, u32[]{:S(2)}) %collective-permute-start.16) | collective-permute-done | bytes 65568 | tf_op jit(solution)/shard_map/ppermute | solution.py:271
  86.7 1.4 %lay_out.1 = bf16[32,8192]{1,0:T(8,128)(2,1)} custom-call(s32[2]{0:T(128)S(1)} %pad_add_fusion.refs_0_, bf16[32,1024]{1,0:T(8,128)(2,1)S(1)} %get-tuple-element.50.refs_3_.refs_1_, bf16[32,1024]{1,0:T(8,128)(2,1)S(1)} %collective-permute-done.6.refs_2_, bf16[32,1024]{1,0:T(8,128)(2,1)S(1)} %get-tuple-element.63.refs_3_, ...), custom_call_target="tpu_custom_call" | custom-call | bytes 1048576 | tf_op jit(solution)/shard_map/lay_out/pallas_call | solution.py:87
Async XLA Ops:
  0.1 1.6 %copy-start.1 = (f32[1024,512]{1,0:T(8,128)S(1)}, f32[1024,512]{1,0:T(8,128)}, u32[]{:S(2)}) copy-start(f32[1024,512]{1,0:T(8,128)} %refs_1_.5) | copy-start | bytes 6291460
  3.3 4.3 %collective-permute-start = (bf16[1024,1024]{1,0:T(8,128)(2,1)S(1)}, bf16[1024,1024]{1,0:T(8,128)(2,1)S(1)}, u32[]{:S(2)}, u32[]{:S(2)}) collective-permute-start(bf16[1024,1024]{1,0:T(8,128)(2,1)S(1)} %split_basis.1.refs_2_), channel_id=1, source_target_pairs={{0,1},{1,0},{2,3},{3,2},{4,5},{5,4},{6,7},{7,6},{8,9},{9,8},{10,11... | collective-permute-start | bytes 6291464 | tf_op jit(solution)/shard_map/ppermute | solution.py:271
  7.6 5.8 %copy-start = (bf16[1,2048,4096]{2,1,0:T(8,128)(2,1)S(1)}, bf16[1,2048,4096]{2,1,0:T(8,128)(2,1)}, u32[]{:S(2)}) copy-start(bf16[1,2048,4096]{2,1,0:T(8,128)(2,1)} %refs_1_.9) | copy-start | bytes 50331652
  18.7 15.9 %collective-permute-start.1 = (bf16[2064,128]{1,0:T(8,128)(2,1)S(1)}, bf16[2064,128]{1,0:T(8,128)(2,1)S(1)}, u32[]{:S(2)}, u32[]{:S(2)}) collective-permute-start(bf16[2064,128]{1,0:T(8,128)(2,1)S(1)} %get-tuple-element.37), channel_id=1, source_target_pairs={{0,2},{1,3},{2,0},{3,1},{4,6},{5,7},{6,4},{7,5},{8,10},{9,11},{10,... | collective-permute-start | bytes 1585160 | tf_op jit(solution)/shard_map/ppermute | solution.py:271
  27.0 17.0 %collective-permute-start.3 = (bf16[2064,128]{1,0:T(8,128)(2,1)S(1)}, bf16[2064,128]{1,0:T(8,128)(2,1)S(1)}, u32[]{:S(2)}, u32[]{:S(2)}) collective-permute-start(bf16[2064,128]{1,0:T(8,128)(2,1)S(1)} %get-tuple-element.43), channel_id=1, source_target_pairs={{0,4},{1,5},{2,6},{3,7},{4,0},{5,1},{6,2},{7,3},{8,12},{9,13},{10,... | collective-permute-start | bytes 1585160 | tf_op jit(solution)/shard_map/ppermute | solution.py:271
  34.0 15.0 %collective-permute-start.5 = (bf16[2064,128]{1,0:T(8,128)(2,1)S(1)}, bf16[2064,128]{1,0:T(8,128)(2,1)S(1)}, u32[]{:S(2)}, u32[]{:S(2)}) collective-permute-start(bf16[2064,128]{1,0:T(8,128)(2,1)S(1)} %get-tuple-element.48), channel_id=1, source_target_pairs={{0,2},{1,3},{2,0},{3,1},{4,6},{5,7},{6,4},{7,5},{8,10},{9,11},{10,... | collective-permute-start | bytes 1585160 | tf_op jit(solution)/shard_map/ppermute | solution.py:271
  35.6 10.9 %collective-permute-start.2 = (bf16[1040,128]{1,0:T(8,128)(2,1)S(1)}, bf16[1040,128]{1,0:T(8,128)(2,1)S(1)}, u32[]{:S(2)}, u32[]{:S(2)}) collective-permute-start(bf16[1040,128]{1,0:T(8,128)(2,1)S(1)} %get-tuple-element.41), channel_id=1, source_target_pairs={{0,4},{1,5},{2,6},{3,7},{4,0},{5,1},{6,2},{7,3},{8,12},{9,13},{10,... | collective-permute-start | bytes 798728 | tf_op jit(solution)/shard_map/ppermute | solution.py:271
  42.2 18.1 %collective-permute-start.8 = (bf16[2064,128]{1,0:T(8,128)(2,1)S(1)}, bf16[2064,128]{1,0:T(8,128)(2,1)S(1)}, u32[]{:S(2)}, u32[]{:S(2)}) collective-permute-start(bf16[2064,128]{1,0:T(8,128)(2,1)S(1)} %get-tuple-element.53), channel_id=1, source_target_pairs={{0,2},{1,3},{2,0},{3,1},{4,6},{5,7},{6,4},{7,5},{8,10},{9,11},{10,... | collective-permute-start | bytes 1585160 | tf_op jit(solution)/shard_map/ppermute | solution.py:271
  50.0 8.6 %collective-permute-start.9 = (bf16[1040,128]{1,0:T(8,128)(2,1)S(1)}, bf16[1040,128]{1,0:T(8,128)(2,1)S(1)}, u32[]{:S(2)}, u32[]{:S(2)}) collective-permute-start(bf16[1040,128]{1,0:T(8,128)(2,1)S(1)} %get-tuple-element.54), channel_id=1, source_target_pairs={{0,4},{1,5},{2,6},{3,7},{4,0},{5,1},{6,2},{7,3},{8,12},{9,13},{10,... | collective-permute-start | bytes 798728 | tf_op jit(solution)/shard_map/ppermute | solution.py:271
  50.5 7.3 %collective-permute-start.4 = (bf16[528,128]{1,0:T(8,128)(2,1)S(1)}, bf16[528,128]{1,0:T(8,128)(2,1)S(1)}, u32[]{:S(2)}, u32[]{:S(2)}) collective-permute-start(bf16[528,128]{1,0:T(8,128)(2,1)S(1)} %get-tuple-element.46), channel_id=1, source_target_pairs={{0,8},{1,9},{2,10},{3,11},{4,12},{5,13},{6,14},{7,15},{8,0},{9,1},... | collective-permute-start | bytes 405512 | tf_op jit(solution)/shard_map/ppermute | solution.py:271
  53.2 11.6 %collective-permute-start.7 = (bf16[1040,128]{1,0:T(8,128)(2,1)S(1)}, bf16[1040,128]{1,0:T(8,128)(2,1)S(1)}, u32[]{:S(2)}, u32[]{:S(2)}) collective-permute-start(bf16[1040,128]{1,0:T(8,128)(2,1)S(1)} %get-tuple-element.52), channel_id=1, source_target_pairs={{0,2},{1,3},{2,0},{3,1},{4,6},{5,7},{6,4},{7,5},{8,10},{9,11},{10,... | collective-permute-start | bytes 798728 | tf_op jit(solution)/shard_map/ppermute | solution.py:271
  61.4 16.6 %collective-permute-start.11 = (bf16[1040,128]{1,0:T(8,128)(2,1)S(1)}, bf16[1040,128]{1,0:T(8,128)(2,1)S(1)}, u32[]{:S(2)}, u32[]{:S(2)}) collective-permute-start(bf16[1040,128]{1,0:T(8,128)(2,1)S(1)} %get-tuple-element.59), channel_id=1, source_target_pairs={{0,4},{1,5},{2,6},{3,7},{4,0},{5,1},{6,2},{7,3},{8,12},{9,13},{10,... | collective-permute-start | bytes 798728 | tf_op jit(solution)/shard_map/ppermute | solution.py:271
  63.8 13.5 %collective-permute-start.12 = (bf16[528,128]{1,0:T(8,128)(2,1)S(1)}, bf16[528,128]{1,0:T(8,128)(2,1)S(1)}, u32[]{:S(2)}, u32[]{:S(2)}) collective-permute-start(bf16[528,128]{1,0:T(8,128)(2,1)S(1)} %get-tuple-element.60), channel_id=1, source_target_pairs={{0,8},{1,9},{2,10},{3,11},{4,12},{5,13},{6,14},{7,15},{8,0},{9,1},... | collective-permute-start | bytes 405512 | tf_op jit(solution)/shard_map/ppermute | solution.py:271
  65.5 14.5 %collective-permute-start.10 = (bf16[528,128]{1,0:T(8,128)(2,1)S(1)}, bf16[528,128]{1,0:T(8,128)(2,1)S(1)}, u32[]{:S(2)}, u32[]{:S(2)}) collective-permute-start(bf16[528,128]{1,0:T(8,128)(2,1)S(1)} %get-tuple-element.57), channel_id=1, source_target_pairs={{0,8},{1,9},{2,10},{3,11},{4,12},{5,13},{6,14},{7,15},{8,0},{9,1},... | collective-permute-start | bytes 405512 | tf_op jit(solution)/shard_map/ppermute | solution.py:271
  78.8 6.0 %collective-permute-start.15 = (bf16[528,128]{1,0:T(8,128)(2,1)S(1)}, bf16[528,128]{1,0:T(8,128)(2,1)S(1)}, u32[]{:S(2)}, u32[]{:S(2)}) collective-permute-start(bf16[528,128]{1,0:T(8,128)(2,1)S(1)} %get-tuple-element.66), channel_id=1, source_target_pairs={{0,8},{1,9},{2,10},{3,11},{4,12},{5,13},{6,14},{7,15},{8,0},{9,1},... | collective-permute-start | bytes 405512 | tf_op jit(solution)/shard_map/ppermute | solution.py:271
  78.8 6.6 %collective-permute-start.6 = (bf16[32,1024]{1,0:T(8,128)(2,1)S(1)}, bf16[32,1024]{1,0:T(8,128)(2,1)S(1)}, u32[]{:S(2)}, u32[]{:S(2)}) collective-permute-start(bf16[32,1024]{1,0:T(8,128)(2,1)S(1)} %get-tuple-element.51), channel_id=1, source_target_pairs={{0,1},{1,0},{2,3},{3,2},{4,5},{5,4},{6,7},{7,6},{8,9},{9,8},{10,11... | collective-permute-start | bytes 196616 | tf_op jit(solution)/shard_map/ppermute | solution.py:271
  78.9 6.6 %collective-permute-start.14 = (bf16[32,1024]{1,0:T(8,128)(2,1)S(1)}, bf16[32,1024]{1,0:T(8,128)(2,1)S(1)}, u32[]{:S(2)}, u32[]{:S(2)}) collective-permute-start(bf16[32,1024]{1,0:T(8,128)(2,1)S(1)} %get-tuple-element.65), channel_id=1, source_target_pairs={{0,1},{1,0},{2,3},{3,2},{4,5},{5,4},{6,7},{7,6},{8,9},{9,8},{10,11... | collective-permute-start | bytes 196616 | tf_op jit(solution)/shard_map/ppermute | solution.py:271
  80.7 4.8 %collective-permute-start.13 = (bf16[32,1024]{1,0:T(8,128)(2,1)S(1)}, bf16[32,1024]{1,0:T(8,128)(2,1)S(1)}, u32[]{:S(2)}, u32[]{:S(2)}) collective-permute-start(bf16[32,1024]{1,0:T(8,128)(2,1)S(1)} %get-tuple-element.64), channel_id=1, source_target_pairs={{0,1},{1,0},{2,3},{3,2},{4,5},{5,4},{6,7},{7,6},{8,9},{9,8},{10,11... | collective-permute-start | bytes 196616 | tf_op jit(solution)/shard_map/ppermute | solution.py:271
  85.4 1.3 %collective-permute-start.16 = (bf16[32,1024]{1,0:T(8,128)(2,1)S(1)}, bf16[32,1024]{1,0:T(8,128)(2,1)S(1)}, u32[]{:S(2)}, u32[]{:S(2)}) collective-permute-start(bf16[32,1024]{1,0:T(8,128)(2,1)S(1)} %get-tuple-element.68), channel_id=1, source_target_pairs={{0,1},{1,0},{2,3},{3,2},{4,5},{5,4},{6,7},{7,6},{8,9},{9,8},{10,11... | collective-permute-start | bytes 196616 | tf_op jit(solution)/shard_map/ppermute | solution.py:271

commit v3 on v2

--- a/solution.py
+++ b/solution.py
@@ -15,6 +15,9 @@
 TINY = 2.0**-110
 MIB = 1 << 20
 
+CHUNKS = [(4, (0, 1, 2)), (4, (1, 0, 2)), (4, (0, 1, 2)), (4, (0, 1, 2))]
+PARTS = 16
+EARLY = 2
 ORDER = [
     (0, 0), (1, 0), (2, 0), (0, 1), (3, 0), (1, 1), (0, 2), (2, 1),
     (0, 3), (2, 2), (3, 1), (1, 2), (2, 3), (3, 2), (1, 3), (3, 3),
@@ -77,17 +80,20 @@
     return bound
 
 
-def call(kernel, name, ins, outs, after, scratch=(), limit=4, cost=(0, 0, 0)):
+def call(kernel, name, ins, outs, after, scratch=(), limit=4, cost=(0, 0, 0), far=0):
     count = len(ins)
 
     def run(*refs):
         kernel(*refs[:count], *refs[count + len(after) :])
 
     vmem = pl.BlockSpec(memory_space=pltpu.VMEM)
+    near = count - far
+    ins = ins[:near] + [pltpu.with_memory_space_constraint(x, pltpu.HBM) for x in ins[near:]]
     return pl.pallas_call(
         run,
         in_specs=[pl.BlockSpec(memory_space=pltpu.SMEM)]
-        + [vmem] * (count - 1)
+        + [vmem] * (count - 1 - far)
+        + [pl.BlockSpec(memory_space=pltpu.HBM)] * far
         + [pl.BlockSpec(memory_space=pl.ANY)] * len(after),
         out_specs=[vmem] * len(outs),
         out_shape=outs,
@@ -100,54 +106,129 @@
     )(*ins, *after)
 
 
-def prepare_kernel(blocks, bits, place_ref, basis_ref, out_ref, turned):
+def prepare_kernel(blocks, bits, wide, place_ref, basis_ref, out_ref, held, turned, sems):
     depth, rows = basis_ref.shape
     step = rows // blocks
-    wide = min(depth, 256)
-    for at in range(0, depth, wide):
-        turned[:, at : at + wide] = basis_ref[at : at + wide, :].T
-    for place in range(blocks):
-        source = jnp.bitwise_xor(place_ref[1], reversed_bits(place, bits))
-        part = turned[pl.ds(pl.multiple_of(source * step, step), step), :]
-        high = part.astype(jnp.bfloat16)
-        low = (part - high.astype(jnp.float32)).astype(jnp.bfloat16)
-        out_ref[place * step : (place + 1) * step, :] = high
-        out_ref[rows + place * step : rows + (place + 1) * step, :] = low
+    copies = []
+    for index, at in enumerate(range(0, depth, wide)):
+        part = pl.ds(at, wide)
+        copies.append(
+            pltpu.make_async_copy(basis_ref.at[part, :], held.at[part, :], sems.at[index])
+        )
+        copies[-1].start()
+    for index, at in enumerate(range(0, depth, wide)):
+        copies[index].wait()
+        turned[:, at : at + wide] = held[at : at + wide, :].T
+        for place in range(blocks):
+            source = jnp.bitwise_xor(place_ref[1], reversed_bits(place, bits))
+            part = turned[pl.ds(pl.multiple_of(source * step, step), step), at : at + wide]
+            high = part.astype(jnp.bfloat16)
+            low = (part - high.astype(jnp.float32)).astype(jnp.bfloat16)
+            out_ref[place * step : (place + 1) * step, at : at + wide] = high
+            out_ref[rows + place * step : rows + (place + 1) * step, at : at + wide] = low
 
 
 def prepare(basis, places, blocks, bits):
     depth, rows = basis.shape
-    return call(
-        functools.partial(prepare_kernel, blocks, bits),
+    wide = min(depth, COLUMNS)
+    return call(
+        functools.partial(prepare_kernel, blocks, bits, wide),
         "split_basis",
         [places, basis],
         [jax.ShapeDtypeStruct((2 * rows, depth), jnp.bfloat16)],
         [],
-        [pltpu.VMEM((rows, depth), jnp.float32)],
-        limit=6,
+        [
+            pltpu.VMEM((depth, rows), jnp.float32),
+            pltpu.VMEM((rows, depth), jnp.float32),
+            pltpu.SemaphoreType.DMA((depth // wide,)),
+        ],
+        limit=10,
         cost=(2 * depth * rows, 8 * depth * rows, 0),
+        far=1,
     )[0]
 
 
-def product_kernel(pieces, start, width, step, leave, stay, place_ref, w_ref, *refs):
+def spans(width, wide):
+    return [(at, min(wide, width - at)) for at in range(0, width, wide)]
+
+
+def halves_added(product):
+    half = product.shape[0] // 2
+    return product[:half] + product[half:]
+
+
+def early_kernel(pieces, width, place_ref, own_ref, w_ref, near_ref, partial_ref, sems):
+    depth = own_ref.shape[1]
+    full = w_ref.shape[2]
+    copies = []
+
+    def bring(distance, at, wide):
+        owner = jnp.bitwise_xor(place_ref[0], distance)
+        rows = pl.ds(pl.multiple_of(owner * depth, depth), depth)
+        copy = pltpu.make_async_copy(
+            w_ref.at[0, rows, pl.ds(at, wide)],
+            near_ref.at[pl.ds(distance * depth, depth), pl.ds(at, wide)],
+            sems.at[len(copies)],
+        )
+        copy.start()
+        copies.append(copy)
+
+    first = spans(width, COLUMNS)
+    for at, wide in first:
+        bring(0, at, wide)
+    for index, (at, wide) in enumerate(first):
+        copies[index].wait()
+        if index == 0:
+            if full > width:
+                bring(0, width, full - width)
+            for distance in range(1, pieces):
+                bring(distance, 0, full)
+        part = jnp.dot(
+            own_ref[...],
+            near_ref[0:depth, at : at + wide],
+            preferred_element_type=jnp.float32,
+        )
+        partial_ref[:, at : at + wide] = halves_added(part)
+    for copy in copies[len(first) :]:
+        copy.wait()
+
+
+def early(own, weights, places, pieces, width, after):
+    rows2, depth = own.shape
+    full = weights.shape[2]
+    return call(
+        functools.partial(early_kernel, pieces, width),
+        "early_products",
+        [places, own, weights],
+        [
+            jax.ShapeDtypeStruct((pieces * depth, full), jnp.bfloat16),
+            jax.ShapeDtypeStruct((rows2 // 2, width), jnp.float32),
+        ],
+        after,
+        [pltpu.SemaphoreType.DMA((len(spans(width, COLUMNS)) + pieces,))],
+        limit=8,
+        cost=(2 * rows2 * depth * width, 2 * pieces * depth * full, 0),
+        far=1,
+    )
+
+
+def product_kernel(pieces, start, width, early, step, leave, stay, place_ref, near_ref, *refs):
     left = refs[:pieces]
-    message_ref, kept_ref = refs[pieces:]
+    message_ref, kept_ref = refs[-2:]
     depth = left[0].shape[1]
-    wide = min(width, COLUMNS)
+    used = left[1:] if early else left
+    low = depth if early else 0
     bounds = []
-    for at in range(0, width, wide):
-        total = None
-        for distance, a_ref in enumerate(left):
-            owner = jnp.bitwise_xor(place_ref[0], distance)
-            rows = pl.ds(pl.multiple_of(owner * depth, depth), depth)
-            part = jnp.dot(
-                a_ref[...],
-                w_ref[0, rows, start + at : start + at + wide],
-                preferred_element_type=jnp.float32,
-            )
-            total = part if total is None else total + part
-        half = total.shape[0] // 2
-        total = total[:half] + total[half:]
+    for at, wide in spans(width, COLUMNS):
+        columns = slice(start + at, start + at + wide)
+        total = jnp.dot(
+            jnp.concatenate([a_ref[...] for a_ref in used], axis=1),
+            near_ref[low : pieces * depth, columns],
+            preferred_element_type=jnp.float32,
+        )
+        total = halves_added(total)
+        if early:
+            total = total + refs[pieces][:, columns]
         for lane in range(0, wide, LANES):
             column = total[:, lane : lane + LANES]
             blocks = {p: column[p * step : (p + 1) * step] for p in leave + stay}
@@ -165,18 +246,22 @@
     ]
 
 
-def product(left, weights, places, start, width, step, leave, stay, after):
+def product(left, near, partial, places, start, width, step, leave, stay, after):
     rows2, depth = left[0].shape
-    return call(
-        functools.partial(product_kernel, len(left), start, width, step, leave, stay),
+    early = partial is not None
+    count = len(left) - 1 if early else len(left)
+    return call(
+        functools.partial(
+            product_kernel, len(left), start, width, early, step, leave, stay
+        ),
         "product",
-        [places, weights, *left],
+        [places, near, *left] + ([partial] if early else []),
         outputs(width, step, leave, stay),
         after,
         limit=8,
         cost=(
-            2 * rows2 * depth * len(left) * width,
-            2 * depth * len(left) * width + 4 * rows2 * width,
+            2 * rows2 * depth * count * width,
+            2 * depth * count * width + 4 * rows2 * width,
             rows2 * width // 4,
         ),
     )
@@ -287,21 +372,27 @@
     own = prepare(basis, places, blocks, bits)
     left = [own] + [swapped(own, distance) for distance in range(1, pieces)]
 
-    chunk = width // 4
-    plain = list(range(bits))
-    orders = [plain] * 4
-    if bits > 1:
-        orders[1] = [1, 0] + plain[2:]
+    cuts = [0]
+    for share, _ in CHUNKS:
+        cuts.append(cuts[-1] + share)
+    cuts = [cut * (width // LANES) // PARTS * LANES for cut in cuts]
+    orders = [[bit for bit in order if bit < bits] for _, order in CHUNKS]
     stages = [split_places(order, bits) for order in orders]
+    near, partial = early(own, weights, places, pieces, cuts[EARLY], [])
 
     state = {}
-    after = []
+    after = [partial]
     finished = {}
     for index, number in ORDER:
         order = orders[index]
+        start = cuts[index]
+        chunk = cuts[index + 1] - start
+        if chunk == 0:
+            continue
         if number == 0:
+            begun = partial if index < EARLY else None
             out = product(
-                left, weights, places, index * chunk, chunk, step, *stages[index][0], after
+                left, near, begun, places, start, chunk, step, *stages[index][0], after
             )
         elif number < bits:
             message, kept = state[index]
@@ -315,7 +406,7 @@
             continue
         state[index] = swapped(out[0], pieces << order[number]), out[1]
         after = [out[1]]
-    return lay([finished[index] for index in range(4)], places, pieces, width)
+    return lay([finished[index] for index in sorted(finished)], places, pieces, width)
 
 
 def solution(mesh):

time: 88.2 us -> 85.5 us (0.969)
  Pallas kernels: 34.4 us -> 42.8 us
  local copies, waits for them, and re-layouts: 7.36 us -> 0 us
  waiting for transfers between devices: 27.2 us -> 20.6 us
  starting transfers between devices: 18.9 us -> 21.6 us
    pallas_call x18 -> x19, Pallas kernels: 34.4 us -> 42.8 us  [call(): pl.pallas_call(run, in_specs=[pl.BlockSpec(memory_space=pltpu.SMEM)] + [v...]
    unnamed x4 -> x0, local copies, waits for them, and re-layouts: 7.36 us -> none
    ppermute x17, waiting for transfers between devices: 27.2 us -> 20.6 us  [swapped(): return lax.ppermute(block, 'row', [(i, i ^ apart) for i in range(count)])]
    ppermute x17, starting transfers between devices: 18.9 us -> 21.6 us  [swapped(): return lax.ppermute(block, 'row', [(i, i ^ apart) for i in range(count)])]
  transfers between devices with their start and end apart: 17 -> 17, of which waited for: 10 -> 8; matrix products, arithmetic and copies ran while one was open for 0% -> 0% of each run, Pallas kernels for 30% -> 42%
where the time goes in v3:
time: 85.5 us; the launch traced here: 85.3 us
  Pallas kernels  42.8 us (50%)
  starting transfers between devices  21.6 us (25%)
  waiting for transfers between devices  20.6 us (24%)
    pallas_call x19, Pallas kernels, call(): pl.pallas_call(run, in_specs=[pl.BlockSpec(memory_space=pltpu.SMEM)] + [v...  42.8 us
    ppermute x17, starting transfers between devices, swapped(): return lax.ppermute(block, 'row', [(i, i ^ apart) for i in range(count)])  21.6 us
    ppermute x17, waiting for transfers between devices, swapped(): return lax.ppermute(block, 'row', [(i, i ^ apart) for i in range(count)])  20.6 us
  transfers between devices with their start and end apart: 17, of which 8 were waited for; matrix products, arithmetic and copies ran while one was open for 0% of the time, Pallas kernels for 42%

profile of v3, /device:TPU:0, one launch (start us, length us, event | category | flops | bytes accessed | tf_op | source)
XLA Modules:
  0.0 85.3 jit_solution(8896807126481828662)
XLA Ops:
  0.0 0.1 pad_add_fusion.refs_0_
  0.1 2.8 %split_basis.1.refs_1_.refs_2_ = bf16[1024,1024]{1,0:T(8,128)(2,1)S(1)} custom-call(s32[2]{0:T(128)S(1)} %pad_add_fusion.refs_0_, f32[1024,512]{1,0:T(8,128)} %refs_1_.1), custom_call_target="tpu_custom_call" | custom-call | flops 1048576 | bytes 4194304 | tf_op jit(solution)/shard_map/split_basis/pallas_call | solution.py:92
  2.9 0.5 collective-permute-start
  3.4 11.6 %early_products.1 = (bf16[2048,4096]{1,0:T(8,128)(2,1)S(1)}, f32[512,2048]{1,0:T(8,128)S(1)}) custom-call(s32[2]{0:T(128)S(1)} %pad_add_fusion.refs_0_, bf16[1024,1024]{1,0:T(8,128)(2,1)S(1)} %split_basis.1.refs_1_.refs_2_, bf16[1,2048,4096]{2,1,0:T(8,128)(2,1)} %refs_2_.1), custom_call_target="tpu_custom_call" | custom-call | flops 4294967296 | bytes 16777216 | tf_op jit(solution)/shard_map/early_products/pallas_call | solution.py:92
  14.9 0.0 collective-permute-done.refs_3_
  15.0 3.2 %product.4 = (bf16[2064,128]{1,0:T(8,128)(2,1)S(1)}, f32[2048,128]{1,0:T(8,128)S(1)}) custom-call(s32[2]{0:T(128)S(1)} %pad_add_fusion.refs_0_, bf16[2048,4096]{1,0:T(8,128)(2,1)S(1)} %get-tuple-element.39.refs_1_, bf16[1024,1024]{1,0:T(8,128)(2,1)S(1)} %split_basis.1.refs_1_.refs_2_, bf16[1024,1024]{1,0:T(8,128)(2,1)S(1)} %collective-permute-done.refs_3_, ...), custom_call_target="tpu_custom_call" | custom-call | flops 2147483648 | bytes 6291456 | tf_op jit(solution)/shard_map/product/pallas_call | solution.py:92
  18.2 2.6 %collective-permute-start.1 = (bf16[2064,128]{1,0:T(8,128)(2,1)S(1)}, bf16[2064,128]{1,0:T(8,128)(2,1)S(1)}, u32[]{:S(2)}, u32[]{:S(2)}) collective-permute-start(bf16[2064,128]{1,0:T(8,128)(2,1)S(1)} %get-tuple-element.41), channel_id=1, source_target_pairs={{0,2},{1,3},{2,0},{3,1},{4,6},{5,7},{6,4},{7,5},{8,10},{9,11},{10,... | collective-permute-start | bytes 1585160 | tf_op jit(solution)/shard_map/ppermute | solution.py:356
  20.8 3.2 %product.5 = (bf16[2064,128]{1,0:T(8,128)(2,1)S(1)}, f32[2048,128]{1,0:T(8,128)S(1)}) custom-call(s32[2]{0:T(128)S(1)} %pad_add_fusion.refs_0_, bf16[2048,4096]{1,0:T(8,128)(2,1)S(1)} %get-tuple-element.39.refs_1_, bf16[1024,1024]{1,0:T(8,128)(2,1)S(1)} %split_basis.1.refs_1_.refs_2_, bf16[1024,1024]{1,0:T(8,128)(2,1)S(1)} %collective-permute-done.refs_3_, ...), custom_call_target="tpu_custom_call" | custom-call | flops 2147483648 | bytes 6291456 | tf_op jit(solution)/shard_map/product/pallas_call | solution.py:92
  24.0 1.6 %collective-permute-start.3 = (bf16[2064,128]{1,0:T(8,128)(2,1)S(1)}, bf16[2064,128]{1,0:T(8,128)(2,1)S(1)}, u32[]{:S(2)}, u32[]{:S(2)}) collective-permute-start(bf16[2064,128]{1,0:T(8,128)(2,1)S(1)} %get-tuple-element.47), channel_id=1, source_target_pairs={{0,4},{1,5},{2,6},{3,7},{4,0},{5,1},{6,2},{7,3},{8,12},{9,13},{10,... | collective-permute-start | bytes 1585160 | tf_op jit(solution)/shard_map/ppermute | solution.py:356
  25.6 5.4 %product.6 = (bf16[2064,128]{1,0:T(8,128)(2,1)S(1)}, f32[2048,128]{1,0:T(8,128)S(1)}) custom-call(s32[2]{0:T(128)S(1)} %pad_add_fusion.refs_0_, bf16[2048,4096]{1,0:T(8,128)(2,1)S(1)} %get-tuple-element.39.refs_1_, bf16[1024,1024]{1,0:T(8,128)(2,1)S(1)} %split_basis.1.refs_1_.refs_2_, bf16[1024,1024]{1,0:T(8,128)(2,1)S(1)} %collective-permute-done.refs_3_, ...), custom_call_target="tpu_custom_call" | custom-call | flops 4294967296 | bytes 8388608 | tf_op jit(solution)/shard_map/product/pallas_call | solution.py:92
  31.0 0.6 collective-permute-start.5
  31.6 1.9 %collective-permute-done.1.refs_1_ = bf16[2064,128]{1,0:T(8,128)(2,1)S(1)} collective-permute-done((bf16[2064,128]{1,0:T(8,128)(2,1)S(1)}, bf16[2064,128]{1,0:T(8,128)(2,1)S(1)}, u32[]{:S(2)}, u32[]{:S(2)}) %collective-permute-start.1) | collective-permute-done | bytes 528416 | tf_op jit(solution)/shard_map/ppermute | solution.py:356
  33.4 1.0 %add_and_split.8 = (bf16[1040,128]{1,0:T(8,128)(2,1)S(1)}, f32[1024,128]{1,0:T(8,128)S(1)}) custom-call(s32[2]{0:T(128)S(1)} %pad_add_fusion.refs_0_, bf16[2064,128]{1,0:T(8,128)(2,1)S(1)} %collective-permute-done.1.refs_1_, f32[2048,128]{1,0:T(8,128)S(1)} %get-tuple-element.42.refs_5_.refs_2_, f32[2048,128]{1,0:T(8,128)S(1)} %get-tuple-element.44.refs_3_.refs_2_), custom_call_target="tpu_custom_call" | custom-call | flops 5242880 | bytes 2359296 | tf_op jit(solution)/shard_map/add_and_split/pallas_call | solution.py:92
  34.5 2.3 %collective-permute-start.2 = (bf16[1040,128]{1,0:T(8,128)(2,1)S(1)}, bf16[1040,128]{1,0:T(8,128)(2,1)S(1)}, u32[]{:S(2)}, u32[]{:S(2)}) collective-permute-start(bf16[1040,128]{1,0:T(8,128)(2,1)S(1)} %get-tuple-element.45), channel_id=1, source_target_pairs={{0,4},{1,5},{2,6},{3,7},{4,0},{5,1},{6,2},{7,3},{8,12},{9,13},{10,... | collective-permute-start | bytes 798728 | tf_op jit(solution)/shard_map/ppermute | solution.py:356
  36.7 5.5 %product.7 = (bf16[2064,128]{1,0:T(8,128)(2,1)S(1)}, f32[2048,128]{1,0:T(8,128)S(1)}) custom-call(s32[2]{0:T(128)S(1)} %pad_add_fusion.refs_0_, bf16[2048,4096]{1,0:T(8,128)(2,1)S(1)} %get-tuple-element.39.refs_1_, bf16[1024,1024]{1,0:T(8,128)(2,1)S(1)} %split_basis.1.refs_1_.refs_2_, bf16[1024,1024]{1,0:T(8,128)(2,1)S(1)} %collective-permute-done.refs_3_, ...), custom_call_target="tpu_custom_call" | custom-call | flops 4294967296 | bytes 8388608 | tf_op jit(solution)/shard_map/product/pallas_call | solution.py:92
  42.3 1.6 %collective-permute-start.8 = (bf16[2064,128]{1,0:T(8,128)(2,1)S(1)}, bf16[2064,128]{1,0:T(8,128)(2,1)S(1)}, u32[]{:S(2)}, u32[]{:S(2)}) collective-permute-start(bf16[2064,128]{1,0:T(8,128)(2,1)S(1)} %get-tuple-element.57), channel_id=1, source_target_pairs={{0,2},{1,3},{2,0},{3,1},{4,6},{5,7},{6,4},{7,5},{8,10},{9,11},{10,... | collective-permute-start | bytes 1585160 | tf_op jit(solution)/shard_map/ppermute | solution.py:356
  43.8 0.0 collective-permute-done.3.refs_1_
  43.8 1.0 %add_and_split.9 = (bf16[1040,128]{1,0:T(8,128)(2,1)S(1)}, f32[1024,128]{1,0:T(8,128)S(1)}) custom-call(s32[2]{0:T(128)S(1)} %pad_add_fusion.refs_0_, bf16[2064,128]{1,0:T(8,128)(2,1)S(1)} %collective-permute-done.3.refs_1_, f32[2048,128]{1,0:T(8,128)S(1)} %get-tuple-element.43.refs_4_.refs_2_, f32[2048,128]{1,0:T(8,128)S(1)} %get-tuple-element.48.refs_3_.refs_2_), custom_call_target="tpu_custom_call" | custom-call | flops 5242880 | bytes 2359296 | tf_op jit(solution)/shard_map/add_and_split/pallas_call | solution.py:92
  44.9 0.0 collective-permute-done.2.refs_1_
  44.9 0.8 add_and_split.10
  45.7 0.1 collective-permute-done.5.refs_1_
  45.8 1.0 %add_and_split.11 = (bf16[1040,128]{1,0:T(8,128)(2,1)S(1)}, f32[1024,128]{1,0:T(8,128)S(1)}) custom-call(s32[2]{0:T(128)S(1)} %pad_add_fusion.refs_0_, bf16[2064,128]{1,0:T(8,128)(2,1)S(1)} %collective-permute-done.5.refs_1_, f32[2048,128]{1,0:T(8,128)S(1)} %get-tuple-element.44.refs_3_.refs_2_, f32[512,128]{1,0:T(8,128)S(1)} %get-tuple-element.51.refs_3_.refs_2_), custom_call_target="tpu_custom_call" | custom-call | flops 5242880 | bytes 2359296 | tf_op jit(solution)/shard_map/add_and_split/pallas_call | solution.py:92
  46.8 1.2 %collective-permute-start.9 = (bf16[1040,128]{1,0:T(8,128)(2,1)S(1)}, bf16[1040,128]{1,0:T(8,128)(2,1)S(1)}, u32[]{:S(2)}, u32[]{:S(2)}) collective-permute-start(bf16[1040,128]{1,0:T(8,128)(2,1)S(1)} %get-tuple-element.58), channel_id=1, source_target_pairs={{0,4},{1,5},{2,6},{3,7},{4,0},{5,1},{6,2},{7,3},{8,12},{9,13},{10,... | collective-permute-start | bytes 798728 | tf_op jit(solution)/shard_map/ppermute | solution.py:356
  48.0 2.6 %collective-permute-start.4 = (bf16[528,128]{1,0:T(8,128)(2,1)S(1)}, bf16[528,128]{1,0:T(8,128)(2,1)S(1)}, u32[]{:S(2)}, u32[]{:S(2)}) collective-permute-start(bf16[528,128]{1,0:T(8,128)(2,1)S(1)} %get-tuple-element.50), channel_id=1, source_target_pairs={{0,8},{1,9},{2,10},{3,11},{4,12},{5,13},{6,14},{7,15},{8,0},{9,1},... | collective-permute-start | bytes 405512 | tf_op jit(solution)/shard_map/ppermute | solution.py:356
  50.6 1.5 %collective-permute-start.7 = (bf16[1040,128]{1,0:T(8,128)(2,1)S(1)}, bf16[1040,128]{1,0:T(8,128)(2,1)S(1)}, u32[]{:S(2)}, u32[]{:S(2)}) collective-permute-start(bf16[1040,128]{1,0:T(8,128)(2,1)S(1)} %get-tuple-element.56), channel_id=1, source_target_pairs={{0,2},{1,3},{2,0},{3,1},{4,6},{5,7},{6,4},{7,5},{8,10},{9,11},{10,... | collective-permute-start | bytes 798728 | tf_op jit(solution)/shard_map/ppermute | solution.py:356
  52.2 3.9 %collective-permute-done.4.refs_1_ = bf16[528,128]{1,0:T(8,128)(2,1)S(1)} collective-permute-done((bf16[528,128]{1,0:T(8,128)(2,1)S(1)}, bf16[528,128]{1,0:T(8,128)(2,1)S(1)}, u32[]{:S(2)}, u32[]{:S(2)}) %collective-permute-start.4) | collective-permute-done | bytes 135200 | tf_op jit(solution)/shard_map/ppermute | solution.py:356
  56.1 0.6 add_last.4
  56.7 0.1 collective-permute-done.9.refs_1_
  56.8 0.8 add_and_split.12
  57.6 0.0 collective-permute-done.8.refs_1_
  57.6 1.0 %add_and_split.13 = (bf16[1040,128]{1,0:T(8,128)(2,1)S(1)}, f32[1024,128]{1,0:T(8,128)S(1)}) custom-call(s32[2]{0:T(128)S(1)} %pad_add_fusion.refs_0_, bf16[2064,128]{1,0:T(8,128)(2,1)S(1)} %collective-permute-done.8.refs_1_, f32[2048,128]{1,0:T(8,128)S(1)} %get-tuple-element.48.refs_3_.refs_2_, f32[512,128]{1,0:T(8,128)S(1)} %get-tuple-element.59.refs_3_.refs_2_), custom_call_target="tpu_custom_call" | custom-call | flops 5242880 | bytes 2359296 | tf_op jit(solution)/shard_map/add_and_split/pallas_call | solution.py:92
  58.7 3.3 %collective-permute-start.11 = (bf16[1040,128]{1,0:T(8,128)(2,1)S(1)}, bf16[1040,128]{1,0:T(8,128)(2,1)S(1)}, u32[]{:S(2)}, u32[]{:S(2)}) collective-permute-start(bf16[1040,128]{1,0:T(8,128)(2,1)S(1)} %get-tuple-element.63), channel_id=1, source_target_pairs={{0,4},{1,5},{2,6},{3,7},{4,0},{5,1},{6,2},{7,3},{8,12},{9,13},{10,... | collective-permute-start | bytes 798728 | tf_op jit(solution)/shard_map/ppermute | solution.py:356
  62.0 1.1 %collective-permute-start.12 = (bf16[528,128]{1,0:T(8,128)(2,1)S(1)}, bf16[528,128]{1,0:T(8,128)(2,1)S(1)}, u32[]{:S(2)}, u32[]{:S(2)}) collective-permute-start(bf16[528,128]{1,0:T(8,128)(2,1)S(1)} %get-tuple-element.64), channel_id=1, source_target_pairs={{0,8},{1,9},{2,10},{3,11},{4,12},{5,13},{6,14},{7,15},{8,0},{9,1},... | collective-permute-start | bytes 405512 | tf_op jit(solution)/shard_map/ppermute | solution.py:356
  63.1 0.0 collective-permute-done.7.refs_1_
  63.1 0.8 add_and_split.14
  63.9 1.9 %collective-permute-start.10 = (bf16[528,128]{1,0:T(8,128)(2,1)S(1)}, bf16[528,128]{1,0:T(8,128)(2,1)S(1)}, u32[]{:S(2)}, u32[]{:S(2)}) collective-permute-start(bf16[528,128]{1,0:T(8,128)(2,1)S(1)} %get-tuple-element.61), channel_id=1, source_target_pairs={{0,8},{1,9},{2,10},{3,11},{4,12},{5,13},{6,14},{7,15},{8,0},{9,1},... | collective-permute-start | bytes 405512 | tf_op jit(solution)/shard_map/ppermute | solution.py:356
  65.8 8.8 %collective-permute-done.12.refs_1_ = bf16[528,128]{1,0:T(8,128)(2,1)S(1)} collective-permute-done((bf16[528,128]{1,0:T(8,128)(2,1)S(1)}, bf16[528,128]{1,0:T(8,128)(2,1)S(1)}, u32[]{:S(2)}, u32[]{:S(2)}) %collective-permute-start.12) | collective-permute-done | bytes 135200 | tf_op jit(solution)/shard_map/ppermute | solution.py:356
  74.5 0.6 add_last.5
  75.2 0.0 collective-permute-done.11.refs_1_
  75.2 0.8 add_and_split.15
  76.0 0.1 collective-permute-start.15
  76.1 0.1 collective-permute-start.6
  76.1 0.5 collective-permute-start.14
  76.6 3.4 %collective-permute-done.10.refs_1_ = bf16[528,128]{1,0:T(8,128)(2,1)S(1)} collective-permute-done((bf16[528,128]{1,0:T(8,128)(2,1)S(1)}, bf16[528,128]{1,0:T(8,128)(2,1)S(1)}, u32[]{:S(2)}, u32[]{:S(2)}) %collective-permute-start.10) | collective-permute-done | bytes 135200 | tf_op jit(solution)/shard_map/ppermute | solution.py:356
  80.0 0.6 add_last.6
  80.7 0.1 collective-permute-start.13
  80.7 1.2 %collective-permute-done.15.refs_1_ = bf16[528,128]{1,0:T(8,128)(2,1)S(1)} collective-permute-done((bf16[528,128]{1,0:T(8,128)(2,1)S(1)}, bf16[528,128]{1,0:T(8,128)(2,1)S(1)}, u32[]{:S(2)}, u32[]{:S(2)}) %collective-permute-start.15) | collective-permute-done | bytes 135200 | tf_op jit(solution)/shard_map/ppermute | solution.py:356
  82.0 0.6 add_last.7
  82.6 0.1 collective-permute-start.16
  82.7 0.0 collective-permute-done.6.refs_2_
  82.7 0.0 collective-permute-done.14.refs_6_
  82.7 0.0 collective-permute-done.13.refs_4_
  82.7 1.2 %collective-permute-done.16.refs_8_ = bf16[32,1024]{1,0:T(8,128)(2,1)S(1)} collective-permute-done((bf16[32,1024]{1,0:T(8,128)(2,1)S(1)}, bf16[32,1024]{1,0:T(8,128)(2,1)S(1)}, u32[]{:S(2)}, u32[]{:S(2)}) %collective-permute-start.16) | collective-permute-done | bytes 65568 | tf_op jit(solution)/shard_map/ppermute | solution.py:356
  83.9 1.4 %lay_out.1 = bf16[32,8192]{1,0:T(8,128)(2,1)} custom-call(s32[2]{0:T(128)S(1)} %pad_add_fusion.refs_0_, bf16[32,1024]{1,0:T(8,128)(2,1)S(1)} %get-tuple-element.54.refs_3_.refs_1_, bf16[32,1024]{1,0:T(8,128)(2,1)S(1)} %collective-permute-done.6.refs_2_, bf16[32,1024]{1,0:T(8,128)(2,1)S(1)} %get-tuple-element.67.refs_3_, ...), custom_call_target="tpu_custom_call" | custom-call | bytes 1048576 | tf_op jit(solution)/shard_map/lay_out/pallas_call | solution.py:92
Async XLA Ops:
  2.9 12.1 %collective-permute-start = (bf16[1024,1024]{1,0:T(8,128)(2,1)S(1)}, bf16[1024,1024]{1,0:T(8,128)(2,1)S(1)}, u32[]{:S(2)}, u32[]{:S(2)}) collective-permute-start(bf16[1024,1024]{1,0:T(8,128)(2,1)S(1)} %split_basis.1.refs_1_.refs_2_), channel_id=1, source_target_pairs={{0,1},{1,0},{2,3},{3,2},{4,5},{5,4},{6,7},{7,6},{8,9},{9,8},{10,11... | collective-permute-start | bytes 6291464 | tf_op jit(solution)/shard_map/ppermute | solution.py:356
  18.2 15.3 %collective-permute-start.1 = (bf16[2064,128]{1,0:T(8,128)(2,1)S(1)}, bf16[2064,128]{1,0:T(8,128)(2,1)S(1)}, u32[]{:S(2)}, u32[]{:S(2)}) collective-permute-start(bf16[2064,128]{1,0:T(8,128)(2,1)S(1)} %get-tuple-element.41), channel_id=1, source_target_pairs={{0,2},{1,3},{2,0},{3,1},{4,6},{5,7},{6,4},{7,5},{8,10},{9,11},{10,... | collective-permute-start | bytes 1585160 | tf_op jit(solution)/shard_map/ppermute | solution.py:356
  24.0 19.9 %collective-permute-start.3 = (bf16[2064,128]{1,0:T(8,128)(2,1)S(1)}, bf16[2064,128]{1,0:T(8,128)(2,1)S(1)}, u32[]{:S(2)}, u32[]{:S(2)}) collective-permute-start(bf16[2064,128]{1,0:T(8,128)(2,1)S(1)} %get-tuple-element.47), channel_id=1, source_target_pairs={{0,4},{1,5},{2,6},{3,7},{4,0},{5,1},{6,2},{7,3},{8,12},{9,13},{10,... | collective-permute-start | bytes 1585160 | tf_op jit(solution)/shard_map/ppermute | solution.py:356
  31.0 14.8 %collective-permute-start.5 = (bf16[2064,128]{1,0:T(8,128)(2,1)S(1)}, bf16[2064,128]{1,0:T(8,128)(2,1)S(1)}, u32[]{:S(2)}, u32[]{:S(2)}) collective-permute-start(bf16[2064,128]{1,0:T(8,128)(2,1)S(1)} %get-tuple-element.52), channel_id=1, source_target_pairs={{0,2},{1,3},{2,0},{3,1},{4,6},{5,7},{6,4},{7,5},{8,10},{9,11},{10,... | collective-permute-start | bytes 1585160 | tf_op jit(solution)/shard_map/ppermute | solution.py:356
  34.5 10.4 %collective-permute-start.2 = (bf16[1040,128]{1,0:T(8,128)(2,1)S(1)}, bf16[1040,128]{1,0:T(8,128)(2,1)S(1)}, u32[]{:S(2)}, u32[]{:S(2)}) collective-permute-start(bf16[1040,128]{1,0:T(8,128)(2,1)S(1)} %get-tuple-element.45), channel_id=1, source_target_pairs={{0,4},{1,5},{2,6},{3,7},{4,0},{5,1},{6,2},{7,3},{8,12},{9,13},{10,... | collective-permute-start | bytes 798728 | tf_op jit(solution)/shard_map/ppermute | solution.py:356
  42.3 15.4 %collective-permute-start.8 = (bf16[2064,128]{1,0:T(8,128)(2,1)S(1)}, bf16[2064,128]{1,0:T(8,128)(2,1)S(1)}, u32[]{:S(2)}, u32[]{:S(2)}) collective-permute-start(bf16[2064,128]{1,0:T(8,128)(2,1)S(1)} %get-tuple-element.57), channel_id=1, source_target_pairs={{0,2},{1,3},{2,0},{3,1},{4,6},{5,7},{6,4},{7,5},{8,10},{9,11},{10,... | collective-permute-start | bytes 1585160 | tf_op jit(solution)/shard_map/ppermute | solution.py:356
  46.8 10.0 %collective-permute-start.9 = (bf16[1040,128]{1,0:T(8,128)(2,1)S(1)}, bf16[1040,128]{1,0:T(8,128)(2,1)S(1)}, u32[]{:S(2)}, u32[]{:S(2)}) collective-permute-start(bf16[1040,128]{1,0:T(8,128)(2,1)S(1)} %get-tuple-element.58), channel_id=1, source_target_pairs={{0,4},{1,5},{2,6},{3,7},{4,0},{5,1},{6,2},{7,3},{8,12},{9,13},{10,... | collective-permute-start | bytes 798728 | tf_op jit(solution)/shard_map/ppermute | solution.py:356
  48.0 8.0 %collective-permute-start.4 = (bf16[528,128]{1,0:T(8,128)(2,1)S(1)}, bf16[528,128]{1,0:T(8,128)(2,1)S(1)}, u32[]{:S(2)}, u32[]{:S(2)}) collective-permute-start(bf16[528,128]{1,0:T(8,128)(2,1)S(1)} %get-tuple-element.50), channel_id=1, source_target_pairs={{0,8},{1,9},{2,10},{3,11},{4,12},{5,13},{6,14},{7,15},{8,0},{9,1},... | collective-permute-start | bytes 405512 | tf_op jit(solution)/shard_map/ppermute | solution.py:356
  50.6 12.4 %collective-permute-start.7 = (bf16[1040,128]{1,0:T(8,128)(2,1)S(1)}, bf16[1040,128]{1,0:T(8,128)(2,1)S(1)}, u32[]{:S(2)}, u32[]{:S(2)}) collective-permute-start(bf16[1040,128]{1,0:T(8,128)(2,1)S(1)} %get-tuple-element.56), channel_id=1, source_target_pairs={{0,2},{1,3},{2,0},{3,1},{4,6},{5,7},{6,4},{7,5},{8,10},{9,11},{10,... | collective-permute-start | bytes 798728 | tf_op jit(solution)/shard_map/ppermute | solution.py:356
  58.7 16.5 %collective-permute-start.11 = (bf16[1040,128]{1,0:T(8,128)(2,1)S(1)}, bf16[1040,128]{1,0:T(8,128)(2,1)S(1)}, u32[]{:S(2)}, u32[]{:S(2)}) collective-permute-start(bf16[1040,128]{1,0:T(8,128)(2,1)S(1)} %get-tuple-element.63), channel_id=1, source_target_pairs={{0,4},{1,5},{2,6},{3,7},{4,0},{5,1},{6,2},{7,3},{8,12},{9,13},{10,... | collective-permute-start | bytes 798728 | tf_op jit(solution)/shard_map/ppermute | solution.py:356
  62.0 12.6 %collective-permute-start.12 = (bf16[528,128]{1,0:T(8,128)(2,1)S(1)}, bf16[528,128]{1,0:T(8,128)(2,1)S(1)}, u32[]{:S(2)}, u32[]{:S(2)}) collective-permute-start(bf16[528,128]{1,0:T(8,128)(2,1)S(1)} %get-tuple-element.64), channel_id=1, source_target_pairs={{0,8},{1,9},{2,10},{3,11},{4,12},{5,13},{6,14},{7,15},{8,0},{9,1},... | collective-permute-start | bytes 405512 | tf_op jit(solution)/shard_map/ppermute | solution.py:356
  63.9 16.2 %collective-permute-start.10 = (bf16[528,128]{1,0:T(8,128)(2,1)S(1)}, bf16[528,128]{1,0:T(8,128)(2,1)S(1)}, u32[]{:S(2)}, u32[]{:S(2)}) collective-permute-start(bf16[528,128]{1,0:T(8,128)(2,1)S(1)} %get-tuple-element.61), channel_id=1, source_target_pairs={{0,8},{1,9},{2,10},{3,11},{4,12},{5,13},{6,14},{7,15},{8,0},{9,1},... | collective-permute-start | bytes 405512 | tf_op jit(solution)/shard_map/ppermute | solution.py:356
  76.0 6.0 %collective-permute-start.15 = (bf16[528,128]{1,0:T(8,128)(2,1)S(1)}, bf16[528,128]{1,0:T(8,128)(2,1)S(1)}, u32[]{:S(2)}, u32[]{:S(2)}) collective-permute-start(bf16[528,128]{1,0:T(8,128)(2,1)S(1)} %get-tuple-element.70), channel_id=1, source_target_pairs={{0,8},{1,9},{2,10},{3,11},{4,12},{5,13},{6,14},{7,15},{8,0},{9,1},... | collective-permute-start | bytes 405512 | tf_op jit(solution)/shard_map/ppermute | solution.py:356
  76.1 6.6 %collective-permute-start.6 = (bf16[32,1024]{1,0:T(8,128)(2,1)S(1)}, bf16[32,1024]{1,0:T(8,128)(2,1)S(1)}, u32[]{:S(2)}, u32[]{:S(2)}) collective-permute-start(bf16[32,1024]{1,0:T(8,128)(2,1)S(1)} %get-tuple-element.55), channel_id=1, source_target_pairs={{0,1},{1,0},{2,3},{3,2},{4,5},{5,4},{6,7},{7,6},{8,9},{9,8},{10,11... | collective-permute-start | bytes 196616 | tf_op jit(solution)/shard_map/ppermute | solution.py:356
  76.1 6.6 %collective-permute-start.14 = (bf16[32,1024]{1,0:T(8,128)(2,1)S(1)}, bf16[32,1024]{1,0:T(8,128)(2,1)S(1)}, u32[]{:S(2)}, u32[]{:S(2)}) collective-permute-start(bf16[32,1024]{1,0:T(8,128)(2,1)S(1)} %get-tuple-element.69), channel_id=1, source_target_pairs={{0,1},{1,0},{2,3},{3,2},{4,5},{5,4},{6,7},{7,6},{8,9},{9,8},{10,11... | collective-permute-start | bytes 196616 | tf_op jit(solution)/shard_map/ppermute | solution.py:356
  80.7 2.0 %collective-permute-start.13 = (bf16[32,1024]{1,0:T(8,128)(2,1)S(1)}, bf16[32,1024]{1,0:T(8,128)(2,1)S(1)}, u32[]{:S(2)}, u32[]{:S(2)}) collective-permute-start(bf16[32,1024]{1,0:T(8,128)(2,1)S(1)} %get-tuple-element.68), channel_id=1, source_target_pairs={{0,1},{1,0},{2,3},{3,2},{4,5},{5,4},{6,7},{7,6},{8,9},{9,8},{10,11... | collective-permute-start | bytes 196616 | tf_op jit(solution)/shard_map/ppermute | solution.py:356
  82.6 1.3 %collective-permute-start.16 = (bf16[32,1024]{1,0:T(8,128)(2,1)S(1)}, bf16[32,1024]{1,0:T(8,128)(2,1)S(1)}, u32[]{:S(2)}, u32[]{:S(2)}) collective-permute-start(bf16[32,1024]{1,0:T(8,128)(2,1)S(1)} %get-tuple-element.72), channel_id=1, source_target_pairs={{0,1},{1,0},{2,3},{3,2},{4,5},{5,4},{6,7},{7,6},{8,9},{9,8},{10,11... | collective-permute-start | bytes 196616 | tf_op jit(solution)/shard_map/ppermute | solution.py:356

commit v4 on v3

--- a/solution.py
+++ b/solution.py
@@ -15,12 +15,19 @@
 TINY = 2.0**-110
 MIB = 1 << 20
 
-CHUNKS = [(4, (0, 1, 2)), (4, (1, 0, 2)), (4, (0, 1, 2)), (4, (0, 1, 2))]
+CHUNKS = [
+    (3, (2, 0, 1)),
+    (4, (0, 1, 2)),
+    (3, (1, 0, 2)),
+    (3, (0, 1, 2)),
+    (3, (0, 1, 2)),
+]
 PARTS = 16
 EARLY = 2
 ORDER = [
-    (0, 0), (1, 0), (2, 0), (0, 1), (3, 0), (1, 1), (0, 2), (2, 1),
-    (0, 3), (2, 2), (3, 1), (1, 2), (2, 3), (3, 2), (1, 3), (3, 3),
+    (0, 0), (1, 0), (2, 0), (3, 0), (1, 1), (4, 0), (3, 1), (1, 2),
+    (2, 1), (4, 1), (3, 2), (0, 1), (2, 2), (4, 2), (0, 2), (3, 3),
+    (2, 3), (1, 3), (4, 3), (0, 3),
 ]
 
 
@@ -157,65 +164,83 @@
     return product[:half] + product[half:]
 
 
+def weight_copies(place_ref, w_ref, near_ref, sems, start, depth, boxes):
+    copies = []
+    for index, (distance, row, rows, at, wide) in enumerate(boxes):
+        owner = jnp.bitwise_xor(place_ref[0], distance)
+        source = pl.ds(pl.multiple_of(owner * depth + row, rows), rows)
+        target = pl.ds(distance * depth + row, rows)
+        copies.append(
+            pltpu.make_async_copy(
+                w_ref.at[0, source, pl.ds(start + at, wide)],
+                near_ref.at[target, pl.ds(at, wide)],
+                sems.at[index],
+            )
+        )
+    return copies
+
+
+def row_boxes(distances, depth, width):
+    return [
+        (distance, row, rows, 0, width)
+        for distance in distances
+        for row, rows in spans(depth, COLUMNS)
+    ]
+
+
+def early_boxes(pieces, depth, width):
+    first = [(0, 0, depth, at, wide) for at, wide in spans(width, 2 * COLUMNS)]
+    return first, row_boxes(range(1, pieces), depth, width)
+
+
 def early_kernel(pieces, width, place_ref, own_ref, w_ref, near_ref, partial_ref, sems):
     depth = own_ref.shape[1]
-    full = w_ref.shape[2]
-    copies = []
-
-    def bring(distance, at, wide):
-        owner = jnp.bitwise_xor(place_ref[0], distance)
-        rows = pl.ds(pl.multiple_of(owner * depth, depth), depth)
-        copy = pltpu.make_async_copy(
-            w_ref.at[0, rows, pl.ds(at, wide)],
-            near_ref.at[pl.ds(distance * depth, depth), pl.ds(at, wide)],
-            sems.at[len(copies)],
-        )
+    first, rest = early_boxes(pieces, depth, width)
+    copies = weight_copies(place_ref, w_ref, near_ref, sems, 0, depth, first + rest)
+    for copy in copies:
         copy.start()
-        copies.append(copy)
-
-    first = spans(width, COLUMNS)
-    for at, wide in first:
-        bring(0, at, wide)
-    for index, (at, wide) in enumerate(first):
-        copies[index].wait()
-        if index == 0:
-            if full > width:
-                bring(0, width, full - width)
-            for distance in range(1, pieces):
-                bring(distance, 0, full)
-        part = jnp.dot(
-            own_ref[...],
-            near_ref[0:depth, at : at + wide],
-            preferred_element_type=jnp.float32,
-        )
-        partial_ref[:, at : at + wide] = halves_added(part)
+    for copy, (_, _, _, start, reach) in zip(copies, first):
+        copy.wait()
+        for at, wide in spans(reach, COLUMNS):
+            columns = slice(start + at, start + at + wide)
+            part = jnp.dot(
+                own_ref[...], near_ref[0:depth, columns], preferred_element_type=jnp.float32
+            )
+            partial_ref[:, columns] = halves_added(part)
     for copy in copies[len(first) :]:
         copy.wait()
 
 
 def early(own, weights, places, pieces, width, after):
     rows2, depth = own.shape
-    full = weights.shape[2]
+    first, rest = early_boxes(pieces, depth, width)
     return call(
         functools.partial(early_kernel, pieces, width),
         "early_products",
         [places, own, weights],
         [
-            jax.ShapeDtypeStruct((pieces * depth, full), jnp.bfloat16),
+            jax.ShapeDtypeStruct((pieces * depth, width), jnp.bfloat16),
             jax.ShapeDtypeStruct((rows2 // 2, width), jnp.float32),
         ],
         after,
-        [pltpu.SemaphoreType.DMA((len(spans(width, COLUMNS)) + pieces,))],
+        [pltpu.SemaphoreType.DMA((len(first) + len(rest),))],
         limit=8,
-        cost=(2 * rows2 * depth * width, 2 * pieces * depth * full, 0),
+        cost=(2 * rows2 * depth * width, 2 * pieces * depth * width, 0),
         far=1,
     )
 
 
-def product_kernel(pieces, start, width, early, step, leave, stay, place_ref, near_ref, *refs):
+def product_kernel(pieces, start, width, early, bring, step, leave, stay, place_ref, near_ref, *refs):
     left = refs[:pieces]
-    message_ref, kept_ref = refs[-2:]
     depth = left[0].shape[1]
+    if bring:
+        w_ref, message_ref, kept_ref, later_ref, sems = refs[-5:]
+        boxes = row_boxes(range(pieces), depth, later_ref.shape[1])
+        copies = weight_copies(place_ref, w_ref, later_ref, sems, bring, depth, boxes)
+        for copy in copies:
+            copy.start()
+    else:
+        message_ref, kept_ref = refs[-2:]
     used = left[1:] if early else left
     low = depth if early else 0
     bounds = []
@@ -235,6 +260,9 @@
             tile = (at + lane) // LANES
             bounds.append(put_tile(message_ref, kept_ref, tile, blocks, step, leave, stay))
     put_bounds(message_ref, bounds, len(leave) * step)
+    if bring:
+        for copy in copies:
+            copy.wait()
 
 
 def outputs(width, step, leave, stay):
@@ -246,24 +274,33 @@
     ]
 
 
-def product(left, near, partial, places, start, width, step, leave, stay, after):
+def product(left, near, partial, weights, places, start, width, bring, step, leave, stay, after):
     rows2, depth = left[0].shape
+    pieces = len(left)
     early = partial is not None
-    count = len(left) - 1 if early else len(left)
+    count = pieces - 1 if early else pieces
+    outs = outputs(width, step, leave, stay)
+    scratch = []
+    if bring:
+        later = weights.shape[2] - bring
+        outs.append(jax.ShapeDtypeStruct((pieces * depth, later), jnp.bfloat16))
+        scratch = [pltpu.SemaphoreType.DMA((len(row_boxes(range(pieces), depth, later)),))]
     return call(
         functools.partial(
-            product_kernel, len(left), start, width, early, step, leave, stay
+            product_kernel, pieces, start, width, early, bring, step, leave, stay
         ),
         "product",
-        [places, near, *left] + ([partial] if early else []),
-        outputs(width, step, leave, stay),
+        [places, near, *left] + ([partial] if early else []) + ([weights] if bring else []),
+        outs,
         after,
+        scratch,
         limit=8,
         cost=(
             2 * rows2 * depth * count * width,
             2 * depth * count * width + 4 * rows2 * width,
             rows2 * width // 4,
         ),
+        far=1 if bring else 0,
     )
 
 
@@ -378,7 +415,8 @@
     cuts = [cut * (width // LANES) // PARTS * LANES for cut in cuts]
     orders = [[bit for bit in order if bit < bits] for _, order in CHUNKS]
     stages = [split_places(order, bits) for order in orders]
-    near, partial = early(own, weights, places, pieces, cuts[EARLY], [])
+    ahead = cuts[EARLY]
+    near, partial = early(own, weights, places, pieces, ahead, [])
 
     state = {}
     after = [partial]
@@ -390,10 +428,22 @@
         if chunk == 0:
             continue
         if number == 0:
-            begun = partial if index < EARLY else None
+            early_one = index < EARLY
             out = product(
-                left, near, begun, places, start, chunk, step, *stages[index][0], after
+                left,
+                near if early_one else later,
+                partial if early_one else None,
+                weights,
+                places,
+                start if early_one else start - ahead,
+                chunk,
+                ahead if index == EARLY - 1 else 0,
+                step,
+                *stages[index][0],
+                after,
             )
+            if index == EARLY - 1:
+                later = out[2]
         elif number < bits:
             message, kept = state[index]
             old = stages[index][number - 1][1]

time: 85.5 us -> 92.2 us (1.078)
  waiting for transfers between devices: 20.6 us -> 23.7 us
  starting transfers between devices: 21.6 us -> 24.2 us
  Pallas kernels: 42.8 us -> 43.9 us
    ppermute x17 -> x21, waiting for transfers between devices: 20.6 us -> 23.7 us  [swapped(): return lax.ppermute(block, 'row', [(i, i ^ apart) for i in range(count)])]
    ppermute x17 -> x21, starting transfers between devices: 21.6 us -> 24.2 us  [swapped(): return lax.ppermute(block, 'row', [(i, i ^ apart) for i in range(count)])]
    pallas_call x19 -> x23, Pallas kernels: 42.8 us -> 43.9 us  [call(): pl.pallas_call(run, in_specs=[pl.BlockSpec(memory_space=pltpu.SMEM)] + [v...]
  transfers between devices with their start and end apart: 17 -> 21, of which waited for: 8 -> 6; matrix products, arithmetic and copies ran while one was open for 0% -> 0% of each run, Pallas kernels for 42% -> 34%
where the time goes in v4:
time: 92.2 us; the launch traced here: 92 us
  Pallas kernels  43.9 us (48%)
  starting transfers between devices  24.2 us (26%)
  waiting for transfers between devices  23.7 us (26%)
    pallas_call x23, Pallas kernels, call(): pl.pallas_call(run, in_specs=[pl.BlockSpec(memory_space=pltpu.SMEM)] + [v...  43.9 us
    ppermute x21, starting transfers between devices, swapped(): return lax.ppermute(block, 'row', [(i, i ^ apart) for i in range(count)])  24.2 us
    ppermute x21, waiting for transfers between devices, swapped(): return lax.ppermute(block, 'row', [(i, i ^ apart) for i in range(count)])  23.7 us
  transfers between devices with their start and end apart: 21, of which 6 were waited for; matrix products, arithmetic and copies ran while one was open for 0% of the time, Pallas kernels for 34%

profile of v4, /device:TPU:0, one launch (start us, length us, event | category | flops | bytes accessed | tf_op | source)
XLA Modules:
  0.0 92.0 jit_solution(8291108538143185502)
XLA Ops:
  0.0 0.1 pad_add_fusion.refs_0_
  0.1 2.8 %split_basis.1.refs_1_.refs_2_ = bf16[1024,1024]{1,0:T(8,128)(2,1)S(1)} custom-call(s32[2]{0:T(128)S(1)} %pad_add_fusion.refs_0_, f32[1024,512]{1,0:T(8,128)} %refs_1_.1), custom_call_target="tpu_custom_call" | custom-call | flops 1048576 | bytes 4194304 | tf_op jit(solution)/shard_map/split_basis/pallas_call | solution.py:99
  2.9 0.5 collective-permute-start
  3.4 7.4 %early_products.1 = (bf16[2048,1792]{1,0:T(8,128)(2,1)S(1)}, f32[512,1792]{1,0:T(8,128)S(1)}) custom-call(s32[2]{0:T(128)S(1)} %pad_add_fusion.refs_0_, bf16[1024,1024]{1,0:T(8,128)(2,1)S(1)} %split_basis.1.refs_1_.refs_2_, bf16[1,2048,4096]{2,1,0:T(8,128)(2,1)} %refs_5_.1), custom_call_target="tpu_custom_call" | custom-call | flops 3758096384 | bytes 7340032 | tf_op jit(solution)/shard_map/early_products/pallas_call | solution.py:99
  10.7 0.0 collective-permute-done.refs_3_
  10.8 2.5 %product.5 = (bf16[1552,128]{1,0:T(8,128)(2,1)S(1)}, f32[1536,128]{1,0:T(8,128)S(1)}) custom-call(s32[2]{0:T(128)S(1)} %pad_add_fusion.refs_0_, bf16[2048,1792]{1,0:T(8,128)(2,1)S(1)} %get-tuple-element.48.refs_1_, bf16[1024,1024]{1,0:T(8,128)(2,1)S(1)} %split_basis.1.refs_1_.refs_2_, bf16[1024,1024]{1,0:T(8,128)(2,1)S(1)} %collective-permute-done.refs_3_, ...), custom_call_target="tpu_custom_call" | custom-call | flops 1610612736 | bytes 4718592 | tf_op jit(solution)/shard_map/product/pallas_call | solution.py:99
  13.3 5.8 %product.6 = (bf16[2064,128]{1,0:T(8,128)(2,1)S(1)}, f32[2048,128]{1,0:T(8,128)S(1)}, bf16[2048,2304]{1,0:T(8,128)(2,1)S(1)}) custom-call(s32[2]{0:T(128)S(1)} %pad_add_fusion.refs_0_, bf16[2048,1792]{1,0:T(8,128)(2,1)S(1)} %get-tuple-element.48.refs_1_, bf16[1024,1024]{1,0:T(8,128)(2,1)S(1)} %split_basis.1.refs_1_.refs_2_, ...), custom_call_target="tpu_custom_call" | custom-call | flops 2147483648 | bytes 6291456 | tf_op jit(solution)/shard_map/product/pallas_call | solution.py:99
  19.1 2.6 %collective-permute-start.3 = (bf16[2064,128]{1,0:T(8,128)(2,1)S(1)}, bf16[2064,128]{1,0:T(8,128)(2,1)S(1)}, u32[]{:S(2)}, u32[]{:S(2)}) collective-permute-start(bf16[2064,128]{1,0:T(8,128)(2,1)S(1)} %get-tuple-element.57), channel_id=1, source_target_pairs={{0,2},{1,3},{2,0},{3,1},{4,6},{5,7},{6,4},{7,5},{8,10},{9,11},{10,... | collective-permute-start | bytes 1585160 | tf_op jit(solution)/shard_map/ppermute | solution.py:393
  21.7 4.1 %product.7 = (bf16[1552,128]{1,0:T(8,128)(2,1)S(1)}, f32[1536,128]{1,0:T(8,128)S(1)}) custom-call(s32[2]{0:T(128)S(1)} %pad_add_fusion.refs_0_, bf16[2048,2304]{1,0:T(8,128)(2,1)S(1)} %get-tuple-element.52.refs_1_, bf16[1024,1024]{1,0:T(8,128)(2,1)S(1)} %split_basis.1.refs_1_.refs_2_, bf16[1024,1024]{1,0:T(8,128)(2,1)S(1)} %collective-permute-done.refs_3_, ...), custom_call_target="tpu_custom_call" | custom-call | flops 3221225472 | bytes 6291456 | tf_op jit(solution)/shard_map/product/pallas_call | solution.py:99
  25.8 1.6 %collective-permute-start.6 = (bf16[1552,128]{1,0:T(8,128)(2,1)S(1)}, bf16[1552,128]{1,0:T(8,128)(2,1)S(1)}, u32[]{:S(2)}, u32[]{:S(2)}) collective-permute-start(bf16[1552,128]{1,0:T(8,128)(2,1)S(1)} %get-tuple-element.63), channel_id=1, source_target_pairs={{0,4},{1,5},{2,6},{3,7},{4,0},{5,1},{6,2},{7,3},{8,12},{9,13},{10,... | collective-permute-start | bytes 1191944 | tf_op jit(solution)/shard_map/ppermute | solution.py:393
  27.5 4.1 %product.8 = (bf16[1552,128]{1,0:T(8,128)(2,1)S(1)}, f32[1536,128]{1,0:T(8,128)S(1)}) custom-call(s32[2]{0:T(128)S(1)} %pad_add_fusion.refs_0_, bf16[2048,2304]{1,0:T(8,128)(2,1)S(1)} %get-tuple-element.52.refs_1_, bf16[1024,1024]{1,0:T(8,128)(2,1)S(1)} %split_basis.1.refs_1_.refs_2_, bf16[1024,1024]{1,0:T(8,128)(2,1)S(1)} %collective-permute-done.refs_3_, ...), custom_call_target="tpu_custom_call" | custom-call | flops 3221225472 | bytes 6291456 | tf_op jit(solution)/shard_map/product/pallas_call | solution.py:99
  31.6 0.6 collective-permute-start.2
  32.2 2.3 %collective-permute-done.3.refs_1_ = bf16[2064,128]{1,0:T(8,128)(2,1)S(1)} collective-permute-done((bf16[2064,128]{1,0:T(8,128)(2,1)S(1)}, bf16[2064,128]{1,0:T(8,128)(2,1)S(1)}, u32[]{:S(2)}, u32[]{:S(2)}) %collective-permute-start.3) | collective-permute-done | bytes 528416 | tf_op jit(solution)/shard_map/ppermute | solution.py:393
  34.5 1.0 %add_and_split.10 = (bf16[1040,128]{1,0:T(8,128)(2,1)S(1)}, f32[1024,128]{1,0:T(8,128)S(1)}) custom-call(s32[2]{0:T(128)S(1)} %pad_add_fusion.refs_0_, bf16[2064,128]{1,0:T(8,128)(2,1)S(1)} %collective-permute-done.3.refs_1_, f32[2048,128]{1,0:T(8,128)S(1)} %get-tuple-element.53.refs_4_.refs_2_, f32[1536,128]{1,0:T(8,128)S(1)} %get-tuple-element.56.refs_3_.refs_2_), custom_call_target="tpu_custom_call" | custom-call | flops 5242880 | bytes 2359296 | tf_op jit(solution)/shard_map/add_and_split/pallas_call | solution.py:99
  35.5 4.3 %product.9 = (bf16[1552,128]{1,0:T(8,128)(2,1)S(1)}, f32[1536,128]{1,0:T(8,128)S(1)}) custom-call(s32[2]{0:T(128)S(1)} %pad_add_fusion.refs_0_, bf16[2048,2304]{1,0:T(8,128)(2,1)S(1)} %get-tuple-element.52.refs_1_, bf16[1024,1024]{1,0:T(8,128)(2,1)S(1)} %split_basis.1.refs_1_.refs_2_, bf16[1024,1024]{1,0:T(8,128)(2,1)S(1)} %collective-permute-done.refs_3_, ...), custom_call_target="tpu_custom_call" | custom-call | flops 3221225472 | bytes 6291456 | tf_op jit(solution)/shard_map/product/pallas_call | solution.py:99
  39.8 2.1 %collective-permute-start.5 = (bf16[1552,128]{1,0:T(8,128)(2,1)S(1)}, bf16[1552,128]{1,0:T(8,128)(2,1)S(1)}, u32[]{:S(2)}, u32[]{:S(2)}) collective-permute-start(bf16[1552,128]{1,0:T(8,128)(2,1)S(1)} %get-tuple-element.62), channel_id=1, source_target_pairs={{0,2},{1,3},{2,0},{3,1},{4,6},{5,7},{6,4},{7,5},{8,10},{9,11},{10,... | collective-permute-start | bytes 1191944 | tf_op jit(solution)/shard_map/ppermute | solution.py:393
  41.9 2.6 %collective-permute-start.1 = (bf16[1552,128]{1,0:T(8,128)(2,1)S(1)}, bf16[1552,128]{1,0:T(8,128)(2,1)S(1)}, u32[]{:S(2)}, u32[]{:S(2)}) collective-permute-start(bf16[1552,128]{1,0:T(8,128)(2,1)S(1)} %get-tuple-element.50), channel_id=1, source_target_pairs={{0,8},{1,9},{2,10},{3,11},{4,12},{5,13},{6,14},{7,15},{8,0},{9,1},... | collective-permute-start | bytes 1191944 | tf_op jit(solution)/shard_map/ppermute | solution.py:393
  44.5 1.6 %collective-permute-start.7 = (bf16[1040,128]{1,0:T(8,128)(2,1)S(1)}, bf16[1040,128]{1,0:T(8,128)(2,1)S(1)}, u32[]{:S(2)}, u32[]{:S(2)}) collective-permute-start(bf16[1040,128]{1,0:T(8,128)(2,1)S(1)} %get-tuple-element.64), channel_id=1, source_target_pairs={{0,4},{1,5},{2,6},{3,7},{4,0},{5,1},{6,2},{7,3},{8,12},{9,13},{10,... | collective-permute-start | bytes 798728 | tf_op jit(solution)/shard_map/ppermute | solution.py:393
  46.1 0.0 collective-permute-done.2.refs_1_
  46.1 0.9 add_and_split.11
  47.0 0.5 collective-permute-start.4
  47.5 12.4 %collective-permute-done.7.refs_1_ = bf16[1040,128]{1,0:T(8,128)(2,1)S(1)} collective-permute-done((bf16[1040,128]{1,0:T(8,128)(2,1)S(1)}, bf16[1040,128]{1,0:T(8,128)(2,1)S(1)}, u32[]{:S(2)}, u32[]{:S(2)}) %collective-permute-start.7) | collective-permute-done | bytes 266272 | tf_op jit(solution)/shard_map/ppermute | solution.py:393
  59.9 0.8 add_and_split.12
  60.7 0.0 collective-permute-done.6.refs_1_
  60.7 0.9 add_and_split.13
  61.6 0.5 collective-permute-start.10
  62.1 0.0 collective-permute-done.5.refs_1_
  62.1 0.9 add_and_split.14
  63.0 2.5 %collective-permute-start.9 = (bf16[784,128]{1,0:T(8,128)(2,1)S(1)}, bf16[784,128]{1,0:T(8,128)(2,1)S(1)}, u32[]{:S(2)}, u32[]{:S(2)}) collective-permute-start(bf16[784,128]{1,0:T(8,128)(2,1)S(1)} %get-tuple-element.71), channel_id=1, source_target_pairs={{0,4},{1,5},{2,6},{3,7},{4,0},{5,1},{6,2},{7,3},{8,12},{9,13},{10,... | collective-permute-start | bytes 602120 | tf_op jit(solution)/shard_map/ppermute | solution.py:393
  65.6 0.0 collective-permute-done.4.refs_1_
  65.6 0.7 add_and_split.15
  66.3 0.0 collective-permute-done.1.refs_1_
  66.3 0.9 add_and_split.16
  67.2 1.7 %collective-permute-start.8 = (bf16[784,128]{1,0:T(8,128)(2,1)S(1)}, bf16[784,128]{1,0:T(8,128)(2,1)S(1)}, u32[]{:S(2)}, u32[]{:S(2)}) collective-permute-start(bf16[784,128]{1,0:T(8,128)(2,1)S(1)} %get-tuple-element.69), channel_id=1, source_target_pairs={{0,2},{1,3},{2,0},{3,1},{4,6},{5,7},{6,4},{7,5},{8,10},{9,11},{10,... | collective-permute-start | bytes 602120 | tf_op jit(solution)/shard_map/ppermute | solution.py:393
  68.9 0.0 collective-permute-start.13
  68.9 2.9 %collective-permute-start.15 = (bf16[400,128]{1,0:T(8,128)(2,1)S(1)}, bf16[400,128]{1,0:T(8,128)(2,1)S(1)}, u32[]{:S(2)}, u32[]{:S(2)}) collective-permute-start(bf16[400,128]{1,0:T(8,128)(2,1)S(1)} %get-tuple-element.80), channel_id=1, source_target_pairs={{0,8},{1,9},{2,10},{3,11},{4,12},{5,13},{6,14},{7,15},{8,0},{9,1},... | collective-permute-start | bytes 307208 | tf_op jit(solution)/shard_map/ppermute | solution.py:393
  71.8 0.0 collective-permute-done.10.refs_1_
  71.8 0.7 add_and_split.17
  72.6 0.1 collective-permute-start.14
  72.7 0.0 collective-permute-done.9.refs_1_
  72.7 0.7 add_and_split.18
  73.4 3.0 %collective-permute-start.12 = (bf16[400,128]{1,0:T(8,128)(2,1)S(1)}, bf16[400,128]{1,0:T(8,128)(2,1)S(1)}, u32[]{:S(2)}, u32[]{:S(2)}) collective-permute-start(bf16[400,128]{1,0:T(8,128)(2,1)S(1)} %get-tuple-element.77), channel_id=1, source_target_pairs={{0,8},{1,9},{2,10},{3,11},{4,12},{5,13},{6,14},{7,15},{8,0},{9,1},... | collective-permute-start | bytes 307208 | tf_op jit(solution)/shard_map/ppermute | solution.py:393
  76.4 0.0 collective-permute-done.8.refs_1_
  76.4 0.7 add_and_split.19
  77.1 0.1 collective-permute-start.11
  77.2 7.4 %collective-permute-done.15.refs_1_ = bf16[400,128]{1,0:T(8,128)(2,1)S(1)} collective-permute-done((bf16[400,128]{1,0:T(8,128)(2,1)S(1)}, bf16[400,128]{1,0:T(8,128)(2,1)S(1)}, u32[]{:S(2)}, u32[]{:S(2)}) %collective-permute-start.15) | collective-permute-done | bytes 102432 | tf_op jit(solution)/shard_map/ppermute | solution.py:393
  84.6 0.6 add_last.5
  85.2 0.5 collective-permute-done.14.refs_1_
  85.7 0.6 add_last.6
  86.3 0.0 collective-permute-done.13.refs_1_
  86.3 0.6 add_last.7
  87.0 0.1 collective-permute-start.17
  87.0 0.5 collective-permute-start.18
  87.5 0.1 collective-permute-start.19
  87.6 0.6 add_last.8
  88.2 0.5 collective-permute-start.20
  88.7 0.0 collective-permute-done.11.refs_1_
  88.7 0.6 add_last.9
  89.4 0.1 collective-permute-start.16
  89.5 0.0 collective-permute-done.18.refs_6_
  89.5 0.0 collective-permute-done.19.refs_8_
  89.5 0.1 collective-permute-done.20.refs_10_
  89.6 1.0 %collective-permute-done.16.refs_2_ = bf16[32,768]{1,0:T(8,128)(2,1)S(1)} collective-permute-done((bf16[32,768]{1,0:T(8,128)(2,1)S(1)}, bf16[32,768]{1,0:T(8,128)(2,1)S(1)}, u32[]{:S(2)}, u32[]{:S(2)}) %collective-permute-start.16) | collective-permute-done | bytes 49184 | tf_op jit(solution)/shard_map/ppermute | solution.py:393
  90.7 1.4 %lay_out.1 = bf16[32,8192]{1,0:T(8,128)(2,1)} custom-call(s32[2]{0:T(128)S(1)} %pad_add_fusion.refs_0_, bf16[32,768]{1,0:T(8,128)(2,1)S(1)} %get-tuple-element.85.refs_1_, bf16[32,768]{1,0:T(8,128)(2,1)S(1)} %collective-permute-done.16.refs_2_, bf16[32,1024]{1,0:T(8,128)(2,1)S(1)} %get-tuple-element.83.refs_3_, ...), custom_call_target="tpu_custom_call" | custom-call | bytes 1048576 | tf_op jit(solution)/shard_map/lay_out/pallas_call | solution.py:99
  (2 shorter events, 0.0 us)
Async XLA Ops:
  2.9 7.9 %collective-permute-start = (bf16[1024,1024]{1,0:T(8,128)(2,1)S(1)}, bf16[1024,1024]{1,0:T(8,128)(2,1)S(1)}, u32[]{:S(2)}, u32[]{:S(2)}) collective-permute-start(bf16[1024,1024]{1,0:T(8,128)(2,1)S(1)} %split_basis.1.refs_1_.refs_2_), channel_id=1, source_target_pairs={{0,1},{1,0},{2,3},{3,2},{4,5},{5,4},{6,7},{7,6},{8,9},{9,8},{10,11... | collective-permute-start | bytes 6291464 | tf_op jit(solution)/shard_map/ppermute | solution.py:393
  19.1 15.4 %collective-permute-start.3 = (bf16[2064,128]{1,0:T(8,128)(2,1)S(1)}, bf16[2064,128]{1,0:T(8,128)(2,1)S(1)}, u32[]{:S(2)}, u32[]{:S(2)}) collective-permute-start(bf16[2064,128]{1,0:T(8,128)(2,1)S(1)} %get-tuple-element.57), channel_id=1, source_target_pairs={{0,2},{1,3},{2,0},{3,1},{4,6},{5,7},{6,4},{7,5},{8,10},{9,11},{10,... | collective-permute-start | bytes 1585160 | tf_op jit(solution)/shard_map/ppermute | solution.py:393
  25.8 34.9 %collective-permute-start.6 = (bf16[1552,128]{1,0:T(8,128)(2,1)S(1)}, bf16[1552,128]{1,0:T(8,128)(2,1)S(1)}, u32[]{:S(2)}, u32[]{:S(2)}) collective-permute-start(bf16[1552,128]{1,0:T(8,128)(2,1)S(1)} %get-tuple-element.63), channel_id=1, source_target_pairs={{0,4},{1,5},{2,6},{3,7},{4,0},{5,1},{6,2},{7,3},{8,12},{9,13},{10,... | collective-permute-start | bytes 1191944 | tf_op jit(solution)/shard_map/ppermute | solution.py:393
  31.6 14.5 %collective-permute-start.2 = (bf16[1552,128]{1,0:T(8,128)(2,1)S(1)}, bf16[1552,128]{1,0:T(8,128)(2,1)S(1)}, u32[]{:S(2)}, u32[]{:S(2)}) collective-permute-start(bf16[1552,128]{1,0:T(8,128)(2,1)S(1)} %get-tuple-element.55), channel_id=1, source_target_pairs={{0,2},{1,3},{2,0},{3,1},{4,6},{5,7},{6,4},{7,5},{8,10},{9,11},{10,... | collective-permute-start | bytes 1191944 | tf_op jit(solution)/shard_map/ppermute | solution.py:393
  39.8 22.3 %collective-permute-start.5 = (bf16[1552,128]{1,0:T(8,128)(2,1)S(1)}, bf16[1552,128]{1,0:T(8,128)(2,1)S(1)}, u32[]{:S(2)}, u32[]{:S(2)}) collective-permute-start(bf16[1552,128]{1,0:T(8,128)(2,1)S(1)} %get-tuple-element.62), channel_id=1, source_target_pairs={{0,2},{1,3},{2,0},{3,1},{4,6},{5,7},{6,4},{7,5},{8,10},{9,11},{10,... | collective-permute-start | bytes 1191944 | tf_op jit(solution)/shard_map/ppermute | solution.py:393
  41.9 24.4 %collective-permute-start.1 = (bf16[1552,128]{1,0:T(8,128)(2,1)S(1)}, bf16[1552,128]{1,0:T(8,128)(2,1)S(1)}, u32[]{:S(2)}, u32[]{:S(2)}) collective-permute-start(bf16[1552,128]{1,0:T(8,128)(2,1)S(1)} %get-tuple-element.50), channel_id=1, source_target_pairs={{0,8},{1,9},{2,10},{3,11},{4,12},{5,13},{6,14},{7,15},{8,0},{9,1},... | collective-permute-start | bytes 1191944 | tf_op jit(solution)/shard_map/ppermute | solution.py:393
  44.5 15.4 %collective-permute-start.7 = (bf16[1040,128]{1,0:T(8,128)(2,1)S(1)}, bf16[1040,128]{1,0:T(8,128)(2,1)S(1)}, u32[]{:S(2)}, u32[]{:S(2)}) collective-permute-start(bf16[1040,128]{1,0:T(8,128)(2,1)S(1)} %get-tuple-element.64), channel_id=1, source_target_pairs={{0,4},{1,5},{2,6},{3,7},{4,0},{5,1},{6,2},{7,3},{8,12},{9,13},{10,... | collective-permute-start | bytes 798728 | tf_op jit(solution)/shard_map/ppermute | solution.py:393
  47.0 18.6 %collective-permute-start.4 = (bf16[784,128]{1,0:T(8,128)(2,1)S(1)}, bf16[784,128]{1,0:T(8,128)(2,1)S(1)}, u32[]{:S(2)}, u32[]{:S(2)}) collective-permute-start(bf16[784,128]{1,0:T(8,128)(2,1)S(1)} %get-tuple-element.60), channel_id=1, source_target_pairs={{0,4},{1,5},{2,6},{3,7},{4,0},{5,1},{6,2},{7,3},{8,12},{9,13},{10,... | collective-permute-start | bytes 602120 | tf_op jit(solution)/shard_map/ppermute | solution.py:393
  61.6 10.2 %collective-permute-start.10 = (bf16[784,128]{1,0:T(8,128)(2,1)S(1)}, bf16[784,128]{1,0:T(8,128)(2,1)S(1)}, u32[]{:S(2)}, u32[]{:S(2)}) collective-permute-start(bf16[784,128]{1,0:T(8,128)(2,1)S(1)} %get-tuple-element.72), channel_id=1, source_target_pairs={{0,2},{1,3},{2,0},{3,1},{4,6},{5,7},{6,4},{7,5},{8,10},{9,11},{10,... | collective-permute-start | bytes 602120 | tf_op jit(solution)/shard_map/ppermute | solution.py:393
  63.0 9.7 %collective-permute-start.9 = (bf16[784,128]{1,0:T(8,128)(2,1)S(1)}, bf16[784,128]{1,0:T(8,128)(2,1)S(1)}, u32[]{:S(2)}, u32[]{:S(2)}) collective-permute-start(bf16[784,128]{1,0:T(8,128)(2,1)S(1)} %get-tuple-element.71), channel_id=1, source_target_pairs={{0,4},{1,5},{2,6},{3,7},{4,0},{5,1},{6,2},{7,3},{8,12},{9,13},{10,... | collective-permute-start | bytes 602120 | tf_op jit(solution)/shard_map/ppermute | solution.py:393
  67.2 9.1 %collective-permute-start.8 = (bf16[784,128]{1,0:T(8,128)(2,1)S(1)}, bf16[784,128]{1,0:T(8,128)(2,1)S(1)}, u32[]{:S(2)}, u32[]{:S(2)}) collective-permute-start(bf16[784,128]{1,0:T(8,128)(2,1)S(1)} %get-tuple-element.69), channel_id=1, source_target_pairs={{0,2},{1,3},{2,0},{3,1},{4,6},{5,7},{6,4},{7,5},{8,10},{9,11},{10,... | collective-permute-start | bytes 602120 | tf_op jit(solution)/shard_map/ppermute | solution.py:393
  68.9 17.4 %collective-permute-start.13 = (bf16[528,128]{1,0:T(8,128)(2,1)S(1)}, bf16[528,128]{1,0:T(8,128)(2,1)S(1)}, u32[]{:S(2)}, u32[]{:S(2)}) collective-permute-start(bf16[528,128]{1,0:T(8,128)(2,1)S(1)} %get-tuple-element.78), channel_id=1, source_target_pairs={{0,8},{1,9},{2,10},{3,11},{4,12},{5,13},{6,14},{7,15},{8,0},{9,1},... | collective-permute-start | bytes 405512 | tf_op jit(solution)/shard_map/ppermute | solution.py:393
  68.9 15.7 %collective-permute-start.15 = (bf16[400,128]{1,0:T(8,128)(2,1)S(1)}, bf16[400,128]{1,0:T(8,128)(2,1)S(1)}, u32[]{:S(2)}, u32[]{:S(2)}) collective-permute-start(bf16[400,128]{1,0:T(8,128)(2,1)S(1)} %get-tuple-element.80), channel_id=1, source_target_pairs={{0,8},{1,9},{2,10},{3,11},{4,12},{5,13},{6,14},{7,15},{8,0},{9,1},... | collective-permute-start | bytes 307208 | tf_op jit(solution)/shard_map/ppermute | solution.py:393
  72.6 13.1 %collective-permute-start.14 = (bf16[400,128]{1,0:T(8,128)(2,1)S(1)}, bf16[400,128]{1,0:T(8,128)(2,1)S(1)}, u32[]{:S(2)}, u32[]{:S(2)}) collective-permute-start(bf16[400,128]{1,0:T(8,128)(2,1)S(1)} %get-tuple-element.79), channel_id=1, source_target_pairs={{0,8},{1,9},{2,10},{3,11},{4,12},{5,13},{6,14},{7,15},{8,0},{9,1},... | collective-permute-start | bytes 307208 | tf_op jit(solution)/shard_map/ppermute | solution.py:393
  73.4 14.2 %collective-permute-start.12 = (bf16[400,128]{1,0:T(8,128)(2,1)S(1)}, bf16[400,128]{1,0:T(8,128)(2,1)S(1)}, u32[]{:S(2)}, u32[]{:S(2)}) collective-permute-start(bf16[400,128]{1,0:T(8,128)(2,1)S(1)} %get-tuple-element.77), channel_id=1, source_target_pairs={{0,8},{1,9},{2,10},{3,11},{4,12},{5,13},{6,14},{7,15},{8,0},{9,1},... | collective-permute-start | bytes 307208 | tf_op jit(solution)/shard_map/ppermute | solution.py:393
  77.1 11.6 %collective-permute-start.11 = (bf16[400,128]{1,0:T(8,128)(2,1)S(1)}, bf16[400,128]{1,0:T(8,128)(2,1)S(1)}, u32[]{:S(2)}, u32[]{:S(2)}) collective-permute-start(bf16[400,128]{1,0:T(8,128)(2,1)S(1)} %get-tuple-element.75), channel_id=1, source_target_pairs={{0,4},{1,5},{2,6},{3,7},{4,0},{5,1},{6,2},{7,3},{8,12},{9,13},{10,... | collective-permute-start | bytes 307208 | tf_op jit(solution)/shard_map/ppermute | solution.py:393
  87.0 2.6 %collective-permute-start.17 = (bf16[32,1024]{1,0:T(8,128)(2,1)S(1)}, bf16[32,1024]{1,0:T(8,128)(2,1)S(1)}, u32[]{:S(2)}, u32[]{:S(2)}) collective-permute-start(bf16[32,1024]{1,0:T(8,128)(2,1)S(1)} %get-tuple-element.87), channel_id=1, source_target_pairs={{0,1},{1,0},{2,3},{3,2},{4,5},{5,4},{6,7},{7,6},{8,9},{9,8},{10,11... | collective-permute-start | bytes 196616 | tf_op jit(solution)/shard_map/ppermute | solution.py:393
  87.0 2.5 %collective-permute-start.18 = (bf16[32,768]{1,0:T(8,128)(2,1)S(1)}, bf16[32,768]{1,0:T(8,128)(2,1)S(1)}, u32[]{:S(2)}, u32[]{:S(2)}) collective-permute-start(bf16[32,768]{1,0:T(8,128)(2,1)S(1)} %get-tuple-element.88), channel_id=1, source_target_pairs={{0,1},{1,0},{2,3},{3,2},{4,5},{5,4},{6,7},{7,6},{8,9},{9,8},{10,11... | collective-permute-start | bytes 147464 | tf_op jit(solution)/shard_map/ppermute | solution.py:393
  87.5 2.0 %collective-permute-start.19 = (bf16[32,768]{1,0:T(8,128)(2,1)S(1)}, bf16[32,768]{1,0:T(8,128)(2,1)S(1)}, u32[]{:S(2)}, u32[]{:S(2)}) collective-permute-start(bf16[32,768]{1,0:T(8,128)(2,1)S(1)} %get-tuple-element.89), channel_id=1, source_target_pairs={{0,1},{1,0},{2,3},{3,2},{4,5},{5,4},{6,7},{7,6},{8,9},{9,8},{10,11... | collective-permute-start | bytes 147464 | tf_op jit(solution)/shard_map/ppermute | solution.py:393
  88.2 1.4 %collective-permute-start.20 = (bf16[32,768]{1,0:T(8,128)(2,1)S(1)}, bf16[32,768]{1,0:T(8,128)(2,1)S(1)}, u32[]{:S(2)}, u32[]{:S(2)}) collective-permute-start(bf16[32,768]{1,0:T(8,128)(2,1)S(1)} %get-tuple-element.90), channel_id=1, source_target_pairs={{0,1},{1,0},{2,3},{3,2},{4,5},{5,4},{6,7},{7,6},{8,9},{9,8},{10,11... | collective-permute-start | bytes 147464 | tf_op jit(solution)/shard_map/ppermute | solution.py:393
  89.4 1.3 %collective-permute-start.16 = (bf16[32,768]{1,0:T(8,128)(2,1)S(1)}, bf16[32,768]{1,0:T(8,128)(2,1)S(1)}, u32[]{:S(2)}, u32[]{:S(2)}) collective-permute-start(bf16[32,768]{1,0:T(8,128)(2,1)S(1)} %get-tuple-element.86), channel_id=1, source_target_pairs={{0,1},{1,0},{2,3},{3,2},{4,5},{5,4},{6,7},{7,6},{8,9},{9,8},{10,11... | collective-permute-start | bytes 147464 | tf_op jit(solution)/shard_map/ppermute | solution.py:393

commit v5 on v4

--- a/solution.py
+++ b/solution.py
@@ -17,17 +17,17 @@
 
 CHUNKS = [
     (3, (2, 0, 1)),
-    (4, (0, 1, 2)),
+    (4, (1, 0, 2)),
+    (3, (0, 2, 1)),
+    (3, (0, 1, 2)),
     (3, (1, 0, 2)),
-    (3, (0, 1, 2)),
-    (3, (0, 1, 2)),
 ]
 PARTS = 16
-EARLY = 2
+EARLY = 1
 ORDER = [
-    (0, 0), (1, 0), (2, 0), (3, 0), (1, 1), (4, 0), (3, 1), (1, 2),
-    (2, 1), (4, 1), (3, 2), (0, 1), (2, 2), (4, 2), (0, 2), (3, 3),
-    (2, 3), (1, 3), (4, 3), (0, 3),
+    (0, 0), (1, 0), (2, 0), (3, 0), (4, 0), (1, 1), (2, 1), (3, 1),
+    (0, 1), (4, 1), (1, 2), (2, 2), (4, 2), (0, 2), (3, 2), (1, 3),
+    (2, 3), (0, 3), (4, 3), (3, 3),
 ]
 
 
@@ -236,7 +236,7 @@
     if bring:
         w_ref, message_ref, kept_ref, later_ref, sems = refs[-5:]
         boxes = row_boxes(range(pieces), depth, later_ref.shape[1])
-        copies = weight_copies(place_ref, w_ref, later_ref, sems, bring, depth, boxes)
+        copies = weight_copies(place_ref, w_ref, later_ref, sems, bring.start, depth, boxes)
         for copy in copies:
             copy.start()
     else:
@@ -282,7 +282,7 @@
     outs = outputs(width, step, leave, stay)
     scratch = []
     if bring:
-        later = weights.shape[2] - bring
+        later = bring.stop - bring.start
         outs.append(jax.ShapeDtypeStruct((pieces * depth, later), jnp.bfloat16))
         scratch = [pltpu.SemaphoreType.DMA((len(row_boxes(range(pieces), depth, later)),))]
     return call(
@@ -415,9 +415,9 @@
     cuts = [cut * (width // LANES) // PARTS * LANES for cut in cuts]
     orders = [[bit for bit in order if bit < bits] for _, order in CHUNKS]
     stages = [split_places(order, bits) for order in orders]
-    ahead = cuts[EARLY]
-    near, partial = early(own, weights, places, pieces, ahead, [])
-
+    near, partial = early(own, weights, places, pieces, cuts[EARLY], [])
+
+    held = {}
     state = {}
     after = [partial]
     finished = {}
@@ -425,25 +425,25 @@
         order = orders[index]
         start = cuts[index]
         chunk = cuts[index + 1] - start
-        if chunk == 0:
-            continue
         if number == 0:
             early_one = index < EARLY
+            ahead = index + EARLY
+            bring = slice(*cuts[ahead : ahead + 2]) if ahead < len(CHUNKS) else None
             out = product(
                 left,
-                near if early_one else later,
+                near if early_one else held[index],
                 partial if early_one else None,
                 weights,
                 places,
-                start if early_one else start - ahead,
+                start if early_one else 0,
                 chunk,
-                ahead if index == EARLY - 1 else 0,
+                bring,
                 step,
                 *stages[index][0],
                 after,
             )
-            if index == EARLY - 1:
-                later = out[2]
+            if bring:
+                held[ahead] = out[2]
         elif number < bits:
             message, kept = state[index]
             old = stages[index][number - 1][1]

time: 92.2 us -> 83.4 us (0.905)
  waiting for transfers between devices: 23.7 us -> 14 us
  Pallas kernels: 43.9 us -> 47.5 us
  starting transfers between devices: 24.2 us -> 21.4 us
    ppermute x21, waiting for transfers between devices: 23.7 us -> 14 us  [swapped(): return lax.ppermute(block, 'row', [(i, i ^ apart) for i in range(count)])]
    pallas_call x23, Pallas kernels: 43.9 us -> 47.5 us  [call(): pl.pallas_call(run, in_specs=[pl.BlockSpec(memory_space=pltpu.SMEM)] + [v...]
    ppermute x21, starting transfers between devices: 24.2 us -> 21.4 us  [swapped(): return lax.ppermute(block, 'row', [(i, i ^ apart) for i in range(count)])]
  transfers between devices with their start and end apart: 21 -> 21, of which waited for: 6 -> 8; matrix products, arithmetic and copies ran while one was open for 0% -> 0% of each run, Pallas kernels for 34% -> 47%
where the time goes in v5:
time: 83.4 us; the launch traced here: 83.2 us
  Pallas kernels  47.5 us (57%)
  starting transfers between devices  21.4 us (26%)
  waiting for transfers between devices  14 us (17%)
    pallas_call x23, Pallas kernels, call(): pl.pallas_call(run, in_specs=[pl.BlockSpec(memory_space=pltpu.SMEM)] + [v...  47.5 us
    ppermute x21, starting transfers between devices, swapped(): return lax.ppermute(block, 'row', [(i, i ^ apart) for i in range(count)])  21.4 us
    ppermute x21, waiting for transfers between devices, swapped(): return lax.ppermute(block, 'row', [(i, i ^ apart) for i in range(count)])  14 us
  transfers between devices with their start and end apart: 21, of which 8 were waited for; matrix products, arithmetic and copies ran while one was open for 0% of the time, Pallas kernels for 47%

profile of v5, /device:TPU:0, one launch (start us, length us, event | category | flops | bytes accessed | tf_op | source)
XLA Modules:
  0.0 83.2 jit_solution(11430265955967400538)
XLA Ops:
  0.0 0.1 pad_add_fusion.refs_0_
  0.1 2.8 %split_basis.1.refs_1_.refs_2_ = bf16[1024,1024]{1,0:T(8,128)(2,1)S(1)} custom-call(s32[2]{0:T(128)S(1)} %pad_add_fusion.refs_0_, f32[1024,512]{1,0:T(8,128)} %refs_1_.1), custom_call_target="tpu_custom_call" | custom-call | flops 1048576 | bytes 4194304 | tf_op jit(solution)/shard_map/split_basis/pallas_call | solution.py:99
  2.9 0.5 collective-permute-start
  3.4 4.9 %early_products.1 = (bf16[2048,768]{1,0:T(8,128)(2,1)S(1)}, f32[512,768]{1,0:T(8,128)S(1)}) custom-call(s32[2]{0:T(128)S(1)} %pad_add_fusion.refs_0_, bf16[1024,1024]{1,0:T(8,128)(2,1)S(1)} %split_basis.1.refs_1_.refs_2_, bf16[1,2048,4096]{2,1,0:T(8,128)(2,1)} %refs_4_.5), custom_call_target="tpu_custom_call" | custom-call | flops 1610612736 | bytes 3145728 | tf_op jit(solution)/shard_map/early_products/pallas_call | solution.py:99
  8.2 0.0 collective-permute-done.refs_3_
  8.3 4.6 %product.5 = (bf16[1552,128]{1,0:T(8,128)(2,1)S(1)}, f32[1536,128]{1,0:T(8,128)S(1)}, bf16[2048,1024]{1,0:T(8,128)(2,1)S(1)}) custom-call(s32[2]{0:T(128)S(1)} %pad_add_fusion.refs_0_, bf16[2048,768]{1,0:T(8,128)(2,1)S(1)} %get-tuple-element.51.refs_1_, bf16[1024,1024]{1,0:T(8,128)(2,1)S(1)} %split_basis.1.refs_1_.refs_2_, ...), custom_call_target="tpu_custom_call" | custom-call | flops 1610612736 | bytes 4718592 | tf_op jit(solution)/shard_map/product/pallas_call | solution.py:99
  12.8 3.7 %collective-permute-start.1 = (bf16[1552,128]{1,0:T(8,128)(2,1)S(1)}, bf16[1552,128]{1,0:T(8,128)(2,1)S(1)}, u32[]{:S(2)}, u32[]{:S(2)}) collective-permute-start(bf16[1552,128]{1,0:T(8,128)(2,1)S(1)} %get-tuple-element.53), channel_id=1, source_target_pairs={{0,8},{1,9},{2,10},{3,11},{4,12},{5,13},{6,14},{7,15},{8,0},{9,1},... | collective-permute-start | bytes 1191944 | tf_op jit(solution)/shard_map/ppermute | solution.py:393
  16.5 7.1 %product.6 = (bf16[2064,128]{1,0:T(8,128)(2,1)S(1)}, f32[2048,128]{1,0:T(8,128)S(1)}, bf16[2048,768]{1,0:T(8,128)(2,1)S(1)}) custom-call(s32[2]{0:T(128)S(1)} %pad_add_fusion.refs_0_, bf16[2048,1024]{1,0:T(8,128)(2,1)S(1)} %get-tuple-element.55.refs_1_, bf16[1024,1024]{1,0:T(8,128)(2,1)S(1)} %split_basis.1.refs_1_.refs_2_, ...), custom_call_target="tpu_custom_call" | custom-call | flops 4294967296 | bytes 8388608 | tf_op jit(solution)/shard_map/product/pallas_call | solution.py:99
  23.6 1.6 %collective-permute-start.4 = (bf16[2064,128]{1,0:T(8,128)(2,1)S(1)}, bf16[2064,128]{1,0:T(8,128)(2,1)S(1)}, u32[]{:S(2)}, u32[]{:S(2)}) collective-permute-start(bf16[2064,128]{1,0:T(8,128)(2,1)S(1)} %get-tuple-element.63), channel_id=1, source_target_pairs={{0,4},{1,5},{2,6},{3,7},{4,0},{5,1},{6,2},{7,3},{8,12},{9,13},{10,... | collective-permute-start | bytes 1585160 | tf_op jit(solution)/shard_map/ppermute | solution.py:393
  25.2 5.5 %product.7 = (bf16[1552,128]{1,0:T(8,128)(2,1)S(1)}, f32[1536,128]{1,0:T(8,128)S(1)}, bf16[2048,768]{1,0:T(8,128)(2,1)S(1)}) custom-call(s32[2]{0:T(128)S(1)} %pad_add_fusion.refs_0_, bf16[2048,768]{1,0:T(8,128)(2,1)S(1)} %get-tuple-element.56.refs_1_, bf16[1024,1024]{1,0:T(8,128)(2,1)S(1)} %split_basis.1.refs_1_.refs_2_, ...), custom_call_target="tpu_custom_call" | custom-call | flops 3221225472 | bytes 6291456 | tf_op jit(solution)/shard_map/product/pallas_call | solution.py:99
  30.8 1.6 %collective-permute-start.3 = (bf16[1552,128]{1,0:T(8,128)(2,1)S(1)}, bf16[1552,128]{1,0:T(8,128)(2,1)S(1)}, u32[]{:S(2)}, u32[]{:S(2)}) collective-permute-start(bf16[1552,128]{1,0:T(8,128)(2,1)S(1)} %get-tuple-element.62), channel_id=1, source_target_pairs={{0,2},{1,3},{2,0},{3,1},{4,6},{5,7},{6,4},{7,5},{8,10},{9,11},{10,... | collective-permute-start | bytes 1191944 | tf_op jit(solution)/shard_map/ppermute | solution.py:393
  32.4 5.5 %product.8 = (bf16[1552,128]{1,0:T(8,128)(2,1)S(1)}, f32[1536,128]{1,0:T(8,128)S(1)}, bf16[2048,768]{1,0:T(8,128)(2,1)S(1)}) custom-call(s32[2]{0:T(128)S(1)} %pad_add_fusion.refs_0_, bf16[2048,768]{1,0:T(8,128)(2,1)S(1)} %get-tuple-element.58.refs_1_, bf16[1024,1024]{1,0:T(8,128)(2,1)S(1)} %split_basis.1.refs_1_.refs_2_, ...), custom_call_target="tpu_custom_call" | custom-call | flops 3221225472 | bytes 6291456 | tf_op jit(solution)/shard_map/product/pallas_call | solution.py:99
  37.9 0.5 collective-permute-start.2
  38.4 4.3 %product.9 = (bf16[1552,128]{1,0:T(8,128)(2,1)S(1)}, f32[1536,128]{1,0:T(8,128)S(1)}) custom-call(s32[2]{0:T(128)S(1)} %pad_add_fusion.refs_0_, bf16[2048,768]{1,0:T(8,128)(2,1)S(1)} %get-tuple-element.64.refs_1_, bf16[1024,1024]{1,0:T(8,128)(2,1)S(1)} %split_basis.1.refs_1_.refs_2_, bf16[1024,1024]{1,0:T(8,128)(2,1)S(1)} %collective-permute-done.refs_3_, ...), custom_call_target="tpu_custom_call" | custom-call | flops 3221225472 | bytes 6291456 | tf_op jit(solution)/shard_map/product/pallas_call | solution.py:99
  42.7 0.5 collective-permute-start.6
  43.3 2.2 %collective-permute-done.4.refs_1_ = bf16[2064,128]{1,0:T(8,128)(2,1)S(1)} collective-permute-done((bf16[2064,128]{1,0:T(8,128)(2,1)S(1)}, bf16[2064,128]{1,0:T(8,128)(2,1)S(1)}, u32[]{:S(2)}, u32[]{:S(2)}) %collective-permute-start.4) | collective-permute-done | bytes 528416 | tf_op jit(solution)/shard_map/ppermute | solution.py:393
  45.4 1.0 %add_and_split.10 = (bf16[1040,128]{1,0:T(8,128)(2,1)S(1)}, f32[1024,128]{1,0:T(8,128)S(1)}) custom-call(s32[2]{0:T(128)S(1)} %pad_add_fusion.refs_0_, bf16[2064,128]{1,0:T(8,128)(2,1)S(1)} %collective-permute-done.4.refs_1_, f32[2048,128]{1,0:T(8,128)S(1)} %get-tuple-element.57.refs_5_.refs_2_, f32[1536,128]{1,0:T(8,128)S(1)} %get-tuple-element.65.refs_3_.refs_2_), custom_call_target="tpu_custom_call" | custom-call | flops 5242880 | bytes 2359296 | tf_op jit(solution)/shard_map/add_and_split/pallas_call | solution.py:99
  46.5 1.7 %collective-permute-start.9 = (bf16[1040,128]{1,0:T(8,128)(2,1)S(1)}, bf16[1040,128]{1,0:T(8,128)(2,1)S(1)}, u32[]{:S(2)}, u32[]{:S(2)}) collective-permute-start(bf16[1040,128]{1,0:T(8,128)(2,1)S(1)} %get-tuple-element.75), channel_id=1, source_target_pairs={{0,2},{1,3},{2,0},{3,1},{4,6},{5,7},{6,4},{7,5},{8,10},{9,11},{10,... | collective-permute-start | bytes 798728 | tf_op jit(solution)/shard_map/ppermute | solution.py:393
  48.2 0.0 collective-permute-done.3.refs_1_
  48.2 0.9 %add_and_split.11 = (bf16[784,128]{1,0:T(8,128)(2,1)S(1)}, f32[768,128]{1,0:T(8,128)S(1)}) custom-call(s32[2]{0:T(128)S(1)} %pad_add_fusion.refs_0_, bf16[1552,128]{1,0:T(8,128)(2,1)S(1)} %collective-permute-done.3.refs_1_, f32[1536,128]{1,0:T(8,128)S(1)} %get-tuple-element.59.refs_5_.refs_2_, f32[1024,128]{1,0:T(8,128)S(1)} %get-tuple-element.66.refs_3_.refs_2_), custom_call_target="tpu_custom_call" | custom-call | flops 3932160 | bytes 1769472 | tf_op jit(solution)/shard_map/add_and_split/pallas_call | solution.py:99
  49.1 0.9 %collective-permute-start.8 = (bf16[784,128]{1,0:T(8,128)(2,1)S(1)}, bf16[784,128]{1,0:T(8,128)(2,1)S(1)}, u32[]{:S(2)}, u32[]{:S(2)}) collective-permute-start(bf16[784,128]{1,0:T(8,128)(2,1)S(1)} %get-tuple-element.74), channel_id=1, source_target_pairs={{0,8},{1,9},{2,10},{3,11},{4,12},{5,13},{6,14},{7,15},{8,0},{9,1},... | collective-permute-start | bytes 602120 | tf_op jit(solution)/shard_map/ppermute | solution.py:393
  50.0 1.5 %collective-permute-done.2.refs_1_ = bf16[1552,128]{1,0:T(8,128)(2,1)S(1)} collective-permute-done((bf16[1552,128]{1,0:T(8,128)(2,1)S(1)}, bf16[1552,128]{1,0:T(8,128)(2,1)S(1)}, u32[]{:S(2)}, u32[]{:S(2)}) %collective-permute-start.2) | collective-permute-done | bytes 397344 | tf_op jit(solution)/shard_map/ppermute | solution.py:393
  51.4 0.9 %add_and_split.12 = (bf16[784,128]{1,0:T(8,128)(2,1)S(1)}, f32[768,128]{1,0:T(8,128)S(1)}) custom-call(s32[2]{0:T(128)S(1)} %pad_add_fusion.refs_0_, bf16[1552,128]{1,0:T(8,128)(2,1)S(1)} %collective-permute-done.2.refs_1_, f32[1536,128]{1,0:T(8,128)S(1)} %get-tuple-element.61.refs_4_.refs_2_, f32[768,128]{1,0:T(8,128)S(1)} %get-tuple-element.67.refs_3_.refs_2_), custom_call_target="tpu_custom_call" | custom-call | flops 3932160 | bytes 1769472 | tf_op jit(solution)/shard_map/add_and_split/pallas_call | solution.py:99
  52.3 0.9 %add_and_split.13 = (bf16[784,128]{1,0:T(8,128)(2,1)S(1)}, f32[768,128]{1,0:T(8,128)S(1)}) custom-call(s32[2]{0:T(128)S(1)} %pad_add_fusion.refs_0_, bf16[1552,128]{1,0:T(8,128)(2,1)S(1)} %collective-permute-done.1.refs_1_, f32[1536,128]{1,0:T(8,128)S(1)} %get-tuple-element.54.refs_5_.refs_2_, f32[768,128]{1,0:T(8,128)S(1)} %get-tuple-element.68.refs_3_.refs_2_), custom_call_target="tpu_custom_call" | custom-call | flops 3932160 | bytes 1769472 | tf_op jit(solution)/shard_map/add_and_split/pallas_call | solution.py:99
  53.2 2.2 %collective-permute-done.6.refs_1_ = bf16[1552,128]{1,0:T(8,128)(2,1)S(1)} collective-permute-done((bf16[1552,128]{1,0:T(8,128)(2,1)S(1)}, bf16[1552,128]{1,0:T(8,128)(2,1)S(1)}, u32[]{:S(2)}, u32[]{:S(2)}) %collective-permute-start.6) | collective-permute-done | bytes 397344 | tf_op jit(solution)/shard_map/ppermute | solution.py:393
  55.4 0.9 %add_and_split.14 = (bf16[784,128]{1,0:T(8,128)(2,1)S(1)}, f32[768,128]{1,0:T(8,128)S(1)}) custom-call(s32[2]{0:T(128)S(1)} %pad_add_fusion.refs_0_, bf16[1552,128]{1,0:T(8,128)(2,1)S(1)} %collective-permute-done.6.refs_1_, f32[1536,128]{1,0:T(8,128)S(1)} %get-tuple-element.65.refs_3_.refs_2_, f32[768,128]{1,0:T(8,128)S(1)} %get-tuple-element.70.refs_3_.refs_2_), custom_call_target="tpu_custom_call" | custom-call | flops 3932160 | bytes 1769472 | tf_op jit(solution)/shard_map/add_and_split/pallas_call | solution.py:99
  56.3 2.7 %collective-permute-start.7 = (bf16[784,128]{1,0:T(8,128)(2,1)S(1)}, bf16[784,128]{1,0:T(8,128)(2,1)S(1)}, u32[]{:S(2)}, u32[]{:S(2)}) collective-permute-start(bf16[784,128]{1,0:T(8,128)(2,1)S(1)} %get-tuple-element.72), channel_id=1, source_target_pairs={{0,2},{1,3},{2,0},{3,1},{4,6},{5,7},{6,4},{7,5},{8,10},{9,11},{10,... | collective-permute-start | bytes 602120 | tf_op jit(solution)/shard_map/ppermute | solution.py:393
  59.0 0.1 collective-permute-start.5
  59.1 0.0 collective-permute-start.13
  59.1 0.0 collective-permute-done.9.refs_1_
  59.1 0.8 add_and_split.15
  59.9 3.1 %collective-permute-start.12 = (bf16[528,128]{1,0:T(8,128)(2,1)S(1)}, bf16[528,128]{1,0:T(8,128)(2,1)S(1)}, u32[]{:S(2)}, u32[]{:S(2)}) collective-permute-start(bf16[528,128]{1,0:T(8,128)(2,1)S(1)} %get-tuple-element.82), channel_id=1, source_target_pairs={{0,8},{1,9},{2,10},{3,11},{4,12},{5,13},{6,14},{7,15},{8,0},{9,1},... | collective-permute-start | bytes 405512 | tf_op jit(solution)/shard_map/ppermute | solution.py:393
  63.0 0.0 collective-permute-done.8.refs_1_
  63.0 0.7 add_and_split.16
  63.7 0.1 collective-permute-start.11
  63.8 1.1 %collective-permute-done.7.refs_1_ = bf16[784,128]{1,0:T(8,128)(2,1)S(1)} collective-permute-done((bf16[784,128]{1,0:T(8,128)(2,1)S(1)}, bf16[784,128]{1,0:T(8,128)(2,1)S(1)}, u32[]{:S(2)}, u32[]{:S(2)}) %collective-permute-start.7) | collective-permute-done | bytes 200736 | tf_op jit(solution)/shard_map/ppermute | solution.py:393
  64.9 0.7 add_and_split.17
  65.7 1.7 %collective-permute-done.5.refs_1_ = bf16[784,128]{1,0:T(8,128)(2,1)S(1)} collective-permute-done((bf16[784,128]{1,0:T(8,128)(2,1)S(1)}, bf16[784,128]{1,0:T(8,128)(2,1)S(1)}, u32[]{:S(2)}, u32[]{:S(2)}) %collective-permute-start.5) | collective-permute-done | bytes 200736 | tf_op jit(solution)/shard_map/ppermute | solution.py:393
  67.3 0.7 add_and_split.18
  68.1 0.1 collective-permute-start.10
  68.2 3.5 %collective-permute-start.18 = (bf16[400,128]{1,0:T(8,128)(2,1)S(1)}, bf16[400,128]{1,0:T(8,128)(2,1)S(1)}, u32[]{:S(2)}, u32[]{:S(2)}) collective-permute-start(bf16[400,128]{1,0:T(8,128)(2,1)S(1)} %get-tuple-element.92), channel_id=1, source_target_pairs={{0,8},{1,9},{2,10},{3,11},{4,12},{5,13},{6,14},{7,15},{8,0},{9,1},... | collective-permute-start | bytes 307208 | tf_op jit(solution)/shard_map/ppermute | solution.py:393
  71.7 0.0 collective-permute-done.13.refs_1_
  71.7 0.7 add_and_split.19
  72.4 0.1 collective-permute-start.17
  72.5 0.0 collective-permute-done.12.refs_1_
  72.5 0.6 add_last.5
  73.2 0.1 collective-permute-start.15
  73.2 0.0 collective-permute-done.11.refs_1_
  73.2 0.6 add_last.6
  73.9 0.0 collective-permute-done.10.refs_1_
  73.9 0.6 add_last.7
  74.5 3.5 %collective-permute-done.18.refs_1_ = bf16[400,128]{1,0:T(8,128)(2,1)S(1)} collective-permute-done((bf16[400,128]{1,0:T(8,128)(2,1)S(1)}, bf16[400,128]{1,0:T(8,128)(2,1)S(1)}, u32[]{:S(2)}, u32[]{:S(2)}) %collective-permute-start.18) | collective-permute-done | bytes 102432 | tf_op jit(solution)/shard_map/ppermute | solution.py:393
  78.0 0.6 add_last.8
  78.7 0.1 collective-permute-start.20
  78.7 0.5 collective-permute-start.14
  79.2 0.1 collective-permute-start.16
  79.3 0.6 collective-permute-done.17.refs_1_
  79.9 0.6 add_last.9
  80.5 0.1 collective-permute-start.19
  80.6 0.0 collective-permute-done.20.refs_10_
  80.6 0.0 collective-permute-done.16.refs_6_
  80.7 1.2 %collective-permute-done.19.refs_8_ = bf16[32,768]{1,0:T(8,128)(2,1)S(1)} collective-permute-done((bf16[32,768]{1,0:T(8,128)(2,1)S(1)}, bf16[32,768]{1,0:T(8,128)(2,1)S(1)}, u32[]{:S(2)}, u32[]{:S(2)}) %collective-permute-start.19) | collective-permute-done | bytes 49184 | tf_op jit(solution)/shard_map/ppermute | solution.py:393
  81.8 0.0 collective-permute-done.15.refs_4_
  81.8 1.4 %lay_out.1 = bf16[32,8192]{1,0:T(8,128)(2,1)} custom-call(s32[2]{0:T(128)S(1)} %pad_add_fusion.refs_0_, bf16[32,768]{1,0:T(8,128)(2,1)S(1)} %get-tuple-element.87.refs_3_.refs_1_, bf16[32,768]{1,0:T(8,128)(2,1)S(1)} %collective-permute-done.14.refs_2_, bf16[32,1024]{1,0:T(8,128)(2,1)S(1)} %get-tuple-element.85.refs_3_, ...), custom_call_target="tpu_custom_call" | custom-call | bytes 1048576 | tf_op jit(solution)/shard_map/lay_out/pallas_call | solution.py:99
  (2 shorter events, 0.0 us)
Async XLA Ops:
  2.9 5.4 %collective-permute-start = (bf16[1024,1024]{1,0:T(8,128)(2,1)S(1)}, bf16[1024,1024]{1,0:T(8,128)(2,1)S(1)}, u32[]{:S(2)}, u32[]{:S(2)}) collective-permute-start(bf16[1024,1024]{1,0:T(8,128)(2,1)S(1)} %split_basis.1.refs_1_.refs_2_), channel_id=1, source_target_pairs={{0,1},{1,0},{2,3},{3,2},{4,5},{5,4},{6,7},{7,6},{8,9},{9,8},{10,11... | collective-permute-start | bytes 6291464 | tf_op jit(solution)/shard_map/ppermute | solution.py:393
  12.8 39.5 %collective-permute-start.1 = (bf16[1552,128]{1,0:T(8,128)(2,1)S(1)}, bf16[1552,128]{1,0:T(8,128)(2,1)S(1)}, u32[]{:S(2)}, u32[]{:S(2)}) collective-permute-start(bf16[1552,128]{1,0:T(8,128)(2,1)S(1)} %get-tuple-element.53), channel_id=1, source_target_pairs={{0,8},{1,9},{2,10},{3,11},{4,12},{5,13},{6,14},{7,15},{8,0},{9,1},... | collective-permute-start | bytes 1191944 | tf_op jit(solution)/shard_map/ppermute | solution.py:393
  23.6 21.8 %collective-permute-start.4 = (bf16[2064,128]{1,0:T(8,128)(2,1)S(1)}, bf16[2064,128]{1,0:T(8,128)(2,1)S(1)}, u32[]{:S(2)}, u32[]{:S(2)}) collective-permute-start(bf16[2064,128]{1,0:T(8,128)(2,1)S(1)} %get-tuple-element.63), channel_id=1, source_target_pairs={{0,4},{1,5},{2,6},{3,7},{4,0},{5,1},{6,2},{7,3},{8,12},{9,13},{10,... | collective-permute-start | bytes 1585160 | tf_op jit(solution)/shard_map/ppermute | solution.py:393
  30.8 17.4 %collective-permute-start.3 = (bf16[1552,128]{1,0:T(8,128)(2,1)S(1)}, bf16[1552,128]{1,0:T(8,128)(2,1)S(1)}, u32[]{:S(2)}, u32[]{:S(2)}) collective-permute-start(bf16[1552,128]{1,0:T(8,128)(2,1)S(1)} %get-tuple-element.62), channel_id=1, source_target_pairs={{0,2},{1,3},{2,0},{3,1},{4,6},{5,7},{6,4},{7,5},{8,10},{9,11},{10,... | collective-permute-start | bytes 1191944 | tf_op jit(solution)/shard_map/ppermute | solution.py:393
  37.9 13.5 %collective-permute-start.2 = (bf16[1552,128]{1,0:T(8,128)(2,1)S(1)}, bf16[1552,128]{1,0:T(8,128)(2,1)S(1)}, u32[]{:S(2)}, u32[]{:S(2)}) collective-permute-start(bf16[1552,128]{1,0:T(8,128)(2,1)S(1)} %get-tuple-element.60), channel_id=1, source_target_pairs={{0,2},{1,3},{2,0},{3,1},{4,6},{5,7},{6,4},{7,5},{8,10},{9,11},{10,... | collective-permute-start | bytes 1191944 | tf_op jit(solution)/shard_map/ppermute | solution.py:393
  42.7 12.7 %collective-permute-start.6 = (bf16[1552,128]{1,0:T(8,128)(2,1)S(1)}, bf16[1552,128]{1,0:T(8,128)(2,1)S(1)}, u32[]{:S(2)}, u32[]{:S(2)}) collective-permute-start(bf16[1552,128]{1,0:T(8,128)(2,1)S(1)} %get-tuple-element.71), channel_id=1, source_target_pairs={{0,4},{1,5},{2,6},{3,7},{4,0},{5,1},{6,2},{7,3},{8,12},{9,13},{10,... | collective-permute-start | bytes 1191944 | tf_op jit(solution)/shard_map/ppermute | solution.py:393
  46.5 12.6 %collective-permute-start.9 = (bf16[1040,128]{1,0:T(8,128)(2,1)S(1)}, bf16[1040,128]{1,0:T(8,128)(2,1)S(1)}, u32[]{:S(2)}, u32[]{:S(2)}) collective-permute-start(bf16[1040,128]{1,0:T(8,128)(2,1)S(1)} %get-tuple-element.75), channel_id=1, source_target_pairs={{0,2},{1,3},{2,0},{3,1},{4,6},{5,7},{6,4},{7,5},{8,10},{9,11},{10,... | collective-permute-start | bytes 798728 | tf_op jit(solution)/shard_map/ppermute | solution.py:393
  49.1 13.9 %collective-permute-start.8 = (bf16[784,128]{1,0:T(8,128)(2,1)S(1)}, bf16[784,128]{1,0:T(8,128)(2,1)S(1)}, u32[]{:S(2)}, u32[]{:S(2)}) collective-permute-start(bf16[784,128]{1,0:T(8,128)(2,1)S(1)} %get-tuple-element.74), channel_id=1, source_target_pairs={{0,8},{1,9},{2,10},{3,11},{4,12},{5,13},{6,14},{7,15},{8,0},{9,1},... | collective-permute-start | bytes 602120 | tf_op jit(solution)/shard_map/ppermute | solution.py:393
  56.3 8.6 %collective-permute-start.7 = (bf16[784,128]{1,0:T(8,128)(2,1)S(1)}, bf16[784,128]{1,0:T(8,128)(2,1)S(1)}, u32[]{:S(2)}, u32[]{:S(2)}) collective-permute-start(bf16[784,128]{1,0:T(8,128)(2,1)S(1)} %get-tuple-element.72), channel_id=1, source_target_pairs={{0,2},{1,3},{2,0},{3,1},{4,6},{5,7},{6,4},{7,5},{8,10},{9,11},{10,... | collective-permute-start | bytes 602120 | tf_op jit(solution)/shard_map/ppermute | solution.py:393
  59.0 8.3 %collective-permute-start.5 = (bf16[784,128]{1,0:T(8,128)(2,1)S(1)}, bf16[784,128]{1,0:T(8,128)(2,1)S(1)}, u32[]{:S(2)}, u32[]{:S(2)}) collective-permute-start(bf16[784,128]{1,0:T(8,128)(2,1)S(1)} %get-tuple-element.69), channel_id=1, source_target_pairs={{0,2},{1,3},{2,0},{3,1},{4,6},{5,7},{6,4},{7,5},{8,10},{9,11},{10,... | collective-permute-start | bytes 602120 | tf_op jit(solution)/shard_map/ppermute | solution.py:393
  59.1 12.6 %collective-permute-start.13 = (bf16[784,128]{1,0:T(8,128)(2,1)S(1)}, bf16[784,128]{1,0:T(8,128)(2,1)S(1)}, u32[]{:S(2)}, u32[]{:S(2)}) collective-permute-start(bf16[784,128]{1,0:T(8,128)(2,1)S(1)} %get-tuple-element.83), channel_id=1, source_target_pairs={{0,4},{1,5},{2,6},{3,7},{4,0},{5,1},{6,2},{7,3},{8,12},{9,13},{10,... | collective-permute-start | bytes 602120 | tf_op jit(solution)/shard_map/ppermute | solution.py:393
  59.9 12.6 %collective-permute-start.12 = (bf16[528,128]{1,0:T(8,128)(2,1)S(1)}, bf16[528,128]{1,0:T(8,128)(2,1)S(1)}, u32[]{:S(2)}, u32[]{:S(2)}) collective-permute-start(bf16[528,128]{1,0:T(8,128)(2,1)S(1)} %get-tuple-element.82), channel_id=1, source_target_pairs={{0,8},{1,9},{2,10},{3,11},{4,12},{5,13},{6,14},{7,15},{8,0},{9,1},... | collective-permute-start | bytes 405512 | tf_op jit(solution)/shard_map/ppermute | solution.py:393
  63.7 9.5 %collective-permute-start.11 = (bf16[400,128]{1,0:T(8,128)(2,1)S(1)}, bf16[400,128]{1,0:T(8,128)(2,1)S(1)}, u32[]{:S(2)}, u32[]{:S(2)}) collective-permute-start(bf16[400,128]{1,0:T(8,128)(2,1)S(1)} %get-tuple-element.81), channel_id=1, source_target_pairs={{0,4},{1,5},{2,6},{3,7},{4,0},{5,1},{6,2},{7,3},{8,12},{9,13},{10,... | collective-permute-start | bytes 307208 | tf_op jit(solution)/shard_map/ppermute | solution.py:393
  68.1 5.8 %collective-permute-start.10 = (bf16[400,128]{1,0:T(8,128)(2,1)S(1)}, bf16[400,128]{1,0:T(8,128)(2,1)S(1)}, u32[]{:S(2)}, u32[]{:S(2)}) collective-permute-start(bf16[400,128]{1,0:T(8,128)(2,1)S(1)} %get-tuple-element.79), channel_id=1, source_target_pairs={{0,4},{1,5},{2,6},{3,7},{4,0},{5,1},{6,2},{7,3},{8,12},{9,13},{10,... | collective-permute-start | bytes 307208 | tf_op jit(solution)/shard_map/ppermute | solution.py:393
  68.2 9.9 %collective-permute-start.18 = (bf16[400,128]{1,0:T(8,128)(2,1)S(1)}, bf16[400,128]{1,0:T(8,128)(2,1)S(1)}, u32[]{:S(2)}, u32[]{:S(2)}) collective-permute-start(bf16[400,128]{1,0:T(8,128)(2,1)S(1)} %get-tuple-element.92), channel_id=1, source_target_pairs={{0,8},{1,9},{2,10},{3,11},{4,12},{5,13},{6,14},{7,15},{8,0},{9,1},... | collective-permute-start | bytes 307208 | tf_op jit(solution)/shard_map/ppermute | solution.py:393
  72.4 7.5 %collective-permute-start.17 = (bf16[400,128]{1,0:T(8,128)(2,1)S(1)}, bf16[400,128]{1,0:T(8,128)(2,1)S(1)}, u32[]{:S(2)}, u32[]{:S(2)}) collective-permute-start(bf16[400,128]{1,0:T(8,128)(2,1)S(1)} %get-tuple-element.91), channel_id=1, source_target_pairs={{0,8},{1,9},{2,10},{3,11},{4,12},{5,13},{6,14},{7,15},{8,0},{9,1},... | collective-permute-start | bytes 307208 | tf_op jit(solution)/shard_map/ppermute | solution.py:393
  73.2 8.7 %collective-permute-start.15 = (bf16[32,1024]{1,0:T(8,128)(2,1)S(1)}, bf16[32,1024]{1,0:T(8,128)(2,1)S(1)}, u32[]{:S(2)}, u32[]{:S(2)}) collective-permute-start(bf16[32,1024]{1,0:T(8,128)(2,1)S(1)} %get-tuple-element.89), channel_id=1, source_target_pairs={{0,1},{1,0},{2,3},{3,2},{4,5},{5,4},{6,7},{7,6},{8,9},{9,8},{10,11... | collective-permute-start | bytes 196616 | tf_op jit(solution)/shard_map/ppermute | solution.py:393
  78.7 2.0 %collective-permute-start.20 = (bf16[32,768]{1,0:T(8,128)(2,1)S(1)}, bf16[32,768]{1,0:T(8,128)(2,1)S(1)}, u32[]{:S(2)}, u32[]{:S(2)}) collective-permute-start(bf16[32,768]{1,0:T(8,128)(2,1)S(1)} %get-tuple-element.96), channel_id=1, source_target_pairs={{0,1},{1,0},{2,3},{3,2},{4,5},{5,4},{6,7},{7,6},{8,9},{9,8},{10,11... | collective-permute-start | bytes 147464 | tf_op jit(solution)/shard_map/ppermute | solution.py:393
  78.7 1.9 %collective-permute-start.14 = (bf16[32,768]{1,0:T(8,128)(2,1)S(1)}, bf16[32,768]{1,0:T(8,128)(2,1)S(1)}, u32[]{:S(2)}, u32[]{:S(2)}) collective-permute-start(bf16[32,768]{1,0:T(8,128)(2,1)S(1)} %get-tuple-element.88), channel_id=1, source_target_pairs={{0,1},{1,0},{2,3},{3,2},{4,5},{5,4},{6,7},{7,6},{8,9},{9,8},{10,11... | collective-permute-start | bytes 147464 | tf_op jit(solution)/shard_map/ppermute | solution.py:393
  79.2 1.4 %collective-permute-start.16 = (bf16[32,768]{1,0:T(8,128)(2,1)S(1)}, bf16[32,768]{1,0:T(8,128)(2,1)S(1)}, u32[]{:S(2)}, u32[]{:S(2)}) collective-permute-start(bf16[32,768]{1,0:T(8,128)(2,1)S(1)} %get-tuple-element.90), channel_id=1, source_target_pairs={{0,1},{1,0},{2,3},{3,2},{4,5},{5,4},{6,7},{7,6},{8,9},{9,8},{10,11... | collective-permute-start | bytes 147464 | tf_op jit(solution)/shard_map/ppermute | solution.py:393
  80.5 1.3 %collective-permute-start.19 = (bf16[32,768]{1,0:T(8,128)(2,1)S(1)}, bf16[32,768]{1,0:T(8,128)(2,1)S(1)}, u32[]{:S(2)}, u32[]{:S(2)}) collective-permute-start(bf16[32,768]{1,0:T(8,128)(2,1)S(1)} %get-tuple-element.95), channel_id=1, source_target_pairs={{0,1},{1,0},{2,3},{3,2},{4,5},{5,4},{6,7},{7,6},{8,9},{9,8},{10,11... | collective-permute-start | bytes 147464 | tf_op jit(solution)/shard_map/ppermute | solution.py:393

commit v6 on v3

--- a/solution.py
+++ b/solution.py
@@ -15,12 +15,19 @@
 TINY = 2.0**-110
 MIB = 1 << 20
 
-CHUNKS = [(4, (0, 1, 2)), (4, (1, 0, 2)), (4, (0, 1, 2)), (4, (0, 1, 2))]
+CHUNKS = [
+    (4, (0, 2, 1)),
+    (4, (1, 0, 2)),
+    (4, (0, 2, 1)),
+    (2, (1, 0, 2)),
+    (2, (0, 1, 2)),
+]
 PARTS = 16
-EARLY = 2
+EARLY = 1
 ORDER = [
-    (0, 0), (1, 0), (2, 0), (0, 1), (3, 0), (1, 1), (0, 2), (2, 1),
-    (0, 3), (2, 2), (3, 1), (1, 2), (2, 3), (3, 2), (1, 3), (3, 3),
+    (0, 0), (1, 0), (2, 0), (0, 1), (3, 0), (4, 0), (1, 1), (2, 1),
+    (0, 2), (3, 1), (4, 1), (1, 2), (2, 2), (0, 3), (3, 2), (4, 2),
+    (1, 3), (2, 3), (3, 3), (4, 3),
 ]
 
 
@@ -99,14 +106,28 @@
         out_shape=outs,
         scratch_shapes=scratch,
         compiler_params=pltpu.CompilerParams(vmem_limit_bytes=limit * MIB),
-        cost_estimate=pl.CostEstimate(
-            flops=cost[0], bytes_accessed=cost[1], transcendentals=cost[2]
-        ),
+        cost_estimate=pl.CostEstimate(flops=1, bytes_accessed=1, transcendentals=0),
         name=name,
     )(*ins, *after)
 
 
-def prepare_kernel(blocks, bits, wide, place_ref, basis_ref, out_ref, held, turned, sems):
+def row_copies(place_ref, w_ref, near_ref, sems, distance, wide):
+    depth = near_ref.shape[0]
+    owner = jnp.bitwise_xor(place_ref[0], distance)
+    copies = []
+    for index, at in enumerate(range(0, depth, wide)):
+        source = pl.ds(pl.multiple_of(owner * depth + at, wide), wide)
+        copies.append(
+            pltpu.make_async_copy(
+                w_ref.at[0, source, :], near_ref.at[pl.ds(at, wide), :], sems.at[index]
+            )
+        )
+    return copies
+
+
+def prepare_kernel(
+    blocks, bits, wide, place_ref, basis_ref, w_ref, out_ref, near_ref, held, turned, sems, w_sems
+):
     depth, rows = basis_ref.shape
     step = rows // blocks
     copies = []
@@ -115,7 +136,9 @@
         copies.append(
             pltpu.make_async_copy(basis_ref.at[part, :], held.at[part, :], sems.at[index])
         )
-        copies[-1].start()
+    weight_copies = row_copies(place_ref, w_ref, near_ref, w_sems, 0, wide)
+    for copy in copies + weight_copies:
+        copy.start()
     for index, at in enumerate(range(0, depth, wide)):
         copies[index].wait()
         turned[:, at : at + wide] = held[at : at + wide, :].T
@@ -126,26 +149,33 @@
             low = (part - high.astype(jnp.float32)).astype(jnp.bfloat16)
             out_ref[place * step : (place + 1) * step, at : at + wide] = high
             out_ref[rows + place * step : rows + (place + 1) * step, at : at + wide] = low
-
-
-def prepare(basis, places, blocks, bits):
+    for copy in weight_copies:
+        copy.wait()
+
+
+def prepare(basis, weights, places, blocks, bits):
     depth, rows = basis.shape
     wide = min(depth, COLUMNS)
+    sems = pltpu.SemaphoreType.DMA((depth // wide,))
     return call(
         functools.partial(prepare_kernel, blocks, bits, wide),
         "split_basis",
-        [places, basis],
-        [jax.ShapeDtypeStruct((2 * rows, depth), jnp.bfloat16)],
+        [places, basis, weights],
+        [
+            jax.ShapeDtypeStruct((2 * rows, depth), jnp.bfloat16),
+            jax.ShapeDtypeStruct((depth, weights.shape[2]), jnp.bfloat16),
+        ],
         [],
         [
             pltpu.VMEM((depth, rows), jnp.float32),
             pltpu.VMEM((rows, depth), jnp.float32),
-            pltpu.SemaphoreType.DMA((depth // wide,)),
+            sems,
+            sems,
         ],
         limit=10,
         cost=(2 * depth * rows, 8 * depth * rows, 0),
-        far=1,
-    )[0]
+        far=2,
+    )
 
 
 def spans(width, wide):
@@ -157,78 +187,58 @@
     return product[:half] + product[half:]
 
 
-def early_kernel(pieces, width, place_ref, own_ref, w_ref, near_ref, partial_ref, sems):
+def early_kernel(pieces, width, place_ref, own_ref, near_ref, w_ref, *refs):
+    *other_refs, partial_ref, sems = refs
     depth = own_ref.shape[1]
-    full = w_ref.shape[2]
+    wide = min(depth, COLUMNS)
     copies = []
-
-    def bring(distance, at, wide):
-        owner = jnp.bitwise_xor(place_ref[0], distance)
-        rows = pl.ds(pl.multiple_of(owner * depth, depth), depth)
-        copy = pltpu.make_async_copy(
-            w_ref.at[0, rows, pl.ds(at, wide)],
-            near_ref.at[pl.ds(distance * depth, depth), pl.ds(at, wide)],
-            sems.at[len(copies)],
+    for distance in range(1, pieces):
+        copies += row_copies(
+            place_ref, w_ref, other_refs[distance - 1], sems.at[distance - 1], distance, wide
         )
+    for copy in copies:
         copy.start()
-        copies.append(copy)
-
-    first = spans(width, COLUMNS)
-    for at, wide in first:
-        bring(0, at, wide)
-    for index, (at, wide) in enumerate(first):
-        copies[index].wait()
-        if index == 0:
-            if full > width:
-                bring(0, width, full - width)
-            for distance in range(1, pieces):
-                bring(distance, 0, full)
-        part = jnp.dot(
-            own_ref[...],
-            near_ref[0:depth, at : at + wide],
-            preferred_element_type=jnp.float32,
-        )
-        partial_ref[:, at : at + wide] = halves_added(part)
-    for copy in copies[len(first) :]:
+    for at, wide in spans(width, COLUMNS):
+        columns = slice(at, at + wide)
+        part = jnp.dot(own_ref[...], near_ref[:, columns], preferred_element_type=jnp.float32)
+        partial_ref[:, columns] = halves_added(part)
+    for copy in copies:
         copy.wait()
 
 
-def early(own, weights, places, pieces, width, after):
+def early(own, near, weights, places, pieces, width):
     rows2, depth = own.shape
     full = weights.shape[2]
-    return call(
+    out = call(
         functools.partial(early_kernel, pieces, width),
         "early_products",
-        [places, own, weights],
-        [
-            jax.ShapeDtypeStruct((pieces * depth, full), jnp.bfloat16),
-            jax.ShapeDtypeStruct((rows2 // 2, width), jnp.float32),
-        ],
-        after,
-        [pltpu.SemaphoreType.DMA((len(spans(width, COLUMNS)) + pieces,))],
+        [places, own, near, weights],
+        [jax.ShapeDtypeStruct((depth, full), jnp.bfloat16)] * (pieces - 1)
+        + [jax.ShapeDtypeStruct((rows2 // 2, width), jnp.float32)],
+        [],
+        [pltpu.SemaphoreType.DMA((pieces - 1, depth // min(depth, COLUMNS)))],
         limit=8,
         cost=(2 * rows2 * depth * width, 2 * pieces * depth * full, 0),
         far=1,
     )
-
-
-def product_kernel(pieces, start, width, early, step, leave, stay, place_ref, near_ref, *refs):
-    left = refs[:pieces]
+    return [near, *out[:-1]], out[-1]
+
+
+def product_kernel(pieces, start, width, early, step, leave, stay, place_ref, *refs):
+    left, right = refs[:pieces], refs[pieces : 2 * pieces]
     message_ref, kept_ref = refs[-2:]
-    depth = left[0].shape[1]
-    used = left[1:] if early else left
-    low = depth if early else 0
+    first = 1 if early else 0
     bounds = []
     for at, wide in spans(width, COLUMNS):
         columns = slice(start + at, start + at + wide)
         total = jnp.dot(
-            jnp.concatenate([a_ref[...] for a_ref in used], axis=1),
-            near_ref[low : pieces * depth, columns],
+            jnp.concatenate([a_ref[...] for a_ref in left[first:]], axis=1),
+            jnp.concatenate([w_ref[:, columns] for w_ref in right[first:]], axis=0),
             preferred_element_type=jnp.float32,
         )
         total = halves_added(total)
         if early:
-            total = total + refs[pieces][:, columns]
+            total = total + refs[2 * pieces][:, columns]
         for lane in range(0, wide, LANES):
             column = total[:, lane : lane + LANES]
             blocks = {p: column[p * step : (p + 1) * step] for p in leave + stay}
@@ -246,16 +256,15 @@
     ]
 
 
-def product(left, near, partial, places, start, width, step, leave, stay, after):
+def product(left, right, partial, places, start, width, step, leave, stay, after):
     rows2, depth = left[0].shape
+    pieces = len(left)
     early = partial is not None
-    count = len(left) - 1 if early else len(left)
+    count = pieces - 1 if early else pieces
     return call(
-        functools.partial(
-            product_kernel, len(left), start, width, early, step, leave, stay
-        ),
+        functools.partial(product_kernel, pieces, start, width, early, step, leave, stay),
         "product",
-        [places, near, *left] + ([partial] if early else []),
+        [places, *left, *right] + ([partial] if early else []),
         outputs(width, step, leave, stay),
         after,
         limit=8,
@@ -369,7 +378,7 @@
     column = jnp.bitwise_and(me, pieces - 1)
     places = jnp.stack([column, jnp.right_shift(me, piece_bits)])
 
-    own = prepare(basis, places, blocks, bits)
+    own, near = prepare(basis, weights, places, blocks, bits)
     left = [own] + [swapped(own, distance) for distance in range(1, pieces)]
 
     cuts = [0]
@@ -378,7 +387,7 @@
     cuts = [cut * (width // LANES) // PARTS * LANES for cut in cuts]
     orders = [[bit for bit in order if bit < bits] for _, order in CHUNKS]
     stages = [split_places(order, bits) for order in orders]
-    near, partial = early(own, weights, places, pieces, cuts[EARLY], [])
+    right, partial = early(own, near, weights, places, pieces, cuts[EARLY])
 
     state = {}
     after = [partial]
@@ -387,12 +396,10 @@
         order = orders[index]
         start = cuts[index]
         chunk = cuts[index + 1] - start
-        if chunk == 0:
-            continue
         if number == 0:
             begun = partial if index < EARLY else None
             out = product(
-                left, near, begun, places, start, chunk, step, *stages[index][0], after
+                left, right, begun, places, start, chunk, step, *stages[index][0], after
             )
         elif number < bits:
             message, kept = state[index]

time: 85.5 us -> 74.7 us (0.87)
  waiting for transfers between devices: 20.6 us -> 8.16 us
  starting transfers between devices: 21.6 us -> 23 us
    ppermute x17 -> x21, waiting for transfers between devices: 20.6 us -> 8.16 us  [swapped(): return lax.ppermute(block, 'row', [(i, i ^ apart) for i in range(count)])]
    ppermute x17 -> x21, starting transfers between devices: 21.6 us -> 23 us  [swapped(): return lax.ppermute(block, 'row', [(i, i ^ apart) for i in range(count)])]
    pallas_call x19 -> x23, Pallas kernels: 42.8 us -> 43.2 us  [call(): pl.pallas_call(run, in_specs=[pl.BlockSpec(memory_space=pltpu.SMEM)] + [v...]
  transfers between devices with their start and end apart: 17 -> 21, of which waited for: 8 -> 9; matrix products, arithmetic and copies ran while one was open for 0% -> 0% of each run, Pallas kernels for 42% -> 46%
where the time goes in v6:
time: 74.7 us; the launch traced here: 74.6 us
  Pallas kernels  43.2 us (58%)
  starting transfers between devices  23 us (31%)
  waiting for transfers between devices  8.16 us (11%)
    pallas_call x23, Pallas kernels, call(): pl.pallas_call(run, in_specs=[pl.BlockSpec(memory_space=pltpu.SMEM)] + [v...  43.2 us
    ppermute x21, starting transfers between devices, swapped(): return lax.ppermute(block, 'row', [(i, i ^ apart) for i in range(count)])  23 us
    ppermute x21, waiting for transfers between devices, swapped(): return lax.ppermute(block, 'row', [(i, i ^ apart) for i in range(count)])  8.16 us
  transfers between devices with their start and end apart: 21, of which 9 were waited for; matrix products, arithmetic and copies ran while one was open for 0% of the time, Pallas kernels for 46%

profile of v6, /device:TPU:0, one launch (start us, length us, event | category | flops | bytes accessed | tf_op | source)
XLA Modules:
  0.0 74.6 jit_solution(14354887560558245280)
XLA Ops:
  0.0 0.1 pad_add_fusion.refs_0_
  0.1 4.7 %split_basis.1 = (bf16[1024,1024]{1,0:T(8,128)(2,1)S(1)}, bf16[1024,4096]{1,0:T(8,128)(2,1)S(1)}) custom-call(s32[2]{0:T(128)S(1)} %pad_add_fusion.refs_0_, f32[1024,512]{1,0:T(8,128)} %refs_1_.1, bf16[1,2048,4096]{2,1,0:T(8,128)(2,1)} %refs_3_.1), custom_call_target="tpu_custom_call" | custom-call | flops 1 | bytes 1 | tf_op jit(solution)/shard_map/split_basis/pallas_call | solution.py:99
  4.8 0.5 collective-permute-start
  5.3 5.6 %early_products.1 = (bf16[1024,4096]{1,0:T(8,128)(2,1)S(1)}, f32[512,1024]{1,0:T(8,128)S(1)}) custom-call(s32[2]{0:T(128)S(1)} %pad_add_fusion.refs_0_, bf16[1024,1024]{1,0:T(8,128)(2,1)S(1)} %get-tuple-element.49.refs_1_, bf16[1024,4096]{1,0:T(8,128)(2,1)S(1)} %get-tuple-element.50.refs_2_.refs_3_, bf16[1,2048,4096]{2,1,0:T(8,128)(2,1)} %refs_3_.1), custom_call_target="tpu_custom_call" | custom-call | flops 1 | bytes 1 | tf_op jit(solution)/shard_map/early_products/pallas_call | solution.py:99
  10.9 0.0 collective-permute-done.refs_2_
  10.9 3.2 %product.5 = (bf16[2064,128]{1,0:T(8,128)(2,1)S(1)}, f32[2048,128]{1,0:T(8,128)S(1)}) custom-call(s32[2]{0:T(128)S(1)} %pad_add_fusion.refs_0_, bf16[1024,1024]{1,0:T(8,128)(2,1)S(1)} %get-tuple-element.49.refs_1_, bf16[1024,1024]{1,0:T(8,128)(2,1)S(1)} %collective-permute-done.refs_2_, bf16[1024,4096]{1,0:T(8,128)(2,1)S(1)} %get-tuple-element.50.refs_2_.refs_3_, ...), custom_call_target="tpu_custom_call" | custom-call | flops 1 | bytes 1 | tf_op jit(solution)/shard_map/product/pallas_call | solution.py:99
  14.1 2.6 %collective-permute-start.1 = (bf16[2064,128]{1,0:T(8,128)(2,1)S(1)}, bf16[2064,128]{1,0:T(8,128)(2,1)S(1)}, u32[]{:S(2)}, u32[]{:S(2)}) collective-permute-start(bf16[2064,128]{1,0:T(8,128)(2,1)S(1)} %get-tuple-element.53), channel_id=1, source_target_pairs={{0,2},{1,3},{2,0},{3,1},{4,6},{5,7},{6,4},{7,5},{8,10},{9,11},{10,... | collective-permute-start | bytes 1585160 | tf_op jit(solution)/shard_map/ppermute | solution.py:365
  16.7 5.3 %product.6 = (bf16[2064,128]{1,0:T(8,128)(2,1)S(1)}, f32[2048,128]{1,0:T(8,128)S(1)}) custom-call(s32[2]{0:T(128)S(1)} %pad_add_fusion.refs_0_, bf16[1024,1024]{1,0:T(8,128)(2,1)S(1)} %get-tuple-element.49.refs_1_, bf16[1024,1024]{1,0:T(8,128)(2,1)S(1)} %collective-permute-done.refs_2_, bf16[1024,4096]{1,0:T(8,128)(2,1)S(1)} %get-tuple-element.50.refs_2_.refs_3_, ...), custom_call_target="tpu_custom_call" | custom-call | flops 1 | bytes 1 | tf_op jit(solution)/shard_map/product/pallas_call | solution.py:99
  22.0 1.7 %collective-permute-start.4 = (bf16[2064,128]{1,0:T(8,128)(2,1)S(1)}, bf16[2064,128]{1,0:T(8,128)(2,1)S(1)}, u32[]{:S(2)}, u32[]{:S(2)}) collective-permute-start(bf16[2064,128]{1,0:T(8,128)(2,1)S(1)} %get-tuple-element.60), channel_id=1, source_target_pairs={{0,4},{1,5},{2,6},{3,7},{4,0},{5,1},{6,2},{7,3},{8,12},{9,13},{10,... | collective-permute-start | bytes 1585160 | tf_op jit(solution)/shard_map/ppermute | solution.py:365
  23.7 5.4 %product.7 = (bf16[2064,128]{1,0:T(8,128)(2,1)S(1)}, f32[2048,128]{1,0:T(8,128)S(1)}) custom-call(s32[2]{0:T(128)S(1)} %pad_add_fusion.refs_0_, bf16[1024,1024]{1,0:T(8,128)(2,1)S(1)} %get-tuple-element.49.refs_1_, bf16[1024,1024]{1,0:T(8,128)(2,1)S(1)} %collective-permute-done.refs_2_, bf16[1024,4096]{1,0:T(8,128)(2,1)S(1)} %get-tuple-element.50.refs_2_.refs_3_, ...), custom_call_target="tpu_custom_call" | custom-call | flops 1 | bytes 1 | tf_op jit(solution)/shard_map/product/pallas_call | solution.py:99
  29.0 0.6 collective-permute-start.3
  29.6 0.0 collective-permute-done.1.refs_1_
  29.6 1.0 %add_and_split.10 = (bf16[1040,128]{1,0:T(8,128)(2,1)S(1)}, f32[1024,128]{1,0:T(8,128)S(1)}) custom-call(s32[2]{0:T(128)S(1)} %pad_add_fusion.refs_0_, bf16[2064,128]{1,0:T(8,128)(2,1)S(1)} %collective-permute-done.1.refs_1_, f32[2048,128]{1,0:T(8,128)S(1)} %get-tuple-element.54.refs_5_.refs_2_, f32[2048,128]{1,0:T(8,128)S(1)} %get-tuple-element.56.refs_3_.refs_2_), custom_call_target="tpu_custom_call" | custom-call | flops 1 | bytes 1 | tf_op jit(solution)/shard_map/add_and_split/pallas_call | solution.py:99
  30.6 2.7 %collective-permute-start.2 = (bf16[1040,128]{1,0:T(8,128)(2,1)S(1)}, bf16[1040,128]{1,0:T(8,128)(2,1)S(1)}, u32[]{:S(2)}, u32[]{:S(2)}) collective-permute-start(bf16[1040,128]{1,0:T(8,128)(2,1)S(1)} %get-tuple-element.57), channel_id=1, source_target_pairs={{0,8},{1,9},{2,10},{3,11},{4,12},{5,13},{6,14},{7,15},{8,0},{9,1},... | collective-permute-start | bytes 798728 | tf_op jit(solution)/shard_map/ppermute | solution.py:365
  33.3 3.0 %product.8 = (bf16[1040,128]{1,0:T(8,128)(2,1)S(1)}, f32[1024,128]{1,0:T(8,128)S(1)}) custom-call(s32[2]{0:T(128)S(1)} %pad_add_fusion.refs_0_, bf16[1024,1024]{1,0:T(8,128)(2,1)S(1)} %get-tuple-element.49.refs_1_, bf16[1024,1024]{1,0:T(8,128)(2,1)S(1)} %collective-permute-done.refs_2_, bf16[1024,4096]{1,0:T(8,128)(2,1)S(1)} %get-tuple-element.50.refs_2_.refs_3_, ...), custom_call_target="tpu_custom_call" | custom-call | flops 1 | bytes 1 | tf_op jit(solution)/shard_map/product/pallas_call | solution.py:99
  36.3 1.6 %collective-permute-start.9 = (bf16[1040,128]{1,0:T(8,128)(2,1)S(1)}, bf16[1040,128]{1,0:T(8,128)(2,1)S(1)}, u32[]{:S(2)}, u32[]{:S(2)}) collective-permute-start(bf16[1040,128]{1,0:T(8,128)(2,1)S(1)} %get-tuple-element.70), channel_id=1, source_target_pairs={{0,4},{1,5},{2,6},{3,7},{4,0},{5,1},{6,2},{7,3},{8,12},{9,13},{10,... | collective-permute-start | bytes 798728 | tf_op jit(solution)/shard_map/ppermute | solution.py:365
  37.9 3.2 %product.9 = (bf16[1040,128]{1,0:T(8,128)(2,1)S(1)}, f32[1024,128]{1,0:T(8,128)S(1)}) custom-call(s32[2]{0:T(128)S(1)} %pad_add_fusion.refs_0_, bf16[1024,1024]{1,0:T(8,128)(2,1)S(1)} %get-tuple-element.49.refs_1_, bf16[1024,1024]{1,0:T(8,128)(2,1)S(1)} %collective-permute-done.refs_2_, bf16[1024,4096]{1,0:T(8,128)(2,1)S(1)} %get-tuple-element.50.refs_2_.refs_3_, ...), custom_call_target="tpu_custom_call" | custom-call | flops 1 | bytes 1 | tf_op jit(solution)/shard_map/product/pallas_call | solution.py:99
  41.1 1.6 %collective-permute-start.8 = (bf16[1040,128]{1,0:T(8,128)(2,1)S(1)}, bf16[1040,128]{1,0:T(8,128)(2,1)S(1)}, u32[]{:S(2)}, u32[]{:S(2)}) collective-permute-start(bf16[1040,128]{1,0:T(8,128)(2,1)S(1)} %get-tuple-element.69), channel_id=1, source_target_pairs={{0,2},{1,3},{2,0},{3,1},{4,6},{5,7},{6,4},{7,5},{8,10},{9,11},{10,... | collective-permute-start | bytes 798728 | tf_op jit(solution)/shard_map/ppermute | solution.py:365
  42.7 0.0 collective-permute-done.4.refs_1_
  42.7 1.0 %add_and_split.11 = (bf16[1040,128]{1,0:T(8,128)(2,1)S(1)}, f32[1024,128]{1,0:T(8,128)S(1)}) custom-call(s32[2]{0:T(128)S(1)} %pad_add_fusion.refs_0_, bf16[2064,128]{1,0:T(8,128)(2,1)S(1)} %collective-permute-done.4.refs_1_, f32[2048,128]{1,0:T(8,128)S(1)} %get-tuple-element.55.refs_5_.refs_2_, f32[1024,128]{1,0:T(8,128)S(1)} %get-tuple-element.62.refs_3_.refs_2_), custom_call_target="tpu_custom_call" | custom-call | flops 1 | bytes 1 | tf_op jit(solution)/shard_map/add_and_split/pallas_call | solution.py:99
  43.7 0.6 collective-permute-start.7
  44.3 0.0 collective-permute-done.3.refs_1_
  44.3 1.0 %add_and_split.12 = (bf16[1040,128]{1,0:T(8,128)(2,1)S(1)}, f32[1024,128]{1,0:T(8,128)S(1)}) custom-call(s32[2]{0:T(128)S(1)} %pad_add_fusion.refs_0_, bf16[2064,128]{1,0:T(8,128)(2,1)S(1)} %collective-permute-done.3.refs_1_, f32[2048,128]{1,0:T(8,128)S(1)} %get-tuple-element.56.refs_3_.refs_2_, f32[1024,128]{1,0:T(8,128)S(1)} %get-tuple-element.63.refs_3_.refs_2_), custom_call_target="tpu_custom_call" | custom-call | flops 1 | bytes 1 | tf_op jit(solution)/shard_map/add_and_split/pallas_call | solution.py:99
  45.3 2.3 %collective-permute-start.6 = (bf16[1040,128]{1,0:T(8,128)(2,1)S(1)}, bf16[1040,128]{1,0:T(8,128)(2,1)S(1)}, u32[]{:S(2)}, u32[]{:S(2)}) collective-permute-start(bf16[1040,128]{1,0:T(8,128)(2,1)S(1)} %get-tuple-element.67), channel_id=1, source_target_pairs={{0,8},{1,9},{2,10},{3,11},{4,12},{5,13},{6,14},{7,15},{8,0},{9,1},... | collective-permute-start | bytes 798728 | tf_op jit(solution)/shard_map/ppermute | solution.py:365
  47.6 0.0 collective-permute-done.2.refs_1_
  47.7 0.8 %add_and_split.13 = (bf16[528,128]{1,0:T(8,128)(2,1)S(1)}, f32[512,128]{1,0:T(8,128)S(1)}) custom-call(s32[2]{0:T(128)S(1)} %pad_add_fusion.refs_0_, bf16[1040,128]{1,0:T(8,128)(2,1)S(1)} %collective-permute-done.2.refs_1_, f32[1024,128]{1,0:T(8,128)S(1)} %get-tuple-element.58.refs_5_.refs_2_, f32[1024,128]{1,0:T(8,128)S(1)} %get-tuple-element.64.refs_3_.refs_2_), custom_call_target="tpu_custom_call" | custom-call | flops 1 | bytes 1 | tf_op jit(solution)/shard_map/add_and_split/pallas_call | solution.py:99
  48.5 0.5 collective-permute-start.5
  49.0 0.1 collective-permute-done.9.refs_1_
  49.1 0.8 %add_and_split.14 = (bf16[528,128]{1,0:T(8,128)(2,1)S(1)}, f32[512,128]{1,0:T(8,128)S(1)}) custom-call(s32[2]{0:T(128)S(1)} %pad_add_fusion.refs_0_, bf16[1040,128]{1,0:T(8,128)(2,1)S(1)} %collective-permute-done.9.refs_1_, f32[1024,128]{1,0:T(8,128)S(1)} %get-tuple-element.61.refs_5_.refs_2_, f32[512,128]{1,0:T(8,128)S(1)} %get-tuple-element.66.refs_3_.refs_2_), custom_call_target="tpu_custom_call" | custom-call | flops 1 | bytes 1 | tf_op jit(solution)/shard_map/add_and_split/pallas_call | solution.py:99
  49.9 0.4 collective-permute-start.13
  50.3 0.2 collective-permute-done.8.refs_1_
  50.5 0.8 %add_and_split.15 = (bf16[528,128]{1,0:T(8,128)(2,1)S(1)}, f32[512,128]{1,0:T(8,128)S(1)}) custom-call(s32[2]{0:T(128)S(1)} %pad_add_fusion.refs_0_, bf16[1040,128]{1,0:T(8,128)(2,1)S(1)} %collective-permute-done.8.refs_1_, f32[1024,128]{1,0:T(8,128)S(1)} %get-tuple-element.62.refs_3_.refs_2_, f32[512,128]{1,0:T(8,128)S(1)} %get-tuple-element.71.refs_3_.refs_2_), custom_call_target="tpu_custom_call" | custom-call | flops 1 | bytes 1 | tf_op jit(solution)/shard_map/add_and_split/pallas_call | solution.py:99
  51.3 1.5 %collective-permute-start.12 = (bf16[528,128]{1,0:T(8,128)(2,1)S(1)}, bf16[528,128]{1,0:T(8,128)(2,1)S(1)}, u32[]{:S(2)}, u32[]{:S(2)}) collective-permute-start(bf16[528,128]{1,0:T(8,128)(2,1)S(1)} %get-tuple-element.78), channel_id=1, source_target_pairs={{0,4},{1,5},{2,6},{3,7},{4,0},{5,1},{6,2},{7,3},{8,12},{9,13},{10,... | collective-permute-start | bytes 405512 | tf_op jit(solution)/shard_map/ppermute | solution.py:365
  52.8 3.0 %collective-permute-done.7.refs_1_ = bf16[1040,128]{1,0:T(8,128)(2,1)S(1)} collective-permute-done((bf16[1040,128]{1,0:T(8,128)(2,1)S(1)}, bf16[1040,128]{1,0:T(8,128)(2,1)S(1)}, u32[]{:S(2)}, u32[]{:S(2)}) %collective-permute-start.7) | collective-permute-done | bytes 266272 | tf_op jit(solution)/shard_map/ppermute | solution.py:365
  55.8 0.8 %add_and_split.16 = (bf16[528,128]{1,0:T(8,128)(2,1)S(1)}, f32[512,128]{1,0:T(8,128)S(1)}) custom-call(s32[2]{0:T(128)S(1)} %pad_add_fusion.refs_0_, bf16[1040,128]{1,0:T(8,128)(2,1)S(1)} %collective-permute-done.7.refs_1_, f32[1024,128]{1,0:T(8,128)S(1)} %get-tuple-element.63.refs_3_.refs_2_, f32[512,128]{1,0:T(8,128)S(1)} %get-tuple-element.72.refs_3_.refs_2_), custom_call_target="tpu_custom_call" | custom-call | flops 1 | bytes 1 | tf_op jit(solution)/shard_map/add_and_split/pallas_call | solution.py:99
  56.6 2.2 %collective-permute-start.11 = (bf16[528,128]{1,0:T(8,128)(2,1)S(1)}, bf16[528,128]{1,0:T(8,128)(2,1)S(1)}, u32[]{:S(2)}, u32[]{:S(2)}) collective-permute-start(bf16[528,128]{1,0:T(8,128)(2,1)S(1)} %get-tuple-element.77), channel_id=1, source_target_pairs={{0,8},{1,9},{2,10},{3,11},{4,12},{5,13},{6,14},{7,15},{8,0},{9,1},... | collective-permute-start | bytes 405512 | tf_op jit(solution)/shard_map/ppermute | solution.py:365
  58.8 1.5 %collective-permute-done.6.refs_1_ = bf16[1040,128]{1,0:T(8,128)(2,1)S(1)} collective-permute-done((bf16[1040,128]{1,0:T(8,128)(2,1)S(1)}, bf16[1040,128]{1,0:T(8,128)(2,1)S(1)}, u32[]{:S(2)}, u32[]{:S(2)}) %collective-permute-start.6) | collective-permute-done | bytes 266272 | tf_op jit(solution)/shard_map/ppermute | solution.py:365
  60.3 0.8 %add_and_split.17 = (bf16[528,128]{1,0:T(8,128)(2,1)S(1)}, f32[512,128]{1,0:T(8,128)S(1)}) custom-call(s32[2]{0:T(128)S(1)} %pad_add_fusion.refs_0_, bf16[1040,128]{1,0:T(8,128)(2,1)S(1)} %collective-permute-done.6.refs_1_, f32[1024,128]{1,0:T(8,128)S(1)} %get-tuple-element.64.refs_3_.refs_2_, f32[512,128]{1,0:T(8,128)S(1)} %get-tuple-element.73.refs_3_.refs_2_), custom_call_target="tpu_custom_call" | custom-call | flops 1 | bytes 1 | tf_op jit(solution)/shard_map/add_and_split/pallas_call | solution.py:99
  61.1 0.1 collective-permute-start.15
  61.2 0.0 collective-permute-done.5.refs_1_
  61.2 0.6 add_last.5
  61.9 0.0 collective-permute-done.13.refs_1_
  61.9 0.7 add_and_split.18
  62.6 1.1 %collective-permute-start.17 = (bf16[272,128]{1,0:T(8,128)(2,1)S(1)}, bf16[272,128]{1,0:T(8,128)(2,1)S(1)}, u32[]{:S(2)}, u32[]{:S(2)}) collective-permute-start(bf16[272,128]{1,0:T(8,128)(2,1)S(1)} %get-tuple-element.87), channel_id=1, source_target_pairs={{0,8},{1,9},{2,10},{3,11},{4,12},{5,13},{6,14},{7,15},{8,0},{9,1},... | collective-permute-start | bytes 208904 | tf_op jit(solution)/shard_map/ppermute | solution.py:365
  63.6 0.0 collective-permute-done.12.refs_1_
  63.6 0.7 add_and_split.19
  64.3 2.0 %collective-permute-start.19 = (bf16[272,128]{1,0:T(8,128)(2,1)S(1)}, bf16[272,128]{1,0:T(8,128)(2,1)S(1)}, u32[]{:S(2)}, u32[]{:S(2)}) collective-permute-start(bf16[272,128]{1,0:T(8,128)(2,1)S(1)} %get-tuple-element.90), channel_id=1, source_target_pairs={{0,8},{1,9},{2,10},{3,11},{4,12},{5,13},{6,14},{7,15},{8,0},{9,1},... | collective-permute-start | bytes 208904 | tf_op jit(solution)/shard_map/ppermute | solution.py:365
  66.3 0.0 collective-permute-start.10
  66.3 0.0 collective-permute-done.11.refs_1_
  66.3 0.6 add_last.6
  66.9 1.6 %collective-permute-done.15.refs_1_ = bf16[528,128]{1,0:T(8,128)(2,1)S(1)} collective-permute-done((bf16[528,128]{1,0:T(8,128)(2,1)S(1)}, bf16[528,128]{1,0:T(8,128)(2,1)S(1)}, u32[]{:S(2)}, u32[]{:S(2)}) %collective-permute-start.15) | collective-permute-done | bytes 135200 | tf_op jit(solution)/shard_map/ppermute | solution.py:365
  68.5 0.6 add_last.7
  69.1 0.1 collective-permute-start.16
  69.2 0.5 collective-permute-start.14
  69.7 0.7 collective-permute-done.17.refs_1_
  70.5 0.6 add_last.8
  71.0 0.1 collective-permute-done.19.refs_1_
  71.2 0.6 add_last.9
  71.8 0.1 collective-permute-start.20
  71.9 0.5 collective-permute-start.18
  72.4 0.0 collective-permute-done.10.refs_2_
  72.4 0.7 collective-permute-done.20.refs_10_
  73.1 0.2 collective-permute-done.18.refs_8_
  73.2 1.4 %lay_out.1 = bf16[32,8192]{1,0:T(8,128)(2,1)} custom-call(s32[2]{0:T(128)S(1)} %pad_add_fusion.refs_0_, bf16[32,1024]{1,0:T(8,128)(2,1)S(1)} %get-tuple-element.75.refs_3_.refs_1_, bf16[32,1024]{1,0:T(8,128)(2,1)S(1)} %collective-permute-done.10.refs_2_, bf16[32,1024]{1,0:T(8,128)(2,1)S(1)} %get-tuple-element.82.refs_3_, ...), custom_call_target="tpu_custom_call" | custom-call | flops 1 | bytes 1 | tf_op jit(solution)/shard_map/lay_out/pallas_call | solution.py:99
  (2 shorter events, 0.0 us)
Async XLA Ops:
  4.8 6.1 %collective-permute-start = (bf16[1024,1024]{1,0:T(8,128)(2,1)S(1)}, bf16[1024,1024]{1,0:T(8,128)(2,1)S(1)}, u32[]{:S(2)}, u32[]{:S(2)}) collective-permute-start(bf16[1024,1024]{1,0:T(8,128)(2,1)S(1)} %get-tuple-element.49.refs_1_), channel_id=1, source_target_pairs={{0,1},{1,0},{2,3},{3,2},{4,5},{5,4},{6,7},{7,6},{8,9},{9,8},{10,11... | collective-permute-start | bytes 6291464 | tf_op jit(solution)/shard_map/ppermute | solution.py:365
  14.1 15.5 %collective-permute-start.1 = (bf16[2064,128]{1,0:T(8,128)(2,1)S(1)}, bf16[2064,128]{1,0:T(8,128)(2,1)S(1)}, u32[]{:S(2)}, u32[]{:S(2)}) collective-permute-start(bf16[2064,128]{1,0:T(8,128)(2,1)S(1)} %get-tuple-element.53), channel_id=1, source_target_pairs={{0,2},{1,3},{2,0},{3,1},{4,6},{5,7},{6,4},{7,5},{8,10},{9,11},{10,... | collective-permute-start | bytes 1585160 | tf_op jit(solution)/shard_map/ppermute | solution.py:365
  22.0 20.7 %collective-permute-start.4 = (bf16[2064,128]{1,0:T(8,128)(2,1)S(1)}, bf16[2064,128]{1,0:T(8,128)(2,1)S(1)}, u32[]{:S(2)}, u32[]{:S(2)}) collective-permute-start(bf16[2064,128]{1,0:T(8,128)(2,1)S(1)} %get-tuple-element.60), channel_id=1, source_target_pairs={{0,4},{1,5},{2,6},{3,7},{4,0},{5,1},{6,2},{7,3},{8,12},{9,13},{10,... | collective-permute-start | bytes 1585160 | tf_op jit(solution)/shard_map/ppermute | solution.py:365
  29.0 15.3 %collective-permute-start.3 = (bf16[2064,128]{1,0:T(8,128)(2,1)S(1)}, bf16[2064,128]{1,0:T(8,128)(2,1)S(1)}, u32[]{:S(2)}, u32[]{:S(2)}) collective-permute-start(bf16[2064,128]{1,0:T(8,128)(2,1)S(1)} %get-tuple-element.59), channel_id=1, source_target_pairs={{0,2},{1,3},{2,0},{3,1},{4,6},{5,7},{6,4},{7,5},{8,10},{9,11},{10,... | collective-permute-start | bytes 1585160 | tf_op jit(solution)/shard_map/ppermute | solution.py:365
  30.6 17.0 %collective-permute-start.2 = (bf16[1040,128]{1,0:T(8,128)(2,1)S(1)}, bf16[1040,128]{1,0:T(8,128)(2,1)S(1)}, u32[]{:S(2)}, u32[]{:S(2)}) collective-permute-start(bf16[1040,128]{1,0:T(8,128)(2,1)S(1)} %get-tuple-element.57), channel_id=1, source_target_pairs={{0,8},{1,9},{2,10},{3,11},{4,12},{5,13},{6,14},{7,15},{8,0},{9,1},... | collective-permute-start | bytes 798728 | tf_op jit(solution)/shard_map/ppermute | solution.py:365
  36.3 12.8 %collective-permute-start.9 = (bf16[1040,128]{1,0:T(8,128)(2,1)S(1)}, bf16[1040,128]{1,0:T(8,128)(2,1)S(1)}, u32[]{:S(2)}, u32[]{:S(2)}) collective-permute-start(bf16[1040,128]{1,0:T(8,128)(2,1)S(1)} %get-tuple-element.70), channel_id=1, source_target_pairs={{0,4},{1,5},{2,6},{3,7},{4,0},{5,1},{6,2},{7,3},{8,12},{9,13},{10,... | collective-permute-start | bytes 798728 | tf_op jit(solution)/shard_map/ppermute | solution.py:365
  41.1 9.4 %collective-permute-start.8 = (bf16[1040,128]{1,0:T(8,128)(2,1)S(1)}, bf16[1040,128]{1,0:T(8,128)(2,1)S(1)}, u32[]{:S(2)}, u32[]{:S(2)}) collective-permute-start(bf16[1040,128]{1,0:T(8,128)(2,1)S(1)} %get-tuple-element.69), channel_id=1, source_target_pairs={{0,2},{1,3},{2,0},{3,1},{4,6},{5,7},{6,4},{7,5},{8,10},{9,11},{10,... | collective-permute-start | bytes 798728 | tf_op jit(solution)/shard_map/ppermute | solution.py:365
  43.7 12.0 %collective-permute-start.7 = (bf16[1040,128]{1,0:T(8,128)(2,1)S(1)}, bf16[1040,128]{1,0:T(8,128)(2,1)S(1)}, u32[]{:S(2)}, u32[]{:S(2)}) collective-permute-start(bf16[1040,128]{1,0:T(8,128)(2,1)S(1)} %get-tuple-element.68), channel_id=1, source_target_pairs={{0,2},{1,3},{2,0},{3,1},{4,6},{5,7},{6,4},{7,5},{8,10},{9,11},{10,... | collective-permute-start | bytes 798728 | tf_op jit(solution)/shard_map/ppermute | solution.py:365
  45.3 15.0 %collective-permute-start.6 = (bf16[1040,128]{1,0:T(8,128)(2,1)S(1)}, bf16[1040,128]{1,0:T(8,128)(2,1)S(1)}, u32[]{:S(2)}, u32[]{:S(2)}) collective-permute-start(bf16[1040,128]{1,0:T(8,128)(2,1)S(1)} %get-tuple-element.67), channel_id=1, source_target_pairs={{0,8},{1,9},{2,10},{3,11},{4,12},{5,13},{6,14},{7,15},{8,0},{9,1},... | collective-permute-start | bytes 798728 | tf_op jit(solution)/shard_map/ppermute | solution.py:365
  48.5 12.8 %collective-permute-start.5 = (bf16[528,128]{1,0:T(8,128)(2,1)S(1)}, bf16[528,128]{1,0:T(8,128)(2,1)S(1)}, u32[]{:S(2)}, u32[]{:S(2)}) collective-permute-start(bf16[528,128]{1,0:T(8,128)(2,1)S(1)} %get-tuple-element.65), channel_id=1, source_target_pairs={{0,4},{1,5},{2,6},{3,7},{4,0},{5,1},{6,2},{7,3},{8,12},{9,13},{10,... | collective-permute-start | bytes 405512 | tf_op jit(solution)/shard_map/ppermute | solution.py:365
  49.9 12.0 %collective-permute-start.13 = (bf16[528,128]{1,0:T(8,128)(2,1)S(1)}, bf16[528,128]{1,0:T(8,128)(2,1)S(1)}, u32[]{:S(2)}, u32[]{:S(2)}) collective-permute-start(bf16[528,128]{1,0:T(8,128)(2,1)S(1)} %get-tuple-element.79), channel_id=1, source_target_pairs={{0,2},{1,3},{2,0},{3,1},{4,6},{5,7},{6,4},{7,5},{8,10},{9,11},{10,... | collective-permute-start | bytes 405512 | tf_op jit(solution)/shard_map/ppermute | solution.py:365
  51.3 12.3 %collective-permute-start.12 = (bf16[528,128]{1,0:T(8,128)(2,1)S(1)}, bf16[528,128]{1,0:T(8,128)(2,1)S(1)}, u32[]{:S(2)}, u32[]{:S(2)}) collective-permute-start(bf16[528,128]{1,0:T(8,128)(2,1)S(1)} %get-tuple-element.78), channel_id=1, source_target_pairs={{0,4},{1,5},{2,6},{3,7},{4,0},{5,1},{6,2},{7,3},{8,12},{9,13},{10,... | collective-permute-start | bytes 405512 | tf_op jit(solution)/shard_map/ppermute | solution.py:365
  56.6 9.7 %collective-permute-start.11 = (bf16[528,128]{1,0:T(8,128)(2,1)S(1)}, bf16[528,128]{1,0:T(8,128)(2,1)S(1)}, u32[]{:S(2)}, u32[]{:S(2)}) collective-permute-start(bf16[528,128]{1,0:T(8,128)(2,1)S(1)} %get-tuple-element.77), channel_id=1, source_target_pairs={{0,8},{1,9},{2,10},{3,11},{4,12},{5,13},{6,14},{7,15},{8,0},{9,1},... | collective-permute-start | bytes 405512 | tf_op jit(solution)/shard_map/ppermute | solution.py:365
  61.1 7.4 %collective-permute-start.15 = (bf16[528,128]{1,0:T(8,128)(2,1)S(1)}, bf16[528,128]{1,0:T(8,128)(2,1)S(1)}, u32[]{:S(2)}, u32[]{:S(2)}) collective-permute-start(bf16[528,128]{1,0:T(8,128)(2,1)S(1)} %get-tuple-element.84), channel_id=1, source_target_pairs={{0,4},{1,5},{2,6},{3,7},{4,0},{5,1},{6,2},{7,3},{8,12},{9,13},{10,... | collective-permute-start | bytes 405512 | tf_op jit(solution)/shard_map/ppermute | solution.py:365
  62.6 7.9 %collective-permute-start.17 = (bf16[272,128]{1,0:T(8,128)(2,1)S(1)}, bf16[272,128]{1,0:T(8,128)(2,1)S(1)}, u32[]{:S(2)}, u32[]{:S(2)}) collective-permute-start(bf16[272,128]{1,0:T(8,128)(2,1)S(1)} %get-tuple-element.87), channel_id=1, source_target_pairs={{0,8},{1,9},{2,10},{3,11},{4,12},{5,13},{6,14},{7,15},{8,0},{9,1},... | collective-permute-start | bytes 208904 | tf_op jit(solution)/shard_map/ppermute | solution.py:365
  64.3 6.9 %collective-permute-start.19 = (bf16[272,128]{1,0:T(8,128)(2,1)S(1)}, bf16[272,128]{1,0:T(8,128)(2,1)S(1)}, u32[]{:S(2)}, u32[]{:S(2)}) collective-permute-start(bf16[272,128]{1,0:T(8,128)(2,1)S(1)} %get-tuple-element.90), channel_id=1, source_target_pairs={{0,8},{1,9},{2,10},{3,11},{4,12},{5,13},{6,14},{7,15},{8,0},{9,1},... | collective-permute-start | bytes 208904 | tf_op jit(solution)/shard_map/ppermute | solution.py:365
  66.3 6.1 %collective-permute-start.10 = (bf16[32,1024]{1,0:T(8,128)(2,1)S(1)}, bf16[32,1024]{1,0:T(8,128)(2,1)S(1)}, u32[]{:S(2)}, u32[]{:S(2)}) collective-permute-start(bf16[32,1024]{1,0:T(8,128)(2,1)S(1)} %get-tuple-element.76), channel_id=1, source_target_pairs={{0,1},{1,0},{2,3},{3,2},{4,5},{5,4},{6,7},{7,6},{8,9},{9,8},{10,11... | collective-permute-start | bytes 196616 | tf_op jit(solution)/shard_map/ppermute | solution.py:365
  69.1 3.2 %collective-permute-start.16 = (bf16[32,1024]{1,0:T(8,128)(2,1)S(1)}, bf16[32,1024]{1,0:T(8,128)(2,1)S(1)}, u32[]{:S(2)}, u32[]{:S(2)}) collective-permute-start(bf16[32,1024]{1,0:T(8,128)(2,1)S(1)} %get-tuple-element.86), channel_id=1, source_target_pairs={{0,1},{1,0},{2,3},{3,2},{4,5},{5,4},{6,7},{7,6},{8,9},{9,8},{10,11... | collective-permute-start | bytes 196616 | tf_op jit(solution)/shard_map/ppermute | solution.py:365
  69.2 3.2 %collective-permute-start.14 = (bf16[32,1024]{1,0:T(8,128)(2,1)S(1)}, bf16[32,1024]{1,0:T(8,128)(2,1)S(1)}, u32[]{:S(2)}, u32[]{:S(2)}) collective-permute-start(bf16[32,1024]{1,0:T(8,128)(2,1)S(1)} %get-tuple-element.83), channel_id=1, source_target_pairs={{0,1},{1,0},{2,3},{3,2},{4,5},{5,4},{6,7},{7,6},{8,9},{9,8},{10,11... | collective-permute-start | bytes 196616 | tf_op jit(solution)/shard_map/ppermute | solution.py:365
  71.8 1.3 %collective-permute-start.20 = (bf16[32,512]{1,0:T(8,128)(2,1)S(1)}, bf16[32,512]{1,0:T(8,128)(2,1)S(1)}, u32[]{:S(2)}, u32[]{:S(2)}) collective-permute-start(bf16[32,512]{1,0:T(8,128)(2,1)S(1)} %get-tuple-element.92), channel_id=1, source_target_pairs={{0,1},{1,0},{2,3},{3,2},{4,5},{5,4},{6,7},{7,6},{8,9},{9,8},{10,11... | collective-permute-start | bytes 98312 | tf_op jit(solution)/shard_map/ppermute | solution.py:365
  71.9 1.4 %collective-permute-start.18 = (bf16[32,512]{1,0:T(8,128)(2,1)S(1)}, bf16[32,512]{1,0:T(8,128)(2,1)S(1)}, u32[]{:S(2)}, u32[]{:S(2)}) collective-permute-start(bf16[32,512]{1,0:T(8,128)(2,1)S(1)} %get-tuple-element.89), channel_id=1, source_target_pairs={{0,1},{1,0},{2,3},{3,2},{4,5},{5,4},{6,7},{7,6},{8,9},{9,8},{10,11... | collective-permute-start | bytes 98312 | tf_op jit(solution)/shard_map/ppermute | solution.py:365

commit v7 on v6

--- a/solution.py
+++ b/solution.py
@@ -23,7 +23,7 @@
     (2, (0, 1, 2)),
 ]
 PARTS = 16
-EARLY = 1
+EARLY = 2
 ORDER = [
     (0, 0), (1, 0), (2, 0), (0, 1), (3, 0), (4, 0), (1, 1), (2, 1),
     (0, 2), (3, 1), (4, 1), (1, 2), (2, 2), (0, 3), (3, 2), (4, 2),
@@ -87,6 +87,11 @@
     return bound
 
 
+def position(pieces):
+    me = lax.axis_index("row").astype(jnp.int32)
+    return jnp.bitwise_and(me, pieces - 1), jnp.right_shift(me, pieces.bit_length() - 1)
+
+
 def call(kernel, name, ins, outs, after, scratch=(), limit=4, cost=(0, 0, 0), far=0):
     count = len(ins)
 
@@ -98,8 +103,7 @@
     ins = ins[:near] + [pltpu.with_memory_space_constraint(x, pltpu.HBM) for x in ins[near:]]
     return pl.pallas_call(
         run,
-        in_specs=[pl.BlockSpec(memory_space=pltpu.SMEM)]
-        + [vmem] * (count - 1 - far)
+        in_specs=[vmem] * (count - far)
         + [pl.BlockSpec(memory_space=pltpu.HBM)] * far
         + [pl.BlockSpec(memory_space=pl.ANY)] * len(after),
         out_specs=[vmem] * len(outs),
@@ -111,9 +115,9 @@
     )(*ins, *after)
 
 
-def row_copies(place_ref, w_ref, near_ref, sems, distance, wide):
+def row_copies(w_ref, near_ref, sems, pieces, distance, wide):
     depth = near_ref.shape[0]
-    owner = jnp.bitwise_xor(place_ref[0], distance)
+    owner = jnp.bitwise_xor(position(pieces)[0], distance)
     copies = []
     for index, at in enumerate(range(0, depth, wide)):
         source = pl.ds(pl.multiple_of(owner * depth + at, wide), wide)
@@ -126,24 +130,25 @@
 
 
 def prepare_kernel(
-    blocks, bits, wide, place_ref, basis_ref, w_ref, out_ref, near_ref, held, turned, sems, w_sems
+    pieces, blocks, bits, wide, basis_ref, w_ref, out_ref, near_ref, held, turned, sems, w_sems
 ):
     depth, rows = basis_ref.shape
     step = rows // blocks
+    mine = position(pieces)[1]
     copies = []
     for index, at in enumerate(range(0, depth, wide)):
         part = pl.ds(at, wide)
         copies.append(
             pltpu.make_async_copy(basis_ref.at[part, :], held.at[part, :], sems.at[index])
         )
-    weight_copies = row_copies(place_ref, w_ref, near_ref, w_sems, 0, wide)
+    weight_copies = row_copies(w_ref, near_ref, w_sems, pieces, 0, wide)
     for copy in copies + weight_copies:
         copy.start()
     for index, at in enumerate(range(0, depth, wide)):
         copies[index].wait()
         turned[:, at : at + wide] = held[at : at + wide, :].T
         for place in range(blocks):
-            source = jnp.bitwise_xor(place_ref[1], reversed_bits(place, bits))
+            source = jnp.bitwise_xor(mine, reversed_bits(place, bits))
             part = turned[pl.ds(pl.multiple_of(source * step, step), step), at : at + wide]
             high = part.astype(jnp.bfloat16)
             low = (part - high.astype(jnp.float32)).astype(jnp.bfloat16)
@@ -153,14 +158,14 @@
         copy.wait()
 
 
-def prepare(basis, weights, places, blocks, bits):
+def prepare(basis, weights, pieces, blocks, bits):
     depth, rows = basis.shape
     wide = min(depth, COLUMNS)
     sems = pltpu.SemaphoreType.DMA((depth // wide,))
     return call(
-        functools.partial(prepare_kernel, blocks, bits, wide),
+        functools.partial(prepare_kernel, pieces, blocks, bits, wide),
         "split_basis",
-        [places, basis, weights],
+        [basis, weights],
         [
             jax.ShapeDtypeStruct((2 * rows, depth), jnp.bfloat16),
             jax.ShapeDtypeStruct((depth, weights.shape[2]), jnp.bfloat16),
@@ -187,14 +192,14 @@
     return product[:half] + product[half:]
 
 
-def early_kernel(pieces, width, place_ref, own_ref, near_ref, w_ref, *refs):
+def early_kernel(pieces, width, own_ref, near_ref, w_ref, *refs):
     *other_refs, partial_ref, sems = refs
     depth = own_ref.shape[1]
     wide = min(depth, COLUMNS)
     copies = []
     for distance in range(1, pieces):
         copies += row_copies(
-            place_ref, w_ref, other_refs[distance - 1], sems.at[distance - 1], distance, wide
+            w_ref, other_refs[distance - 1], sems.at[distance - 1], pieces, distance, wide
         )
     for copy in copies:
         copy.start()
@@ -206,13 +211,13 @@
         copy.wait()
 
 
-def early(own, near, weights, places, pieces, width):
+def early(own, near, weights, pieces, width):
     rows2, depth = own.shape
     full = weights.shape[2]
     out = call(
         functools.partial(early_kernel, pieces, width),
         "early_products",
-        [places, own, near, weights],
+        [own, near, weights],
         [jax.ShapeDtypeStruct((depth, full), jnp.bfloat16)] * (pieces - 1)
         + [jax.ShapeDtypeStruct((rows2 // 2, width), jnp.float32)],
         [],
@@ -224,7 +229,7 @@
     return [near, *out[:-1]], out[-1]
 
 
-def product_kernel(pieces, start, width, early, step, leave, stay, place_ref, *refs):
+def product_kernel(pieces, start, width, early, step, leave, stay, *refs):
     left, right = refs[:pieces], refs[pieces : 2 * pieces]
     message_ref, kept_ref = refs[-2:]
     first = 1 if early else 0
@@ -256,7 +261,7 @@
     ]
 
 
-def product(left, right, partial, places, start, width, step, leave, stay, after):
+def product(left, right, partial, start, width, step, leave, stay, after):
     rows2, depth = left[0].shape
     pieces = len(left)
     early = partial is not None
@@ -264,7 +269,7 @@
     return call(
         functools.partial(product_kernel, pieces, start, width, early, step, leave, stay),
         "product",
-        [places, *left, *right] + ([partial] if early else []),
+        [*left, *right] + ([partial] if early else []),
         outputs(width, step, leave, stay),
         after,
         limit=8,
@@ -285,7 +290,7 @@
     return kept_ref[tile * count : (tile + 1) * count, :] + decode(coded, bound)
 
 
-def middle_kernel(tiles, step, old, leave, stay, place_ref, message_ref, kept_ref, out_ref, next_ref):
+def middle_kernel(tiles, step, old, leave, stay, message_ref, kept_ref, out_ref, next_ref):
     bounds = []
     for tile in range(tiles):
         column = received(message_ref, kept_ref, tile, tiles, len(old) * step)
@@ -294,19 +299,19 @@
     put_bounds(out_ref, bounds, len(leave) * step)
 
 
-def middle(message, kept, places, width, step, old, leave, stay, after):
+def middle(message, kept, width, step, old, leave, stay, after):
     size = width * len(old) * step
     return call(
         functools.partial(middle_kernel, width // LANES, step, old, leave, stay),
         "add_and_split",
-        [places, message, kept],
+        [message, kept],
         outputs(width, step, leave, stay),
         after,
         cost=(20 * size, 9 * size, 2 * size),
     )
 
 
-def last_kernel(tiles, pieces, place_ref, message_ref, kept_ref, *refs):
+def last_kernel(tiles, pieces, message_ref, kept_ref, *refs):
     outs = refs[:pieces]
     whole = refs[pieces]
     count = whole.shape[0]
@@ -316,18 +321,18 @@
             message_ref, kept_ref, tile, tiles, count
         )
     for distance in range(pieces):
-        owner = jnp.bitwise_xor(place_ref[0], distance)
+        owner = jnp.bitwise_xor(position(pieces)[0], distance)
         rows = whole[pl.ds(pl.multiple_of(owner * share, share), share), :]
         outs[distance][...] = rows.astype(jnp.bfloat16)
 
 
-def last(message, kept, places, width, step, pieces, after):
+def last(message, kept, width, step, pieces, after):
     size = width * step
     share = jax.ShapeDtypeStruct((step // pieces, width), jnp.bfloat16)
     return call(
         functools.partial(last_kernel, width // LANES, pieces),
         "add_last",
-        [places, message, kept],
+        [message, kept],
         [share] * pieces,
         after,
         [pltpu.VMEM((step, width), jnp.float32)],
@@ -335,25 +340,25 @@
     )
 
 
-def lay_kernel(pieces, width, place_ref, *refs):
+def lay_kernel(pieces, width, *refs):
     out_ref = refs[-1]
     at = 0
     for first in range(0, len(refs) - 1, pieces):
         for distance in range(pieces):
             part = refs[first + distance]
-            owner = jnp.bitwise_xor(place_ref[0], distance)
+            owner = jnp.bitwise_xor(position(pieces)[0], distance)
             columns = pl.ds(pl.multiple_of(owner * width + at, LANES), part.shape[1])
             out_ref[:, columns] = part[...]
         at += part.shape[1]
 
 
-def lay(parts, places, pieces, width):
+def lay(parts, pieces, width):
     flat = [part for chunk in parts for part in chunk]
     rows = flat[0].shape[0]
     return call(
         functools.partial(lay_kernel, pieces, width),
         "lay_out",
-        [places, *flat],
+        [*flat],
         [jax.ShapeDtypeStruct((rows, pieces * width), jnp.bfloat16)],
         [],
         cost=(0, 4 * rows * pieces * width, 0),
@@ -371,14 +376,10 @@
     pieces = weights.shape[1] // depth
     blocks = axis_len // pieces
     bits = blocks.bit_length() - 1
-    piece_bits = pieces.bit_length() - 1
     step = rows // blocks
     width = weights.shape[2]
-    me = lax.axis_index("row").astype(jnp.int32)
-    column = jnp.bitwise_and(me, pieces - 1)
-    places = jnp.stack([column, jnp.right_shift(me, piece_bits)])
-
-    own, near = prepare(basis, weights, places, blocks, bits)
+
+    own, near = prepare(basis, weights, pieces, blocks, bits)
     left = [own] + [swapped(own, distance) for distance in range(1, pieces)]
 
     cuts = [0]
@@ -387,7 +388,7 @@
     cuts = [cut * (width // LANES) // PARTS * LANES for cut in cuts]
     orders = [[bit for bit in order if bit < bits] for _, order in CHUNKS]
     stages = [split_places(order, bits) for order in orders]
-    right, partial = early(own, near, weights, places, pieces, cuts[EARLY])
+    right, partial = early(own, near, weights, pieces, cuts[EARLY])
 
     state = {}
     after = [partial]
@@ -399,21 +400,21 @@
         if number == 0:
             begun = partial if index < EARLY else None
             out = product(
-                left, right, begun, places, start, chunk, step, *stages[index][0], after
+                left, right, begun, start, chunk, step, *stages[index][0], after
             )
         elif number < bits:
             message, kept = state[index]
             old = stages[index][number - 1][1]
-            out = middle(message, kept, places, chunk, step, old, *stages[index][number], after)
+            out = middle(message, kept, chunk, step, old, *stages[index][number], after)
         else:
             message, kept = state[index]
-            out = last(message, kept, places, chunk, step, pieces, after)
+            out = last(message, kept, chunk, step, pieces, after)
             finished[index] = [out[0]] + [swapped(out[d], d) for d in range(1, pieces)]
             after = [out[0]]
             continue
         state[index] = swapped(out[0], pieces << order[number]), out[1]
         after = [out[1]]
-    return lay([finished[index] for index in sorted(finished)], places, pieces, width)
+    return lay([finished[index] for index in sorted(finished)], pieces, width)
 
 
 def solution(mesh):

time: 74.7 us -> 71.9 us (0.963)
  Pallas kernels: 43.2 us -> 31.4 us
  waiting for transfers between devices: 8.16 us -> 14.4 us
  starting transfers between devices: 23 us -> 25.2 us
    pallas_call x23, Pallas kernels: 43.2 us -> 31.4 us  [call(): pl.pallas_call(run, in_specs=[vmem] * (count - far) + [pl.BlockSpec(memor...]
    ppermute x21, waiting for transfers between devices: 8.16 us -> 14.4 us  [swapped(): return lax.ppermute(block, 'row', [(i, i ^ apart) for i in range(count)])]
    ppermute x21, starting transfers between devices: 23 us -> 25.2 us  [swapped(): return lax.ppermute(block, 'row', [(i, i ^ apart) for i in range(count)])]
  transfers between devices with their start and end apart: 21 -> 21, of which waited for: 9 -> 9; matrix products, arithmetic and copies ran while one was open for 0% -> 0% of each run, Pallas kernels for 46% -> 33%
where the time goes in v7:
time: 71.9 us; the launch traced here: 71.2 us
  Pallas kernels  31.4 us (44%)
  starting transfers between devices  25.2 us (35%)
  waiting for transfers between devices  14.4 us (20%)
    pallas_call x23, Pallas kernels, call(): pl.pallas_call(run, in_specs=[vmem] * (count - far) + [pl.BlockSpec(memor...  31.4 us
    ppermute x21, starting transfers between devices, swapped(): return lax.ppermute(block, 'row', [(i, i ^ apart) for i in range(count)])  25.2 us
    ppermute x21, waiting for transfers between devices, swapped(): return lax.ppermute(block, 'row', [(i, i ^ apart) for i in range(count)])  14.4 us
  transfers between devices with their start and end apart: 21, of which 9 were waited for; matrix products, arithmetic and copies ran while one was open for 0% of the time, Pallas kernels for 33%

profile of v7, /device:TPU:0, one launch (start us, length us, event | category | flops | bytes accessed | tf_op | source)
XLA Modules:
  0.0 71.2 jit_solution(14366579351068671904)
XLA Ops:
  0.0 4.2 %split_basis.1 = (bf16[1024,1024]{1,0:T(8,128)(2,1)S(1)}, bf16[1024,4096]{1,0:T(8,128)(2,1)S(1)}) custom-call(f32[1024,512]{1,0:T(8,128)} %refs_0_.1, bf16[1,2048,4096]{2,1,0:T(8,128)(2,1)} %refs_2_.1), custom_call_target="tpu_custom_call" | custom-call | flops 1 | bytes 1 | tf_op jit(solution)/shard_map/split_basis/pallas_call | solution.py:104
  4.2 0.5 collective-permute-start
  4.7 7.8 %early_products.1 = (bf16[1024,4096]{1,0:T(8,128)(2,1)S(1)}, f32[512,2048]{1,0:T(8,128)S(1)}) custom-call(bf16[1024,1024]{1,0:T(8,128)(2,1)S(1)} %get-tuple-element.49.refs_0_, bf16[1024,4096]{1,0:T(8,128)(2,1)S(1)} %get-tuple-element.50.refs_1_.refs_2_, bf16[1,2048,4096]{2,1,0:T(8,128)(2,1)} %refs_2_.1), custom_call_target="tpu_custom_call" | custom-call | flops 1 | bytes 1 | tf_op jit(solution)/shard_map/early_products/pallas_call | solution.py:104
  12.5 0.0 collective-permute-done.refs_1_
  12.5 2.6 %product.5 = (bf16[2064,128]{1,0:T(8,128)(2,1)S(1)}, f32[2048,128]{1,0:T(8,128)S(1)}) custom-call(bf16[1024,1024]{1,0:T(8,128)(2,1)S(1)} %get-tuple-element.49.refs_0_, bf16[1024,1024]{1,0:T(8,128)(2,1)S(1)} %collective-permute-done.refs_1_, bf16[1024,4096]{1,0:T(8,128)(2,1)S(1)} %get-tuple-element.50.refs_1_.refs_2_, ...), custom_call_target="tpu_custom_call" | custom-call | flops 1 | bytes 1 | tf_op jit(solution)/shard_map/product/pallas_call | solution.py:104
  15.1 2.6 %collective-permute-start.1 = (bf16[2064,128]{1,0:T(8,128)(2,1)S(1)}, bf16[2064,128]{1,0:T(8,128)(2,1)S(1)}, u32[]{:S(2)}, u32[]{:S(2)}) collective-permute-start(bf16[2064,128]{1,0:T(8,128)(2,1)S(1)} %get-tuple-element.53), channel_id=1, source_target_pairs={{0,2},{1,3},{2,0},{3,1},{4,6},{5,7},{6,4},{7,5},{8,10},{9,11},{10,... | collective-permute-start | bytes 1585160 | tf_op jit(solution)/shard_map/ppermute | solution.py:370
  17.7 2.6 %product.6 = (bf16[2064,128]{1,0:T(8,128)(2,1)S(1)}, f32[2048,128]{1,0:T(8,128)S(1)}) custom-call(bf16[1024,1024]{1,0:T(8,128)(2,1)S(1)} %get-tuple-element.49.refs_0_, bf16[1024,1024]{1,0:T(8,128)(2,1)S(1)} %collective-permute-done.refs_1_, bf16[1024,4096]{1,0:T(8,128)(2,1)S(1)} %get-tuple-element.50.refs_1_.refs_2_, ...), custom_call_target="tpu_custom_call" | custom-call | flops 1 | bytes 1 | tf_op jit(solution)/shard_map/product/pallas_call | solution.py:104
  20.4 1.7 %collective-permute-start.4 = (bf16[2064,128]{1,0:T(8,128)(2,1)S(1)}, bf16[2064,128]{1,0:T(8,128)(2,1)S(1)}, u32[]{:S(2)}, u32[]{:S(2)}) collective-permute-start(bf16[2064,128]{1,0:T(8,128)(2,1)S(1)} %get-tuple-element.60), channel_id=1, source_target_pairs={{0,4},{1,5},{2,6},{3,7},{4,0},{5,1},{6,2},{7,3},{8,12},{9,13},{10,... | collective-permute-start | bytes 1585160 | tf_op jit(solution)/shard_map/ppermute | solution.py:370
  22.0 4.8 %product.7 = (bf16[2064,128]{1,0:T(8,128)(2,1)S(1)}, f32[2048,128]{1,0:T(8,128)S(1)}) custom-call(bf16[1024,1024]{1,0:T(8,128)(2,1)S(1)} %get-tuple-element.49.refs_0_, bf16[1024,1024]{1,0:T(8,128)(2,1)S(1)} %collective-permute-done.refs_1_, bf16[1024,4096]{1,0:T(8,128)(2,1)S(1)} %get-tuple-element.50.refs_1_.refs_2_, ...), custom_call_target="tpu_custom_call" | custom-call | flops 1 | bytes 1 | tf_op jit(solution)/shard_map/product/pallas_call | solution.py:104
  26.8 0.6 collective-permute-start.3
  27.4 3.2 %collective-permute-done.1.refs_0_ = bf16[2064,128]{1,0:T(8,128)(2,1)S(1)} collective-permute-done((bf16[2064,128]{1,0:T(8,128)(2,1)S(1)}, bf16[2064,128]{1,0:T(8,128)(2,1)S(1)}, u32[]{:S(2)}, u32[]{:S(2)}) %collective-permute-start.1) | collective-permute-done | bytes 528416 | tf_op jit(solution)/shard_map/ppermute | solution.py:370
  30.6 0.5 add_and_split.10
  31.1 3.1 %collective-permute-start.2 = (bf16[1040,128]{1,0:T(8,128)(2,1)S(1)}, bf16[1040,128]{1,0:T(8,128)(2,1)S(1)}, u32[]{:S(2)}, u32[]{:S(2)}) collective-permute-start(bf16[1040,128]{1,0:T(8,128)(2,1)S(1)} %get-tuple-element.57), channel_id=1, source_target_pairs={{0,8},{1,9},{2,10},{3,11},{4,12},{5,13},{6,14},{7,15},{8,0},{9,1},... | collective-permute-start | bytes 798728 | tf_op jit(solution)/shard_map/ppermute | solution.py:370
  34.2 2.5 %product.8 = (bf16[1040,128]{1,0:T(8,128)(2,1)S(1)}, f32[1024,128]{1,0:T(8,128)S(1)}) custom-call(bf16[1024,1024]{1,0:T(8,128)(2,1)S(1)} %get-tuple-element.49.refs_0_, bf16[1024,1024]{1,0:T(8,128)(2,1)S(1)} %collective-permute-done.refs_1_, bf16[1024,4096]{1,0:T(8,128)(2,1)S(1)} %get-tuple-element.50.refs_1_.refs_2_, ...), custom_call_target="tpu_custom_call" | custom-call | flops 1 | bytes 1 | tf_op jit(solution)/shard_map/product/pallas_call | solution.py:104
  36.6 1.6 %collective-permute-start.9 = (bf16[1040,128]{1,0:T(8,128)(2,1)S(1)}, bf16[1040,128]{1,0:T(8,128)(2,1)S(1)}, u32[]{:S(2)}, u32[]{:S(2)}) collective-permute-start(bf16[1040,128]{1,0:T(8,128)(2,1)S(1)} %get-tuple-element.70), channel_id=1, source_target_pairs={{0,4},{1,5},{2,6},{3,7},{4,0},{5,1},{6,2},{7,3},{8,12},{9,13},{10,... | collective-permute-start | bytes 798728 | tf_op jit(solution)/shard_map/ppermute | solution.py:370
  38.3 2.7 %product.9 = (bf16[1040,128]{1,0:T(8,128)(2,1)S(1)}, f32[1024,128]{1,0:T(8,128)S(1)}) custom-call(bf16[1024,1024]{1,0:T(8,128)(2,1)S(1)} %get-tuple-element.49.refs_0_, bf16[1024,1024]{1,0:T(8,128)(2,1)S(1)} %collective-permute-done.refs_1_, bf16[1024,4096]{1,0:T(8,128)(2,1)S(1)} %get-tuple-element.50.refs_1_.refs_2_, ...), custom_call_target="tpu_custom_call" | custom-call | flops 1 | bytes 1 | tf_op jit(solution)/shard_map/product/pallas_call | solution.py:104
  41.0 1.6 %collective-permute-start.8 = (bf16[1040,128]{1,0:T(8,128)(2,1)S(1)}, bf16[1040,128]{1,0:T(8,128)(2,1)S(1)}, u32[]{:S(2)}, u32[]{:S(2)}) collective-permute-start(bf16[1040,128]{1,0:T(8,128)(2,1)S(1)} %get-tuple-element.69), channel_id=1, source_target_pairs={{0,2},{1,3},{2,0},{3,1},{4,6},{5,7},{6,4},{7,5},{8,10},{9,11},{10,... | collective-permute-start | bytes 798728 | tf_op jit(solution)/shard_map/ppermute | solution.py:370
  42.5 0.0 collective-permute-done.4.refs_0_
  42.5 0.5 add_and_split.11
  43.0 0.6 collective-permute-start.7
  43.6 0.0 collective-permute-done.3.refs_0_
  43.6 0.5 add_and_split.12
  44.1 1.4 %collective-permute-start.6 = (bf16[1040,128]{1,0:T(8,128)(2,1)S(1)}, bf16[1040,128]{1,0:T(8,128)(2,1)S(1)}, u32[]{:S(2)}, u32[]{:S(2)}) collective-permute-start(bf16[1040,128]{1,0:T(8,128)(2,1)S(1)} %get-tuple-element.67), channel_id=1, source_target_pairs={{0,8},{1,9},{2,10},{3,11},{4,12},{5,13},{6,14},{7,15},{8,0},{9,1},... | collective-permute-start | bytes 798728 | tf_op jit(solution)/shard_map/ppermute | solution.py:370
  45.5 0.5 collective-permute-done.2.refs_0_
  45.9 0.3 add_and_split.13
  46.2 1.2 %collective-permute-start.5 = (bf16[528,128]{1,0:T(8,128)(2,1)S(1)}, bf16[528,128]{1,0:T(8,128)(2,1)S(1)}, u32[]{:S(2)}, u32[]{:S(2)}) collective-permute-start(bf16[528,128]{1,0:T(8,128)(2,1)S(1)} %get-tuple-element.65), channel_id=1, source_target_pairs={{0,4},{1,5},{2,6},{3,7},{4,0},{5,1},{6,2},{7,3},{8,12},{9,13},{10,... | collective-permute-start | bytes 405512 | tf_op jit(solution)/shard_map/ppermute | solution.py:370
  47.4 3.7 %collective-permute-done.9.refs_0_ = bf16[1040,128]{1,0:T(8,128)(2,1)S(1)} collective-permute-done((bf16[1040,128]{1,0:T(8,128)(2,1)S(1)}, bf16[1040,128]{1,0:T(8,128)(2,1)S(1)}, u32[]{:S(2)}, u32[]{:S(2)}) %collective-permute-start.9) | collective-permute-done | bytes 266272 | tf_op jit(solution)/shard_map/ppermute | solution.py:370
  51.1 0.2 add_and_split.14
  51.3 1.7 %collective-permute-start.13 = (bf16[528,128]{1,0:T(8,128)(2,1)S(1)}, bf16[528,128]{1,0:T(8,128)(2,1)S(1)}, u32[]{:S(2)}, u32[]{:S(2)}) collective-permute-start(bf16[528,128]{1,0:T(8,128)(2,1)S(1)} %get-tuple-element.79), channel_id=1, source_target_pairs={{0,2},{1,3},{2,0},{3,1},{4,6},{5,7},{6,4},{7,5},{8,10},{9,11},{10,... | collective-permute-start | bytes 405512 | tf_op jit(solution)/shard_map/ppermute | solution.py:370
  53.0 0.0 collective-permute-done.8.refs_0_
  53.0 0.2 add_and_split.15
  53.3 0.1 collective-permute-start.12
  53.4 1.9 %collective-permute-done.7.refs_0_ = bf16[1040,128]{1,0:T(8,128)(2,1)S(1)} collective-permute-done((bf16[1040,128]{1,0:T(8,128)(2,1)S(1)}, bf16[1040,128]{1,0:T(8,128)(2,1)S(1)}, u32[]{:S(2)}, u32[]{:S(2)}) %collective-permute-start.7) | collective-permute-done | bytes 266272 | tf_op jit(solution)/shard_map/ppermute | solution.py:370
  55.2 0.3 add_and_split.16
  55.5 1.2 %collective-permute-start.11 = (bf16[528,128]{1,0:T(8,128)(2,1)S(1)}, bf16[528,128]{1,0:T(8,128)(2,1)S(1)}, u32[]{:S(2)}, u32[]{:S(2)}) collective-permute-start(bf16[528,128]{1,0:T(8,128)(2,1)S(1)} %get-tuple-element.77), channel_id=1, source_target_pairs={{0,8},{1,9},{2,10},{3,11},{4,12},{5,13},{6,14},{7,15},{8,0},{9,1},... | collective-permute-start | bytes 405512 | tf_op jit(solution)/shard_map/ppermute | solution.py:370
  56.7 1.1 %collective-permute-done.6.refs_0_ = bf16[1040,128]{1,0:T(8,128)(2,1)S(1)} collective-permute-done((bf16[1040,128]{1,0:T(8,128)(2,1)S(1)}, bf16[1040,128]{1,0:T(8,128)(2,1)S(1)}, u32[]{:S(2)}, u32[]{:S(2)}) %collective-permute-start.6) | collective-permute-done | bytes 266272 | tf_op jit(solution)/shard_map/ppermute | solution.py:370
  57.8 0.3 add_and_split.17
  58.1 0.6 collective-permute-start.15
  58.6 0.0 collective-permute-done.5.refs_0_
  58.6 0.1 add_last.5
  58.7 0.0 collective-permute-done.13.refs_0_
  58.8 0.1 add_and_split.18
  58.9 3.9 %collective-permute-start.17 = (bf16[272,128]{1,0:T(8,128)(2,1)S(1)}, bf16[272,128]{1,0:T(8,128)(2,1)S(1)}, u32[]{:S(2)}, u32[]{:S(2)}) collective-permute-start(bf16[272,128]{1,0:T(8,128)(2,1)S(1)} %get-tuple-element.87), channel_id=1, source_target_pairs={{0,8},{1,9},{2,10},{3,11},{4,12},{5,13},{6,14},{7,15},{8,0},{9,1},... | collective-permute-start | bytes 208904 | tf_op jit(solution)/shard_map/ppermute | solution.py:370
  62.8 0.0 collective-permute-done.12.refs_0_
  62.8 0.1 add_and_split.19
  62.9 2.3 %collective-permute-start.19 = (bf16[272,128]{1,0:T(8,128)(2,1)S(1)}, bf16[272,128]{1,0:T(8,128)(2,1)S(1)}, u32[]{:S(2)}, u32[]{:S(2)}) collective-permute-start(bf16[272,128]{1,0:T(8,128)(2,1)S(1)} %get-tuple-element.90), channel_id=1, source_target_pairs={{0,8},{1,9},{2,10},{3,11},{4,12},{5,13},{6,14},{7,15},{8,0},{9,1},... | collective-permute-start | bytes 208904 | tf_op jit(solution)/shard_map/ppermute | solution.py:370
  65.2 0.0 collective-permute-start.10
  65.2 0.0 collective-permute-done.11.refs_0_
  65.2 0.1 add_last.6
  65.3 0.6 collective-permute-start.14
  65.8 0.6 collective-permute-done.15.refs_0_
  66.5 0.1 add_last.7
  66.6 0.1 collective-permute-start.16
  66.6 1.2 %collective-permute-done.17.refs_0_ = bf16[272,128]{1,0:T(8,128)(2,1)S(1)} collective-permute-done((bf16[272,128]{1,0:T(8,128)(2,1)S(1)}, bf16[272,128]{1,0:T(8,128)(2,1)S(1)}, u32[]{:S(2)}, u32[]{:S(2)}) %collective-permute-start.17) | collective-permute-done | bytes 69664 | tf_op jit(solution)/shard_map/ppermute | solution.py:370
  67.9 0.1 add_last.8
  67.9 0.1 collective-permute-start.18
  68.0 1.1 %collective-permute-done.19.refs_0_ = bf16[272,128]{1,0:T(8,128)(2,1)S(1)} collective-permute-done((bf16[272,128]{1,0:T(8,128)(2,1)S(1)}, bf16[272,128]{1,0:T(8,128)(2,1)S(1)}, u32[]{:S(2)}, u32[]{:S(2)}) %collective-permute-start.19) | collective-permute-done | bytes 69664 | tf_op jit(solution)/shard_map/ppermute | solution.py:370
  69.1 0.1 add_last.9
  69.1 0.1 collective-permute-start.20
  69.2 0.0 collective-permute-done.10.refs_1_
  69.2 0.0 collective-permute-done.14.refs_3_
  69.2 0.0 collective-permute-done.18.refs_7_
  69.3 1.2 %collective-permute-done.20.refs_9_ = bf16[32,512]{1,0:T(8,128)(2,1)S(1)} collective-permute-done((bf16[32,512]{1,0:T(8,128)(2,1)S(1)}, bf16[32,512]{1,0:T(8,128)(2,1)S(1)}, u32[]{:S(2)}, u32[]{:S(2)}) %collective-permute-start.20) | collective-permute-done | bytes 32800 | tf_op jit(solution)/shard_map/ppermute | solution.py:370
  70.4 0.8 %lay_out.1 = bf16[32,8192]{1,0:T(8,128)(2,1)} custom-call(bf16[32,1024]{1,0:T(8,128)(2,1)S(1)} %get-tuple-element.75.refs_2_.refs_0_, bf16[32,1024]{1,0:T(8,128)(2,1)S(1)} %collective-permute-done.10.refs_1_, bf16[32,1024]{1,0:T(8,128)(2,1)S(1)} %get-tuple-element.82.refs_2_, bf16[32,1024]{1,0:T(8,128)(2,1)S(1)} %collective-permute-done.14.refs_3_, ...), custom_call_target="tpu_custom_call" | custom-call | flops 1 | bytes 1 | tf_op jit(solution)/shard_map/lay_out/pallas_call | solution.py:104
  (1 shorter events, 0.0 us)
Async XLA Ops:
  4.2 8.3 %collective-permute-start = (bf16[1024,1024]{1,0:T(8,128)(2,1)S(1)}, bf16[1024,1024]{1,0:T(8,128)(2,1)S(1)}, u32[]{:S(2)}, u32[]{:S(2)}) collective-permute-start(bf16[1024,1024]{1,0:T(8,128)(2,1)S(1)} %get-tuple-element.49.refs_0_), channel_id=1, source_target_pairs={{0,1},{1,0},{2,3},{3,2},{4,5},{5,4},{6,7},{7,6},{8,9},{9,8},{10,11... | collective-permute-start | bytes 6291464 | tf_op jit(solution)/shard_map/ppermute | solution.py:370
  15.1 15.5 %collective-permute-start.1 = (bf16[2064,128]{1,0:T(8,128)(2,1)S(1)}, bf16[2064,128]{1,0:T(8,128)(2,1)S(1)}, u32[]{:S(2)}, u32[]{:S(2)}) collective-permute-start(bf16[2064,128]{1,0:T(8,128)(2,1)S(1)} %get-tuple-element.53), channel_id=1, source_target_pairs={{0,2},{1,3},{2,0},{3,1},{4,6},{5,7},{6,4},{7,5},{8,10},{9,11},{10,... | collective-permute-start | bytes 1585160 | tf_op jit(solution)/shard_map/ppermute | solution.py:370
  20.4 22.2 %collective-permute-start.4 = (bf16[2064,128]{1,0:T(8,128)(2,1)S(1)}, bf16[2064,128]{1,0:T(8,128)(2,1)S(1)}, u32[]{:S(2)}, u32[]{:S(2)}) collective-permute-start(bf16[2064,128]{1,0:T(8,128)(2,1)S(1)} %get-tuple-element.60), channel_id=1, source_target_pairs={{0,4},{1,5},{2,6},{3,7},{4,0},{5,1},{6,2},{7,3},{8,12},{9,13},{10,... | collective-permute-start | bytes 1585160 | tf_op jit(solution)/shard_map/ppermute | solution.py:370
  26.8 16.8 %collective-permute-start.3 = (bf16[2064,128]{1,0:T(8,128)(2,1)S(1)}, bf16[2064,128]{1,0:T(8,128)(2,1)S(1)}, u32[]{:S(2)}, u32[]{:S(2)}) collective-permute-start(bf16[2064,128]{1,0:T(8,128)(2,1)S(1)} %get-tuple-element.59), channel_id=1, source_target_pairs={{0,2},{1,3},{2,0},{3,1},{4,6},{5,7},{6,4},{7,5},{8,10},{9,11},{10,... | collective-permute-start | bytes 1585160 | tf_op jit(solution)/shard_map/ppermute | solution.py:370
  31.1 14.9 %collective-permute-start.2 = (bf16[1040,128]{1,0:T(8,128)(2,1)S(1)}, bf16[1040,128]{1,0:T(8,128)(2,1)S(1)}, u32[]{:S(2)}, u32[]{:S(2)}) collective-permute-start(bf16[1040,128]{1,0:T(8,128)(2,1)S(1)} %get-tuple-element.57), channel_id=1, source_target_pairs={{0,8},{1,9},{2,10},{3,11},{4,12},{5,13},{6,14},{7,15},{8,0},{9,1},... | collective-permute-start | bytes 798728 | tf_op jit(solution)/shard_map/ppermute | solution.py:370
  36.6 14.4 %collective-permute-start.9 = (bf16[1040,128]{1,0:T(8,128)(2,1)S(1)}, bf16[1040,128]{1,0:T(8,128)(2,1)S(1)}, u32[]{:S(2)}, u32[]{:S(2)}) collective-permute-start(bf16[1040,128]{1,0:T(8,128)(2,1)S(1)} %get-tuple-element.70), channel_id=1, source_target_pairs={{0,4},{1,5},{2,6},{3,7},{4,0},{5,1},{6,2},{7,3},{8,12},{9,13},{10,... | collective-permute-start | bytes 798728 | tf_op jit(solution)/shard_map/ppermute | solution.py:370
  41.0 12.1 %collective-permute-start.8 = (bf16[1040,128]{1,0:T(8,128)(2,1)S(1)}, bf16[1040,128]{1,0:T(8,128)(2,1)S(1)}, u32[]{:S(2)}, u32[]{:S(2)}) collective-permute-start(bf16[1040,128]{1,0:T(8,128)(2,1)S(1)} %get-tuple-element.69), channel_id=1, source_target_pairs={{0,2},{1,3},{2,0},{3,1},{4,6},{5,7},{6,4},{7,5},{8,10},{9,11},{10,... | collective-permute-start | bytes 798728 | tf_op jit(solution)/shard_map/ppermute | solution.py:370
  43.0 12.2 %collective-permute-start.7 = (bf16[1040,128]{1,0:T(8,128)(2,1)S(1)}, bf16[1040,128]{1,0:T(8,128)(2,1)S(1)}, u32[]{:S(2)}, u32[]{:S(2)}) collective-permute-start(bf16[1040,128]{1,0:T(8,128)(2,1)S(1)} %get-tuple-element.68), channel_id=1, source_target_pairs={{0,2},{1,3},{2,0},{3,1},{4,6},{5,7},{6,4},{7,5},{8,10},{9,11},{10,... | collective-permute-start | bytes 798728 | tf_op jit(solution)/shard_map/ppermute | solution.py:370
  44.1 13.7 %collective-permute-start.6 = (bf16[1040,128]{1,0:T(8,128)(2,1)S(1)}, bf16[1040,128]{1,0:T(8,128)(2,1)S(1)}, u32[]{:S(2)}, u32[]{:S(2)}) collective-permute-start(bf16[1040,128]{1,0:T(8,128)(2,1)S(1)} %get-tuple-element.67), channel_id=1, source_target_pairs={{0,8},{1,9},{2,10},{3,11},{4,12},{5,13},{6,14},{7,15},{8,0},{9,1},... | collective-permute-start | bytes 798728 | tf_op jit(solution)/shard_map/ppermute | solution.py:370
  46.2 12.4 %collective-permute-start.5 = (bf16[528,128]{1,0:T(8,128)(2,1)S(1)}, bf16[528,128]{1,0:T(8,128)(2,1)S(1)}, u32[]{:S(2)}, u32[]{:S(2)}) collective-permute-start(bf16[528,128]{1,0:T(8,128)(2,1)S(1)} %get-tuple-element.65), channel_id=1, source_target_pairs={{0,4},{1,5},{2,6},{3,7},{4,0},{5,1},{6,2},{7,3},{8,12},{9,13},{10,... | collective-permute-start | bytes 405512 | tf_op jit(solution)/shard_map/ppermute | solution.py:370
  51.3 7.4 %collective-permute-start.13 = (bf16[528,128]{1,0:T(8,128)(2,1)S(1)}, bf16[528,128]{1,0:T(8,128)(2,1)S(1)}, u32[]{:S(2)}, u32[]{:S(2)}) collective-permute-start(bf16[528,128]{1,0:T(8,128)(2,1)S(1)} %get-tuple-element.79), channel_id=1, source_target_pairs={{0,2},{1,3},{2,0},{3,1},{4,6},{5,7},{6,4},{7,5},{8,10},{9,11},{10,... | collective-permute-start | bytes 405512 | tf_op jit(solution)/shard_map/ppermute | solution.py:370
  53.3 9.5 %collective-permute-start.12 = (bf16[528,128]{1,0:T(8,128)(2,1)S(1)}, bf16[528,128]{1,0:T(8,128)(2,1)S(1)}, u32[]{:S(2)}, u32[]{:S(2)}) collective-permute-start(bf16[528,128]{1,0:T(8,128)(2,1)S(1)} %get-tuple-element.78), channel_id=1, source_target_pairs={{0,4},{1,5},{2,6},{3,7},{4,0},{5,1},{6,2},{7,3},{8,12},{9,13},{10,... | collective-permute-start | bytes 405512 | tf_op jit(solution)/shard_map/ppermute | solution.py:370
  55.5 9.7 %collective-permute-start.11 = (bf16[528,128]{1,0:T(8,128)(2,1)S(1)}, bf16[528,128]{1,0:T(8,128)(2,1)S(1)}, u32[]{:S(2)}, u32[]{:S(2)}) collective-permute-start(bf16[528,128]{1,0:T(8,128)(2,1)S(1)} %get-tuple-element.77), channel_id=1, source_target_pairs={{0,8},{1,9},{2,10},{3,11},{4,12},{5,13},{6,14},{7,15},{8,0},{9,1},... | collective-permute-start | bytes 405512 | tf_op jit(solution)/shard_map/ppermute | solution.py:370
  58.1 8.4 %collective-permute-start.15 = (bf16[528,128]{1,0:T(8,128)(2,1)S(1)}, bf16[528,128]{1,0:T(8,128)(2,1)S(1)}, u32[]{:S(2)}, u32[]{:S(2)}) collective-permute-start(bf16[528,128]{1,0:T(8,128)(2,1)S(1)} %get-tuple-element.84), channel_id=1, source_target_pairs={{0,4},{1,5},{2,6},{3,7},{4,0},{5,1},{6,2},{7,3},{8,12},{9,13},{10,... | collective-permute-start | bytes 405512 | tf_op jit(solution)/shard_map/ppermute | solution.py:370
  58.9 9.0 %collective-permute-start.17 = (bf16[272,128]{1,0:T(8,128)(2,1)S(1)}, bf16[272,128]{1,0:T(8,128)(2,1)S(1)}, u32[]{:S(2)}, u32[]{:S(2)}) collective-permute-start(bf16[272,128]{1,0:T(8,128)(2,1)S(1)} %get-tuple-element.87), channel_id=1, source_target_pairs={{0,8},{1,9},{2,10},{3,11},{4,12},{5,13},{6,14},{7,15},{8,0},{9,1},... | collective-permute-start | bytes 208904 | tf_op jit(solution)/shard_map/ppermute | solution.py:370
  62.9 6.2 %collective-permute-start.19 = (bf16[272,128]{1,0:T(8,128)(2,1)S(1)}, bf16[272,128]{1,0:T(8,128)(2,1)S(1)}, u32[]{:S(2)}, u32[]{:S(2)}) collective-permute-start(bf16[272,128]{1,0:T(8,128)(2,1)S(1)} %get-tuple-element.90), channel_id=1, source_target_pairs={{0,8},{1,9},{2,10},{3,11},{4,12},{5,13},{6,14},{7,15},{8,0},{9,1},... | collective-permute-start | bytes 208904 | tf_op jit(solution)/shard_map/ppermute | solution.py:370
  65.2 4.1 %collective-permute-start.10 = (bf16[32,1024]{1,0:T(8,128)(2,1)S(1)}, bf16[32,1024]{1,0:T(8,128)(2,1)S(1)}, u32[]{:S(2)}, u32[]{:S(2)}) collective-permute-start(bf16[32,1024]{1,0:T(8,128)(2,1)S(1)} %get-tuple-element.76), channel_id=1, source_target_pairs={{0,1},{1,0},{2,3},{3,2},{4,5},{5,4},{6,7},{7,6},{8,9},{9,8},{10,11... | collective-permute-start | bytes 196616 | tf_op jit(solution)/shard_map/ppermute | solution.py:370
  65.3 4.0 %collective-permute-start.14 = (bf16[32,1024]{1,0:T(8,128)(2,1)S(1)}, bf16[32,1024]{1,0:T(8,128)(2,1)S(1)}, u32[]{:S(2)}, u32[]{:S(2)}) collective-permute-start(bf16[32,1024]{1,0:T(8,128)(2,1)S(1)} %get-tuple-element.83), channel_id=1, source_target_pairs={{0,1},{1,0},{2,3},{3,2},{4,5},{5,4},{6,7},{7,6},{8,9},{9,8},{10,11... | collective-permute-start | bytes 196616 | tf_op jit(solution)/shard_map/ppermute | solution.py:370
  66.6 2.7 %collective-permute-start.16 = (bf16[32,1024]{1,0:T(8,128)(2,1)S(1)}, bf16[32,1024]{1,0:T(8,128)(2,1)S(1)}, u32[]{:S(2)}, u32[]{:S(2)}) collective-permute-start(bf16[32,1024]{1,0:T(8,128)(2,1)S(1)} %get-tuple-element.86), channel_id=1, source_target_pairs={{0,1},{1,0},{2,3},{3,2},{4,5},{5,4},{6,7},{7,6},{8,9},{9,8},{10,11... | collective-permute-start | bytes 196616 | tf_op jit(solution)/shard_map/ppermute | solution.py:370
  67.9 1.3 %collective-permute-start.18 = (bf16[32,512]{1,0:T(8,128)(2,1)S(1)}, bf16[32,512]{1,0:T(8,128)(2,1)S(1)}, u32[]{:S(2)}, u32[]{:S(2)}) collective-permute-start(bf16[32,512]{1,0:T(8,128)(2,1)S(1)} %get-tuple-element.89), channel_id=1, source_target_pairs={{0,1},{1,0},{2,3},{3,2},{4,5},{5,4},{6,7},{7,6},{8,9},{9,8},{10,11... | collective-permute-start | bytes 98312 | tf_op jit(solution)/shard_map/ppermute | solution.py:370
  69.1 1.3 %collective-permute-start.20 = (bf16[32,512]{1,0:T(8,128)(2,1)S(1)}, bf16[32,512]{1,0:T(8,128)(2,1)S(1)}, u32[]{:S(2)}, u32[]{:S(2)}) collective-permute-start(bf16[32,512]{1,0:T(8,128)(2,1)S(1)} %get-tuple-element.92), channel_id=1, source_target_pairs={{0,1},{1,0},{2,3},{3,2},{4,5},{5,4},{6,7},{7,6},{8,9},{9,8},{10,11... | collective-permute-start | bytes 98312 | tf_op jit(solution)/shard_map/ppermute | solution.py:370

commit v8 on v7

--- a/solution.py
+++ b/solution.py
@@ -10,6 +10,7 @@
 LANES = 128
 SCALE_ROWS = 16
 COLUMNS = 256
+TILE = 512
 HALF_SPAN = 125.0
 SPAN = 250.0
 TINY = 2.0**-110
@@ -23,7 +24,7 @@
     (2, (0, 1, 2)),
 ]
 PARTS = 16
-EARLY = 2
+EARLY = 1
 ORDER = [
     (0, 0), (1, 0), (2, 0), (0, 1), (3, 0), (4, 0), (1, 1), (2, 1),
     (0, 2), (3, 1), (4, 1), (1, 2), (2, 2), (0, 3), (3, 2), (4, 2),
@@ -203,7 +204,7 @@
         )
     for copy in copies:
         copy.start()
-    for at, wide in spans(width, COLUMNS):
+    for at, wide in spans(width, TILE):
         columns = slice(at, at + wide)
         part = jnp.dot(own_ref[...], near_ref[:, columns], preferred_element_type=jnp.float32)
         partial_ref[:, columns] = halves_added(part)
@@ -222,7 +223,7 @@
         + [jax.ShapeDtypeStruct((rows2 // 2, width), jnp.float32)],
         [],
         [pltpu.SemaphoreType.DMA((pieces - 1, depth // min(depth, COLUMNS)))],
-        limit=8,
+        limit=12,
         cost=(2 * rows2 * depth * width, 2 * pieces * depth * full, 0),
         far=1,
     )
@@ -234,7 +235,7 @@
     message_ref, kept_ref = refs[-2:]
     first = 1 if early else 0
     bounds = []
-    for at, wide in spans(width, COLUMNS):
+    for at, wide in spans(width, TILE):
         columns = slice(start + at, start + at + wide)
         total = jnp.dot(
             jnp.concatenate([a_ref[...] for a_ref in left[first:]], axis=1),
@@ -272,7 +273,7 @@
         [*left, *right] + ([partial] if early else []),
         outputs(width, step, leave, stay),
         after,
-        limit=8,
+        limit=12,
         cost=(
             2 * rows2 * depth * count * width,
             2 * depth * count * width + 4 * rows2 * width,

time: 71.9 us -> 71.6 us (level)
  starting transfers between devices: 25.2 us -> 26 us
    ppermute x21, starting transfers between devices: 25.2 us -> 26 us  [swapped(): return lax.ppermute(block, 'row', [(i, i ^ apart) for i in range(count)])]
where the time goes in v8:
time: 71.6 us; the launch traced here: 71.5 us
  Pallas kernels  31.4 us (44%)
  starting transfers between devices  26 us (36%)
  waiting for transfers between devices  13.9 us (19%)
    pallas_call x23, Pallas kernels, call(): pl.pallas_call(run, in_specs=[vmem] * (count - far) + [pl.BlockSpec(memor...  31.4 us
    ppermute x21, starting transfers between devices, swapped(): return lax.ppermute(block, 'row', [(i, i ^ apart) for i in range(count)])  26 us
    ppermute x21, waiting for transfers between devices, swapped(): return lax.ppermute(block, 'row', [(i, i ^ apart) for i in range(count)])  13.9 us
  transfers between devices with their start and end apart: 21, of which 9 were waited for; matrix products, arithmetic and copies ran while one was open for 0% of the time, Pallas kernels for 33%

profile of v8, /device:TPU:0, one launch (start us, length us, event | category | flops | bytes accessed | tf_op | source)
XLA Modules:
  0.0 71.5 jit_solution(16615157101783633031)
XLA Ops:
  0.0 4.2 %split_basis.1 = (bf16[1024,1024]{1,0:T(8,128)(2,1)S(1)}, bf16[1024,4096]{1,0:T(8,128)(2,1)S(1)}) custom-call(f32[1024,512]{1,0:T(8,128)} %refs_0_.1, bf16[1,2048,4096]{2,1,0:T(8,128)(2,1)} %refs_2_.1), custom_call_target="tpu_custom_call" | custom-call | flops 1 | bytes 1 | tf_op jit(solution)/shard_map/split_basis/pallas_call | solution.py:105
  4.2 0.5 collective-permute-start
  4.7 5.6 %early_products.1 = (bf16[1024,4096]{1,0:T(8,128)(2,1)S(1)}, f32[512,1024]{1,0:T(8,128)S(1)}) custom-call(bf16[1024,1024]{1,0:T(8,128)(2,1)S(1)} %get-tuple-element.49.refs_0_, bf16[1024,4096]{1,0:T(8,128)(2,1)S(1)} %get-tuple-element.50.refs_1_.refs_2_, bf16[1,2048,4096]{2,1,0:T(8,128)(2,1)} %refs_2_.1), custom_call_target="tpu_custom_call" | custom-call | flops 1 | bytes 1 | tf_op jit(solution)/shard_map/early_products/pallas_call | solution.py:105
  10.3 0.0 collective-permute-done.refs_1_
  10.3 2.6 %product.5 = (bf16[2064,128]{1,0:T(8,128)(2,1)S(1)}, f32[2048,128]{1,0:T(8,128)S(1)}) custom-call(bf16[1024,1024]{1,0:T(8,128)(2,1)S(1)} %get-tuple-element.49.refs_0_, bf16[1024,1024]{1,0:T(8,128)(2,1)S(1)} %collective-permute-done.refs_1_, bf16[1024,4096]{1,0:T(8,128)(2,1)S(1)} %get-tuple-element.50.refs_1_.refs_2_, ...), custom_call_target="tpu_custom_call" | custom-call | flops 1 | bytes 1 | tf_op jit(solution)/shard_map/product/pallas_call | solution.py:105
  13.0 2.6 %collective-permute-start.1 = (bf16[2064,128]{1,0:T(8,128)(2,1)S(1)}, bf16[2064,128]{1,0:T(8,128)(2,1)S(1)}, u32[]{:S(2)}, u32[]{:S(2)}) collective-permute-start(bf16[2064,128]{1,0:T(8,128)(2,1)S(1)} %get-tuple-element.53), channel_id=1, source_target_pairs={{0,2},{1,3},{2,0},{3,1},{4,6},{5,7},{6,4},{7,5},{8,10},{9,11},{10,... | collective-permute-start | bytes 1585160 | tf_op jit(solution)/shard_map/ppermute | solution.py:371
  15.6 4.8 %product.6 = (bf16[2064,128]{1,0:T(8,128)(2,1)S(1)}, f32[2048,128]{1,0:T(8,128)S(1)}) custom-call(bf16[1024,1024]{1,0:T(8,128)(2,1)S(1)} %get-tuple-element.49.refs_0_, bf16[1024,1024]{1,0:T(8,128)(2,1)S(1)} %collective-permute-done.refs_1_, bf16[1024,4096]{1,0:T(8,128)(2,1)S(1)} %get-tuple-element.50.refs_1_.refs_2_, ...), custom_call_target="tpu_custom_call" | custom-call | flops 1 | bytes 1 | tf_op jit(solution)/shard_map/product/pallas_call | solution.py:105
  20.4 1.6 %collective-permute-start.4 = (bf16[2064,128]{1,0:T(8,128)(2,1)S(1)}, bf16[2064,128]{1,0:T(8,128)(2,1)S(1)}, u32[]{:S(2)}, u32[]{:S(2)}) collective-permute-start(bf16[2064,128]{1,0:T(8,128)(2,1)S(1)} %get-tuple-element.60), channel_id=1, source_target_pairs={{0,4},{1,5},{2,6},{3,7},{4,0},{5,1},{6,2},{7,3},{8,12},{9,13},{10,... | collective-permute-start | bytes 1585160 | tf_op jit(solution)/shard_map/ppermute | solution.py:371
  22.0 4.8 %product.7 = (bf16[2064,128]{1,0:T(8,128)(2,1)S(1)}, f32[2048,128]{1,0:T(8,128)S(1)}) custom-call(bf16[1024,1024]{1,0:T(8,128)(2,1)S(1)} %get-tuple-element.49.refs_0_, bf16[1024,1024]{1,0:T(8,128)(2,1)S(1)} %collective-permute-done.refs_1_, bf16[1024,4096]{1,0:T(8,128)(2,1)S(1)} %get-tuple-element.50.refs_1_.refs_2_, ...), custom_call_target="tpu_custom_call" | custom-call | flops 1 | bytes 1 | tf_op jit(solution)/shard_map/product/pallas_call | solution.py:105
  26.8 0.6 collective-permute-start.3
  27.4 0.8 %collective-permute-done.1.refs_0_ = bf16[2064,128]{1,0:T(8,128)(2,1)S(1)} collective-permute-done((bf16[2064,128]{1,0:T(8,128)(2,1)S(1)}, bf16[2064,128]{1,0:T(8,128)(2,1)S(1)}, u32[]{:S(2)}, u32[]{:S(2)}) %collective-permute-start.1) | collective-permute-done | bytes 528416 | tf_op jit(solution)/shard_map/ppermute | solution.py:371
  28.2 0.5 add_and_split.10
  28.7 2.9 %collective-permute-start.2 = (bf16[1040,128]{1,0:T(8,128)(2,1)S(1)}, bf16[1040,128]{1,0:T(8,128)(2,1)S(1)}, u32[]{:S(2)}, u32[]{:S(2)}) collective-permute-start(bf16[1040,128]{1,0:T(8,128)(2,1)S(1)} %get-tuple-element.57), channel_id=1, source_target_pairs={{0,8},{1,9},{2,10},{3,11},{4,12},{5,13},{6,14},{7,15},{8,0},{9,1},... | collective-permute-start | bytes 798728 | tf_op jit(solution)/shard_map/ppermute | solution.py:371
  31.6 2.5 %product.8 = (bf16[1040,128]{1,0:T(8,128)(2,1)S(1)}, f32[1024,128]{1,0:T(8,128)S(1)}) custom-call(bf16[1024,1024]{1,0:T(8,128)(2,1)S(1)} %get-tuple-element.49.refs_0_, bf16[1024,1024]{1,0:T(8,128)(2,1)S(1)} %collective-permute-done.refs_1_, bf16[1024,4096]{1,0:T(8,128)(2,1)S(1)} %get-tuple-element.50.refs_1_.refs_2_, ...), custom_call_target="tpu_custom_call" | custom-call | flops 1 | bytes 1 | tf_op jit(solution)/shard_map/product/pallas_call | solution.py:105
  34.1 1.7 %collective-permute-start.9 = (bf16[1040,128]{1,0:T(8,128)(2,1)S(1)}, bf16[1040,128]{1,0:T(8,128)(2,1)S(1)}, u32[]{:S(2)}, u32[]{:S(2)}) collective-permute-start(bf16[1040,128]{1,0:T(8,128)(2,1)S(1)} %get-tuple-element.70), channel_id=1, source_target_pairs={{0,4},{1,5},{2,6},{3,7},{4,0},{5,1},{6,2},{7,3},{8,12},{9,13},{10,... | collective-permute-start | bytes 798728 | tf_op jit(solution)/shard_map/ppermute | solution.py:371
  35.8 2.7 %product.9 = (bf16[1040,128]{1,0:T(8,128)(2,1)S(1)}, f32[1024,128]{1,0:T(8,128)S(1)}) custom-call(bf16[1024,1024]{1,0:T(8,128)(2,1)S(1)} %get-tuple-element.49.refs_0_, bf16[1024,1024]{1,0:T(8,128)(2,1)S(1)} %collective-permute-done.refs_1_, bf16[1024,4096]{1,0:T(8,128)(2,1)S(1)} %get-tuple-element.50.refs_1_.refs_2_, ...), custom_call_target="tpu_custom_call" | custom-call | flops 1 | bytes 1 | tf_op jit(solution)/shard_map/product/pallas_call | solution.py:105
  38.5 1.9 %collective-permute-start.8 = (bf16[1040,128]{1,0:T(8,128)(2,1)S(1)}, bf16[1040,128]{1,0:T(8,128)(2,1)S(1)}, u32[]{:S(2)}, u32[]{:S(2)}) collective-permute-start(bf16[1040,128]{1,0:T(8,128)(2,1)S(1)} %get-tuple-element.69), channel_id=1, source_target_pairs={{0,2},{1,3},{2,0},{3,1},{4,6},{5,7},{6,4},{7,5},{8,10},{9,11},{10,... | collective-permute-start | bytes 798728 | tf_op jit(solution)/shard_map/ppermute | solution.py:371
  40.4 0.5 add_and_split.11
  40.9 0.2 collective-permute-start.7
  41.1 0.1 collective-permute-done.3.refs_0_
  41.2 0.5 add_and_split.12
  41.7 3.2 %collective-permute-start.6 = (bf16[1040,128]{1,0:T(8,128)(2,1)S(1)}, bf16[1040,128]{1,0:T(8,128)(2,1)S(1)}, u32[]{:S(2)}, u32[]{:S(2)}) collective-permute-start(bf16[1040,128]{1,0:T(8,128)(2,1)S(1)} %get-tuple-element.67), channel_id=1, source_target_pairs={{0,8},{1,9},{2,10},{3,11},{4,12},{5,13},{6,14},{7,15},{8,0},{9,1},... | collective-permute-start | bytes 798728 | tf_op jit(solution)/shard_map/ppermute | solution.py:371
  44.9 0.0 collective-permute-done.2.refs_0_
  44.9 0.3 add_and_split.13
  45.2 0.5 collective-permute-start.5
  45.7 5.3 %collective-permute-done.9.refs_0_ = bf16[1040,128]{1,0:T(8,128)(2,1)S(1)} collective-permute-done((bf16[1040,128]{1,0:T(8,128)(2,1)S(1)}, bf16[1040,128]{1,0:T(8,128)(2,1)S(1)}, u32[]{:S(2)}, u32[]{:S(2)}) %collective-permute-start.9) | collective-permute-done | bytes 266272 | tf_op jit(solution)/shard_map/ppermute | solution.py:371
  51.0 0.2 add_and_split.14
  51.2 0.1 collective-permute-start.13
  51.3 0.0 collective-permute-done.8.refs_0_
  51.3 0.2 add_and_split.15
  51.6 0.1 collective-permute-start.12
  51.7 0.5 collective-permute-done.7.refs_0_
  52.1 0.3 add_and_split.16
  52.4 3.7 %collective-permute-start.11 = (bf16[528,128]{1,0:T(8,128)(2,1)S(1)}, bf16[528,128]{1,0:T(8,128)(2,1)S(1)}, u32[]{:S(2)}, u32[]{:S(2)}) collective-permute-start(bf16[528,128]{1,0:T(8,128)(2,1)S(1)} %get-tuple-element.77), channel_id=1, source_target_pairs={{0,8},{1,9},{2,10},{3,11},{4,12},{5,13},{6,14},{7,15},{8,0},{9,1},... | collective-permute-start | bytes 405512 | tf_op jit(solution)/shard_map/ppermute | solution.py:371
  56.1 0.0 collective-permute-done.6.refs_0_
  56.1 0.3 add_and_split.17
  56.4 0.8 %collective-permute-start.15 = (bf16[528,128]{1,0:T(8,128)(2,1)S(1)}, bf16[528,128]{1,0:T(8,128)(2,1)S(1)}, u32[]{:S(2)}, u32[]{:S(2)}) collective-permute-start(bf16[528,128]{1,0:T(8,128)(2,1)S(1)} %get-tuple-element.84), channel_id=1, source_target_pairs={{0,4},{1,5},{2,6},{3,7},{4,0},{5,1},{6,2},{7,3},{8,12},{9,13},{10,... | collective-permute-start | bytes 405512 | tf_op jit(solution)/shard_map/ppermute | solution.py:371
  57.1 0.0 collective-permute-done.5.refs_0_
  57.1 0.1 add_last.5
  57.2 0.0 collective-permute-done.13.refs_0_
  57.2 0.1 add_and_split.18
  57.4 3.5 %collective-permute-start.17 = (bf16[272,128]{1,0:T(8,128)(2,1)S(1)}, bf16[272,128]{1,0:T(8,128)(2,1)S(1)}, u32[]{:S(2)}, u32[]{:S(2)}) collective-permute-start(bf16[272,128]{1,0:T(8,128)(2,1)S(1)} %get-tuple-element.87), channel_id=1, source_target_pairs={{0,8},{1,9},{2,10},{3,11},{4,12},{5,13},{6,14},{7,15},{8,0},{9,1},... | collective-permute-start | bytes 208904 | tf_op jit(solution)/shard_map/ppermute | solution.py:371
  60.9 0.9 %collective-permute-done.12.refs_0_ = bf16[528,128]{1,0:T(8,128)(2,1)S(1)} collective-permute-done((bf16[528,128]{1,0:T(8,128)(2,1)S(1)}, bf16[528,128]{1,0:T(8,128)(2,1)S(1)}, u32[]{:S(2)}, u32[]{:S(2)}) %collective-permute-start.12) | collective-permute-done | bytes 135200 | tf_op jit(solution)/shard_map/ppermute | solution.py:371
  61.8 0.1 add_and_split.19
  61.9 0.9 %collective-permute-start.19 = (bf16[272,128]{1,0:T(8,128)(2,1)S(1)}, bf16[272,128]{1,0:T(8,128)(2,1)S(1)}, u32[]{:S(2)}, u32[]{:S(2)}) collective-permute-start(bf16[272,128]{1,0:T(8,128)(2,1)S(1)} %get-tuple-element.90), channel_id=1, source_target_pairs={{0,8},{1,9},{2,10},{3,11},{4,12},{5,13},{6,14},{7,15},{8,0},{9,1},... | collective-permute-start | bytes 208904 | tf_op jit(solution)/shard_map/ppermute | solution.py:371
  62.8 0.0 collective-permute-start.10
  62.8 0.0 collective-permute-done.11.refs_0_
  62.8 0.1 add_last.6
  63.0 2.6 %collective-permute-done.15.refs_0_ = bf16[528,128]{1,0:T(8,128)(2,1)S(1)} collective-permute-done((bf16[528,128]{1,0:T(8,128)(2,1)S(1)}, bf16[528,128]{1,0:T(8,128)(2,1)S(1)}, u32[]{:S(2)}, u32[]{:S(2)}) %collective-permute-start.15) | collective-permute-done | bytes 135200 | tf_op jit(solution)/shard_map/ppermute | solution.py:371
  65.5 0.1 add_last.7
  65.6 0.1 collective-permute-start.16
  65.7 0.5 collective-permute-start.14
  66.2 0.0 collective-permute-done.17.refs_0_
  66.2 0.1 add_last.8
  66.2 2.9 %collective-permute-done.19.refs_0_ = bf16[272,128]{1,0:T(8,128)(2,1)S(1)} collective-permute-done((bf16[272,128]{1,0:T(8,128)(2,1)S(1)}, bf16[272,128]{1,0:T(8,128)(2,1)S(1)}, u32[]{:S(2)}, u32[]{:S(2)}) %collective-permute-start.19) | collective-permute-done | bytes 69664 | tf_op jit(solution)/shard_map/ppermute | solution.py:371
  69.2 0.1 add_last.9
  69.2 0.1 collective-permute-start.20
  69.3 0.5 collective-permute-start.18
  69.8 0.0 collective-permute-done.10.refs_1_
  69.8 0.0 collective-permute-done.16.refs_5_
  69.8 0.0 collective-permute-done.14.refs_3_
  69.8 0.7 collective-permute-done.20.refs_9_
  70.5 0.2 collective-permute-done.18.refs_7_
  70.7 0.8 %lay_out.1 = bf16[32,8192]{1,0:T(8,128)(2,1)} custom-call(bf16[32,1024]{1,0:T(8,128)(2,1)S(1)} %get-tuple-element.75.refs_2_.refs_0_, bf16[32,1024]{1,0:T(8,128)(2,1)S(1)} %collective-permute-done.10.refs_1_, bf16[32,1024]{1,0:T(8,128)(2,1)S(1)} %get-tuple-element.82.refs_2_, bf16[32,1024]{1,0:T(8,128)(2,1)S(1)} %collective-permute-done.14.refs_3_, ...), custom_call_target="tpu_custom_call" | custom-call | flops 1 | bytes 1 | tf_op jit(solution)/shard_map/lay_out/pallas_call | solution.py:105
  (1 shorter events, 0.0 us)
Async XLA Ops:
  4.2 6.1 %collective-permute-start = (bf16[1024,1024]{1,0:T(8,128)(2,1)S(1)}, bf16[1024,1024]{1,0:T(8,128)(2,1)S(1)}, u32[]{:S(2)}, u32[]{:S(2)}) collective-permute-start(bf16[1024,1024]{1,0:T(8,128)(2,1)S(1)} %get-tuple-element.49.refs_0_), channel_id=1, source_target_pairs={{0,1},{1,0},{2,3},{3,2},{4,5},{5,4},{6,7},{7,6},{8,9},{9,8},{10,11... | collective-permute-start | bytes 6291464 | tf_op jit(solution)/shard_map/ppermute | solution.py:371
  13.0 15.3 %collective-permute-start.1 = (bf16[2064,128]{1,0:T(8,128)(2,1)S(1)}, bf16[2064,128]{1,0:T(8,128)(2,1)S(1)}, u32[]{:S(2)}, u32[]{:S(2)}) collective-permute-start(bf16[2064,128]{1,0:T(8,128)(2,1)S(1)} %get-tuple-element.53), channel_id=1, source_target_pairs={{0,2},{1,3},{2,0},{3,1},{4,6},{5,7},{6,4},{7,5},{8,10},{9,11},{10,... | collective-permute-start | bytes 1585160 | tf_op jit(solution)/shard_map/ppermute | solution.py:371
  20.4 20.0 %collective-permute-start.4 = (bf16[2064,128]{1,0:T(8,128)(2,1)S(1)}, bf16[2064,128]{1,0:T(8,128)(2,1)S(1)}, u32[]{:S(2)}, u32[]{:S(2)}) collective-permute-start(bf16[2064,128]{1,0:T(8,128)(2,1)S(1)} %get-tuple-element.60), channel_id=1, source_target_pairs={{0,4},{1,5},{2,6},{3,7},{4,0},{5,1},{6,2},{7,3},{8,12},{9,13},{10,... | collective-permute-start | bytes 1585160 | tf_op jit(solution)/shard_map/ppermute | solution.py:371
  26.8 14.4 %collective-permute-start.3 = (bf16[2064,128]{1,0:T(8,128)(2,1)S(1)}, bf16[2064,128]{1,0:T(8,128)(2,1)S(1)}, u32[]{:S(2)}, u32[]{:S(2)}) collective-permute-start(bf16[2064,128]{1,0:T(8,128)(2,1)S(1)} %get-tuple-element.59), channel_id=1, source_target_pairs={{0,2},{1,3},{2,0},{3,1},{4,6},{5,7},{6,4},{7,5},{8,10},{9,11},{10,... | collective-permute-start | bytes 1585160 | tf_op jit(solution)/shard_map/ppermute | solution.py:371
  28.7 16.2 %collective-permute-start.2 = (bf16[1040,128]{1,0:T(8,128)(2,1)S(1)}, bf16[1040,128]{1,0:T(8,128)(2,1)S(1)}, u32[]{:S(2)}, u32[]{:S(2)}) collective-permute-start(bf16[1040,128]{1,0:T(8,128)(2,1)S(1)} %get-tuple-element.57), channel_id=1, source_target_pairs={{0,8},{1,9},{2,10},{3,11},{4,12},{5,13},{6,14},{7,15},{8,0},{9,1},... | collective-permute-start | bytes 798728 | tf_op jit(solution)/shard_map/ppermute | solution.py:371
  34.1 16.9 %collective-permute-start.9 = (bf16[1040,128]{1,0:T(8,128)(2,1)S(1)}, bf16[1040,128]{1,0:T(8,128)(2,1)S(1)}, u32[]{:S(2)}, u32[]{:S(2)}) collective-permute-start(bf16[1040,128]{1,0:T(8,128)(2,1)S(1)} %get-tuple-element.70), channel_id=1, source_target_pairs={{0,4},{1,5},{2,6},{3,7},{4,0},{5,1},{6,2},{7,3},{8,12},{9,13},{10,... | collective-permute-start | bytes 798728 | tf_op jit(solution)/shard_map/ppermute | solution.py:371
  38.5 12.9 %collective-permute-start.8 = (bf16[1040,128]{1,0:T(8,128)(2,1)S(1)}, bf16[1040,128]{1,0:T(8,128)(2,1)S(1)}, u32[]{:S(2)}, u32[]{:S(2)}) collective-permute-start(bf16[1040,128]{1,0:T(8,128)(2,1)S(1)} %get-tuple-element.69), channel_id=1, source_target_pairs={{0,2},{1,3},{2,0},{3,1},{4,6},{5,7},{6,4},{7,5},{8,10},{9,11},{10,... | collective-permute-start | bytes 798728 | tf_op jit(solution)/shard_map/ppermute | solution.py:371
  40.9 11.3 %collective-permute-start.7 = (bf16[1040,128]{1,0:T(8,128)(2,1)S(1)}, bf16[1040,128]{1,0:T(8,128)(2,1)S(1)}, u32[]{:S(2)}, u32[]{:S(2)}) collective-permute-start(bf16[1040,128]{1,0:T(8,128)(2,1)S(1)} %get-tuple-element.68), channel_id=1, source_target_pairs={{0,2},{1,3},{2,0},{3,1},{4,6},{5,7},{6,4},{7,5},{8,10},{9,11},{10,... | collective-permute-start | bytes 798728 | tf_op jit(solution)/shard_map/ppermute | solution.py:371
  41.7 14.4 %collective-permute-start.6 = (bf16[1040,128]{1,0:T(8,128)(2,1)S(1)}, bf16[1040,128]{1,0:T(8,128)(2,1)S(1)}, u32[]{:S(2)}, u32[]{:S(2)}) collective-permute-start(bf16[1040,128]{1,0:T(8,128)(2,1)S(1)} %get-tuple-element.67), channel_id=1, source_target_pairs={{0,8},{1,9},{2,10},{3,11},{4,12},{5,13},{6,14},{7,15},{8,0},{9,1},... | collective-permute-start | bytes 798728 | tf_op jit(solution)/shard_map/ppermute | solution.py:371
  45.2 12.0 %collective-permute-start.5 = (bf16[528,128]{1,0:T(8,128)(2,1)S(1)}, bf16[528,128]{1,0:T(8,128)(2,1)S(1)}, u32[]{:S(2)}, u32[]{:S(2)}) collective-permute-start(bf16[528,128]{1,0:T(8,128)(2,1)S(1)} %get-tuple-element.65), channel_id=1, source_target_pairs={{0,4},{1,5},{2,6},{3,7},{4,0},{5,1},{6,2},{7,3},{8,12},{9,13},{10,... | collective-permute-start | bytes 405512 | tf_op jit(solution)/shard_map/ppermute | solution.py:371
  51.2 6.0 %collective-permute-start.13 = (bf16[528,128]{1,0:T(8,128)(2,1)S(1)}, bf16[528,128]{1,0:T(8,128)(2,1)S(1)}, u32[]{:S(2)}, u32[]{:S(2)}) collective-permute-start(bf16[528,128]{1,0:T(8,128)(2,1)S(1)} %get-tuple-element.79), channel_id=1, source_target_pairs={{0,2},{1,3},{2,0},{3,1},{4,6},{5,7},{6,4},{7,5},{8,10},{9,11},{10,... | collective-permute-start | bytes 405512 | tf_op jit(solution)/shard_map/ppermute | solution.py:371
  51.6 10.2 %collective-permute-start.12 = (bf16[528,128]{1,0:T(8,128)(2,1)S(1)}, bf16[528,128]{1,0:T(8,128)(2,1)S(1)}, u32[]{:S(2)}, u32[]{:S(2)}) collective-permute-start(bf16[528,128]{1,0:T(8,128)(2,1)S(1)} %get-tuple-element.78), channel_id=1, source_target_pairs={{0,4},{1,5},{2,6},{3,7},{4,0},{5,1},{6,2},{7,3},{8,12},{9,13},{10,... | collective-permute-start | bytes 405512 | tf_op jit(solution)/shard_map/ppermute | solution.py:371
  52.4 10.4 %collective-permute-start.11 = (bf16[528,128]{1,0:T(8,128)(2,1)S(1)}, bf16[528,128]{1,0:T(8,128)(2,1)S(1)}, u32[]{:S(2)}, u32[]{:S(2)}) collective-permute-start(bf16[528,128]{1,0:T(8,128)(2,1)S(1)} %get-tuple-element.77), channel_id=1, source_target_pairs={{0,8},{1,9},{2,10},{3,11},{4,12},{5,13},{6,14},{7,15},{8,0},{9,1},... | collective-permute-start | bytes 405512 | tf_op jit(solution)/shard_map/ppermute | solution.py:371
  56.4 9.2 %collective-permute-start.15 = (bf16[528,128]{1,0:T(8,128)(2,1)S(1)}, bf16[528,128]{1,0:T(8,128)(2,1)S(1)}, u32[]{:S(2)}, u32[]{:S(2)}) collective-permute-start(bf16[528,128]{1,0:T(8,128)(2,1)S(1)} %get-tuple-element.84), channel_id=1, source_target_pairs={{0,4},{1,5},{2,6},{3,7},{4,0},{5,1},{6,2},{7,3},{8,12},{9,13},{10,... | collective-permute-start | bytes 405512 | tf_op jit(solution)/shard_map/ppermute | solution.py:371
  57.4 8.8 %collective-permute-start.17 = (bf16[272,128]{1,0:T(8,128)(2,1)S(1)}, bf16[272,128]{1,0:T(8,128)(2,1)S(1)}, u32[]{:S(2)}, u32[]{:S(2)}) collective-permute-start(bf16[272,128]{1,0:T(8,128)(2,1)S(1)} %get-tuple-element.87), channel_id=1, source_target_pairs={{0,8},{1,9},{2,10},{3,11},{4,12},{5,13},{6,14},{7,15},{8,0},{9,1},... | collective-permute-start | bytes 208904 | tf_op jit(solution)/shard_map/ppermute | solution.py:371
  61.9 7.2 %collective-permute-start.19 = (bf16[272,128]{1,0:T(8,128)(2,1)S(1)}, bf16[272,128]{1,0:T(8,128)(2,1)S(1)}, u32[]{:S(2)}, u32[]{:S(2)}) collective-permute-start(bf16[272,128]{1,0:T(8,128)(2,1)S(1)} %get-tuple-element.90), channel_id=1, source_target_pairs={{0,8},{1,9},{2,10},{3,11},{4,12},{5,13},{6,14},{7,15},{8,0},{9,1},... | collective-permute-start | bytes 208904 | tf_op jit(solution)/shard_map/ppermute | solution.py:371
  62.8 7.0 %collective-permute-start.10 = (bf16[32,1024]{1,0:T(8,128)(2,1)S(1)}, bf16[32,1024]{1,0:T(8,128)(2,1)S(1)}, u32[]{:S(2)}, u32[]{:S(2)}) collective-permute-start(bf16[32,1024]{1,0:T(8,128)(2,1)S(1)} %get-tuple-element.76), channel_id=1, source_target_pairs={{0,1},{1,0},{2,3},{3,2},{4,5},{5,4},{6,7},{7,6},{8,9},{9,8},{10,11... | collective-permute-start | bytes 196616 | tf_op jit(solution)/shard_map/ppermute | solution.py:371
  65.6 4.2 %collective-permute-start.16 = (bf16[32,1024]{1,0:T(8,128)(2,1)S(1)}, bf16[32,1024]{1,0:T(8,128)(2,1)S(1)}, u32[]{:S(2)}, u32[]{:S(2)}) collective-permute-start(bf16[32,1024]{1,0:T(8,128)(2,1)S(1)} %get-tuple-element.86), channel_id=1, source_target_pairs={{0,1},{1,0},{2,3},{3,2},{4,5},{5,4},{6,7},{7,6},{8,9},{9,8},{10,11... | collective-permute-start | bytes 196616 | tf_op jit(solution)/shard_map/ppermute | solution.py:371
  65.7 4.1 %collective-permute-start.14 = (bf16[32,1024]{1,0:T(8,128)(2,1)S(1)}, bf16[32,1024]{1,0:T(8,128)(2,1)S(1)}, u32[]{:S(2)}, u32[]{:S(2)}) collective-permute-start(bf16[32,1024]{1,0:T(8,128)(2,1)S(1)} %get-tuple-element.83), channel_id=1, source_target_pairs={{0,1},{1,0},{2,3},{3,2},{4,5},{5,4},{6,7},{7,6},{8,9},{9,8},{10,11... | collective-permute-start | bytes 196616 | tf_op jit(solution)/shard_map/ppermute | solution.py:371
  69.2 1.3 %collective-permute-start.20 = (bf16[32,512]{1,0:T(8,128)(2,1)S(1)}, bf16[32,512]{1,0:T(8,128)(2,1)S(1)}, u32[]{:S(2)}, u32[]{:S(2)}) collective-permute-start(bf16[32,512]{1,0:T(8,128)(2,1)S(1)} %get-tuple-element.92), channel_id=1, source_target_pairs={{0,1},{1,0},{2,3},{3,2},{4,5},{5,4},{6,7},{7,6},{8,9},{9,8},{10,11... | collective-permute-start | bytes 98312 | tf_op jit(solution)/shard_map/ppermute | solution.py:371
  69.3 1.4 %collective-permute-start.18 = (bf16[32,512]{1,0:T(8,128)(2,1)S(1)}, bf16[32,512]{1,0:T(8,128)(2,1)S(1)}, u32[]{:S(2)}, u32[]{:S(2)}) collective-permute-start(bf16[32,512]{1,0:T(8,128)(2,1)S(1)} %get-tuple-element.89), channel_id=1, source_target_pairs={{0,1},{1,0},{2,3},{3,2},{4,5},{5,4},{6,7},{7,6},{8,9},{9,8},{10,11... | collective-permute-start | bytes 98312 | tf_op jit(solution)/shard_map/ppermute | solution.py:371

commit v9 on v8

--- a/solution.py
+++ b/solution.py
@@ -24,7 +24,7 @@
     (2, (0, 1, 2)),
 ]
 PARTS = 16
-EARLY = 1
+EARLY = 2
 ORDER = [
     (0, 0), (1, 0), (2, 0), (0, 1), (3, 0), (4, 0), (1, 1), (2, 1),
     (0, 2), (3, 1), (4, 1), (1, 2), (2, 2), (0, 3), (3, 2), (4, 2),
@@ -204,10 +204,19 @@
         )
     for copy in copies:
         copy.start()
-    for at, wide in spans(width, TILE):
-        columns = slice(at, at + wide)
+
+    def multiply(columns):
         part = jnp.dot(own_ref[...], near_ref[:, columns], preferred_element_type=jnp.float32)
         partial_ref[:, columns] = halves_added(part)
+
+    tiles = width // COLUMNS
+
+    @pl.loop(0, tiles)
+    def _(tile):
+        multiply(pl.ds(pl.multiple_of(tile * COLUMNS, COLUMNS), COLUMNS))
+
+    if tiles * COLUMNS < width:
+        multiply(slice(tiles * COLUMNS, width))
     for copy in copies:
         copy.wait()
 

time: 71.6 us -> 69.9 us (0.976)
  Pallas kernels: 31.4 us -> 29.2 us
    pallas_call x23, Pallas kernels: 31.4 us -> 29.2 us  [call(): pl.pallas_call(run, in_specs=[vmem] * (count - far) + [pl.BlockSpec(memor...]
  transfers between devices with their start and end apart: 21 -> 21, of which waited for: 9 -> 8; matrix products, arithmetic and copies ran while one was open for 0% -> 0% of each run, Pallas kernels for 33% -> 31%
where the time goes in v9:
time: 69.9 us; the launch traced here: 69.2 us
  Pallas kernels  29.2 us (42%)
  starting transfers between devices  26.1 us (37%)
  waiting for transfers between devices  13.6 us (19%)
    pallas_call x23, Pallas kernels, call(): pl.pallas_call(run, in_specs=[vmem] * (count - far) + [pl.BlockSpec(memor...  29.2 us
    ppermute x21, starting transfers between devices, swapped(): return lax.ppermute(block, 'row', [(i, i ^ apart) for i in range(count)])  26.1 us
    ppermute x21, waiting for transfers between devices, swapped(): return lax.ppermute(block, 'row', [(i, i ^ apart) for i in range(count)])  13.6 us
  transfers between devices with their start and end apart: 21, of which 8 were waited for; matrix products, arithmetic and copies ran while one was open for 0% of the time, Pallas kernels for 31%

profile of v9, /device:TPU:0, one launch (start us, length us, event | category | flops | bytes accessed | tf_op | source)
XLA Modules:
  0.0 69.2 jit_solution(9637815130135069638)
XLA Ops:
  0.0 4.2 %split_basis.1 = (bf16[1024,1024]{1,0:T(8,128)(2,1)S(1)}, bf16[1024,4096]{1,0:T(8,128)(2,1)S(1)}) custom-call(f32[1024,512]{1,0:T(8,128)} %refs_0_.1, bf16[1,2048,4096]{2,1,0:T(8,128)(2,1)} %refs_2_.1), custom_call_target="tpu_custom_call" | custom-call | flops 1 | bytes 1 | tf_op jit(solution)/shard_map/split_basis/pallas_call | solution.py:105
  4.2 0.5 collective-permute-start
  4.7 5.8 %early_products.1 = (bf16[1024,4096]{1,0:T(8,128)(2,1)S(1)}, f32[512,2048]{1,0:T(8,128)S(1)}) custom-call(bf16[1024,1024]{1,0:T(8,128)(2,1)S(1)} %get-tuple-element.49.refs_0_, bf16[1024,4096]{1,0:T(8,128)(2,1)S(1)} %get-tuple-element.50.refs_1_.refs_2_, bf16[1,2048,4096]{2,1,0:T(8,128)(2,1)} %refs_2_.1), custom_call_target="tpu_custom_call" | custom-call | flops 1 | bytes 1 | tf_op jit(solution)/shard_map/early_products/pallas_call | solution.py:105
  10.5 0.0 collective-permute-done.refs_1_
  10.5 2.6 %product.5 = (bf16[2064,128]{1,0:T(8,128)(2,1)S(1)}, f32[2048,128]{1,0:T(8,128)S(1)}) custom-call(bf16[1024,1024]{1,0:T(8,128)(2,1)S(1)} %get-tuple-element.49.refs_0_, bf16[1024,1024]{1,0:T(8,128)(2,1)S(1)} %collective-permute-done.refs_1_, bf16[1024,4096]{1,0:T(8,128)(2,1)S(1)} %get-tuple-element.50.refs_1_.refs_2_, ...), custom_call_target="tpu_custom_call" | custom-call | flops 1 | bytes 1 | tf_op jit(solution)/shard_map/product/pallas_call | solution.py:105
  13.2 2.6 %collective-permute-start.1 = (bf16[2064,128]{1,0:T(8,128)(2,1)S(1)}, bf16[2064,128]{1,0:T(8,128)(2,1)S(1)}, u32[]{:S(2)}, u32[]{:S(2)}) collective-permute-start(bf16[2064,128]{1,0:T(8,128)(2,1)S(1)} %get-tuple-element.53), channel_id=1, source_target_pairs={{0,2},{1,3},{2,0},{3,1},{4,6},{5,7},{6,4},{7,5},{8,10},{9,11},{10,... | collective-permute-start | bytes 1585160 | tf_op jit(solution)/shard_map/ppermute | solution.py:380
  15.8 2.6 %product.6 = (bf16[2064,128]{1,0:T(8,128)(2,1)S(1)}, f32[2048,128]{1,0:T(8,128)S(1)}) custom-call(bf16[1024,1024]{1,0:T(8,128)(2,1)S(1)} %get-tuple-element.49.refs_0_, bf16[1024,1024]{1,0:T(8,128)(2,1)S(1)} %collective-permute-done.refs_1_, bf16[1024,4096]{1,0:T(8,128)(2,1)S(1)} %get-tuple-element.50.refs_1_.refs_2_, ...), custom_call_target="tpu_custom_call" | custom-call | flops 1 | bytes 1 | tf_op jit(solution)/shard_map/product/pallas_call | solution.py:105
  18.4 1.6 %collective-permute-start.4 = (bf16[2064,128]{1,0:T(8,128)(2,1)S(1)}, bf16[2064,128]{1,0:T(8,128)(2,1)S(1)}, u32[]{:S(2)}, u32[]{:S(2)}) collective-permute-start(bf16[2064,128]{1,0:T(8,128)(2,1)S(1)} %get-tuple-element.60), channel_id=1, source_target_pairs={{0,4},{1,5},{2,6},{3,7},{4,0},{5,1},{6,2},{7,3},{8,12},{9,13},{10,... | collective-permute-start | bytes 1585160 | tf_op jit(solution)/shard_map/ppermute | solution.py:380
  20.1 4.8 %product.7 = (bf16[2064,128]{1,0:T(8,128)(2,1)S(1)}, f32[2048,128]{1,0:T(8,128)S(1)}) custom-call(bf16[1024,1024]{1,0:T(8,128)(2,1)S(1)} %get-tuple-element.49.refs_0_, bf16[1024,1024]{1,0:T(8,128)(2,1)S(1)} %collective-permute-done.refs_1_, bf16[1024,4096]{1,0:T(8,128)(2,1)S(1)} %get-tuple-element.50.refs_1_.refs_2_, ...), custom_call_target="tpu_custom_call" | custom-call | flops 1 | bytes 1 | tf_op jit(solution)/shard_map/product/pallas_call | solution.py:105
  24.9 0.6 collective-permute-start.3
  25.5 3.2 %collective-permute-done.1.refs_0_ = bf16[2064,128]{1,0:T(8,128)(2,1)S(1)} collective-permute-done((bf16[2064,128]{1,0:T(8,128)(2,1)S(1)}, bf16[2064,128]{1,0:T(8,128)(2,1)S(1)}, u32[]{:S(2)}, u32[]{:S(2)}) %collective-permute-start.1) | collective-permute-done | bytes 528416 | tf_op jit(solution)/shard_map/ppermute | solution.py:380
  28.6 0.5 add_and_split.10
  29.1 3.1 %collective-permute-start.2 = (bf16[1040,128]{1,0:T(8,128)(2,1)S(1)}, bf16[1040,128]{1,0:T(8,128)(2,1)S(1)}, u32[]{:S(2)}, u32[]{:S(2)}) collective-permute-start(bf16[1040,128]{1,0:T(8,128)(2,1)S(1)} %get-tuple-element.57), channel_id=1, source_target_pairs={{0,8},{1,9},{2,10},{3,11},{4,12},{5,13},{6,14},{7,15},{8,0},{9,1},... | collective-permute-start | bytes 798728 | tf_op jit(solution)/shard_map/ppermute | solution.py:380
  32.2 2.5 %product.8 = (bf16[1040,128]{1,0:T(8,128)(2,1)S(1)}, f32[1024,128]{1,0:T(8,128)S(1)}) custom-call(bf16[1024,1024]{1,0:T(8,128)(2,1)S(1)} %get-tuple-element.49.refs_0_, bf16[1024,1024]{1,0:T(8,128)(2,1)S(1)} %collective-permute-done.refs_1_, bf16[1024,4096]{1,0:T(8,128)(2,1)S(1)} %get-tuple-element.50.refs_1_.refs_2_, ...), custom_call_target="tpu_custom_call" | custom-call | flops 1 | bytes 1 | tf_op jit(solution)/shard_map/product/pallas_call | solution.py:105
  34.7 1.7 %collective-permute-start.9 = (bf16[1040,128]{1,0:T(8,128)(2,1)S(1)}, bf16[1040,128]{1,0:T(8,128)(2,1)S(1)}, u32[]{:S(2)}, u32[]{:S(2)}) collective-permute-start(bf16[1040,128]{1,0:T(8,128)(2,1)S(1)} %get-tuple-element.70), channel_id=1, source_target_pairs={{0,4},{1,5},{2,6},{3,7},{4,0},{5,1},{6,2},{7,3},{8,12},{9,13},{10,... | collective-permute-start | bytes 798728 | tf_op jit(solution)/shard_map/ppermute | solution.py:380
  36.3 2.5 %product.9 = (bf16[1040,128]{1,0:T(8,128)(2,1)S(1)}, f32[1024,128]{1,0:T(8,128)S(1)}) custom-call(bf16[1024,1024]{1,0:T(8,128)(2,1)S(1)} %get-tuple-element.49.refs_0_, bf16[1024,1024]{1,0:T(8,128)(2,1)S(1)} %collective-permute-done.refs_1_, bf16[1024,4096]{1,0:T(8,128)(2,1)S(1)} %get-tuple-element.50.refs_1_.refs_2_, ...), custom_call_target="tpu_custom_call" | custom-call | flops 1 | bytes 1 | tf_op jit(solution)/shard_map/product/pallas_call | solution.py:105
  38.8 1.6 %collective-permute-start.8 = (bf16[1040,128]{1,0:T(8,128)(2,1)S(1)}, bf16[1040,128]{1,0:T(8,128)(2,1)S(1)}, u32[]{:S(2)}, u32[]{:S(2)}) collective-permute-start(bf16[1040,128]{1,0:T(8,128)(2,1)S(1)} %get-tuple-element.69), channel_id=1, source_target_pairs={{0,2},{1,3},{2,0},{3,1},{4,6},{5,7},{6,4},{7,5},{8,10},{9,11},{10,... | collective-permute-start | bytes 798728 | tf_op jit(solution)/shard_map/ppermute | solution.py:380
  40.4 0.0 collective-permute-done.4.refs_0_
  40.4 0.5 add_and_split.11
  40.9 0.6 collective-permute-start.7
  41.5 0.0 collective-permute-done.3.refs_0_
  41.5 0.5 add_and_split.12
  42.0 1.6 %collective-permute-start.6 = (bf16[1040,128]{1,0:T(8,128)(2,1)S(1)}, bf16[1040,128]{1,0:T(8,128)(2,1)S(1)}, u32[]{:S(2)}, u32[]{:S(2)}) collective-permute-start(bf16[1040,128]{1,0:T(8,128)(2,1)S(1)} %get-tuple-element.67), channel_id=1, source_target_pairs={{0,8},{1,9},{2,10},{3,11},{4,12},{5,13},{6,14},{7,15},{8,0},{9,1},... | collective-permute-start | bytes 798728 | tf_op jit(solution)/shard_map/ppermute | solution.py:380
  43.5 0.5 collective-permute-done.2.refs_0_
  44.0 0.3 add_and_split.13
  44.3 1.1 %collective-permute-start.5 = (bf16[528,128]{1,0:T(8,128)(2,1)S(1)}, bf16[528,128]{1,0:T(8,128)(2,1)S(1)}, u32[]{:S(2)}, u32[]{:S(2)}) collective-permute-start(bf16[528,128]{1,0:T(8,128)(2,1)S(1)} %get-tuple-element.65), channel_id=1, source_target_pairs={{0,4},{1,5},{2,6},{3,7},{4,0},{5,1},{6,2},{7,3},{8,12},{9,13},{10,... | collective-permute-start | bytes 405512 | tf_op jit(solution)/shard_map/ppermute | solution.py:380
  45.4 3.7 %collective-permute-done.9.refs_0_ = bf16[1040,128]{1,0:T(8,128)(2,1)S(1)} collective-permute-done((bf16[1040,128]{1,0:T(8,128)(2,1)S(1)}, bf16[1040,128]{1,0:T(8,128)(2,1)S(1)}, u32[]{:S(2)}, u32[]{:S(2)}) %collective-permute-start.9) | collective-permute-done | bytes 266272 | tf_op jit(solution)/shard_map/ppermute | solution.py:380
  49.1 0.2 add_and_split.14
  49.3 1.7 %collective-permute-start.13 = (bf16[528,128]{1,0:T(8,128)(2,1)S(1)}, bf16[528,128]{1,0:T(8,128)(2,1)S(1)}, u32[]{:S(2)}, u32[]{:S(2)}) collective-permute-start(bf16[528,128]{1,0:T(8,128)(2,1)S(1)} %get-tuple-element.79), channel_id=1, source_target_pairs={{0,2},{1,3},{2,0},{3,1},{4,6},{5,7},{6,4},{7,5},{8,10},{9,11},{10,... | collective-permute-start | bytes 405512 | tf_op jit(solution)/shard_map/ppermute | solution.py:380
  51.1 0.0 collective-permute-done.8.refs_0_
  51.1 0.2 add_and_split.15
  51.3 0.1 collective-permute-start.12
  51.4 1.7 %collective-permute-done.7.refs_0_ = bf16[1040,128]{1,0:T(8,128)(2,1)S(1)} collective-permute-done((bf16[1040,128]{1,0:T(8,128)(2,1)S(1)}, bf16[1040,128]{1,0:T(8,128)(2,1)S(1)}, u32[]{:S(2)}, u32[]{:S(2)}) %collective-permute-start.7) | collective-permute-done | bytes 266272 | tf_op jit(solution)/shard_map/ppermute | solution.py:380
  53.1 0.3 add_and_split.16
  53.3 1.4 %collective-permute-start.11 = (bf16[528,128]{1,0:T(8,128)(2,1)S(1)}, bf16[528,128]{1,0:T(8,128)(2,1)S(1)}, u32[]{:S(2)}, u32[]{:S(2)}) collective-permute-start(bf16[528,128]{1,0:T(8,128)(2,1)S(1)} %get-tuple-element.77), channel_id=1, source_target_pairs={{0,8},{1,9},{2,10},{3,11},{4,12},{5,13},{6,14},{7,15},{8,0},{9,1},... | collective-permute-start | bytes 405512 | tf_op jit(solution)/shard_map/ppermute | solution.py:380
  54.7 1.1 %collective-permute-done.6.refs_0_ = bf16[1040,128]{1,0:T(8,128)(2,1)S(1)} collective-permute-done((bf16[1040,128]{1,0:T(8,128)(2,1)S(1)}, bf16[1040,128]{1,0:T(8,128)(2,1)S(1)}, u32[]{:S(2)}, u32[]{:S(2)}) %collective-permute-start.6) | collective-permute-done | bytes 266272 | tf_op jit(solution)/shard_map/ppermute | solution.py:380
  55.8 0.3 add_and_split.17
  56.0 0.7 collective-permute-start.15
  56.7 0.0 collective-permute-done.5.refs_0_
  56.7 0.1 add_last.5
  56.8 0.0 collective-permute-done.13.refs_0_
  56.8 0.1 add_and_split.18
  56.9 3.9 %collective-permute-start.17 = (bf16[272,128]{1,0:T(8,128)(2,1)S(1)}, bf16[272,128]{1,0:T(8,128)(2,1)S(1)}, u32[]{:S(2)}, u32[]{:S(2)}) collective-permute-start(bf16[272,128]{1,0:T(8,128)(2,1)S(1)} %get-tuple-element.87), channel_id=1, source_target_pairs={{0,8},{1,9},{2,10},{3,11},{4,12},{5,13},{6,14},{7,15},{8,0},{9,1},... | collective-permute-start | bytes 208904 | tf_op jit(solution)/shard_map/ppermute | solution.py:380
  60.8 0.0 collective-permute-done.12.refs_0_
  60.8 0.1 add_and_split.19
  60.9 2.3 %collective-permute-start.19 = (bf16[272,128]{1,0:T(8,128)(2,1)S(1)}, bf16[272,128]{1,0:T(8,128)(2,1)S(1)}, u32[]{:S(2)}, u32[]{:S(2)}) collective-permute-start(bf16[272,128]{1,0:T(8,128)(2,1)S(1)} %get-tuple-element.90), channel_id=1, source_target_pairs={{0,8},{1,9},{2,10},{3,11},{4,12},{5,13},{6,14},{7,15},{8,0},{9,1},... | collective-permute-start | bytes 208904 | tf_op jit(solution)/shard_map/ppermute | solution.py:380
  63.2 0.0 collective-permute-start.10
  63.2 0.0 collective-permute-done.11.refs_0_
  63.2 0.1 add_last.6
  63.3 0.6 collective-permute-start.14
  63.9 0.7 collective-permute-done.15.refs_0_
  64.6 0.1 add_last.7
  64.7 0.1 collective-permute-start.16
  64.7 0.0 collective-permute-done.17.refs_0_
  64.7 0.1 add_last.8
  64.8 0.6 collective-permute-start.18
  65.4 1.6 %collective-permute-done.19.refs_0_ = bf16[272,128]{1,0:T(8,128)(2,1)S(1)} collective-permute-done((bf16[272,128]{1,0:T(8,128)(2,1)S(1)}, bf16[272,128]{1,0:T(8,128)(2,1)S(1)}, u32[]{:S(2)}, u32[]{:S(2)}) %collective-permute-start.19) | collective-permute-done | bytes 69664 | tf_op jit(solution)/shard_map/ppermute | solution.py:380
  67.0 0.1 add_last.9
  67.1 0.1 collective-permute-start.20
  67.1 0.0 collective-permute-done.10.refs_1_
  67.1 0.0 collective-permute-done.14.refs_3_
  67.2 0.0 collective-permute-done.16.refs_5_
  67.2 1.2 %collective-permute-done.20.refs_9_ = bf16[32,512]{1,0:T(8,128)(2,1)S(1)} collective-permute-done((bf16[32,512]{1,0:T(8,128)(2,1)S(1)}, bf16[32,512]{1,0:T(8,128)(2,1)S(1)}, u32[]{:S(2)}, u32[]{:S(2)}) %collective-permute-start.20) | collective-permute-done | bytes 32800 | tf_op jit(solution)/shard_map/ppermute | solution.py:380
  68.3 0.8 %lay_out.1 = bf16[32,8192]{1,0:T(8,128)(2,1)} custom-call(bf16[32,1024]{1,0:T(8,128)(2,1)S(1)} %get-tuple-element.75.refs_2_.refs_0_, bf16[32,1024]{1,0:T(8,128)(2,1)S(1)} %collective-permute-done.10.refs_1_, bf16[32,1024]{1,0:T(8,128)(2,1)S(1)} %get-tuple-element.82.refs_2_, bf16[32,1024]{1,0:T(8,128)(2,1)S(1)} %collective-permute-done.14.refs_3_, ...), custom_call_target="tpu_custom_call" | custom-call | flops 1 | bytes 1 | tf_op jit(solution)/shard_map/lay_out/pallas_call | solution.py:105
  (1 shorter events, 0.0 us)
Async XLA Ops:
  4.2 6.4 %collective-permute-start = (bf16[1024,1024]{1,0:T(8,128)(2,1)S(1)}, bf16[1024,1024]{1,0:T(8,128)(2,1)S(1)}, u32[]{:S(2)}, u32[]{:S(2)}) collective-permute-start(bf16[1024,1024]{1,0:T(8,128)(2,1)S(1)} %get-tuple-element.49.refs_0_), channel_id=1, source_target_pairs={{0,1},{1,0},{2,3},{3,2},{4,5},{5,4},{6,7},{7,6},{8,9},{9,8},{10,11... | collective-permute-start | bytes 6291464 | tf_op jit(solution)/shard_map/ppermute | solution.py:380
  13.2 15.5 %collective-permute-start.1 = (bf16[2064,128]{1,0:T(8,128)(2,1)S(1)}, bf16[2064,128]{1,0:T(8,128)(2,1)S(1)}, u32[]{:S(2)}, u32[]{:S(2)}) collective-permute-start(bf16[2064,128]{1,0:T(8,128)(2,1)S(1)} %get-tuple-element.53), channel_id=1, source_target_pairs={{0,2},{1,3},{2,0},{3,1},{4,6},{5,7},{6,4},{7,5},{8,10},{9,11},{10,... | collective-permute-start | bytes 1585160 | tf_op jit(solution)/shard_map/ppermute | solution.py:380
  18.4 22.0 %collective-permute-start.4 = (bf16[2064,128]{1,0:T(8,128)(2,1)S(1)}, bf16[2064,128]{1,0:T(8,128)(2,1)S(1)}, u32[]{:S(2)}, u32[]{:S(2)}) collective-permute-start(bf16[2064,128]{1,0:T(8,128)(2,1)S(1)} %get-tuple-element.60), channel_id=1, source_target_pairs={{0,4},{1,5},{2,6},{3,7},{4,0},{5,1},{6,2},{7,3},{8,12},{9,13},{10,... | collective-permute-start | bytes 1585160 | tf_op jit(solution)/shard_map/ppermute | solution.py:380
  24.9 16.6 %collective-permute-start.3 = (bf16[2064,128]{1,0:T(8,128)(2,1)S(1)}, bf16[2064,128]{1,0:T(8,128)(2,1)S(1)}, u32[]{:S(2)}, u32[]{:S(2)}) collective-permute-start(bf16[2064,128]{1,0:T(8,128)(2,1)S(1)} %get-tuple-element.59), channel_id=1, source_target_pairs={{0,2},{1,3},{2,0},{3,1},{4,6},{5,7},{6,4},{7,5},{8,10},{9,11},{10,... | collective-permute-start | bytes 1585160 | tf_op jit(solution)/shard_map/ppermute | solution.py:380
  29.1 14.9 %collective-permute-start.2 = (bf16[1040,128]{1,0:T(8,128)(2,1)S(1)}, bf16[1040,128]{1,0:T(8,128)(2,1)S(1)}, u32[]{:S(2)}, u32[]{:S(2)}) collective-permute-start(bf16[1040,128]{1,0:T(8,128)(2,1)S(1)} %get-tuple-element.57), channel_id=1, source_target_pairs={{0,8},{1,9},{2,10},{3,11},{4,12},{5,13},{6,14},{7,15},{8,0},{9,1},... | collective-permute-start | bytes 798728 | tf_op jit(solution)/shard_map/ppermute | solution.py:380
  34.7 14.4 %collective-permute-start.9 = (bf16[1040,128]{1,0:T(8,128)(2,1)S(1)}, bf16[1040,128]{1,0:T(8,128)(2,1)S(1)}, u32[]{:S(2)}, u32[]{:S(2)}) collective-permute-start(bf16[1040,128]{1,0:T(8,128)(2,1)S(1)} %get-tuple-element.70), channel_id=1, source_target_pairs={{0,4},{1,5},{2,6},{3,7},{4,0},{5,1},{6,2},{7,3},{8,12},{9,13},{10,... | collective-permute-start | bytes 798728 | tf_op jit(solution)/shard_map/ppermute | solution.py:380
  38.8 12.2 %collective-permute-start.8 = (bf16[1040,128]{1,0:T(8,128)(2,1)S(1)}, bf16[1040,128]{1,0:T(8,128)(2,1)S(1)}, u32[]{:S(2)}, u32[]{:S(2)}) collective-permute-start(bf16[1040,128]{1,0:T(8,128)(2,1)S(1)} %get-tuple-element.69), channel_id=1, source_target_pairs={{0,2},{1,3},{2,0},{3,1},{4,6},{5,7},{6,4},{7,5},{8,10},{9,11},{10,... | collective-permute-start | bytes 798728 | tf_op jit(solution)/shard_map/ppermute | solution.py:380
  40.9 12.2 %collective-permute-start.7 = (bf16[1040,128]{1,0:T(8,128)(2,1)S(1)}, bf16[1040,128]{1,0:T(8,128)(2,1)S(1)}, u32[]{:S(2)}, u32[]{:S(2)}) collective-permute-start(bf16[1040,128]{1,0:T(8,128)(2,1)S(1)} %get-tuple-element.68), channel_id=1, source_target_pairs={{0,2},{1,3},{2,0},{3,1},{4,6},{5,7},{6,4},{7,5},{8,10},{9,11},{10,... | collective-permute-start | bytes 798728 | tf_op jit(solution)/shard_map/ppermute | solution.py:380
  42.0 13.8 %collective-permute-start.6 = (bf16[1040,128]{1,0:T(8,128)(2,1)S(1)}, bf16[1040,128]{1,0:T(8,128)(2,1)S(1)}, u32[]{:S(2)}, u32[]{:S(2)}) collective-permute-start(bf16[1040,128]{1,0:T(8,128)(2,1)S(1)} %get-tuple-element.67), channel_id=1, source_target_pairs={{0,8},{1,9},{2,10},{3,11},{4,12},{5,13},{6,14},{7,15},{8,0},{9,1},... | collective-permute-start | bytes 798728 | tf_op jit(solution)/shard_map/ppermute | solution.py:380
  44.3 12.4 %collective-permute-start.5 = (bf16[528,128]{1,0:T(8,128)(2,1)S(1)}, bf16[528,128]{1,0:T(8,128)(2,1)S(1)}, u32[]{:S(2)}, u32[]{:S(2)}) collective-permute-start(bf16[528,128]{1,0:T(8,128)(2,1)S(1)} %get-tuple-element.65), channel_id=1, source_target_pairs={{0,4},{1,5},{2,6},{3,7},{4,0},{5,1},{6,2},{7,3},{8,12},{9,13},{10,... | collective-permute-start | bytes 405512 | tf_op jit(solution)/shard_map/ppermute | solution.py:380
  49.3 7.4 %collective-permute-start.13 = (bf16[528,128]{1,0:T(8,128)(2,1)S(1)}, bf16[528,128]{1,0:T(8,128)(2,1)S(1)}, u32[]{:S(2)}, u32[]{:S(2)}) collective-permute-start(bf16[528,128]{1,0:T(8,128)(2,1)S(1)} %get-tuple-element.79), channel_id=1, source_target_pairs={{0,2},{1,3},{2,0},{3,1},{4,6},{5,7},{6,4},{7,5},{8,10},{9,11},{10,... | collective-permute-start | bytes 405512 | tf_op jit(solution)/shard_map/ppermute | solution.py:380
  51.3 9.5 %collective-permute-start.12 = (bf16[528,128]{1,0:T(8,128)(2,1)S(1)}, bf16[528,128]{1,0:T(8,128)(2,1)S(1)}, u32[]{:S(2)}, u32[]{:S(2)}) collective-permute-start(bf16[528,128]{1,0:T(8,128)(2,1)S(1)} %get-tuple-element.78), channel_id=1, source_target_pairs={{0,4},{1,5},{2,6},{3,7},{4,0},{5,1},{6,2},{7,3},{8,12},{9,13},{10,... | collective-permute-start | bytes 405512 | tf_op jit(solution)/shard_map/ppermute | solution.py:380
  53.3 9.9 %collective-permute-start.11 = (bf16[528,128]{1,0:T(8,128)(2,1)S(1)}, bf16[528,128]{1,0:T(8,128)(2,1)S(1)}, u32[]{:S(2)}, u32[]{:S(2)}) collective-permute-start(bf16[528,128]{1,0:T(8,128)(2,1)S(1)} %get-tuple-element.77), channel_id=1, source_target_pairs={{0,8},{1,9},{2,10},{3,11},{4,12},{5,13},{6,14},{7,15},{8,0},{9,1},... | collective-permute-start | bytes 405512 | tf_op jit(solution)/shard_map/ppermute | solution.py:380
  56.0 8.5 %collective-permute-start.15 = (bf16[528,128]{1,0:T(8,128)(2,1)S(1)}, bf16[528,128]{1,0:T(8,128)(2,1)S(1)}, u32[]{:S(2)}, u32[]{:S(2)}) collective-permute-start(bf16[528,128]{1,0:T(8,128)(2,1)S(1)} %get-tuple-element.84), channel_id=1, source_target_pairs={{0,4},{1,5},{2,6},{3,7},{4,0},{5,1},{6,2},{7,3},{8,12},{9,13},{10,... | collective-permute-start | bytes 405512 | tf_op jit(solution)/shard_map/ppermute | solution.py:380
  56.9 7.8 %collective-permute-start.17 = (bf16[272,128]{1,0:T(8,128)(2,1)S(1)}, bf16[272,128]{1,0:T(8,128)(2,1)S(1)}, u32[]{:S(2)}, u32[]{:S(2)}) collective-permute-start(bf16[272,128]{1,0:T(8,128)(2,1)S(1)} %get-tuple-element.87), channel_id=1, source_target_pairs={{0,8},{1,9},{2,10},{3,11},{4,12},{5,13},{6,14},{7,15},{8,0},{9,1},... | collective-permute-start | bytes 208904 | tf_op jit(solution)/shard_map/ppermute | solution.py:380
  60.9 6.1 %collective-permute-start.19 = (bf16[272,128]{1,0:T(8,128)(2,1)S(1)}, bf16[272,128]{1,0:T(8,128)(2,1)S(1)}, u32[]{:S(2)}, u32[]{:S(2)}) collective-permute-start(bf16[272,128]{1,0:T(8,128)(2,1)S(1)} %get-tuple-element.90), channel_id=1, source_target_pairs={{0,8},{1,9},{2,10},{3,11},{4,12},{5,13},{6,14},{7,15},{8,0},{9,1},... | collective-permute-start | bytes 208904 | tf_op jit(solution)/shard_map/ppermute | solution.py:380
  63.2 3.9 %collective-permute-start.10 = (bf16[32,1024]{1,0:T(8,128)(2,1)S(1)}, bf16[32,1024]{1,0:T(8,128)(2,1)S(1)}, u32[]{:S(2)}, u32[]{:S(2)}) collective-permute-start(bf16[32,1024]{1,0:T(8,128)(2,1)S(1)} %get-tuple-element.76), channel_id=1, source_target_pairs={{0,1},{1,0},{2,3},{3,2},{4,5},{5,4},{6,7},{7,6},{8,9},{9,8},{10,11... | collective-permute-start | bytes 196616 | tf_op jit(solution)/shard_map/ppermute | solution.py:380
  63.3 3.8 %collective-permute-start.14 = (bf16[32,1024]{1,0:T(8,128)(2,1)S(1)}, bf16[32,1024]{1,0:T(8,128)(2,1)S(1)}, u32[]{:S(2)}, u32[]{:S(2)}) collective-permute-start(bf16[32,1024]{1,0:T(8,128)(2,1)S(1)} %get-tuple-element.83), channel_id=1, source_target_pairs={{0,1},{1,0},{2,3},{3,2},{4,5},{5,4},{6,7},{7,6},{8,9},{9,8},{10,11... | collective-permute-start | bytes 196616 | tf_op jit(solution)/shard_map/ppermute | solution.py:380
  64.7 2.5 %collective-permute-start.16 = (bf16[32,1024]{1,0:T(8,128)(2,1)S(1)}, bf16[32,1024]{1,0:T(8,128)(2,1)S(1)}, u32[]{:S(2)}, u32[]{:S(2)}) collective-permute-start(bf16[32,1024]{1,0:T(8,128)(2,1)S(1)} %get-tuple-element.86), channel_id=1, source_target_pairs={{0,1},{1,0},{2,3},{3,2},{4,5},{5,4},{6,7},{7,6},{8,9},{9,8},{10,11... | collective-permute-start | bytes 196616 | tf_op jit(solution)/shard_map/ppermute | solution.py:380
  64.8 2.4 %collective-permute-start.18 = (bf16[32,512]{1,0:T(8,128)(2,1)S(1)}, bf16[32,512]{1,0:T(8,128)(2,1)S(1)}, u32[]{:S(2)}, u32[]{:S(2)}) collective-permute-start(bf16[32,512]{1,0:T(8,128)(2,1)S(1)} %get-tuple-element.89), channel_id=1, source_target_pairs={{0,1},{1,0},{2,3},{3,2},{4,5},{5,4},{6,7},{7,6},{8,9},{9,8},{10,11... | collective-permute-start | bytes 98312 | tf_op jit(solution)/shard_map/ppermute | solution.py:380
  67.1 1.3 %collective-permute-start.20 = (bf16[32,512]{1,0:T(8,128)(2,1)S(1)}, bf16[32,512]{1,0:T(8,128)(2,1)S(1)}, u32[]{:S(2)}, u32[]{:S(2)}) collective-permute-start(bf16[32,512]{1,0:T(8,128)(2,1)S(1)} %get-tuple-element.92), channel_id=1, source_target_pairs={{0,1},{1,0},{2,3},{3,2},{4,5},{5,4},{6,7},{7,6},{8,9},{9,8},{10,11... | collective-permute-start | bytes 98312 | tf_op jit(solution)/shard_map/ppermute | solution.py:380

commit v10 on v9

--- a/solution.py
+++ b/solution.py
@@ -116,15 +116,17 @@
     )(*ins, *after)
 
 
-def row_copies(w_ref, near_ref, sems, pieces, distance, wide):
-    depth = near_ref.shape[0]
+def row_copies(w_ref, near_ref, sems, pieces, distance, wide, first=0):
+    depth, width = near_ref.shape
     owner = jnp.bitwise_xor(position(pieces)[0], distance)
     copies = []
     for index, at in enumerate(range(0, depth, wide)):
         source = pl.ds(pl.multiple_of(owner * depth + at, wide), wide)
         copies.append(
             pltpu.make_async_copy(
-                w_ref.at[0, source, :], near_ref.at[pl.ds(at, wide), :], sems.at[index]
+                w_ref.at[0, source, pl.ds(first, width)],
+                near_ref.at[pl.ds(at, wide), :],
+                sems.at[index],
             )
         )
     return copies
@@ -159,7 +161,7 @@
         copy.wait()
 
 
-def prepare(basis, weights, pieces, blocks, bits):
+def prepare(basis, weights, pieces, blocks, bits, width):
     depth, rows = basis.shape
     wide = min(depth, COLUMNS)
     sems = pltpu.SemaphoreType.DMA((depth // wide,))
@@ -169,7 +171,7 @@
         [basis, weights],
         [
             jax.ShapeDtypeStruct((2 * rows, depth), jnp.bfloat16),
-            jax.ShapeDtypeStruct((depth, weights.shape[2]), jnp.bfloat16),
+            jax.ShapeDtypeStruct((depth, width), jnp.bfloat16),
         ],
         [],
         [
@@ -194,13 +196,14 @@
 
 
 def early_kernel(pieces, width, own_ref, near_ref, w_ref, *refs):
-    *other_refs, partial_ref, sems = refs
+    *later_refs, partial_ref, sems = refs
     depth = own_ref.shape[1]
     wide = min(depth, COLUMNS)
     copies = []
-    for distance in range(1, pieces):
+    for distance in [*range(1, pieces), 0]:
+        first = 0 if distance else width
         copies += row_copies(
-            w_ref, other_refs[distance - 1], sems.at[distance - 1], pieces, distance, wide
+            w_ref, later_refs[distance], sems.at[distance], pieces, distance, wide, first
         )
     for copy in copies:
         copy.start()
@@ -228,27 +231,32 @@
         functools.partial(early_kernel, pieces, width),
         "early_products",
         [own, near, weights],
-        [jax.ShapeDtypeStruct((depth, full), jnp.bfloat16)] * (pieces - 1)
+        [jax.ShapeDtypeStruct((depth, full - width), jnp.bfloat16)]
+        + [jax.ShapeDtypeStruct((depth, full), jnp.bfloat16)] * (pieces - 1)
         + [jax.ShapeDtypeStruct((rows2 // 2, width), jnp.float32)],
         [],
-        [pltpu.SemaphoreType.DMA((pieces - 1, depth // min(depth, COLUMNS)))],
+        [pltpu.SemaphoreType.DMA((pieces, depth // min(depth, COLUMNS)))],
         limit=12,
         cost=(2 * rows2 * depth * width, 2 * pieces * depth * full, 0),
         far=1,
     )
-    return [near, *out[:-1]], out[-1]
-
-
-def product_kernel(pieces, start, width, early, step, leave, stay, *refs):
+    return out[:-1], out[-1]
+
+
+def product_kernel(pieces, start, width, skip, early, step, leave, stay, *refs):
     left, right = refs[:pieces], refs[pieces : 2 * pieces]
     message_ref, kept_ref = refs[-2:]
     first = 1 if early else 0
     bounds = []
     for at, wide in spans(width, TILE):
         columns = slice(start + at, start + at + wide)
+        own_columns = slice(columns.start - skip, columns.stop - skip)
+        taken = [w_ref[:, columns] for w_ref in right[1:]]
+        if not early:
+            taken = [right[0][:, own_columns]] + taken
         total = jnp.dot(
             jnp.concatenate([a_ref[...] for a_ref in left[first:]], axis=1),
-            jnp.concatenate([w_ref[:, columns] for w_ref in right[first:]], axis=0),
+            jnp.concatenate(taken, axis=0),
             preferred_element_type=jnp.float32,
         )
         total = halves_added(total)
@@ -275,9 +283,10 @@
     rows2, depth = left[0].shape
     pieces = len(left)
     early = partial is not None
+    skip = right[1].shape[1] - right[0].shape[1]
     count = pieces - 1 if early else pieces
     return call(
-        functools.partial(product_kernel, pieces, start, width, early, step, leave, stay),
+        functools.partial(product_kernel, pieces, start, width, skip, early, step, leave, stay),
         "product",
         [*left, *right] + ([partial] if early else []),
         outputs(width, step, leave, stay),
@@ -389,16 +398,16 @@
     step = rows // blocks
     width = weights.shape[2]
 
-    own, near = prepare(basis, weights, pieces, blocks, bits)
-    left = [own] + [swapped(own, distance) for distance in range(1, pieces)]
-
     cuts = [0]
     for share, _ in CHUNKS:
         cuts.append(cuts[-1] + share)
     cuts = [cut * (width // LANES) // PARTS * LANES for cut in cuts]
+    ahead = cuts[EARLY]
     orders = [[bit for bit in order if bit < bits] for _, order in CHUNKS]
     stages = [split_places(order, bits) for order in orders]
-    right, partial = early(own, near, weights, pieces, cuts[EARLY])
+    own, near = prepare(basis, weights, pieces, blocks, bits, ahead)
+    left = [own] + [swapped(own, distance) for distance in range(1, pieces)]
+    right, partial = early(own, near, weights, pieces, ahead)
 
     state = {}
     after = [partial]

time: 69.9 us -> 69 us (0.987)
  waiting for transfers between devices: 13.6 us -> 16.3 us
  starting transfers between devices: 26.1 us -> 24.3 us
  Pallas kernels: 29.2 us -> 28.1 us
    ppermute x21, waiting for transfers between devices: 13.6 us -> 16.3 us  [swapped(): return lax.ppermute(block, 'row', [(i, i ^ apart) for i in range(count)])]
    ppermute x21, starting transfers between devices: 26.1 us -> 24.3 us  [swapped(): return lax.ppermute(block, 'row', [(i, i ^ apart) for i in range(count)])]
    pallas_call x23, Pallas kernels: 29.2 us -> 28.1 us  [call(): pl.pallas_call(run, in_specs=[vmem] * (count - far) + [pl.BlockSpec(memor...]
  transfers between devices with their start and end apart: 21 -> 21, of which waited for: 8 -> 10; matrix products, arithmetic and copies ran while one was open for 0% -> 0% of each run, Pallas kernels for 31% -> 32%
where the time goes in v10:
time: 69 us; the launch traced here: 68.9 us
  Pallas kernels  28.1 us (41%)
  starting transfers between devices  24.3 us (35%)
  waiting for transfers between devices  16.3 us (24%)
    pallas_call x23, Pallas kernels, call(): pl.pallas_call(run, in_specs=[vmem] * (count - far) + [pl.BlockSpec(memor...  28.1 us
    ppermute x21, starting transfers between devices, swapped(): return lax.ppermute(block, 'row', [(i, i ^ apart) for i in range(count)])  24.3 us
    ppermute x21, waiting for transfers between devices, swapped(): return lax.ppermute(block, 'row', [(i, i ^ apart) for i in range(count)])  16.3 us
  transfers between devices with their start and end apart: 21, of which 10 were waited for; matrix products, arithmetic and copies ran while one was open for 0% of the time, Pallas kernels for 32%

profile of v10, /device:TPU:0, one launch (start us, length us, event | category | flops | bytes accessed | tf_op | source)
XLA Modules:
  0.0 68.9 jit_solution(1579884784563919668)
XLA Ops:
  0.0 2.9 %split_basis.1 = (bf16[1024,1024]{1,0:T(8,128)(2,1)S(1)}, bf16[1024,2048]{1,0:T(8,128)(2,1)S(1)}) custom-call(f32[1024,512]{1,0:T(8,128)} %refs_0_.1, bf16[1,2048,4096]{2,1,0:T(8,128)(2,1)} %refs_2_.1), custom_call_target="tpu_custom_call" | custom-call | flops 1 | bytes 1 | tf_op jit(solution)/shard_map/split_basis/pallas_call | solution.py:105
  2.9 0.5 collective-permute-start
  3.4 5.9 %early_products.1 = (bf16[1024,2048]{1,0:T(8,128)(2,1)S(1)}, bf16[1024,4096]{1,0:T(8,128)(2,1)S(1)}, f32[512,2048]{1,0:T(8,128)S(1)}) custom-call(bf16[1024,1024]{1,0:T(8,128)(2,1)S(1)} %get-tuple-element.50.refs_0_, bf16[1024,2048]{1,0:T(8,128)(2,1)S(1)} %get-tuple-element.51.refs_1_, bf16[1,2048,4096]{2,1,0:T(8,128)(2,1)} %refs_2_.1), custom_call_target="tpu_custom_call" | custom-call | flops 1 | bytes 1 | tf_op jit(solution)/shard_map/early_products/pallas_call | solution.py:105
  9.3 0.0 collective-permute-done.refs_1_
  9.3 2.7 %product.5 = (bf16[2064,128]{1,0:T(8,128)(2,1)S(1)}, f32[2048,128]{1,0:T(8,128)S(1)}) custom-call(bf16[1024,1024]{1,0:T(8,128)(2,1)S(1)} %get-tuple-element.50.refs_0_, bf16[1024,1024]{1,0:T(8,128)(2,1)S(1)} %collective-permute-done.refs_1_, bf16[1024,2048]{1,0:T(8,128)(2,1)S(1)} %get-tuple-element.52.refs_2_, ...), custom_call_target="tpu_custom_call" | custom-call | flops 1 | bytes 1 | tf_op jit(solution)/shard_map/product/pallas_call | solution.py:105
  11.9 2.6 %collective-permute-start.1 = (bf16[2064,128]{1,0:T(8,128)(2,1)S(1)}, bf16[2064,128]{1,0:T(8,128)(2,1)S(1)}, u32[]{:S(2)}, u32[]{:S(2)}) collective-permute-start(bf16[2064,128]{1,0:T(8,128)(2,1)S(1)} %get-tuple-element.55), channel_id=1, source_target_pairs={{0,2},{1,3},{2,0},{3,1},{4,6},{5,7},{6,4},{7,5},{8,10},{9,11},{10,... | collective-permute-start | bytes 1585160 | tf_op jit(solution)/shard_map/ppermute | solution.py:389
  14.6 2.7 %product.6 = (bf16[2064,128]{1,0:T(8,128)(2,1)S(1)}, f32[2048,128]{1,0:T(8,128)S(1)}) custom-call(bf16[1024,1024]{1,0:T(8,128)(2,1)S(1)} %get-tuple-element.50.refs_0_, bf16[1024,1024]{1,0:T(8,128)(2,1)S(1)} %collective-permute-done.refs_1_, bf16[1024,2048]{1,0:T(8,128)(2,1)S(1)} %get-tuple-element.52.refs_2_, ...), custom_call_target="tpu_custom_call" | custom-call | flops 1 | bytes 1 | tf_op jit(solution)/shard_map/product/pallas_call | solution.py:105
  17.2 1.6 %collective-permute-start.4 = (bf16[2064,128]{1,0:T(8,128)(2,1)S(1)}, bf16[2064,128]{1,0:T(8,128)(2,1)S(1)}, u32[]{:S(2)}, u32[]{:S(2)}) collective-permute-start(bf16[2064,128]{1,0:T(8,128)(2,1)S(1)} %get-tuple-element.62), channel_id=1, source_target_pairs={{0,4},{1,5},{2,6},{3,7},{4,0},{5,1},{6,2},{7,3},{8,12},{9,13},{10,... | collective-permute-start | bytes 1585160 | tf_op jit(solution)/shard_map/ppermute | solution.py:389
  18.9 4.8 %product.7 = (bf16[2064,128]{1,0:T(8,128)(2,1)S(1)}, f32[2048,128]{1,0:T(8,128)S(1)}) custom-call(bf16[1024,1024]{1,0:T(8,128)(2,1)S(1)} %get-tuple-element.50.refs_0_, bf16[1024,1024]{1,0:T(8,128)(2,1)S(1)} %collective-permute-done.refs_1_, bf16[1024,2048]{1,0:T(8,128)(2,1)S(1)} %get-tuple-element.52.refs_2_, ...), custom_call_target="tpu_custom_call" | custom-call | flops 1 | bytes 1 | tf_op jit(solution)/shard_map/product/pallas_call | solution.py:105
  23.7 0.6 collective-permute-start.3
  24.3 3.1 %collective-permute-done.1.refs_0_ = bf16[2064,128]{1,0:T(8,128)(2,1)S(1)} collective-permute-done((bf16[2064,128]{1,0:T(8,128)(2,1)S(1)}, bf16[2064,128]{1,0:T(8,128)(2,1)S(1)}, u32[]{:S(2)}, u32[]{:S(2)}) %collective-permute-start.1) | collective-permute-done | bytes 528416 | tf_op jit(solution)/shard_map/ppermute | solution.py:389
  27.4 0.5 add_and_split.10
  27.9 3.1 %collective-permute-start.2 = (bf16[1040,128]{1,0:T(8,128)(2,1)S(1)}, bf16[1040,128]{1,0:T(8,128)(2,1)S(1)}, u32[]{:S(2)}, u32[]{:S(2)}) collective-permute-start(bf16[1040,128]{1,0:T(8,128)(2,1)S(1)} %get-tuple-element.59), channel_id=1, source_target_pairs={{0,8},{1,9},{2,10},{3,11},{4,12},{5,13},{6,14},{7,15},{8,0},{9,1},... | collective-permute-start | bytes 798728 | tf_op jit(solution)/shard_map/ppermute | solution.py:389
  31.0 2.5 %product.8 = (bf16[1040,128]{1,0:T(8,128)(2,1)S(1)}, f32[1024,128]{1,0:T(8,128)S(1)}) custom-call(bf16[1024,1024]{1,0:T(8,128)(2,1)S(1)} %get-tuple-element.50.refs_0_, bf16[1024,1024]{1,0:T(8,128)(2,1)S(1)} %collective-permute-done.refs_1_, bf16[1024,2048]{1,0:T(8,128)(2,1)S(1)} %get-tuple-element.52.refs_2_, ...), custom_call_target="tpu_custom_call" | custom-call | flops 1 | bytes 1 | tf_op jit(solution)/shard_map/product/pallas_call | solution.py:105
  33.5 1.6 %collective-permute-start.9 = (bf16[1040,128]{1,0:T(8,128)(2,1)S(1)}, bf16[1040,128]{1,0:T(8,128)(2,1)S(1)}, u32[]{:S(2)}, u32[]{:S(2)}) collective-permute-start(bf16[1040,128]{1,0:T(8,128)(2,1)S(1)} %get-tuple-element.72), channel_id=1, source_target_pairs={{0,4},{1,5},{2,6},{3,7},{4,0},{5,1},{6,2},{7,3},{8,12},{9,13},{10,... | collective-permute-start | bytes 798728 | tf_op jit(solution)/shard_map/ppermute | solution.py:389
  35.1 2.5 %product.9 = (bf16[1040,128]{1,0:T(8,128)(2,1)S(1)}, f32[1024,128]{1,0:T(8,128)S(1)}) custom-call(bf16[1024,1024]{1,0:T(8,128)(2,1)S(1)} %get-tuple-element.50.refs_0_, bf16[1024,1024]{1,0:T(8,128)(2,1)S(1)} %collective-permute-done.refs_1_, bf16[1024,2048]{1,0:T(8,128)(2,1)S(1)} %get-tuple-element.52.refs_2_, ...), custom_call_target="tpu_custom_call" | custom-call | flops 1 | bytes 1 | tf_op jit(solution)/shard_map/product/pallas_call | solution.py:105
  37.6 1.6 %collective-permute-start.8 = (bf16[1040,128]{1,0:T(8,128)(2,1)S(1)}, bf16[1040,128]{1,0:T(8,128)(2,1)S(1)}, u32[]{:S(2)}, u32[]{:S(2)}) collective-permute-start(bf16[1040,128]{1,0:T(8,128)(2,1)S(1)} %get-tuple-element.71), channel_id=1, source_target_pairs={{0,2},{1,3},{2,0},{3,1},{4,6},{5,7},{6,4},{7,5},{8,10},{9,11},{10,... | collective-permute-start | bytes 798728 | tf_op jit(solution)/shard_map/ppermute | solution.py:389
  39.2 0.0 collective-permute-done.4.refs_0_
  39.2 0.5 add_and_split.11
  39.7 0.6 collective-permute-start.7
  40.3 0.0 collective-permute-done.3.refs_0_
  40.3 0.5 add_and_split.12
  40.8 1.6 %collective-permute-start.6 = (bf16[1040,128]{1,0:T(8,128)(2,1)S(1)}, bf16[1040,128]{1,0:T(8,128)(2,1)S(1)}, u32[]{:S(2)}, u32[]{:S(2)}) collective-permute-start(bf16[1040,128]{1,0:T(8,128)(2,1)S(1)} %get-tuple-element.69), channel_id=1, source_target_pairs={{0,8},{1,9},{2,10},{3,11},{4,12},{5,13},{6,14},{7,15},{8,0},{9,1},... | collective-permute-start | bytes 798728 | tf_op jit(solution)/shard_map/ppermute | solution.py:389
  42.3 0.5 collective-permute-done.2.refs_0_
  42.8 0.3 add_and_split.13
  43.1 1.1 %collective-permute-start.5 = (bf16[528,128]{1,0:T(8,128)(2,1)S(1)}, bf16[528,128]{1,0:T(8,128)(2,1)S(1)}, u32[]{:S(2)}, u32[]{:S(2)}) collective-permute-start(bf16[528,128]{1,0:T(8,128)(2,1)S(1)} %get-tuple-element.67), channel_id=1, source_target_pairs={{0,4},{1,5},{2,6},{3,7},{4,0},{5,1},{6,2},{7,3},{8,12},{9,13},{10,... | collective-permute-start | bytes 405512 | tf_op jit(solution)/shard_map/ppermute | solution.py:389
  44.2 3.6 %collective-permute-done.9.refs_0_ = bf16[1040,128]{1,0:T(8,128)(2,1)S(1)} collective-permute-done((bf16[1040,128]{1,0:T(8,128)(2,1)S(1)}, bf16[1040,128]{1,0:T(8,128)(2,1)S(1)}, u32[]{:S(2)}, u32[]{:S(2)}) %collective-permute-start.9) | collective-permute-done | bytes 266272 | tf_op jit(solution)/shard_map/ppermute | solution.py:389
  47.8 0.2 add_and_split.14
  48.1 1.7 %collective-permute-start.13 = (bf16[528,128]{1,0:T(8,128)(2,1)S(1)}, bf16[528,128]{1,0:T(8,128)(2,1)S(1)}, u32[]{:S(2)}, u32[]{:S(2)}) collective-permute-start(bf16[528,128]{1,0:T(8,128)(2,1)S(1)} %get-tuple-element.81), channel_id=1, source_target_pairs={{0,2},{1,3},{2,0},{3,1},{4,6},{5,7},{6,4},{7,5},{8,10},{9,11},{10,... | collective-permute-start | bytes 405512 | tf_op jit(solution)/shard_map/ppermute | solution.py:389
  49.8 0.0 collective-permute-done.8.refs_0_
  49.8 0.2 add_and_split.15
  50.1 0.1 collective-permute-start.12
  50.2 1.7 %collective-permute-done.7.refs_0_ = bf16[1040,128]{1,0:T(8,128)(2,1)S(1)} collective-permute-done((bf16[1040,128]{1,0:T(8,128)(2,1)S(1)}, bf16[1040,128]{1,0:T(8,128)(2,1)S(1)}, u32[]{:S(2)}, u32[]{:S(2)}) %collective-permute-start.7) | collective-permute-done | bytes 266272 | tf_op jit(solution)/shard_map/ppermute | solution.py:389
  51.8 0.3 add_and_split.16
  52.1 1.4 %collective-permute-start.11 = (bf16[528,128]{1,0:T(8,128)(2,1)S(1)}, bf16[528,128]{1,0:T(8,128)(2,1)S(1)}, u32[]{:S(2)}, u32[]{:S(2)}) collective-permute-start(bf16[528,128]{1,0:T(8,128)(2,1)S(1)} %get-tuple-element.79), channel_id=1, source_target_pairs={{0,8},{1,9},{2,10},{3,11},{4,12},{5,13},{6,14},{7,15},{8,0},{9,1},... | collective-permute-start | bytes 405512 | tf_op jit(solution)/shard_map/ppermute | solution.py:389
  53.5 1.1 %collective-permute-done.6.refs_0_ = bf16[1040,128]{1,0:T(8,128)(2,1)S(1)} collective-permute-done((bf16[1040,128]{1,0:T(8,128)(2,1)S(1)}, bf16[1040,128]{1,0:T(8,128)(2,1)S(1)}, u32[]{:S(2)}, u32[]{:S(2)}) %collective-permute-start.6) | collective-permute-done | bytes 266272 | tf_op jit(solution)/shard_map/ppermute | solution.py:389
  54.6 0.3 add_and_split.17
  54.8 0.6 collective-permute-start.15
  55.5 0.0 collective-permute-done.5.refs_0_
  55.5 0.1 add_last.5
  55.6 0.0 collective-permute-done.13.refs_0_
  55.6 0.1 add_and_split.18
  55.7 3.9 %collective-permute-start.17 = (bf16[272,128]{1,0:T(8,128)(2,1)S(1)}, bf16[272,128]{1,0:T(8,128)(2,1)S(1)}, u32[]{:S(2)}, u32[]{:S(2)}) collective-permute-start(bf16[272,128]{1,0:T(8,128)(2,1)S(1)} %get-tuple-element.89), channel_id=1, source_target_pairs={{0,8},{1,9},{2,10},{3,11},{4,12},{5,13},{6,14},{7,15},{8,0},{9,1},... | collective-permute-start | bytes 208904 | tf_op jit(solution)/shard_map/ppermute | solution.py:389
  59.6 0.0 collective-permute-done.12.refs_0_
  59.6 0.1 add_and_split.19
  59.7 0.4 collective-permute-start.19
  60.2 1.2 %collective-permute-done.11.refs_0_ = bf16[528,128]{1,0:T(8,128)(2,1)S(1)} collective-permute-done((bf16[528,128]{1,0:T(8,128)(2,1)S(1)}, bf16[528,128]{1,0:T(8,128)(2,1)S(1)}, u32[]{:S(2)}, u32[]{:S(2)}) %collective-permute-start.11) | collective-permute-done | bytes 135200 | tf_op jit(solution)/shard_map/ppermute | solution.py:389
  61.4 0.1 add_last.6
  61.5 1.8 %collective-permute-done.15.refs_0_ = bf16[528,128]{1,0:T(8,128)(2,1)S(1)} collective-permute-done((bf16[528,128]{1,0:T(8,128)(2,1)S(1)}, bf16[528,128]{1,0:T(8,128)(2,1)S(1)}, u32[]{:S(2)}, u32[]{:S(2)}) %collective-permute-start.15) | collective-permute-done | bytes 135200 | tf_op jit(solution)/shard_map/ppermute | solution.py:389
  63.3 0.1 add_last.7
  63.4 0.1 collective-permute-start.16
  63.5 0.5 collective-permute-start.14
  64.0 0.1 collective-permute-start.10
  64.1 0.0 collective-permute-done.17.refs_0_
  64.1 0.1 add_last.8
  64.1 2.4 %collective-permute-done.19.refs_0_ = bf16[272,128]{1,0:T(8,128)(2,1)S(1)} collective-permute-done((bf16[272,128]{1,0:T(8,128)(2,1)S(1)}, bf16[272,128]{1,0:T(8,128)(2,1)S(1)}, u32[]{:S(2)}, u32[]{:S(2)}) %collective-permute-start.19) | collective-permute-done | bytes 69664 | tf_op jit(solution)/shard_map/ppermute | solution.py:389
  66.5 0.1 add_last.9
  66.6 0.1 collective-permute-start.20
  66.7 0.5 collective-permute-start.18
  67.2 0.0 collective-permute-done.16.refs_5_
  67.2 0.0 collective-permute-done.14.refs_3_
  67.2 0.7 collective-permute-done.20.refs_9_
  67.9 0.2 collective-permute-done.18.refs_7_
  68.0 0.8 %lay_out.1 = bf16[32,8192]{1,0:T(8,128)(2,1)} custom-call(bf16[32,1024]{1,0:T(8,128)(2,1)S(1)} %get-tuple-element.77.refs_2_.refs_0_, bf16[32,1024]{1,0:T(8,128)(2,1)S(1)} %collective-permute-done.10.refs_1_, bf16[32,1024]{1,0:T(8,128)(2,1)S(1)} %get-tuple-element.84.refs_2_, bf16[32,1024]{1,0:T(8,128)(2,1)S(1)} %collective-permute-done.14.refs_3_, ...), custom_call_target="tpu_custom_call" | custom-call | flops 1 | bytes 1 | tf_op jit(solution)/shard_map/lay_out/pallas_call | solution.py:105
  (1 shorter events, 0.0 us)
Async XLA Ops:
  2.9 6.4 %collective-permute-start = (bf16[1024,1024]{1,0:T(8,128)(2,1)S(1)}, bf16[1024,1024]{1,0:T(8,128)(2,1)S(1)}, u32[]{:S(2)}, u32[]{:S(2)}) collective-permute-start(bf16[1024,1024]{1,0:T(8,128)(2,1)S(1)} %get-tuple-element.50.refs_0_), channel_id=1, source_target_pairs={{0,1},{1,0},{2,3},{3,2},{4,5},{5,4},{6,7},{7,6},{8,9},{9,8},{10,11... | collective-permute-start | bytes 6291464 | tf_op jit(solution)/shard_map/ppermute | solution.py:389
  11.9 15.5 %collective-permute-start.1 = (bf16[2064,128]{1,0:T(8,128)(2,1)S(1)}, bf16[2064,128]{1,0:T(8,128)(2,1)S(1)}, u32[]{:S(2)}, u32[]{:S(2)}) collective-permute-start(bf16[2064,128]{1,0:T(8,128)(2,1)S(1)} %get-tuple-element.55), channel_id=1, source_target_pairs={{0,2},{1,3},{2,0},{3,1},{4,6},{5,7},{6,4},{7,5},{8,10},{9,11},{10,... | collective-permute-start | bytes 1585160 | tf_op jit(solution)/shard_map/ppermute | solution.py:389
  17.2 22.0 %collective-permute-start.4 = (bf16[2064,128]{1,0:T(8,128)(2,1)S(1)}, bf16[2064,128]{1,0:T(8,128)(2,1)S(1)}, u32[]{:S(2)}, u32[]{:S(2)}) collective-permute-start(bf16[2064,128]{1,0:T(8,128)(2,1)S(1)} %get-tuple-element.62), channel_id=1, source_target_pairs={{0,4},{1,5},{2,6},{3,7},{4,0},{5,1},{6,2},{7,3},{8,12},{9,13},{10,... | collective-permute-start | bytes 1585160 | tf_op jit(solution)/shard_map/ppermute | solution.py:389
  23.7 16.6 %collective-permute-start.3 = (bf16[2064,128]{1,0:T(8,128)(2,1)S(1)}, bf16[2064,128]{1,0:T(8,128)(2,1)S(1)}, u32[]{:S(2)}, u32[]{:S(2)}) collective-permute-start(bf16[2064,128]{1,0:T(8,128)(2,1)S(1)} %get-tuple-element.61), channel_id=1, source_target_pairs={{0,2},{1,3},{2,0},{3,1},{4,6},{5,7},{6,4},{7,5},{8,10},{9,11},{10,... | collective-permute-start | bytes 1585160 | tf_op jit(solution)/shard_map/ppermute | solution.py:389
  27.9 14.9 %collective-permute-start.2 = (bf16[1040,128]{1,0:T(8,128)(2,1)S(1)}, bf16[1040,128]{1,0:T(8,128)(2,1)S(1)}, u32[]{:S(2)}, u32[]{:S(2)}) collective-permute-start(bf16[1040,128]{1,0:T(8,128)(2,1)S(1)} %get-tuple-element.59), channel_id=1, source_target_pairs={{0,8},{1,9},{2,10},{3,11},{4,12},{5,13},{6,14},{7,15},{8,0},{9,1},... | collective-permute-start | bytes 798728 | tf_op jit(solution)/shard_map/ppermute | solution.py:389
  33.5 14.3 %collective-permute-start.9 = (bf16[1040,128]{1,0:T(8,128)(2,1)S(1)}, bf16[1040,128]{1,0:T(8,128)(2,1)S(1)}, u32[]{:S(2)}, u32[]{:S(2)}) collective-permute-start(bf16[1040,128]{1,0:T(8,128)(2,1)S(1)} %get-tuple-element.72), channel_id=1, source_target_pairs={{0,4},{1,5},{2,6},{3,7},{4,0},{5,1},{6,2},{7,3},{8,12},{9,13},{10,... | collective-permute-start | bytes 798728 | tf_op jit(solution)/shard_map/ppermute | solution.py:389
  37.6 12.2 %collective-permute-start.8 = (bf16[1040,128]{1,0:T(8,128)(2,1)S(1)}, bf16[1040,128]{1,0:T(8,128)(2,1)S(1)}, u32[]{:S(2)}, u32[]{:S(2)}) collective-permute-start(bf16[1040,128]{1,0:T(8,128)(2,1)S(1)} %get-tuple-element.71), channel_id=1, source_target_pairs={{0,2},{1,3},{2,0},{3,1},{4,6},{5,7},{6,4},{7,5},{8,10},{9,11},{10,... | collective-permute-start | bytes 798728 | tf_op jit(solution)/shard_map/ppermute | solution.py:389
  39.7 12.1 %collective-permute-start.7 = (bf16[1040,128]{1,0:T(8,128)(2,1)S(1)}, bf16[1040,128]{1,0:T(8,128)(2,1)S(1)}, u32[]{:S(2)}, u32[]{:S(2)}) collective-permute-start(bf16[1040,128]{1,0:T(8,128)(2,1)S(1)} %get-tuple-element.70), channel_id=1, source_target_pairs={{0,2},{1,3},{2,0},{3,1},{4,6},{5,7},{6,4},{7,5},{8,10},{9,11},{10,... | collective-permute-start | bytes 798728 | tf_op jit(solution)/shard_map/ppermute | solution.py:389
  40.8 13.8 %collective-permute-start.6 = (bf16[1040,128]{1,0:T(8,128)(2,1)S(1)}, bf16[1040,128]{1,0:T(8,128)(2,1)S(1)}, u32[]{:S(2)}, u32[]{:S(2)}) collective-permute-start(bf16[1040,128]{1,0:T(8,128)(2,1)S(1)} %get-tuple-element.69), channel_id=1, source_target_pairs={{0,8},{1,9},{2,10},{3,11},{4,12},{5,13},{6,14},{7,15},{8,0},{9,1},... | collective-permute-start | bytes 798728 | tf_op jit(solution)/shard_map/ppermute | solution.py:389
  43.1 12.4 %collective-permute-start.5 = (bf16[528,128]{1,0:T(8,128)(2,1)S(1)}, bf16[528,128]{1,0:T(8,128)(2,1)S(1)}, u32[]{:S(2)}, u32[]{:S(2)}) collective-permute-start(bf16[528,128]{1,0:T(8,128)(2,1)S(1)} %get-tuple-element.67), channel_id=1, source_target_pairs={{0,4},{1,5},{2,6},{3,7},{4,0},{5,1},{6,2},{7,3},{8,12},{9,13},{10,... | collective-permute-start | bytes 405512 | tf_op jit(solution)/shard_map/ppermute | solution.py:389
  48.1 7.5 %collective-permute-start.13 = (bf16[528,128]{1,0:T(8,128)(2,1)S(1)}, bf16[528,128]{1,0:T(8,128)(2,1)S(1)}, u32[]{:S(2)}, u32[]{:S(2)}) collective-permute-start(bf16[528,128]{1,0:T(8,128)(2,1)S(1)} %get-tuple-element.81), channel_id=1, source_target_pairs={{0,2},{1,3},{2,0},{3,1},{4,6},{5,7},{6,4},{7,5},{8,10},{9,11},{10,... | collective-permute-start | bytes 405512 | tf_op jit(solution)/shard_map/ppermute | solution.py:389
  50.1 9.5 %collective-permute-start.12 = (bf16[528,128]{1,0:T(8,128)(2,1)S(1)}, bf16[528,128]{1,0:T(8,128)(2,1)S(1)}, u32[]{:S(2)}, u32[]{:S(2)}) collective-permute-start(bf16[528,128]{1,0:T(8,128)(2,1)S(1)} %get-tuple-element.80), channel_id=1, source_target_pairs={{0,4},{1,5},{2,6},{3,7},{4,0},{5,1},{6,2},{7,3},{8,12},{9,13},{10,... | collective-permute-start | bytes 405512 | tf_op jit(solution)/shard_map/ppermute | solution.py:389
  52.1 9.3 %collective-permute-start.11 = (bf16[528,128]{1,0:T(8,128)(2,1)S(1)}, bf16[528,128]{1,0:T(8,128)(2,1)S(1)}, u32[]{:S(2)}, u32[]{:S(2)}) collective-permute-start(bf16[528,128]{1,0:T(8,128)(2,1)S(1)} %get-tuple-element.79), channel_id=1, source_target_pairs={{0,8},{1,9},{2,10},{3,11},{4,12},{5,13},{6,14},{7,15},{8,0},{9,1},... | collective-permute-start | bytes 405512 | tf_op jit(solution)/shard_map/ppermute | solution.py:389
  54.8 8.5 %collective-permute-start.15 = (bf16[528,128]{1,0:T(8,128)(2,1)S(1)}, bf16[528,128]{1,0:T(8,128)(2,1)S(1)}, u32[]{:S(2)}, u32[]{:S(2)}) collective-permute-start(bf16[528,128]{1,0:T(8,128)(2,1)S(1)} %get-tuple-element.86), channel_id=1, source_target_pairs={{0,4},{1,5},{2,6},{3,7},{4,0},{5,1},{6,2},{7,3},{8,12},{9,13},{10,... | collective-permute-start | bytes 405512 | tf_op jit(solution)/shard_map/ppermute | solution.py:389
  55.7 8.4 %collective-permute-start.17 = (bf16[272,128]{1,0:T(8,128)(2,1)S(1)}, bf16[272,128]{1,0:T(8,128)(2,1)S(1)}, u32[]{:S(2)}, u32[]{:S(2)}) collective-permute-start(bf16[272,128]{1,0:T(8,128)(2,1)S(1)} %get-tuple-element.89), channel_id=1, source_target_pairs={{0,8},{1,9},{2,10},{3,11},{4,12},{5,13},{6,14},{7,15},{8,0},{9,1},... | collective-permute-start | bytes 208904 | tf_op jit(solution)/shard_map/ppermute | solution.py:389
  59.7 6.8 %collective-permute-start.19 = (bf16[272,128]{1,0:T(8,128)(2,1)S(1)}, bf16[272,128]{1,0:T(8,128)(2,1)S(1)}, u32[]{:S(2)}, u32[]{:S(2)}) collective-permute-start(bf16[272,128]{1,0:T(8,128)(2,1)S(1)} %get-tuple-element.92), channel_id=1, source_target_pairs={{0,8},{1,9},{2,10},{3,11},{4,12},{5,13},{6,14},{7,15},{8,0},{9,1},... | collective-permute-start | bytes 208904 | tf_op jit(solution)/shard_map/ppermute | solution.py:389
  63.4 3.8 %collective-permute-start.16 = (bf16[32,1024]{1,0:T(8,128)(2,1)S(1)}, bf16[32,1024]{1,0:T(8,128)(2,1)S(1)}, u32[]{:S(2)}, u32[]{:S(2)}) collective-permute-start(bf16[32,1024]{1,0:T(8,128)(2,1)S(1)} %get-tuple-element.88), channel_id=1, source_target_pairs={{0,1},{1,0},{2,3},{3,2},{4,5},{5,4},{6,7},{7,6},{8,9},{9,8},{10,11... | collective-permute-start | bytes 196616 | tf_op jit(solution)/shard_map/ppermute | solution.py:389
  63.5 3.7 %collective-permute-start.14 = (bf16[32,1024]{1,0:T(8,128)(2,1)S(1)}, bf16[32,1024]{1,0:T(8,128)(2,1)S(1)}, u32[]{:S(2)}, u32[]{:S(2)}) collective-permute-start(bf16[32,1024]{1,0:T(8,128)(2,1)S(1)} %get-tuple-element.85), channel_id=1, source_target_pairs={{0,1},{1,0},{2,3},{3,2},{4,5},{5,4},{6,7},{7,6},{8,9},{9,8},{10,11... | collective-permute-start | bytes 196616 | tf_op jit(solution)/shard_map/ppermute | solution.py:389
  64.0 3.2 %collective-permute-start.10 = (bf16[32,1024]{1,0:T(8,128)(2,1)S(1)}, bf16[32,1024]{1,0:T(8,128)(2,1)S(1)}, u32[]{:S(2)}, u32[]{:S(2)}) collective-permute-start(bf16[32,1024]{1,0:T(8,128)(2,1)S(1)} %get-tuple-element.78), channel_id=1, source_target_pairs={{0,1},{1,0},{2,3},{3,2},{4,5},{5,4},{6,7},{7,6},{8,9},{9,8},{10,11... | collective-permute-start | bytes 196616 | tf_op jit(solution)/shard_map/ppermute | solution.py:389
  66.6 1.3 %collective-permute-start.20 = (bf16[32,512]{1,0:T(8,128)(2,1)S(1)}, bf16[32,512]{1,0:T(8,128)(2,1)S(1)}, u32[]{:S(2)}, u32[]{:S(2)}) collective-permute-start(bf16[32,512]{1,0:T(8,128)(2,1)S(1)} %get-tuple-element.94), channel_id=1, source_target_pairs={{0,1},{1,0},{2,3},{3,2},{4,5},{5,4},{6,7},{7,6},{8,9},{9,8},{10,11... | collective-permute-start | bytes 98312 | tf_op jit(solution)/shard_map/ppermute | solution.py:389
  66.7 1.4 %collective-permute-start.18 = (bf16[32,512]{1,0:T(8,128)(2,1)S(1)}, bf16[32,512]{1,0:T(8,128)(2,1)S(1)}, u32[]{:S(2)}, u32[]{:S(2)}) collective-permute-start(bf16[32,512]{1,0:T(8,128)(2,1)S(1)} %get-tuple-element.91), channel_id=1, source_target_pairs={{0,1},{1,0},{2,3},{3,2},{4,5},{5,4},{6,7},{7,6},{8,9},{9,8},{10,11... | collective-permute-start | bytes 98312 | tf_op jit(solution)/shard_map/ppermute | solution.py:389

commit v11 on v10

--- a/solution.py
+++ b/solution.py
@@ -212,14 +212,17 @@
         part = jnp.dot(own_ref[...], near_ref[:, columns], preferred_element_type=jnp.float32)
         partial_ref[:, columns] = halves_added(part)
 
-    tiles = width // COLUMNS
-
-    @pl.loop(0, tiles)
-    def _(tile):
-        multiply(pl.ds(pl.multiple_of(tile * COLUMNS, COLUMNS), COLUMNS))
-
-    if tiles * COLUMNS < width:
-        multiply(slice(tiles * COLUMNS, width))
+    turn = 4 * COLUMNS
+    turns = width // turn
+
+    def multiply_turn(index):
+        for at in range(0, turn, COLUMNS):
+            multiply(pl.ds(pl.multiple_of(index * turn + at, COLUMNS), COLUMNS))
+
+    if turns:
+        pl.loop(0, turns)(multiply_turn)
+    for at, wide in spans(width - turns * turn, COLUMNS):
+        multiply(pl.ds(turns * turn + at, wide))
     for copy in copies:
         copy.wait()
 

time: 69 us -> 68.3 us (0.990)
  Pallas kernels: 28.1 us -> 27.4 us
    pallas_call x23, Pallas kernels: 28.1 us -> 27.4 us  [call(): pl.pallas_call(run, in_specs=[vmem] * (count - far) + [pl.BlockSpec(memor...]
  transfers between devices with their start and end apart: 21 -> 21, of which waited for: 10 -> 10; matrix products, arithmetic and copies ran while one was open for 0% -> 0% of each run, Pallas kernels for 32% -> 31%
where the time goes in v11:
time: 68.3 us; the launch traced here: 68.2 us
  Pallas kernels  27.4 us (40%)
  starting transfers between devices  24.2 us (35%)
  waiting for transfers between devices  16.5 us (24%)
    pallas_call x23, Pallas kernels, call(): pl.pallas_call(run, in_specs=[vmem] * (count - far) + [pl.BlockSpec(memor...  27.4 us
    ppermute x21, starting transfers between devices, swapped(): return lax.ppermute(block, 'row', [(i, i ^ apart) for i in range(count)])  24.2 us
    ppermute x21, waiting for transfers between devices, swapped(): return lax.ppermute(block, 'row', [(i, i ^ apart) for i in range(count)])  16.5 us
  transfers between devices with their start and end apart: 21, of which 10 were waited for; matrix products, arithmetic and copies ran while one was open for 0% of the time, Pallas kernels for 31%

profile of v11, /device:TPU:0, one launch (start us, length us, event | category | flops | bytes accessed | tf_op | source)
XLA Modules:
  0.0 68.2 jit_solution(7120999744162536074)
XLA Ops:
  0.0 2.9 %split_basis.1 = (bf16[1024,1024]{1,0:T(8,128)(2,1)S(1)}, bf16[1024,2048]{1,0:T(8,128)(2,1)S(1)}) custom-call(f32[1024,512]{1,0:T(8,128)} %refs_0_.1, bf16[1,2048,4096]{2,1,0:T(8,128)(2,1)} %refs_2_.1), custom_call_target="tpu_custom_call" | custom-call | flops 1 | bytes 1 | tf_op jit(solution)/shard_map/split_basis/pallas_call | solution.py:105
  2.9 0.5 collective-permute-start
  3.4 5.1 %early_products.1 = (bf16[1024,2048]{1,0:T(8,128)(2,1)S(1)}, bf16[1024,4096]{1,0:T(8,128)(2,1)S(1)}, f32[512,2048]{1,0:T(8,128)S(1)}) custom-call(bf16[1024,1024]{1,0:T(8,128)(2,1)S(1)} %get-tuple-element.50.refs_0_, bf16[1024,2048]{1,0:T(8,128)(2,1)S(1)} %get-tuple-element.51.refs_1_, bf16[1,2048,4096]{2,1,0:T(8,128)(2,1)} %refs_2_.1), custom_call_target="tpu_custom_call" | custom-call | flops 1 | bytes 1 | tf_op jit(solution)/shard_map/early_products/pallas_call | solution.py:105
  8.6 0.0 collective-permute-done.refs_1_
  8.6 2.7 %product.5 = (bf16[2064,128]{1,0:T(8,128)(2,1)S(1)}, f32[2048,128]{1,0:T(8,128)S(1)}) custom-call(bf16[1024,1024]{1,0:T(8,128)(2,1)S(1)} %get-tuple-element.50.refs_0_, bf16[1024,1024]{1,0:T(8,128)(2,1)S(1)} %collective-permute-done.refs_1_, bf16[1024,2048]{1,0:T(8,128)(2,1)S(1)} %get-tuple-element.52.refs_2_, ...), custom_call_target="tpu_custom_call" | custom-call | flops 1 | bytes 1 | tf_op jit(solution)/shard_map/product/pallas_call | solution.py:105
  11.2 2.6 %collective-permute-start.1 = (bf16[2064,128]{1,0:T(8,128)(2,1)S(1)}, bf16[2064,128]{1,0:T(8,128)(2,1)S(1)}, u32[]{:S(2)}, u32[]{:S(2)}) collective-permute-start(bf16[2064,128]{1,0:T(8,128)(2,1)S(1)} %get-tuple-element.55), channel_id=1, source_target_pairs={{0,2},{1,3},{2,0},{3,1},{4,6},{5,7},{6,4},{7,5},{8,10},{9,11},{10,... | collective-permute-start | bytes 1585160 | tf_op jit(solution)/shard_map/ppermute | solution.py:392
  13.9 2.7 %product.6 = (bf16[2064,128]{1,0:T(8,128)(2,1)S(1)}, f32[2048,128]{1,0:T(8,128)S(1)}) custom-call(bf16[1024,1024]{1,0:T(8,128)(2,1)S(1)} %get-tuple-element.50.refs_0_, bf16[1024,1024]{1,0:T(8,128)(2,1)S(1)} %collective-permute-done.refs_1_, bf16[1024,2048]{1,0:T(8,128)(2,1)S(1)} %get-tuple-element.52.refs_2_, ...), custom_call_target="tpu_custom_call" | custom-call | flops 1 | bytes 1 | tf_op jit(solution)/shard_map/product/pallas_call | solution.py:105
  16.5 1.6 %collective-permute-start.4 = (bf16[2064,128]{1,0:T(8,128)(2,1)S(1)}, bf16[2064,128]{1,0:T(8,128)(2,1)S(1)}, u32[]{:S(2)}, u32[]{:S(2)}) collective-permute-start(bf16[2064,128]{1,0:T(8,128)(2,1)S(1)} %get-tuple-element.62), channel_id=1, source_target_pairs={{0,4},{1,5},{2,6},{3,7},{4,0},{5,1},{6,2},{7,3},{8,12},{9,13},{10,... | collective-permute-start | bytes 1585160 | tf_op jit(solution)/shard_map/ppermute | solution.py:392
  18.2 4.8 %product.7 = (bf16[2064,128]{1,0:T(8,128)(2,1)S(1)}, f32[2048,128]{1,0:T(8,128)S(1)}) custom-call(bf16[1024,1024]{1,0:T(8,128)(2,1)S(1)} %get-tuple-element.50.refs_0_, bf16[1024,1024]{1,0:T(8,128)(2,1)S(1)} %collective-permute-done.refs_1_, bf16[1024,2048]{1,0:T(8,128)(2,1)S(1)} %get-tuple-element.52.refs_2_, ...), custom_call_target="tpu_custom_call" | custom-call | flops 1 | bytes 1 | tf_op jit(solution)/shard_map/product/pallas_call | solution.py:105
  23.0 0.6 collective-permute-start.3
  23.6 3.1 %collective-permute-done.1.refs_0_ = bf16[2064,128]{1,0:T(8,128)(2,1)S(1)} collective-permute-done((bf16[2064,128]{1,0:T(8,128)(2,1)S(1)}, bf16[2064,128]{1,0:T(8,128)(2,1)S(1)}, u32[]{:S(2)}, u32[]{:S(2)}) %collective-permute-start.1) | collective-permute-done | bytes 528416 | tf_op jit(solution)/shard_map/ppermute | solution.py:392
  26.7 0.5 add_and_split.10
  27.2 3.1 %collective-permute-start.2 = (bf16[1040,128]{1,0:T(8,128)(2,1)S(1)}, bf16[1040,128]{1,0:T(8,128)(2,1)S(1)}, u32[]{:S(2)}, u32[]{:S(2)}) collective-permute-start(bf16[1040,128]{1,0:T(8,128)(2,1)S(1)} %get-tuple-element.59), channel_id=1, source_target_pairs={{0,8},{1,9},{2,10},{3,11},{4,12},{5,13},{6,14},{7,15},{8,0},{9,1},... | collective-permute-start | bytes 798728 | tf_op jit(solution)/shard_map/ppermute | solution.py:392
  30.3 2.5 %product.8 = (bf16[1040,128]{1,0:T(8,128)(2,1)S(1)}, f32[1024,128]{1,0:T(8,128)S(1)}) custom-call(bf16[1024,1024]{1,0:T(8,128)(2,1)S(1)} %get-tuple-element.50.refs_0_, bf16[1024,1024]{1,0:T(8,128)(2,1)S(1)} %collective-permute-done.refs_1_, bf16[1024,2048]{1,0:T(8,128)(2,1)S(1)} %get-tuple-element.52.refs_2_, ...), custom_call_target="tpu_custom_call" | custom-call | flops 1 | bytes 1 | tf_op jit(solution)/shard_map/product/pallas_call | solution.py:105
  32.8 1.6 %collective-permute-start.9 = (bf16[1040,128]{1,0:T(8,128)(2,1)S(1)}, bf16[1040,128]{1,0:T(8,128)(2,1)S(1)}, u32[]{:S(2)}, u32[]{:S(2)}) collective-permute-start(bf16[1040,128]{1,0:T(8,128)(2,1)S(1)} %get-tuple-element.72), channel_id=1, source_target_pairs={{0,4},{1,5},{2,6},{3,7},{4,0},{5,1},{6,2},{7,3},{8,12},{9,13},{10,... | collective-permute-start | bytes 798728 | tf_op jit(solution)/shard_map/ppermute | solution.py:392
  34.4 2.5 %product.9 = (bf16[1040,128]{1,0:T(8,128)(2,1)S(1)}, f32[1024,128]{1,0:T(8,128)S(1)}) custom-call(bf16[1024,1024]{1,0:T(8,128)(2,1)S(1)} %get-tuple-element.50.refs_0_, bf16[1024,1024]{1,0:T(8,128)(2,1)S(1)} %collective-permute-done.refs_1_, bf16[1024,2048]{1,0:T(8,128)(2,1)S(1)} %get-tuple-element.52.refs_2_, ...), custom_call_target="tpu_custom_call" | custom-call | flops 1 | bytes 1 | tf_op jit(solution)/shard_map/product/pallas_call | solution.py:105
  36.9 1.6 %collective-permute-start.8 = (bf16[1040,128]{1,0:T(8,128)(2,1)S(1)}, bf16[1040,128]{1,0:T(8,128)(2,1)S(1)}, u32[]{:S(2)}, u32[]{:S(2)}) collective-permute-start(bf16[1040,128]{1,0:T(8,128)(2,1)S(1)} %get-tuple-element.71), channel_id=1, source_target_pairs={{0,2},{1,3},{2,0},{3,1},{4,6},{5,7},{6,4},{7,5},{8,10},{9,11},{10,... | collective-permute-start | bytes 798728 | tf_op jit(solution)/shard_map/ppermute | solution.py:392
  38.5 0.0 collective-permute-done.4.refs_0_
  38.5 0.5 add_and_split.11
  39.0 0.6 collective-permute-start.7
  39.6 0.0 collective-permute-done.3.refs_0_
  39.6 0.5 add_and_split.12
  40.1 1.5 %collective-permute-start.6 = (bf16[1040,128]{1,0:T(8,128)(2,1)S(1)}, bf16[1040,128]{1,0:T(8,128)(2,1)S(1)}, u32[]{:S(2)}, u32[]{:S(2)}) collective-permute-start(bf16[1040,128]{1,0:T(8,128)(2,1)S(1)} %get-tuple-element.69), channel_id=1, source_target_pairs={{0,8},{1,9},{2,10},{3,11},{4,12},{5,13},{6,14},{7,15},{8,0},{9,1},... | collective-permute-start | bytes 798728 | tf_op jit(solution)/shard_map/ppermute | solution.py:392
  41.6 0.5 collective-permute-done.2.refs_0_
  42.1 0.3 add_and_split.13
  42.4 1.1 %collective-permute-start.5 = (bf16[528,128]{1,0:T(8,128)(2,1)S(1)}, bf16[528,128]{1,0:T(8,128)(2,1)S(1)}, u32[]{:S(2)}, u32[]{:S(2)}) collective-permute-start(bf16[528,128]{1,0:T(8,128)(2,1)S(1)} %get-tuple-element.67), channel_id=1, source_target_pairs={{0,4},{1,5},{2,6},{3,7},{4,0},{5,1},{6,2},{7,3},{8,12},{9,13},{10,... | collective-permute-start | bytes 405512 | tf_op jit(solution)/shard_map/ppermute | solution.py:392
  43.5 3.6 %collective-permute-done.9.refs_0_ = bf16[1040,128]{1,0:T(8,128)(2,1)S(1)} collective-permute-done((bf16[1040,128]{1,0:T(8,128)(2,1)S(1)}, bf16[1040,128]{1,0:T(8,128)(2,1)S(1)}, u32[]{:S(2)}, u32[]{:S(2)}) %collective-permute-start.9) | collective-permute-done | bytes 266272 | tf_op jit(solution)/shard_map/ppermute | solution.py:392
  47.1 0.2 add_and_split.14
  47.4 1.7 %collective-permute-start.13 = (bf16[528,128]{1,0:T(8,128)(2,1)S(1)}, bf16[528,128]{1,0:T(8,128)(2,1)S(1)}, u32[]{:S(2)}, u32[]{:S(2)}) collective-permute-start(bf16[528,128]{1,0:T(8,128)(2,1)S(1)} %get-tuple-element.81), channel_id=1, source_target_pairs={{0,2},{1,3},{2,0},{3,1},{4,6},{5,7},{6,4},{7,5},{8,10},{9,11},{10,... | collective-permute-start | bytes 405512 | tf_op jit(solution)/shard_map/ppermute | solution.py:392
  49.1 0.0 collective-permute-done.8.refs_0_
  49.1 0.2 add_and_split.15
  49.3 0.1 collective-permute-start.12
  49.4 1.7 %collective-permute-done.7.refs_0_ = bf16[1040,128]{1,0:T(8,128)(2,1)S(1)} collective-permute-done((bf16[1040,128]{1,0:T(8,128)(2,1)S(1)}, bf16[1040,128]{1,0:T(8,128)(2,1)S(1)}, u32[]{:S(2)}, u32[]{:S(2)}) %collective-permute-start.7) | collective-permute-done | bytes 266272 | tf_op jit(solution)/shard_map/ppermute | solution.py:392
  51.1 0.3 add_and_split.16
  51.4 1.4 %collective-permute-start.11 = (bf16[528,128]{1,0:T(8,128)(2,1)S(1)}, bf16[528,128]{1,0:T(8,128)(2,1)S(1)}, u32[]{:S(2)}, u32[]{:S(2)}) collective-permute-start(bf16[528,128]{1,0:T(8,128)(2,1)S(1)} %get-tuple-element.79), channel_id=1, source_target_pairs={{0,8},{1,9},{2,10},{3,11},{4,12},{5,13},{6,14},{7,15},{8,0},{9,1},... | collective-permute-start | bytes 405512 | tf_op jit(solution)/shard_map/ppermute | solution.py:392
  52.8 1.1 %collective-permute-done.6.refs_0_ = bf16[1040,128]{1,0:T(8,128)(2,1)S(1)} collective-permute-done((bf16[1040,128]{1,0:T(8,128)(2,1)S(1)}, bf16[1040,128]{1,0:T(8,128)(2,1)S(1)}, u32[]{:S(2)}, u32[]{:S(2)}) %collective-permute-start.6) | collective-permute-done | bytes 266272 | tf_op jit(solution)/shard_map/ppermute | solution.py:392
  53.9 0.3 add_and_split.17
  54.1 0.6 collective-permute-start.15
  54.7 0.0 collective-permute-done.5.refs_0_
  54.7 0.1 add_last.5
  54.8 0.0 collective-permute-done.13.refs_0_
  54.9 0.1 add_and_split.18
  55.0 3.9 %collective-permute-start.17 = (bf16[272,128]{1,0:T(8,128)(2,1)S(1)}, bf16[272,128]{1,0:T(8,128)(2,1)S(1)}, u32[]{:S(2)}, u32[]{:S(2)}) collective-permute-start(bf16[272,128]{1,0:T(8,128)(2,1)S(1)} %get-tuple-element.89), channel_id=1, source_target_pairs={{0,8},{1,9},{2,10},{3,11},{4,12},{5,13},{6,14},{7,15},{8,0},{9,1},... | collective-permute-start | bytes 208904 | tf_op jit(solution)/shard_map/ppermute | solution.py:392
  58.9 0.0 collective-permute-done.12.refs_0_
  58.9 0.1 add_and_split.19
  59.0 0.3 collective-permute-start.19
  59.4 1.3 %collective-permute-done.11.refs_0_ = bf16[528,128]{1,0:T(8,128)(2,1)S(1)} collective-permute-done((bf16[528,128]{1,0:T(8,128)(2,1)S(1)}, bf16[528,128]{1,0:T(8,128)(2,1)S(1)}, u32[]{:S(2)}, u32[]{:S(2)}) %collective-permute-start.11) | collective-permute-done | bytes 135200 | tf_op jit(solution)/shard_map/ppermute | solution.py:392
  60.7 0.1 add_last.6
  60.8 1.8 %collective-permute-done.15.refs_0_ = bf16[528,128]{1,0:T(8,128)(2,1)S(1)} collective-permute-done((bf16[528,128]{1,0:T(8,128)(2,1)S(1)}, bf16[528,128]{1,0:T(8,128)(2,1)S(1)}, u32[]{:S(2)}, u32[]{:S(2)}) %collective-permute-start.15) | collective-permute-done | bytes 135200 | tf_op jit(solution)/shard_map/ppermute | solution.py:392
  62.6 0.1 add_last.7
  62.7 0.1 collective-permute-start.16
  62.8 0.5 collective-permute-start.14
  63.3 0.1 collective-permute-start.10
  63.4 0.0 collective-permute-done.17.refs_0_
  63.4 0.1 add_last.8
  63.4 2.4 %collective-permute-done.19.refs_0_ = bf16[272,128]{1,0:T(8,128)(2,1)S(1)} collective-permute-done((bf16[272,128]{1,0:T(8,128)(2,1)S(1)}, bf16[272,128]{1,0:T(8,128)(2,1)S(1)}, u32[]{:S(2)}, u32[]{:S(2)}) %collective-permute-start.19) | collective-permute-done | bytes 69664 | tf_op jit(solution)/shard_map/ppermute | solution.py:392
  65.8 0.1 add_last.9
  65.9 0.1 collective-permute-start.20
  66.0 0.5 collective-permute-start.18
  66.5 0.0 collective-permute-done.16.refs_5_
  66.5 0.0 collective-permute-done.10.refs_1_
  66.5 0.7 %collective-permute-done.20.refs_9_ = bf16[32,512]{1,0:T(8,128)(2,1)S(1)} collective-permute-done((bf16[32,512]{1,0:T(8,128)(2,1)S(1)}, bf16[32,512]{1,0:T(8,128)(2,1)S(1)}, u32[]{:S(2)}, u32[]{:S(2)}) %collective-permute-start.20) | collective-permute-done | bytes 32800 | tf_op jit(solution)/shard_map/ppermute | solution.py:392
  67.2 0.2 collective-permute-done.18.refs_7_
  67.3 0.8 %lay_out.1 = bf16[32,8192]{1,0:T(8,128)(2,1)} custom-call(bf16[32,1024]{1,0:T(8,128)(2,1)S(1)} %get-tuple-element.77.refs_2_.refs_0_, bf16[32,1024]{1,0:T(8,128)(2,1)S(1)} %collective-permute-done.10.refs_1_, bf16[32,1024]{1,0:T(8,128)(2,1)S(1)} %get-tuple-element.84.refs_2_, bf16[32,1024]{1,0:T(8,128)(2,1)S(1)} %collective-permute-done.14.refs_3_, ...), custom_call_target="tpu_custom_call" | custom-call | flops 1 | bytes 1 | tf_op jit(solution)/shard_map/lay_out/pallas_call | solution.py:105
  (1 shorter events, 0.0 us)
Async XLA Ops:
  2.9 5.7 %collective-permute-start = (bf16[1024,1024]{1,0:T(8,128)(2,1)S(1)}, bf16[1024,1024]{1,0:T(8,128)(2,1)S(1)}, u32[]{:S(2)}, u32[]{:S(2)}) collective-permute-start(bf16[1024,1024]{1,0:T(8,128)(2,1)S(1)} %get-tuple-element.50.refs_0_), channel_id=1, source_target_pairs={{0,1},{1,0},{2,3},{3,2},{4,5},{5,4},{6,7},{7,6},{8,9},{9,8},{10,11... | collective-permute-start | bytes 6291464 | tf_op jit(solution)/shard_map/ppermute | solution.py:392
  11.2 15.5 %collective-permute-start.1 = (bf16[2064,128]{1,0:T(8,128)(2,1)S(1)}, bf16[2064,128]{1,0:T(8,128)(2,1)S(1)}, u32[]{:S(2)}, u32[]{:S(2)}) collective-permute-start(bf16[2064,128]{1,0:T(8,128)(2,1)S(1)} %get-tuple-element.55), channel_id=1, source_target_pairs={{0,2},{1,3},{2,0},{3,1},{4,6},{5,7},{6,4},{7,5},{8,10},{9,11},{10,... | collective-permute-start | bytes 1585160 | tf_op jit(solution)/shard_map/ppermute | solution.py:392
  16.5 22.0 %collective-permute-start.4 = (bf16[2064,128]{1,0:T(8,128)(2,1)S(1)}, bf16[2064,128]{1,0:T(8,128)(2,1)S(1)}, u32[]{:S(2)}, u32[]{:S(2)}) collective-permute-start(bf16[2064,128]{1,0:T(8,128)(2,1)S(1)} %get-tuple-element.62), channel_id=1, source_target_pairs={{0,4},{1,5},{2,6},{3,7},{4,0},{5,1},{6,2},{7,3},{8,12},{9,13},{10,... | collective-permute-start | bytes 1585160 | tf_op jit(solution)/shard_map/ppermute | solution.py:392
  23.0 16.6 %collective-permute-start.3 = (bf16[2064,128]{1,0:T(8,128)(2,1)S(1)}, bf16[2064,128]{1,0:T(8,128)(2,1)S(1)}, u32[]{:S(2)}, u32[]{:S(2)}) collective-permute-start(bf16[2064,128]{1,0:T(8,128)(2,1)S(1)} %get-tuple-element.61), channel_id=1, source_target_pairs={{0,2},{1,3},{2,0},{3,1},{4,6},{5,7},{6,4},{7,5},{8,10},{9,11},{10,... | collective-permute-start | bytes 1585160 | tf_op jit(solution)/shard_map/ppermute | solution.py:392
  27.2 14.9 %collective-permute-start.2 = (bf16[1040,128]{1,0:T(8,128)(2,1)S(1)}, bf16[1040,128]{1,0:T(8,128)(2,1)S(1)}, u32[]{:S(2)}, u32[]{:S(2)}) collective-permute-start(bf16[1040,128]{1,0:T(8,128)(2,1)S(1)} %get-tuple-element.59), channel_id=1, source_target_pairs={{0,8},{1,9},{2,10},{3,11},{4,12},{5,13},{6,14},{7,15},{8,0},{9,1},... | collective-permute-start | bytes 798728 | tf_op jit(solution)/shard_map/ppermute | solution.py:392
  32.8 14.3 %collective-permute-start.9 = (bf16[1040,128]{1,0:T(8,128)(2,1)S(1)}, bf16[1040,128]{1,0:T(8,128)(2,1)S(1)}, u32[]{:S(2)}, u32[]{:S(2)}) collective-permute-start(bf16[1040,128]{1,0:T(8,128)(2,1)S(1)} %get-tuple-element.72), channel_id=1, source_target_pairs={{0,4},{1,5},{2,6},{3,7},{4,0},{5,1},{6,2},{7,3},{8,12},{9,13},{10,... | collective-permute-start | bytes 798728 | tf_op jit(solution)/shard_map/ppermute | solution.py:392
  36.9 12.2 %collective-permute-start.8 = (bf16[1040,128]{1,0:T(8,128)(2,1)S(1)}, bf16[1040,128]{1,0:T(8,128)(2,1)S(1)}, u32[]{:S(2)}, u32[]{:S(2)}) collective-permute-start(bf16[1040,128]{1,0:T(8,128)(2,1)S(1)} %get-tuple-element.71), channel_id=1, source_target_pairs={{0,2},{1,3},{2,0},{3,1},{4,6},{5,7},{6,4},{7,5},{8,10},{9,11},{10,... | collective-permute-start | bytes 798728 | tf_op jit(solution)/shard_map/ppermute | solution.py:392
  39.0 12.1 %collective-permute-start.7 = (bf16[1040,128]{1,0:T(8,128)(2,1)S(1)}, bf16[1040,128]{1,0:T(8,128)(2,1)S(1)}, u32[]{:S(2)}, u32[]{:S(2)}) collective-permute-start(bf16[1040,128]{1,0:T(8,128)(2,1)S(1)} %get-tuple-element.70), channel_id=1, source_target_pairs={{0,2},{1,3},{2,0},{3,1},{4,6},{5,7},{6,4},{7,5},{8,10},{9,11},{10,... | collective-permute-start | bytes 798728 | tf_op jit(solution)/shard_map/ppermute | solution.py:392
  40.1 13.8 %collective-permute-start.6 = (bf16[1040,128]{1,0:T(8,128)(2,1)S(1)}, bf16[1040,128]{1,0:T(8,128)(2,1)S(1)}, u32[]{:S(2)}, u32[]{:S(2)}) collective-permute-start(bf16[1040,128]{1,0:T(8,128)(2,1)S(1)} %get-tuple-element.69), channel_id=1, source_target_pairs={{0,8},{1,9},{2,10},{3,11},{4,12},{5,13},{6,14},{7,15},{8,0},{9,1},... | collective-permute-start | bytes 798728 | tf_op jit(solution)/shard_map/ppermute | solution.py:392
  42.4 12.4 %collective-permute-start.5 = (bf16[528,128]{1,0:T(8,128)(2,1)S(1)}, bf16[528,128]{1,0:T(8,128)(2,1)S(1)}, u32[]{:S(2)}, u32[]{:S(2)}) collective-permute-start(bf16[528,128]{1,0:T(8,128)(2,1)S(1)} %get-tuple-element.67), channel_id=1, source_target_pairs={{0,4},{1,5},{2,6},{3,7},{4,0},{5,1},{6,2},{7,3},{8,12},{9,13},{10,... | collective-permute-start | bytes 405512 | tf_op jit(solution)/shard_map/ppermute | solution.py:392
  47.4 7.5 %collective-permute-start.13 = (bf16[528,128]{1,0:T(8,128)(2,1)S(1)}, bf16[528,128]{1,0:T(8,128)(2,1)S(1)}, u32[]{:S(2)}, u32[]{:S(2)}) collective-permute-start(bf16[528,128]{1,0:T(8,128)(2,1)S(1)} %get-tuple-element.81), channel_id=1, source_target_pairs={{0,2},{1,3},{2,0},{3,1},{4,6},{5,7},{6,4},{7,5},{8,10},{9,11},{10,... | collective-permute-start | bytes 405512 | tf_op jit(solution)/shard_map/ppermute | solution.py:392
  49.3 9.6 %collective-permute-start.12 = (bf16[528,128]{1,0:T(8,128)(2,1)S(1)}, bf16[528,128]{1,0:T(8,128)(2,1)S(1)}, u32[]{:S(2)}, u32[]{:S(2)}) collective-permute-start(bf16[528,128]{1,0:T(8,128)(2,1)S(1)} %get-tuple-element.80), channel_id=1, source_target_pairs={{0,4},{1,5},{2,6},{3,7},{4,0},{5,1},{6,2},{7,3},{8,12},{9,13},{10,... | collective-permute-start | bytes 405512 | tf_op jit(solution)/shard_map/ppermute | solution.py:392
  51.4 9.3 %collective-permute-start.11 = (bf16[528,128]{1,0:T(8,128)(2,1)S(1)}, bf16[528,128]{1,0:T(8,128)(2,1)S(1)}, u32[]{:S(2)}, u32[]{:S(2)}) collective-permute-start(bf16[528,128]{1,0:T(8,128)(2,1)S(1)} %get-tuple-element.79), channel_id=1, source_target_pairs={{0,8},{1,9},{2,10},{3,11},{4,12},{5,13},{6,14},{7,15},{8,0},{9,1},... | collective-permute-start | bytes 405512 | tf_op jit(solution)/shard_map/ppermute | solution.py:392
  54.1 8.5 %collective-permute-start.15 = (bf16[528,128]{1,0:T(8,128)(2,1)S(1)}, bf16[528,128]{1,0:T(8,128)(2,1)S(1)}, u32[]{:S(2)}, u32[]{:S(2)}) collective-permute-start(bf16[528,128]{1,0:T(8,128)(2,1)S(1)} %get-tuple-element.86), channel_id=1, source_target_pairs={{0,4},{1,5},{2,6},{3,7},{4,0},{5,1},{6,2},{7,3},{8,12},{9,13},{10,... | collective-permute-start | bytes 405512 | tf_op jit(solution)/shard_map/ppermute | solution.py:392
  55.0 8.4 %collective-permute-start.17 = (bf16[272,128]{1,0:T(8,128)(2,1)S(1)}, bf16[272,128]{1,0:T(8,128)(2,1)S(1)}, u32[]{:S(2)}, u32[]{:S(2)}) collective-permute-start(bf16[272,128]{1,0:T(8,128)(2,1)S(1)} %get-tuple-element.89), channel_id=1, source_target_pairs={{0,8},{1,9},{2,10},{3,11},{4,12},{5,13},{6,14},{7,15},{8,0},{9,1},... | collective-permute-start | bytes 208904 | tf_op jit(solution)/shard_map/ppermute | solution.py:392
  59.0 6.8 %collective-permute-start.19 = (bf16[272,128]{1,0:T(8,128)(2,1)S(1)}, bf16[272,128]{1,0:T(8,128)(2,1)S(1)}, u32[]{:S(2)}, u32[]{:S(2)}) collective-permute-start(bf16[272,128]{1,0:T(8,128)(2,1)S(1)} %get-tuple-element.92), channel_id=1, source_target_pairs={{0,8},{1,9},{2,10},{3,11},{4,12},{5,13},{6,14},{7,15},{8,0},{9,1},... | collective-permute-start | bytes 208904 | tf_op jit(solution)/shard_map/ppermute | solution.py:392
  62.7 3.7 %collective-permute-start.16 = (bf16[32,1024]{1,0:T(8,128)(2,1)S(1)}, bf16[32,1024]{1,0:T(8,128)(2,1)S(1)}, u32[]{:S(2)}, u32[]{:S(2)}) collective-permute-start(bf16[32,1024]{1,0:T(8,128)(2,1)S(1)} %get-tuple-element.88), channel_id=1, source_target_pairs={{0,1},{1,0},{2,3},{3,2},{4,5},{5,4},{6,7},{7,6},{8,9},{9,8},{10,11... | collective-permute-start | bytes 196616 | tf_op jit(solution)/shard_map/ppermute | solution.py:392
  62.8 3.7 %collective-permute-start.14 = (bf16[32,1024]{1,0:T(8,128)(2,1)S(1)}, bf16[32,1024]{1,0:T(8,128)(2,1)S(1)}, u32[]{:S(2)}, u32[]{:S(2)}) collective-permute-start(bf16[32,1024]{1,0:T(8,128)(2,1)S(1)} %get-tuple-element.85), channel_id=1, source_target_pairs={{0,1},{1,0},{2,3},{3,2},{4,5},{5,4},{6,7},{7,6},{8,9},{9,8},{10,11... | collective-permute-start | bytes 196616 | tf_op jit(solution)/shard_map/ppermute | solution.py:392
  63.3 3.2 %collective-permute-start.10 = (bf16[32,1024]{1,0:T(8,128)(2,1)S(1)}, bf16[32,1024]{1,0:T(8,128)(2,1)S(1)}, u32[]{:S(2)}, u32[]{:S(2)}) collective-permute-start(bf16[32,1024]{1,0:T(8,128)(2,1)S(1)} %get-tuple-element.78), channel_id=1, source_target_pairs={{0,1},{1,0},{2,3},{3,2},{4,5},{5,4},{6,7},{7,6},{8,9},{9,8},{10,11... | collective-permute-start | bytes 196616 | tf_op jit(solution)/shard_map/ppermute | solution.py:392
  65.9 1.3 %collective-permute-start.20 = (bf16[32,512]{1,0:T(8,128)(2,1)S(1)}, bf16[32,512]{1,0:T(8,128)(2,1)S(1)}, u32[]{:S(2)}, u32[]{:S(2)}) collective-permute-start(bf16[32,512]{1,0:T(8,128)(2,1)S(1)} %get-tuple-element.94), channel_id=1, source_target_pairs={{0,1},{1,0},{2,3},{3,2},{4,5},{5,4},{6,7},{7,6},{8,9},{9,8},{10,11... | collective-permute-start | bytes 98312 | tf_op jit(solution)/shard_map/ppermute | solution.py:392
  66.0 1.4 %collective-permute-start.18 = (bf16[32,512]{1,0:T(8,128)(2,1)S(1)}, bf16[32,512]{1,0:T(8,128)(2,1)S(1)}, u32[]{:S(2)}, u32[]{:S(2)}) collective-permute-start(bf16[32,512]{1,0:T(8,128)(2,1)S(1)} %get-tuple-element.91), channel_id=1, source_target_pairs={{0,1},{1,0},{2,3},{3,2},{4,5},{5,4},{6,7},{7,6},{8,9},{9,8},{10,11... | collective-permute-start | bytes 98312 | tf_op jit(solution)/shard_map/ppermute | solution.py:392

commit v12 on v11

--- a/solution.py
+++ b/solution.py
@@ -190,6 +190,11 @@
     return [(at, min(wide, width - at)) for at in range(0, width, wide)]
 
 
+def terms(a_ref):
+    half = a_ref.shape[0] // 2
+    return a_ref[:half, :], a_ref[half:, :]
+
+
 def halves_added(product):
     half = product.shape[0] // 2
     return product[:half] + product[half:]
@@ -258,11 +263,10 @@
         if not early:
             taken = [right[0][:, own_columns]] + taken
         total = jnp.dot(
-            jnp.concatenate([a_ref[...] for a_ref in left[first:]], axis=1),
-            jnp.concatenate(taken, axis=0),
+            jnp.concatenate([term for a_ref in left[first:] for term in terms(a_ref)], axis=1),
+            jnp.concatenate([rows for rows in taken for _ in range(2)], axis=0),
             preferred_element_type=jnp.float32,
         )
-        total = halves_added(total)
         if early:
             total = total + refs[2 * pieces][:, columns]
         for lane in range(0, wide, LANES):

time: 68.3 us -> 68.3 us (level)
  no operation moved by 1% of the time
where the time goes in v12:
time: 68.3 us; the launch traced here: 68.2 us
  Pallas kernels  27.3 us (40%)
  starting transfers between devices  24 us (35%)
  waiting for transfers between devices  16.6 us (24%)
    pallas_call x23, Pallas kernels, call(): pl.pallas_call(run, in_specs=[vmem] * (count - far) + [pl.BlockSpec(memor...  27.3 us
    ppermute x21, starting transfers between devices, swapped(): return lax.ppermute(block, 'row', [(i, i ^ apart) for i in range(count)])  24 us
    ppermute x21, waiting for transfers between devices, swapped(): return lax.ppermute(block, 'row', [(i, i ^ apart) for i in range(count)])  16.6 us
  transfers between devices with their start and end apart: 21, of which 10 were waited for; matrix products, arithmetic and copies ran while one was open for 0% of the time, Pallas kernels for 31%

profile of v12, /device:TPU:0, one launch (start us, length us, event | category | flops | bytes accessed | tf_op | source)
XLA Modules:
  0.0 68.2 jit_solution(15997449077923436569)
XLA Ops:
  0.0 2.9 %split_basis.1 = (bf16[1024,1024]{1,0:T(8,128)(2,1)S(1)}, bf16[1024,2048]{1,0:T(8,128)(2,1)S(1)}) custom-call(f32[1024,512]{1,0:T(8,128)} %refs_0_.1, bf16[1,2048,4096]{2,1,0:T(8,128)(2,1)} %refs_2_.1), custom_call_target="tpu_custom_call" | custom-call | flops 1 | bytes 1 | tf_op jit(solution)/shard_map/split_basis/pallas_call | solution.py:105
  2.9 0.5 collective-permute-start
  3.4 5.1 %early_products.1 = (bf16[1024,2048]{1,0:T(8,128)(2,1)S(1)}, bf16[1024,4096]{1,0:T(8,128)(2,1)S(1)}, f32[512,2048]{1,0:T(8,128)S(1)}) custom-call(bf16[1024,1024]{1,0:T(8,128)(2,1)S(1)} %get-tuple-element.50.refs_0_, bf16[1024,2048]{1,0:T(8,128)(2,1)S(1)} %get-tuple-element.51.refs_1_, bf16[1,2048,4096]{2,1,0:T(8,128)(2,1)} %refs_2_.1), custom_call_target="tpu_custom_call" | custom-call | flops 1 | bytes 1 | tf_op jit(solution)/shard_map/early_products/pallas_call | solution.py:105
  8.6 0.0 collective-permute-done.refs_1_
  8.6 2.7 %product.5 = (bf16[2064,128]{1,0:T(8,128)(2,1)S(1)}, f32[2048,128]{1,0:T(8,128)S(1)}) custom-call(bf16[1024,1024]{1,0:T(8,128)(2,1)S(1)} %get-tuple-element.50.refs_0_, bf16[1024,1024]{1,0:T(8,128)(2,1)S(1)} %collective-permute-done.refs_1_, bf16[1024,2048]{1,0:T(8,128)(2,1)S(1)} %get-tuple-element.52.refs_2_, ...), custom_call_target="tpu_custom_call" | custom-call | flops 1 | bytes 1 | tf_op jit(solution)/shard_map/product/pallas_call | solution.py:105
  11.2 2.6 %collective-permute-start.1 = (bf16[2064,128]{1,0:T(8,128)(2,1)S(1)}, bf16[2064,128]{1,0:T(8,128)(2,1)S(1)}, u32[]{:S(2)}, u32[]{:S(2)}) collective-permute-start(bf16[2064,128]{1,0:T(8,128)(2,1)S(1)} %get-tuple-element.55), channel_id=1, source_target_pairs={{0,2},{1,3},{2,0},{3,1},{4,6},{5,7},{6,4},{7,5},{8,10},{9,11},{10,... | collective-permute-start | bytes 1585160 | tf_op jit(solution)/shard_map/ppermute | solution.py:396
  13.8 2.7 %product.6 = (bf16[2064,128]{1,0:T(8,128)(2,1)S(1)}, f32[2048,128]{1,0:T(8,128)S(1)}) custom-call(bf16[1024,1024]{1,0:T(8,128)(2,1)S(1)} %get-tuple-element.50.refs_0_, bf16[1024,1024]{1,0:T(8,128)(2,1)S(1)} %collective-permute-done.refs_1_, bf16[1024,2048]{1,0:T(8,128)(2,1)S(1)} %get-tuple-element.52.refs_2_, ...), custom_call_target="tpu_custom_call" | custom-call | flops 1 | bytes 1 | tf_op jit(solution)/shard_map/product/pallas_call | solution.py:105
  16.5 1.7 %collective-permute-start.4 = (bf16[2064,128]{1,0:T(8,128)(2,1)S(1)}, bf16[2064,128]{1,0:T(8,128)(2,1)S(1)}, u32[]{:S(2)}, u32[]{:S(2)}) collective-permute-start(bf16[2064,128]{1,0:T(8,128)(2,1)S(1)} %get-tuple-element.62), channel_id=1, source_target_pairs={{0,4},{1,5},{2,6},{3,7},{4,0},{5,1},{6,2},{7,3},{8,12},{9,13},{10,... | collective-permute-start | bytes 1585160 | tf_op jit(solution)/shard_map/ppermute | solution.py:396
  18.2 4.8 %product.7 = (bf16[2064,128]{1,0:T(8,128)(2,1)S(1)}, f32[2048,128]{1,0:T(8,128)S(1)}) custom-call(bf16[1024,1024]{1,0:T(8,128)(2,1)S(1)} %get-tuple-element.50.refs_0_, bf16[1024,1024]{1,0:T(8,128)(2,1)S(1)} %collective-permute-done.refs_1_, bf16[1024,2048]{1,0:T(8,128)(2,1)S(1)} %get-tuple-element.52.refs_2_, ...), custom_call_target="tpu_custom_call" | custom-call | flops 1 | bytes 1 | tf_op jit(solution)/shard_map/product/pallas_call | solution.py:105
  23.0 0.6 collective-permute-start.3
  23.6 3.1 %collective-permute-done.1.refs_0_ = bf16[2064,128]{1,0:T(8,128)(2,1)S(1)} collective-permute-done((bf16[2064,128]{1,0:T(8,128)(2,1)S(1)}, bf16[2064,128]{1,0:T(8,128)(2,1)S(1)}, u32[]{:S(2)}, u32[]{:S(2)}) %collective-permute-start.1) | collective-permute-done | bytes 528416 | tf_op jit(solution)/shard_map/ppermute | solution.py:396
  26.7 0.5 add_and_split.10
  27.2 3.1 %collective-permute-start.2 = (bf16[1040,128]{1,0:T(8,128)(2,1)S(1)}, bf16[1040,128]{1,0:T(8,128)(2,1)S(1)}, u32[]{:S(2)}, u32[]{:S(2)}) collective-permute-start(bf16[1040,128]{1,0:T(8,128)(2,1)S(1)} %get-tuple-element.59), channel_id=1, source_target_pairs={{0,8},{1,9},{2,10},{3,11},{4,12},{5,13},{6,14},{7,15},{8,0},{9,1},... | collective-permute-start | bytes 798728 | tf_op jit(solution)/shard_map/ppermute | solution.py:396
  30.3 2.5 %product.8 = (bf16[1040,128]{1,0:T(8,128)(2,1)S(1)}, f32[1024,128]{1,0:T(8,128)S(1)}) custom-call(bf16[1024,1024]{1,0:T(8,128)(2,1)S(1)} %get-tuple-element.50.refs_0_, bf16[1024,1024]{1,0:T(8,128)(2,1)S(1)} %collective-permute-done.refs_1_, bf16[1024,2048]{1,0:T(8,128)(2,1)S(1)} %get-tuple-element.52.refs_2_, ...), custom_call_target="tpu_custom_call" | custom-call | flops 1 | bytes 1 | tf_op jit(solution)/shard_map/product/pallas_call | solution.py:105
  32.8 1.6 %collective-permute-start.9 = (bf16[1040,128]{1,0:T(8,128)(2,1)S(1)}, bf16[1040,128]{1,0:T(8,128)(2,1)S(1)}, u32[]{:S(2)}, u32[]{:S(2)}) collective-permute-start(bf16[1040,128]{1,0:T(8,128)(2,1)S(1)} %get-tuple-element.72), channel_id=1, source_target_pairs={{0,4},{1,5},{2,6},{3,7},{4,0},{5,1},{6,2},{7,3},{8,12},{9,13},{10,... | collective-permute-start | bytes 798728 | tf_op jit(solution)/shard_map/ppermute | solution.py:396
  34.4 2.5 %product.9 = (bf16[1040,128]{1,0:T(8,128)(2,1)S(1)}, f32[1024,128]{1,0:T(8,128)S(1)}) custom-call(bf16[1024,1024]{1,0:T(8,128)(2,1)S(1)} %get-tuple-element.50.refs_0_, bf16[1024,1024]{1,0:T(8,128)(2,1)S(1)} %collective-permute-done.refs_1_, bf16[1024,2048]{1,0:T(8,128)(2,1)S(1)} %get-tuple-element.52.refs_2_, ...), custom_call_target="tpu_custom_call" | custom-call | flops 1 | bytes 1 | tf_op jit(solution)/shard_map/product/pallas_call | solution.py:105
  36.9 1.6 %collective-permute-start.8 = (bf16[1040,128]{1,0:T(8,128)(2,1)S(1)}, bf16[1040,128]{1,0:T(8,128)(2,1)S(1)}, u32[]{:S(2)}, u32[]{:S(2)}) collective-permute-start(bf16[1040,128]{1,0:T(8,128)(2,1)S(1)} %get-tuple-element.71), channel_id=1, source_target_pairs={{0,2},{1,3},{2,0},{3,1},{4,6},{5,7},{6,4},{7,5},{8,10},{9,11},{10,... | collective-permute-start | bytes 798728 | tf_op jit(solution)/shard_map/ppermute | solution.py:396
  38.5 0.0 collective-permute-done.4.refs_0_
  38.5 0.5 add_and_split.11
  39.0 0.6 collective-permute-start.7
  39.6 0.0 collective-permute-done.3.refs_0_
  39.6 0.5 add_and_split.12
  40.1 1.6 %collective-permute-start.6 = (bf16[1040,128]{1,0:T(8,128)(2,1)S(1)}, bf16[1040,128]{1,0:T(8,128)(2,1)S(1)}, u32[]{:S(2)}, u32[]{:S(2)}) collective-permute-start(bf16[1040,128]{1,0:T(8,128)(2,1)S(1)} %get-tuple-element.69), channel_id=1, source_target_pairs={{0,8},{1,9},{2,10},{3,11},{4,12},{5,13},{6,14},{7,15},{8,0},{9,1},... | collective-permute-start | bytes 798728 | tf_op jit(solution)/shard_map/ppermute | solution.py:396
  41.6 0.5 collective-permute-done.2.refs_0_
  42.1 0.3 add_and_split.13
  42.4 1.1 %collective-permute-start.5 = (bf16[528,128]{1,0:T(8,128)(2,1)S(1)}, bf16[528,128]{1,0:T(8,128)(2,1)S(1)}, u32[]{:S(2)}, u32[]{:S(2)}) collective-permute-start(bf16[528,128]{1,0:T(8,128)(2,1)S(1)} %get-tuple-element.67), channel_id=1, source_target_pairs={{0,4},{1,5},{2,6},{3,7},{4,0},{5,1},{6,2},{7,3},{8,12},{9,13},{10,... | collective-permute-start | bytes 405512 | tf_op jit(solution)/shard_map/ppermute | solution.py:396
  43.5 3.6 %collective-permute-done.9.refs_0_ = bf16[1040,128]{1,0:T(8,128)(2,1)S(1)} collective-permute-done((bf16[1040,128]{1,0:T(8,128)(2,1)S(1)}, bf16[1040,128]{1,0:T(8,128)(2,1)S(1)}, u32[]{:S(2)}, u32[]{:S(2)}) %collective-permute-start.9) | collective-permute-done | bytes 266272 | tf_op jit(solution)/shard_map/ppermute | solution.py:396
  47.2 0.2 add_and_split.14
  47.4 1.7 %collective-permute-start.13 = (bf16[528,128]{1,0:T(8,128)(2,1)S(1)}, bf16[528,128]{1,0:T(8,128)(2,1)S(1)}, u32[]{:S(2)}, u32[]{:S(2)}) collective-permute-start(bf16[528,128]{1,0:T(8,128)(2,1)S(1)} %get-tuple-element.81), channel_id=1, source_target_pairs={{0,2},{1,3},{2,0},{3,1},{4,6},{5,7},{6,4},{7,5},{8,10},{9,11},{10,... | collective-permute-start | bytes 405512 | tf_op jit(solution)/shard_map/ppermute | solution.py:396
  49.1 0.0 collective-permute-done.8.refs_0_
  49.1 0.2 add_and_split.15
  49.4 0.1 collective-permute-start.12
  49.4 1.7 %collective-permute-done.7.refs_0_ = bf16[1040,128]{1,0:T(8,128)(2,1)S(1)} collective-permute-done((bf16[1040,128]{1,0:T(8,128)(2,1)S(1)}, bf16[1040,128]{1,0:T(8,128)(2,1)S(1)}, u32[]{:S(2)}, u32[]{:S(2)}) %collective-permute-start.7) | collective-permute-done | bytes 266272 | tf_op jit(solution)/shard_map/ppermute | solution.py:396
  51.2 0.3 add_and_split.16
  51.4 1.4 %collective-permute-start.11 = (bf16[528,128]{1,0:T(8,128)(2,1)S(1)}, bf16[528,128]{1,0:T(8,128)(2,1)S(1)}, u32[]{:S(2)}, u32[]{:S(2)}) collective-permute-start(bf16[528,128]{1,0:T(8,128)(2,1)S(1)} %get-tuple-element.79), channel_id=1, source_target_pairs={{0,8},{1,9},{2,10},{3,11},{4,12},{5,13},{6,14},{7,15},{8,0},{9,1},... | collective-permute-start | bytes 405512 | tf_op jit(solution)/shard_map/ppermute | solution.py:396
  52.8 1.1 %collective-permute-done.6.refs_0_ = bf16[1040,128]{1,0:T(8,128)(2,1)S(1)} collective-permute-done((bf16[1040,128]{1,0:T(8,128)(2,1)S(1)}, bf16[1040,128]{1,0:T(8,128)(2,1)S(1)}, u32[]{:S(2)}, u32[]{:S(2)}) %collective-permute-start.6) | collective-permute-done | bytes 266272 | tf_op jit(solution)/shard_map/ppermute | solution.py:396
  53.9 0.3 add_and_split.17
  54.2 0.6 collective-permute-start.15
  54.7 0.0 collective-permute-done.5.refs_0_
  54.8 0.1 add_last.5
  54.9 0.0 collective-permute-done.13.refs_0_
  54.9 0.1 add_and_split.18
  55.0 3.9 %collective-permute-start.17 = (bf16[272,128]{1,0:T(8,128)(2,1)S(1)}, bf16[272,128]{1,0:T(8,128)(2,1)S(1)}, u32[]{:S(2)}, u32[]{:S(2)}) collective-permute-start(bf16[272,128]{1,0:T(8,128)(2,1)S(1)} %get-tuple-element.89), channel_id=1, source_target_pairs={{0,8},{1,9},{2,10},{3,11},{4,12},{5,13},{6,14},{7,15},{8,0},{9,1},... | collective-permute-start | bytes 208904 | tf_op jit(solution)/shard_map/ppermute | solution.py:396
  58.9 0.0 collective-permute-done.12.refs_0_
  58.9 0.1 add_and_split.19
  59.1 0.3 collective-permute-start.19
  59.3 1.4 %collective-permute-done.11.refs_0_ = bf16[528,128]{1,0:T(8,128)(2,1)S(1)} collective-permute-done((bf16[528,128]{1,0:T(8,128)(2,1)S(1)}, bf16[528,128]{1,0:T(8,128)(2,1)S(1)}, u32[]{:S(2)}, u32[]{:S(2)}) %collective-permute-start.11) | collective-permute-done | bytes 135200 | tf_op jit(solution)/shard_map/ppermute | solution.py:396
  60.7 0.1 add_last.6
  60.8 1.8 %collective-permute-done.15.refs_0_ = bf16[528,128]{1,0:T(8,128)(2,1)S(1)} collective-permute-done((bf16[528,128]{1,0:T(8,128)(2,1)S(1)}, bf16[528,128]{1,0:T(8,128)(2,1)S(1)}, u32[]{:S(2)}, u32[]{:S(2)}) %collective-permute-start.15) | collective-permute-done | bytes 135200 | tf_op jit(solution)/shard_map/ppermute | solution.py:396
  62.6 0.1 add_last.7
  62.7 0.1 collective-permute-start.16
  62.8 0.5 collective-permute-start.14
  63.3 0.1 collective-permute-start.10
  63.4 0.1 add_last.8
  63.4 2.4 %collective-permute-done.19.refs_0_ = bf16[272,128]{1,0:T(8,128)(2,1)S(1)} collective-permute-done((bf16[272,128]{1,0:T(8,128)(2,1)S(1)}, bf16[272,128]{1,0:T(8,128)(2,1)S(1)}, u32[]{:S(2)}, u32[]{:S(2)}) %collective-permute-start.19) | collective-permute-done | bytes 69664 | tf_op jit(solution)/shard_map/ppermute | solution.py:396
  65.8 0.1 add_last.9
  65.9 0.1 collective-permute-start.20
  66.0 0.5 collective-permute-start.18
  66.5 0.0 collective-permute-done.16.refs_5_
  66.5 0.0 collective-permute-done.14.refs_3_
  66.5 0.0 collective-permute-done.10.refs_1_
  66.5 0.7 %collective-permute-done.20.refs_9_ = bf16[32,512]{1,0:T(8,128)(2,1)S(1)} collective-permute-done((bf16[32,512]{1,0:T(8,128)(2,1)S(1)}, bf16[32,512]{1,0:T(8,128)(2,1)S(1)}, u32[]{:S(2)}, u32[]{:S(2)}) %collective-permute-start.20) | collective-permute-done | bytes 32800 | tf_op jit(solution)/shard_map/ppermute | solution.py:396
  67.2 0.2 collective-permute-done.18.refs_7_
  67.3 0.8 %lay_out.1 = bf16[32,8192]{1,0:T(8,128)(2,1)} custom-call(bf16[32,1024]{1,0:T(8,128)(2,1)S(1)} %get-tuple-element.77.refs_2_.refs_0_, bf16[32,1024]{1,0:T(8,128)(2,1)S(1)} %collective-permute-done.10.refs_1_, bf16[32,1024]{1,0:T(8,128)(2,1)S(1)} %get-tuple-element.84.refs_2_, bf16[32,1024]{1,0:T(8,128)(2,1)S(1)} %collective-permute-done.14.refs_3_, ...), custom_call_target="tpu_custom_call" | custom-call | flops 1 | bytes 1 | tf_op jit(solution)/shard_map/lay_out/pallas_call | solution.py:105
  (1 shorter events, 0.0 us)
Async XLA Ops:
  2.9 5.7 %collective-permute-start = (bf16[1024,1024]{1,0:T(8,128)(2,1)S(1)}, bf16[1024,1024]{1,0:T(8,128)(2,1)S(1)}, u32[]{:S(2)}, u32[]{:S(2)}) collective-permute-start(bf16[1024,1024]{1,0:T(8,128)(2,1)S(1)} %get-tuple-element.50.refs_0_), channel_id=1, source_target_pairs={{0,1},{1,0},{2,3},{3,2},{4,5},{5,4},{6,7},{7,6},{8,9},{9,8},{10,11... | collective-permute-start | bytes 6291464 | tf_op jit(solution)/shard_map/ppermute | solution.py:396
  11.2 15.5 %collective-permute-start.1 = (bf16[2064,128]{1,0:T(8,128)(2,1)S(1)}, bf16[2064,128]{1,0:T(8,128)(2,1)S(1)}, u32[]{:S(2)}, u32[]{:S(2)}) collective-permute-start(bf16[2064,128]{1,0:T(8,128)(2,1)S(1)} %get-tuple-element.55), channel_id=1, source_target_pairs={{0,2},{1,3},{2,0},{3,1},{4,6},{5,7},{6,4},{7,5},{8,10},{9,11},{10,... | collective-permute-start | bytes 1585160 | tf_op jit(solution)/shard_map/ppermute | solution.py:396
  16.5 22.0 %collective-permute-start.4 = (bf16[2064,128]{1,0:T(8,128)(2,1)S(1)}, bf16[2064,128]{1,0:T(8,128)(2,1)S(1)}, u32[]{:S(2)}, u32[]{:S(2)}) collective-permute-start(bf16[2064,128]{1,0:T(8,128)(2,1)S(1)} %get-tuple-element.62), channel_id=1, source_target_pairs={{0,4},{1,5},{2,6},{3,7},{4,0},{5,1},{6,2},{7,3},{8,12},{9,13},{10,... | collective-permute-start | bytes 1585160 | tf_op jit(solution)/shard_map/ppermute | solution.py:396
  23.0 16.6 %collective-permute-start.3 = (bf16[2064,128]{1,0:T(8,128)(2,1)S(1)}, bf16[2064,128]{1,0:T(8,128)(2,1)S(1)}, u32[]{:S(2)}, u32[]{:S(2)}) collective-permute-start(bf16[2064,128]{1,0:T(8,128)(2,1)S(1)} %get-tuple-element.61), channel_id=1, source_target_pairs={{0,2},{1,3},{2,0},{3,1},{4,6},{5,7},{6,4},{7,5},{8,10},{9,11},{10,... | collective-permute-start | bytes 1585160 | tf_op jit(solution)/shard_map/ppermute | solution.py:396
  27.2 14.9 %collective-permute-start.2 = (bf16[1040,128]{1,0:T(8,128)(2,1)S(1)}, bf16[1040,128]{1,0:T(8,128)(2,1)S(1)}, u32[]{:S(2)}, u32[]{:S(2)}) collective-permute-start(bf16[1040,128]{1,0:T(8,128)(2,1)S(1)} %get-tuple-element.59), channel_id=1, source_target_pairs={{0,8},{1,9},{2,10},{3,11},{4,12},{5,13},{6,14},{7,15},{8,0},{9,1},... | collective-permute-start | bytes 798728 | tf_op jit(solution)/shard_map/ppermute | solution.py:396
  32.8 14.4 %collective-permute-start.9 = (bf16[1040,128]{1,0:T(8,128)(2,1)S(1)}, bf16[1040,128]{1,0:T(8,128)(2,1)S(1)}, u32[]{:S(2)}, u32[]{:S(2)}) collective-permute-start(bf16[1040,128]{1,0:T(8,128)(2,1)S(1)} %get-tuple-element.72), channel_id=1, source_target_pairs={{0,4},{1,5},{2,6},{3,7},{4,0},{5,1},{6,2},{7,3},{8,12},{9,13},{10,... | collective-permute-start | bytes 798728 | tf_op jit(solution)/shard_map/ppermute | solution.py:396
  36.9 12.2 %collective-permute-start.8 = (bf16[1040,128]{1,0:T(8,128)(2,1)S(1)}, bf16[1040,128]{1,0:T(8,128)(2,1)S(1)}, u32[]{:S(2)}, u32[]{:S(2)}) collective-permute-start(bf16[1040,128]{1,0:T(8,128)(2,1)S(1)} %get-tuple-element.71), channel_id=1, source_target_pairs={{0,2},{1,3},{2,0},{3,1},{4,6},{5,7},{6,4},{7,5},{8,10},{9,11},{10,... | collective-permute-start | bytes 798728 | tf_op jit(solution)/shard_map/ppermute | solution.py:396
  39.0 12.2 %collective-permute-start.7 = (bf16[1040,128]{1,0:T(8,128)(2,1)S(1)}, bf16[1040,128]{1,0:T(8,128)(2,1)S(1)}, u32[]{:S(2)}, u32[]{:S(2)}) collective-permute-start(bf16[1040,128]{1,0:T(8,128)(2,1)S(1)} %get-tuple-element.70), channel_id=1, source_target_pairs={{0,2},{1,3},{2,0},{3,1},{4,6},{5,7},{6,4},{7,5},{8,10},{9,11},{10,... | collective-permute-start | bytes 798728 | tf_op jit(solution)/shard_map/ppermute | solution.py:396
  40.1 13.8 %collective-permute-start.6 = (bf16[1040,128]{1,0:T(8,128)(2,1)S(1)}, bf16[1040,128]{1,0:T(8,128)(2,1)S(1)}, u32[]{:S(2)}, u32[]{:S(2)}) collective-permute-start(bf16[1040,128]{1,0:T(8,128)(2,1)S(1)} %get-tuple-element.69), channel_id=1, source_target_pairs={{0,8},{1,9},{2,10},{3,11},{4,12},{5,13},{6,14},{7,15},{8,0},{9,1},... | collective-permute-start | bytes 798728 | tf_op jit(solution)/shard_map/ppermute | solution.py:396
  42.4 12.4 %collective-permute-start.5 = (bf16[528,128]{1,0:T(8,128)(2,1)S(1)}, bf16[528,128]{1,0:T(8,128)(2,1)S(1)}, u32[]{:S(2)}, u32[]{:S(2)}) collective-permute-start(bf16[528,128]{1,0:T(8,128)(2,1)S(1)} %get-tuple-element.67), channel_id=1, source_target_pairs={{0,4},{1,5},{2,6},{3,7},{4,0},{5,1},{6,2},{7,3},{8,12},{9,13},{10,... | collective-permute-start | bytes 405512 | tf_op jit(solution)/shard_map/ppermute | solution.py:396
  47.4 7.5 %collective-permute-start.13 = (bf16[528,128]{1,0:T(8,128)(2,1)S(1)}, bf16[528,128]{1,0:T(8,128)(2,1)S(1)}, u32[]{:S(2)}, u32[]{:S(2)}) collective-permute-start(bf16[528,128]{1,0:T(8,128)(2,1)S(1)} %get-tuple-element.81), channel_id=1, source_target_pairs={{0,2},{1,3},{2,0},{3,1},{4,6},{5,7},{6,4},{7,5},{8,10},{9,11},{10,... | collective-permute-start | bytes 405512 | tf_op jit(solution)/shard_map/ppermute | solution.py:396
  49.4 9.6 %collective-permute-start.12 = (bf16[528,128]{1,0:T(8,128)(2,1)S(1)}, bf16[528,128]{1,0:T(8,128)(2,1)S(1)}, u32[]{:S(2)}, u32[]{:S(2)}) collective-permute-start(bf16[528,128]{1,0:T(8,128)(2,1)S(1)} %get-tuple-element.80), channel_id=1, source_target_pairs={{0,4},{1,5},{2,6},{3,7},{4,0},{5,1},{6,2},{7,3},{8,12},{9,13},{10,... | collective-permute-start | bytes 405512 | tf_op jit(solution)/shard_map/ppermute | solution.py:396
  51.4 9.3 %collective-permute-start.11 = (bf16[528,128]{1,0:T(8,128)(2,1)S(1)}, bf16[528,128]{1,0:T(8,128)(2,1)S(1)}, u32[]{:S(2)}, u32[]{:S(2)}) collective-permute-start(bf16[528,128]{1,0:T(8,128)(2,1)S(1)} %get-tuple-element.79), channel_id=1, source_target_pairs={{0,8},{1,9},{2,10},{3,11},{4,12},{5,13},{6,14},{7,15},{8,0},{9,1},... | collective-permute-start | bytes 405512 | tf_op jit(solution)/shard_map/ppermute | solution.py:396
  54.2 8.5 %collective-permute-start.15 = (bf16[528,128]{1,0:T(8,128)(2,1)S(1)}, bf16[528,128]{1,0:T(8,128)(2,1)S(1)}, u32[]{:S(2)}, u32[]{:S(2)}) collective-permute-start(bf16[528,128]{1,0:T(8,128)(2,1)S(1)} %get-tuple-element.86), channel_id=1, source_target_pairs={{0,4},{1,5},{2,6},{3,7},{4,0},{5,1},{6,2},{7,3},{8,12},{9,13},{10,... | collective-permute-start | bytes 405512 | tf_op jit(solution)/shard_map/ppermute | solution.py:396
  55.0 8.4 %collective-permute-start.17 = (bf16[272,128]{1,0:T(8,128)(2,1)S(1)}, bf16[272,128]{1,0:T(8,128)(2,1)S(1)}, u32[]{:S(2)}, u32[]{:S(2)}) collective-permute-start(bf16[272,128]{1,0:T(8,128)(2,1)S(1)} %get-tuple-element.89), channel_id=1, source_target_pairs={{0,8},{1,9},{2,10},{3,11},{4,12},{5,13},{6,14},{7,15},{8,0},{9,1},... | collective-permute-start | bytes 208904 | tf_op jit(solution)/shard_map/ppermute | solution.py:396
  59.1 6.8 %collective-permute-start.19 = (bf16[272,128]{1,0:T(8,128)(2,1)S(1)}, bf16[272,128]{1,0:T(8,128)(2,1)S(1)}, u32[]{:S(2)}, u32[]{:S(2)}) collective-permute-start(bf16[272,128]{1,0:T(8,128)(2,1)S(1)} %get-tuple-element.92), channel_id=1, source_target_pairs={{0,8},{1,9},{2,10},{3,11},{4,12},{5,13},{6,14},{7,15},{8,0},{9,1},... | collective-permute-start | bytes 208904 | tf_op jit(solution)/shard_map/ppermute | solution.py:396
  62.7 3.7 %collective-permute-start.16 = (bf16[32,1024]{1,0:T(8,128)(2,1)S(1)}, bf16[32,1024]{1,0:T(8,128)(2,1)S(1)}, u32[]{:S(2)}, u32[]{:S(2)}) collective-permute-start(bf16[32,1024]{1,0:T(8,128)(2,1)S(1)} %get-tuple-element.88), channel_id=1, source_target_pairs={{0,1},{1,0},{2,3},{3,2},{4,5},{5,4},{6,7},{7,6},{8,9},{9,8},{10,11... | collective-permute-start | bytes 196616 | tf_op jit(solution)/shard_map/ppermute | solution.py:396
  62.8 3.7 %collective-permute-start.14 = (bf16[32,1024]{1,0:T(8,128)(2,1)S(1)}, bf16[32,1024]{1,0:T(8,128)(2,1)S(1)}, u32[]{:S(2)}, u32[]{:S(2)}) collective-permute-start(bf16[32,1024]{1,0:T(8,128)(2,1)S(1)} %get-tuple-element.85), channel_id=1, source_target_pairs={{0,1},{1,0},{2,3},{3,2},{4,5},{5,4},{6,7},{7,6},{8,9},{9,8},{10,11... | collective-permute-start | bytes 196616 | tf_op jit(solution)/shard_map/ppermute | solution.py:396
  63.3 3.2 %collective-permute-start.10 = (bf16[32,1024]{1,0:T(8,128)(2,1)S(1)}, bf16[32,1024]{1,0:T(8,128)(2,1)S(1)}, u32[]{:S(2)}, u32[]{:S(2)}) collective-permute-start(bf16[32,1024]{1,0:T(8,128)(2,1)S(1)} %get-tuple-element.78), channel_id=1, source_target_pairs={{0,1},{1,0},{2,3},{3,2},{4,5},{5,4},{6,7},{7,6},{8,9},{9,8},{10,11... | collective-permute-start | bytes 196616 | tf_op jit(solution)/shard_map/ppermute | solution.py:396
  65.9 1.3 %collective-permute-start.20 = (bf16[32,512]{1,0:T(8,128)(2,1)S(1)}, bf16[32,512]{1,0:T(8,128)(2,1)S(1)}, u32[]{:S(2)}, u32[]{:S(2)}) collective-permute-start(bf16[32,512]{1,0:T(8,128)(2,1)S(1)} %get-tuple-element.94), channel_id=1, source_target_pairs={{0,1},{1,0},{2,3},{3,2},{4,5},{5,4},{6,7},{7,6},{8,9},{9,8},{10,11... | collective-permute-start | bytes 98312 | tf_op jit(solution)/shard_map/ppermute | solution.py:396
  66.0 1.4 %collective-permute-start.18 = (bf16[32,512]{1,0:T(8,128)(2,1)S(1)}, bf16[32,512]{1,0:T(8,128)(2,1)S(1)}, u32[]{:S(2)}, u32[]{:S(2)}) collective-permute-start(bf16[32,512]{1,0:T(8,128)(2,1)S(1)} %get-tuple-element.91), channel_id=1, source_target_pairs={{0,1},{1,0},{2,3},{3,2},{4,5},{5,4},{6,7},{7,6},{8,9},{9,8},{10,11... | collective-permute-start | bytes 98312 | tf_op jit(solution)/shard_map/ppermute | solution.py:396

commit v13 on v11

--- a/solution.py
+++ b/solution.py
@@ -363,28 +363,37 @@
 
 
 def lay_kernel(pieces, width, *refs):
-    out_ref = refs[-1]
+    *parts, out_ref, sems = refs
+    copies = []
     at = 0
-    for first in range(0, len(refs) - 1, pieces):
+    for first in range(0, len(parts), pieces):
         for distance in range(pieces):
-            part = refs[first + distance]
+            part = parts[first + distance]
             owner = jnp.bitwise_xor(position(pieces)[0], distance)
             columns = pl.ds(pl.multiple_of(owner * width + at, LANES), part.shape[1])
-            out_ref[:, columns] = part[...]
+            copies.append(
+                pltpu.make_async_copy(part, out_ref.at[:, columns], sems.at[len(copies)])
+            )
         at += part.shape[1]
+    for copy in copies:
+        copy.start()
+    for copy in copies:
+        copy.wait()
 
 
 def lay(parts, pieces, width):
     flat = [part for chunk in parts for part in chunk]
     rows = flat[0].shape[0]
-    return call(
+    return pl.pallas_call(
         functools.partial(lay_kernel, pieces, width),
-        "lay_out",
-        [*flat],
-        [jax.ShapeDtypeStruct((rows, pieces * width), jnp.bfloat16)],
-        [],
-        cost=(0, 4 * rows * pieces * width, 0),
-    )[0]
+        in_specs=[pl.BlockSpec(memory_space=pltpu.VMEM)] * len(flat),
+        out_specs=pl.BlockSpec(memory_space=pltpu.HBM),
+        out_shape=jax.ShapeDtypeStruct((rows, pieces * width), jnp.bfloat16),
+        scratch_shapes=[pltpu.SemaphoreType.DMA((len(flat),))],
+        compiler_params=pltpu.CompilerParams(vmem_limit_bytes=4 * MIB),
+        cost_estimate=pl.CostEstimate(flops=1, bytes_accessed=1, transcendentals=0),
+        name="lay_out",
+    )(*flat)
 
 
 def swapped(block, apart):

time: 68.3 us -> 68.5 us (level)
    pallas_call x0 -> x1, Pallas kernels: none -> 0.86 us  [lay(): pl.pallas_call(functools.partial(lay_kernel, pieces, width), in_specs=[pl...]
    pallas_call x23 -> x22, Pallas kernels: 27.4 us -> 26.5 us  [call(): pl.pallas_call(run, in_specs=[vmem] * (count - far) + [pl.BlockSpec(memor...]
where the time goes in v13:
time: 68.5 us; the launch traced here: 68.3 us
  Pallas kernels  27.4 us (40%)
  starting transfers between devices  24.2 us (35%)
  waiting for transfers between devices  16.5 us (24%)
    pallas_call x22, Pallas kernels, call(): pl.pallas_call(run, in_specs=[vmem] * (count - far) + [pl.BlockSpec(memor...  26.5 us
    ppermute x21, starting transfers between devices, swapped(): return lax.ppermute(block, 'row', [(i, i ^ apart) for i in range(count)])  24.2 us
    ppermute x21, waiting for transfers between devices, swapped(): return lax.ppermute(block, 'row', [(i, i ^ apart) for i in range(count)])  16.5 us
  transfers between devices with their start and end apart: 21, of which 10 were waited for; matrix products, arithmetic and copies ran while one was open for 0% of the time, Pallas kernels for 31%

profile of v13, /device:TPU:0, one launch (start us, length us, event | category | flops | bytes accessed | tf_op | source)
XLA Modules:
  0.0 68.3 jit_solution(13074157284065138931)
XLA Ops:
  0.0 2.9 %split_basis.1 = (bf16[1024,1024]{1,0:T(8,128)(2,1)S(1)}, bf16[1024,2048]{1,0:T(8,128)(2,1)S(1)}) custom-call(f32[1024,512]{1,0:T(8,128)} %refs_0_.1, bf16[1,2048,4096]{2,1,0:T(8,128)(2,1)} %refs_2_.1), custom_call_target="tpu_custom_call" | custom-call | flops 1 | bytes 1 | tf_op jit(solution)/shard_map/split_basis/pallas_call | solution.py:105
  2.9 0.5 collective-permute-start
  3.4 5.1 %early_products.1 = (bf16[1024,2048]{1,0:T(8,128)(2,1)S(1)}, bf16[1024,4096]{1,0:T(8,128)(2,1)S(1)}, f32[512,2048]{1,0:T(8,128)S(1)}) custom-call(bf16[1024,1024]{1,0:T(8,128)(2,1)S(1)} %get-tuple-element.50.refs_0_, bf16[1024,2048]{1,0:T(8,128)(2,1)S(1)} %get-tuple-element.51.refs_1_, bf16[1,2048,4096]{2,1,0:T(8,128)(2,1)} %refs_2_.1), custom_call_target="tpu_custom_call" | custom-call | flops 1 | bytes 1 | tf_op jit(solution)/shard_map/early_products/pallas_call | solution.py:105
  8.6 0.0 collective-permute-done.refs_1_
  8.6 2.7 %product.5 = (bf16[2064,128]{1,0:T(8,128)(2,1)S(1)}, f32[2048,128]{1,0:T(8,128)S(1)}) custom-call(bf16[1024,1024]{1,0:T(8,128)(2,1)S(1)} %get-tuple-element.50.refs_0_, bf16[1024,1024]{1,0:T(8,128)(2,1)S(1)} %collective-permute-done.refs_1_, bf16[1024,2048]{1,0:T(8,128)(2,1)S(1)} %get-tuple-element.52.refs_2_, ...), custom_call_target="tpu_custom_call" | custom-call | flops 1 | bytes 1 | tf_op jit(solution)/shard_map/product/pallas_call | solution.py:105
  11.2 2.6 %collective-permute-start.1 = (bf16[2064,128]{1,0:T(8,128)(2,1)S(1)}, bf16[2064,128]{1,0:T(8,128)(2,1)S(1)}, u32[]{:S(2)}, u32[]{:S(2)}) collective-permute-start(bf16[2064,128]{1,0:T(8,128)(2,1)S(1)} %get-tuple-element.55), channel_id=1, source_target_pairs={{0,2},{1,3},{2,0},{3,1},{4,6},{5,7},{6,4},{7,5},{8,10},{9,11},{10,... | collective-permute-start | bytes 1585160 | tf_op jit(solution)/shard_map/ppermute | solution.py:401
  13.9 2.7 %product.6 = (bf16[2064,128]{1,0:T(8,128)(2,1)S(1)}, f32[2048,128]{1,0:T(8,128)S(1)}) custom-call(bf16[1024,1024]{1,0:T(8,128)(2,1)S(1)} %get-tuple-element.50.refs_0_, bf16[1024,1024]{1,0:T(8,128)(2,1)S(1)} %collective-permute-done.refs_1_, bf16[1024,2048]{1,0:T(8,128)(2,1)S(1)} %get-tuple-element.52.refs_2_, ...), custom_call_target="tpu_custom_call" | custom-call | flops 1 | bytes 1 | tf_op jit(solution)/shard_map/product/pallas_call | solution.py:105
  16.5 1.6 %collective-permute-start.4 = (bf16[2064,128]{1,0:T(8,128)(2,1)S(1)}, bf16[2064,128]{1,0:T(8,128)(2,1)S(1)}, u32[]{:S(2)}, u32[]{:S(2)}) collective-permute-start(bf16[2064,128]{1,0:T(8,128)(2,1)S(1)} %get-tuple-element.62), channel_id=1, source_target_pairs={{0,4},{1,5},{2,6},{3,7},{4,0},{5,1},{6,2},{7,3},{8,12},{9,13},{10,... | collective-permute-start | bytes 1585160 | tf_op jit(solution)/shard_map/ppermute | solution.py:401
  18.2 4.8 %product.7 = (bf16[2064,128]{1,0:T(8,128)(2,1)S(1)}, f32[2048,128]{1,0:T(8,128)S(1)}) custom-call(bf16[1024,1024]{1,0:T(8,128)(2,1)S(1)} %get-tuple-element.50.refs_0_, bf16[1024,1024]{1,0:T(8,128)(2,1)S(1)} %collective-permute-done.refs_1_, bf16[1024,2048]{1,0:T(8,128)(2,1)S(1)} %get-tuple-element.52.refs_2_, ...), custom_call_target="tpu_custom_call" | custom-call | flops 1 | bytes 1 | tf_op jit(solution)/shard_map/product/pallas_call | solution.py:105
  23.0 0.6 collective-permute-start.3
  23.6 3.1 %collective-permute-done.1.refs_0_ = bf16[2064,128]{1,0:T(8,128)(2,1)S(1)} collective-permute-done((bf16[2064,128]{1,0:T(8,128)(2,1)S(1)}, bf16[2064,128]{1,0:T(8,128)(2,1)S(1)}, u32[]{:S(2)}, u32[]{:S(2)}) %collective-permute-start.1) | collective-permute-done | bytes 528416 | tf_op jit(solution)/shard_map/ppermute | solution.py:401
  26.7 0.5 add_and_split.10
  27.2 3.1 %collective-permute-start.2 = (bf16[1040,128]{1,0:T(8,128)(2,1)S(1)}, bf16[1040,128]{1,0:T(8,128)(2,1)S(1)}, u32[]{:S(2)}, u32[]{:S(2)}) collective-permute-start(bf16[1040,128]{1,0:T(8,128)(2,1)S(1)} %get-tuple-element.59), channel_id=1, source_target_pairs={{0,8},{1,9},{2,10},{3,11},{4,12},{5,13},{6,14},{7,15},{8,0},{9,1},... | collective-permute-start | bytes 798728 | tf_op jit(solution)/shard_map/ppermute | solution.py:401
  30.3 2.5 %product.8 = (bf16[1040,128]{1,0:T(8,128)(2,1)S(1)}, f32[1024,128]{1,0:T(8,128)S(1)}) custom-call(bf16[1024,1024]{1,0:T(8,128)(2,1)S(1)} %get-tuple-element.50.refs_0_, bf16[1024,1024]{1,0:T(8,128)(2,1)S(1)} %collective-permute-done.refs_1_, bf16[1024,2048]{1,0:T(8,128)(2,1)S(1)} %get-tuple-element.52.refs_2_, ...), custom_call_target="tpu_custom_call" | custom-call | flops 1 | bytes 1 | tf_op jit(solution)/shard_map/product/pallas_call | solution.py:105
  32.8 1.6 %collective-permute-start.9 = (bf16[1040,128]{1,0:T(8,128)(2,1)S(1)}, bf16[1040,128]{1,0:T(8,128)(2,1)S(1)}, u32[]{:S(2)}, u32[]{:S(2)}) collective-permute-start(bf16[1040,128]{1,0:T(8,128)(2,1)S(1)} %get-tuple-element.72), channel_id=1, source_target_pairs={{0,4},{1,5},{2,6},{3,7},{4,0},{5,1},{6,2},{7,3},{8,12},{9,13},{10,... | collective-permute-start | bytes 798728 | tf_op jit(solution)/shard_map/ppermute | solution.py:401
  34.4 2.5 %product.9 = (bf16[1040,128]{1,0:T(8,128)(2,1)S(1)}, f32[1024,128]{1,0:T(8,128)S(1)}) custom-call(bf16[1024,1024]{1,0:T(8,128)(2,1)S(1)} %get-tuple-element.50.refs_0_, bf16[1024,1024]{1,0:T(8,128)(2,1)S(1)} %collective-permute-done.refs_1_, bf16[1024,2048]{1,0:T(8,128)(2,1)S(1)} %get-tuple-element.52.refs_2_, ...), custom_call_target="tpu_custom_call" | custom-call | flops 1 | bytes 1 | tf_op jit(solution)/shard_map/product/pallas_call | solution.py:105
  36.9 1.6 %collective-permute-start.8 = (bf16[1040,128]{1,0:T(8,128)(2,1)S(1)}, bf16[1040,128]{1,0:T(8,128)(2,1)S(1)}, u32[]{:S(2)}, u32[]{:S(2)}) collective-permute-start(bf16[1040,128]{1,0:T(8,128)(2,1)S(1)} %get-tuple-element.71), channel_id=1, source_target_pairs={{0,2},{1,3},{2,0},{3,1},{4,6},{5,7},{6,4},{7,5},{8,10},{9,11},{10,... | collective-permute-start | bytes 798728 | tf_op jit(solution)/shard_map/ppermute | solution.py:401
  38.5 0.0 collective-permute-done.4.refs_0_
  38.5 0.5 add_and_split.11
  39.0 0.6 collective-permute-start.7
  39.6 0.0 collective-permute-done.3.refs_0_
  39.6 0.5 add_and_split.12
  40.1 1.5 %collective-permute-start.6 = (bf16[1040,128]{1,0:T(8,128)(2,1)S(1)}, bf16[1040,128]{1,0:T(8,128)(2,1)S(1)}, u32[]{:S(2)}, u32[]{:S(2)}) collective-permute-start(bf16[1040,128]{1,0:T(8,128)(2,1)S(1)} %get-tuple-element.69), channel_id=1, source_target_pairs={{0,8},{1,9},{2,10},{3,11},{4,12},{5,13},{6,14},{7,15},{8,0},{9,1},... | collective-permute-start | bytes 798728 | tf_op jit(solution)/shard_map/ppermute | solution.py:401
  41.6 0.5 collective-permute-done.2.refs_0_
  42.1 0.3 add_and_split.13
  42.4 1.1 %collective-permute-start.5 = (bf16[528,128]{1,0:T(8,128)(2,1)S(1)}, bf16[528,128]{1,0:T(8,128)(2,1)S(1)}, u32[]{:S(2)}, u32[]{:S(2)}) collective-permute-start(bf16[528,128]{1,0:T(8,128)(2,1)S(1)} %get-tuple-element.67), channel_id=1, source_target_pairs={{0,4},{1,5},{2,6},{3,7},{4,0},{5,1},{6,2},{7,3},{8,12},{9,13},{10,... | collective-permute-start | bytes 405512 | tf_op jit(solution)/shard_map/ppermute | solution.py:401
  43.5 3.6 %collective-permute-done.9.refs_0_ = bf16[1040,128]{1,0:T(8,128)(2,1)S(1)} collective-permute-done((bf16[1040,128]{1,0:T(8,128)(2,1)S(1)}, bf16[1040,128]{1,0:T(8,128)(2,1)S(1)}, u32[]{:S(2)}, u32[]{:S(2)}) %collective-permute-start.9) | collective-permute-done | bytes 266272 | tf_op jit(solution)/shard_map/ppermute | solution.py:401
  47.1 0.2 add_and_split.14
  47.4 1.7 %collective-permute-start.13 = (bf16[528,128]{1,0:T(8,128)(2,1)S(1)}, bf16[528,128]{1,0:T(8,128)(2,1)S(1)}, u32[]{:S(2)}, u32[]{:S(2)}) collective-permute-start(bf16[528,128]{1,0:T(8,128)(2,1)S(1)} %get-tuple-element.81), channel_id=1, source_target_pairs={{0,2},{1,3},{2,0},{3,1},{4,6},{5,7},{6,4},{7,5},{8,10},{9,11},{10,... | collective-permute-start | bytes 405512 | tf_op jit(solution)/shard_map/ppermute | solution.py:401
  49.1 0.0 collective-permute-done.8.refs_0_
  49.1 0.2 add_and_split.15
  49.3 0.1 collective-permute-start.12
  49.4 1.7 %collective-permute-done.7.refs_0_ = bf16[1040,128]{1,0:T(8,128)(2,1)S(1)} collective-permute-done((bf16[1040,128]{1,0:T(8,128)(2,1)S(1)}, bf16[1040,128]{1,0:T(8,128)(2,1)S(1)}, u32[]{:S(2)}, u32[]{:S(2)}) %collective-permute-start.7) | collective-permute-done | bytes 266272 | tf_op jit(solution)/shard_map/ppermute | solution.py:401
  51.1 0.3 add_and_split.16
  51.4 1.4 %collective-permute-start.11 = (bf16[528,128]{1,0:T(8,128)(2,1)S(1)}, bf16[528,128]{1,0:T(8,128)(2,1)S(1)}, u32[]{:S(2)}, u32[]{:S(2)}) collective-permute-start(bf16[528,128]{1,0:T(8,128)(2,1)S(1)} %get-tuple-element.79), channel_id=1, source_target_pairs={{0,8},{1,9},{2,10},{3,11},{4,12},{5,13},{6,14},{7,15},{8,0},{9,1},... | collective-permute-start | bytes 405512 | tf_op jit(solution)/shard_map/ppermute | solution.py:401
  52.8 1.1 %collective-permute-done.6.refs_0_ = bf16[1040,128]{1,0:T(8,128)(2,1)S(1)} collective-permute-done((bf16[1040,128]{1,0:T(8,128)(2,1)S(1)}, bf16[1040,128]{1,0:T(8,128)(2,1)S(1)}, u32[]{:S(2)}, u32[]{:S(2)}) %collective-permute-start.6) | collective-permute-done | bytes 266272 | tf_op jit(solution)/shard_map/ppermute | solution.py:401
  53.9 0.3 add_and_split.17
  54.1 0.6 collective-permute-start.15
  54.7 0.0 collective-permute-done.5.refs_0_
  54.7 0.1 add_last.5
  54.8 0.0 collective-permute-done.13.refs_0_
  54.9 0.1 add_and_split.18
  55.0 3.9 %collective-permute-start.17 = (bf16[272,128]{1,0:T(8,128)(2,1)S(1)}, bf16[272,128]{1,0:T(8,128)(2,1)S(1)}, u32[]{:S(2)}, u32[]{:S(2)}) collective-permute-start(bf16[272,128]{1,0:T(8,128)(2,1)S(1)} %get-tuple-element.89), channel_id=1, source_target_pairs={{0,8},{1,9},{2,10},{3,11},{4,12},{5,13},{6,14},{7,15},{8,0},{9,1},... | collective-permute-start | bytes 208904 | tf_op jit(solution)/shard_map/ppermute | solution.py:401
  58.9 0.0 collective-permute-done.12.refs_0_
  58.9 0.1 add_and_split.19
  59.0 0.3 collective-permute-start.19
  59.4 1.3 %collective-permute-done.11.refs_0_ = bf16[528,128]{1,0:T(8,128)(2,1)S(1)} collective-permute-done((bf16[528,128]{1,0:T(8,128)(2,1)S(1)}, bf16[528,128]{1,0:T(8,128)(2,1)S(1)}, u32[]{:S(2)}, u32[]{:S(2)}) %collective-permute-start.11) | collective-permute-done | bytes 135200 | tf_op jit(solution)/shard_map/ppermute | solution.py:401
  60.7 0.1 add_last.6
  60.8 1.8 %collective-permute-done.15.refs_0_ = bf16[528,128]{1,0:T(8,128)(2,1)S(1)} collective-permute-done((bf16[528,128]{1,0:T(8,128)(2,1)S(1)}, bf16[528,128]{1,0:T(8,128)(2,1)S(1)}, u32[]{:S(2)}, u32[]{:S(2)}) %collective-permute-start.15) | collective-permute-done | bytes 135200 | tf_op jit(solution)/shard_map/ppermute | solution.py:401
  62.6 0.1 add_last.7
  62.7 0.1 collective-permute-start.16
  62.8 0.5 collective-permute-start.14
  63.3 0.1 collective-permute-start.10
  63.4 0.1 add_last.8
  63.4 2.4 %collective-permute-done.19.refs_0_ = bf16[272,128]{1,0:T(8,128)(2,1)S(1)} collective-permute-done((bf16[272,128]{1,0:T(8,128)(2,1)S(1)}, bf16[272,128]{1,0:T(8,128)(2,1)S(1)}, u32[]{:S(2)}, u32[]{:S(2)}) %collective-permute-start.19) | collective-permute-done | bytes 69664 | tf_op jit(solution)/shard_map/ppermute | solution.py:401
  65.8 0.1 add_last.9
  65.9 0.1 collective-permute-start.20
  66.0 0.5 collective-permute-start.18
  66.5 0.0 collective-permute-done.16.refs_5_
  66.5 0.0 collective-permute-done.14.refs_3_
  66.5 0.0 collective-permute-done.10.refs_1_
  66.5 0.7 %collective-permute-done.20.refs_9_ = bf16[32,512]{1,0:T(8,128)(2,1)S(1)} collective-permute-done((bf16[32,512]{1,0:T(8,128)(2,1)S(1)}, bf16[32,512]{1,0:T(8,128)(2,1)S(1)}, u32[]{:S(2)}, u32[]{:S(2)}) %collective-permute-start.20) | collective-permute-done | bytes 32800 | tf_op jit(solution)/shard_map/ppermute | solution.py:401
  67.2 0.2 collective-permute-done.18.refs_7_
  67.3 0.9 %lay_out.1 = bf16[32,8192]{1,0:T(8,128)(2,1)} custom-call(bf16[32,1024]{1,0:T(8,128)(2,1)S(1)} %get-tuple-element.77.refs_2_.refs_0_, bf16[32,1024]{1,0:T(8,128)(2,1)S(1)} %collective-permute-done.10.refs_1_, bf16[32,1024]{1,0:T(8,128)(2,1)S(1)} %get-tuple-element.84.refs_2_, bf16[32,1024]{1,0:T(8,128)(2,1)S(1)} %collective-permute-done.14.refs_3_, ...), custom_call_target="tpu_custom_call" | custom-call | flops 1 | bytes 1 | tf_op jit(solution)/shard_map/lay_out/pallas_call | solution.py:387
  (1 shorter events, 0.0 us)
Async XLA Ops:
  2.9 5.7 %collective-permute-start = (bf16[1024,1024]{1,0:T(8,128)(2,1)S(1)}, bf16[1024,1024]{1,0:T(8,128)(2,1)S(1)}, u32[]{:S(2)}, u32[]{:S(2)}) collective-permute-start(bf16[1024,1024]{1,0:T(8,128)(2,1)S(1)} %get-tuple-element.50.refs_0_), channel_id=1, source_target_pairs={{0,1},{1,0},{2,3},{3,2},{4,5},{5,4},{6,7},{7,6},{8,9},{9,8},{10,11... | collective-permute-start | bytes 6291464 | tf_op jit(solution)/shard_map/ppermute | solution.py:401
  11.2 15.5 %collective-permute-start.1 = (bf16[2064,128]{1,0:T(8,128)(2,1)S(1)}, bf16[2064,128]{1,0:T(8,128)(2,1)S(1)}, u32[]{:S(2)}, u32[]{:S(2)}) collective-permute-start(bf16[2064,128]{1,0:T(8,128)(2,1)S(1)} %get-tuple-element.55), channel_id=1, source_target_pairs={{0,2},{1,3},{2,0},{3,1},{4,6},{5,7},{6,4},{7,5},{8,10},{9,11},{10,... | collective-permute-start | bytes 1585160 | tf_op jit(solution)/shard_map/ppermute | solution.py:401
  16.5 22.0 %collective-permute-start.4 = (bf16[2064,128]{1,0:T(8,128)(2,1)S(1)}, bf16[2064,128]{1,0:T(8,128)(2,1)S(1)}, u32[]{:S(2)}, u32[]{:S(2)}) collective-permute-start(bf16[2064,128]{1,0:T(8,128)(2,1)S(1)} %get-tuple-element.62), channel_id=1, source_target_pairs={{0,4},{1,5},{2,6},{3,7},{4,0},{5,1},{6,2},{7,3},{8,12},{9,13},{10,... | collective-permute-start | bytes 1585160 | tf_op jit(solution)/shard_map/ppermute | solution.py:401
  23.0 16.6 %collective-permute-start.3 = (bf16[2064,128]{1,0:T(8,128)(2,1)S(1)}, bf16[2064,128]{1,0:T(8,128)(2,1)S(1)}, u32[]{:S(2)}, u32[]{:S(2)}) collective-permute-start(bf16[2064,128]{1,0:T(8,128)(2,1)S(1)} %get-tuple-element.61), channel_id=1, source_target_pairs={{0,2},{1,3},{2,0},{3,1},{4,6},{5,7},{6,4},{7,5},{8,10},{9,11},{10,... | collective-permute-start | bytes 1585160 | tf_op jit(solution)/shard_map/ppermute | solution.py:401
  27.2 14.9 %collective-permute-start.2 = (bf16[1040,128]{1,0:T(8,128)(2,1)S(1)}, bf16[1040,128]{1,0:T(8,128)(2,1)S(1)}, u32[]{:S(2)}, u32[]{:S(2)}) collective-permute-start(bf16[1040,128]{1,0:T(8,128)(2,1)S(1)} %get-tuple-element.59), channel_id=1, source_target_pairs={{0,8},{1,9},{2,10},{3,11},{4,12},{5,13},{6,14},{7,15},{8,0},{9,1},... | collective-permute-start | bytes 798728 | tf_op jit(solution)/shard_map/ppermute | solution.py:401
  32.8 14.3 %collective-permute-start.9 = (bf16[1040,128]{1,0:T(8,128)(2,1)S(1)}, bf16[1040,128]{1,0:T(8,128)(2,1)S(1)}, u32[]{:S(2)}, u32[]{:S(2)}) collective-permute-start(bf16[1040,128]{1,0:T(8,128)(2,1)S(1)} %get-tuple-element.72), channel_id=1, source_target_pairs={{0,4},{1,5},{2,6},{3,7},{4,0},{5,1},{6,2},{7,3},{8,12},{9,13},{10,... | collective-permute-start | bytes 798728 | tf_op jit(solution)/shard_map/ppermute | solution.py:401
  36.9 12.2 %collective-permute-start.8 = (bf16[1040,128]{1,0:T(8,128)(2,1)S(1)}, bf16[1040,128]{1,0:T(8,128)(2,1)S(1)}, u32[]{:S(2)}, u32[]{:S(2)}) collective-permute-start(bf16[1040,128]{1,0:T(8,128)(2,1)S(1)} %get-tuple-element.71), channel_id=1, source_target_pairs={{0,2},{1,3},{2,0},{3,1},{4,6},{5,7},{6,4},{7,5},{8,10},{9,11},{10,... | collective-permute-start | bytes 798728 | tf_op jit(solution)/shard_map/ppermute | solution.py:401
  39.0 12.1 %collective-permute-start.7 = (bf16[1040,128]{1,0:T(8,128)(2,1)S(1)}, bf16[1040,128]{1,0:T(8,128)(2,1)S(1)}, u32[]{:S(2)}, u32[]{:S(2)}) collective-permute-start(bf16[1040,128]{1,0:T(8,128)(2,1)S(1)} %get-tuple-element.70), channel_id=1, source_target_pairs={{0,2},{1,3},{2,0},{3,1},{4,6},{5,7},{6,4},{7,5},{8,10},{9,11},{10,... | collective-permute-start | bytes 798728 | tf_op jit(solution)/shard_map/ppermute | solution.py:401
  40.1 13.8 %collective-permute-start.6 = (bf16[1040,128]{1,0:T(8,128)(2,1)S(1)}, bf16[1040,128]{1,0:T(8,128)(2,1)S(1)}, u32[]{:S(2)}, u32[]{:S(2)}) collective-permute-start(bf16[1040,128]{1,0:T(8,128)(2,1)S(1)} %get-tuple-element.69), channel_id=1, source_target_pairs={{0,8},{1,9},{2,10},{3,11},{4,12},{5,13},{6,14},{7,15},{8,0},{9,1},... | collective-permute-start | bytes 798728 | tf_op jit(solution)/shard_map/ppermute | solution.py:401
  42.4 12.4 %collective-permute-start.5 = (bf16[528,128]{1,0:T(8,128)(2,1)S(1)}, bf16[528,128]{1,0:T(8,128)(2,1)S(1)}, u32[]{:S(2)}, u32[]{:S(2)}) collective-permute-start(bf16[528,128]{1,0:T(8,128)(2,1)S(1)} %get-tuple-element.67), channel_id=1, source_target_pairs={{0,4},{1,5},{2,6},{3,7},{4,0},{5,1},{6,2},{7,3},{8,12},{9,13},{10,... | collective-permute-start | bytes 405512 | tf_op jit(solution)/shard_map/ppermute | solution.py:401
  47.4 7.5 %collective-permute-start.13 = (bf16[528,128]{1,0:T(8,128)(2,1)S(1)}, bf16[528,128]{1,0:T(8,128)(2,1)S(1)}, u32[]{:S(2)}, u32[]{:S(2)}) collective-permute-start(bf16[528,128]{1,0:T(8,128)(2,1)S(1)} %get-tuple-element.81), channel_id=1, source_target_pairs={{0,2},{1,3},{2,0},{3,1},{4,6},{5,7},{6,4},{7,5},{8,10},{9,11},{10,... | collective-permute-start | bytes 405512 | tf_op jit(solution)/shard_map/ppermute | solution.py:401
  49.3 9.6 %collective-permute-start.12 = (bf16[528,128]{1,0:T(8,128)(2,1)S(1)}, bf16[528,128]{1,0:T(8,128)(2,1)S(1)}, u32[]{:S(2)}, u32[]{:S(2)}) collective-permute-start(bf16[528,128]{1,0:T(8,128)(2,1)S(1)} %get-tuple-element.80), channel_id=1, source_target_pairs={{0,4},{1,5},{2,6},{3,7},{4,0},{5,1},{6,2},{7,3},{8,12},{9,13},{10,... | collective-permute-start | bytes 405512 | tf_op jit(solution)/shard_map/ppermute | solution.py:401
  51.4 9.3 %collective-permute-start.11 = (bf16[528,128]{1,0:T(8,128)(2,1)S(1)}, bf16[528,128]{1,0:T(8,128)(2,1)S(1)}, u32[]{:S(2)}, u32[]{:S(2)}) collective-permute-start(bf16[528,128]{1,0:T(8,128)(2,1)S(1)} %get-tuple-element.79), channel_id=1, source_target_pairs={{0,8},{1,9},{2,10},{3,11},{4,12},{5,13},{6,14},{7,15},{8,0},{9,1},... | collective-permute-start | bytes 405512 | tf_op jit(solution)/shard_map/ppermute | solution.py:401
  54.1 8.5 %collective-permute-start.15 = (bf16[528,128]{1,0:T(8,128)(2,1)S(1)}, bf16[528,128]{1,0:T(8,128)(2,1)S(1)}, u32[]{:S(2)}, u32[]{:S(2)}) collective-permute-start(bf16[528,128]{1,0:T(8,128)(2,1)S(1)} %get-tuple-element.86), channel_id=1, source_target_pairs={{0,4},{1,5},{2,6},{3,7},{4,0},{5,1},{6,2},{7,3},{8,12},{9,13},{10,... | collective-permute-start | bytes 405512 | tf_op jit(solution)/shard_map/ppermute | solution.py:401
  55.0 8.4 %collective-permute-start.17 = (bf16[272,128]{1,0:T(8,128)(2,1)S(1)}, bf16[272,128]{1,0:T(8,128)(2,1)S(1)}, u32[]{:S(2)}, u32[]{:S(2)}) collective-permute-start(bf16[272,128]{1,0:T(8,128)(2,1)S(1)} %get-tuple-element.89), channel_id=1, source_target_pairs={{0,8},{1,9},{2,10},{3,11},{4,12},{5,13},{6,14},{7,15},{8,0},{9,1},... | collective-permute-start | bytes 208904 | tf_op jit(solution)/shard_map/ppermute | solution.py:401
  59.0 6.8 %collective-permute-start.19 = (bf16[272,128]{1,0:T(8,128)(2,1)S(1)}, bf16[272,128]{1,0:T(8,128)(2,1)S(1)}, u32[]{:S(2)}, u32[]{:S(2)}) collective-permute-start(bf16[272,128]{1,0:T(8,128)(2,1)S(1)} %get-tuple-element.92), channel_id=1, source_target_pairs={{0,8},{1,9},{2,10},{3,11},{4,12},{5,13},{6,14},{7,15},{8,0},{9,1},... | collective-permute-start | bytes 208904 | tf_op jit(solution)/shard_map/ppermute | solution.py:401
  62.7 3.7 %collective-permute-start.16 = (bf16[32,1024]{1,0:T(8,128)(2,1)S(1)}, bf16[32,1024]{1,0:T(8,128)(2,1)S(1)}, u32[]{:S(2)}, u32[]{:S(2)}) collective-permute-start(bf16[32,1024]{1,0:T(8,128)(2,1)S(1)} %get-tuple-element.88), channel_id=1, source_target_pairs={{0,1},{1,0},{2,3},{3,2},{4,5},{5,4},{6,7},{7,6},{8,9},{9,8},{10,11... | collective-permute-start | bytes 196616 | tf_op jit(solution)/shard_map/ppermute | solution.py:401
  62.8 3.7 %collective-permute-start.14 = (bf16[32,1024]{1,0:T(8,128)(2,1)S(1)}, bf16[32,1024]{1,0:T(8,128)(2,1)S(1)}, u32[]{:S(2)}, u32[]{:S(2)}) collective-permute-start(bf16[32,1024]{1,0:T(8,128)(2,1)S(1)} %get-tuple-element.85), channel_id=1, source_target_pairs={{0,1},{1,0},{2,3},{3,2},{4,5},{5,4},{6,7},{7,6},{8,9},{9,8},{10,11... | collective-permute-start | bytes 196616 | tf_op jit(solution)/shard_map/ppermute | solution.py:401
  63.3 3.2 %collective-permute-start.10 = (bf16[32,1024]{1,0:T(8,128)(2,1)S(1)}, bf16[32,1024]{1,0:T(8,128)(2,1)S(1)}, u32[]{:S(2)}, u32[]{:S(2)}) collective-permute-start(bf16[32,1024]{1,0:T(8,128)(2,1)S(1)} %get-tuple-element.78), channel_id=1, source_target_pairs={{0,1},{1,0},{2,3},{3,2},{4,5},{5,4},{6,7},{7,6},{8,9},{9,8},{10,11... | collective-permute-start | bytes 196616 | tf_op jit(solution)/shard_map/ppermute | solution.py:401
  65.9 1.3 %collective-permute-start.20 = (bf16[32,512]{1,0:T(8,128)(2,1)S(1)}, bf16[32,512]{1,0:T(8,128)(2,1)S(1)}, u32[]{:S(2)}, u32[]{:S(2)}) collective-permute-start(bf16[32,512]{1,0:T(8,128)(2,1)S(1)} %get-tuple-element.94), channel_id=1, source_target_pairs={{0,1},{1,0},{2,3},{3,2},{4,5},{5,4},{6,7},{7,6},{8,9},{9,8},{10,11... | collective-permute-start | bytes 98312 | tf_op jit(solution)/shard_map/ppermute | solution.py:401
  66.0 1.4 %collective-permute-start.18 = (bf16[32,512]{1,0:T(8,128)(2,1)S(1)}, bf16[32,512]{1,0:T(8,128)(2,1)S(1)}, u32[]{:S(2)}, u32[]{:S(2)}) collective-permute-start(bf16[32,512]{1,0:T(8,128)(2,1)S(1)} %get-tuple-element.91), channel_id=1, source_target_pairs={{0,1},{1,0},{2,3},{3,2},{4,5},{5,4},{6,7},{7,6},{8,9},{9,8},{10,11... | collective-permute-start | bytes 98312 | tf_op jit(solution)/shard_map/ppermute | solution.py:401
